TPU v7x, 32 devices: a whole 2x2x4 slice. The times are simulated.
32 devices in a mesh: group: 2 (over x), fsdp: 16 (over z, y, core).
Axes of the slice: x: 2, y: 2, z: 4, core: 2. Of those that a mesh axis runs over, the one named last changes fastest.
Arguments:
- acts: bfloat16 [4096, 8192], P(('group', 'fsdp')), parts along dimension 0, may hold values from -6 to 6
- cotangent: bfloat16 [4096, 8192], P(('group', 'fsdp')), parts along dimension 0, may hold values from -6 to 6
- down_weight_slots: bfloat16 [16, 16, 8192], P('fsdp'), may hold values from -0.25 to 0.25
- up_weight_slots: bfloat16 [16, 16, 8192], P('fsdp'), may hold values from -0.125 to 0.125
- adapter_per_tile: int32 [32], P(('group', 'fsdp')), parts along dimension 0, may hold values from 0 to 15, each once
- adapter_storage_slot: int32 [16], replicated, may hold values from 0 to 15, each once
Outputs:
- grad_acts: bfloat16 [4096, 8192], P(('group', 'fsdp')), parts along dimension 0
- grad_a: bfloat16 [32, 16, 8192], P(('group', 'fsdp')), parts along dimension 0
- grad_b: bfloat16 [32, 16, 8192], P(('group', 'fsdp')), parts along dimension 0
There are 2 independent parts, one for each index of `group`. A program takes and returns all parts, laid end to end along the dimension named above; an argument that names none is the same for every part. Nothing has to cross between parts.
Inputs may be any that keep to these rules, and one draw needn't show every extreme that they name: `adapter_per_tile`: within each group's 16 entries every adapter appears exactly once. `adapter_storage_slot`: every slot holds exactly one adapter.
All inputs are finite; a program needn't handle non-finite values.
Results may differ from a plain program's by a relative error of at most 0.005.
Values may be sent and summed in bfloat16 or wider, within the bound.
No kernel may reach another device: no remote copies, remote signals or barrier semaphores. Data moves between devices by JAX's collectives and lax.ppermute only.
A program may use at most 64 MiB of HBM per device.

v0:
```python
import jax
import jax.numpy as jnp
from jax import lax
from jax.sharding import PartitionSpec as P

TILE = 128


def shards(
    acts, cotangent, down_weight_slots, up_weight_slots, adapter_per_tile, adapter_storage_slot
):
    n_dev = lax.axis_size("fsdp")
    tok_rows, width = acts.shape
    tile_rows = TILE
    own_tiles = tok_rows // tile_rows
    all_tiles_n = own_tiles * n_dev
    slices = width // n_dev
    adapter_n = adapter_storage_slot.shape[0]
    stacked_factors = jnp.stack([down_weight_slots, up_weight_slots], 1)
    factor_cols = lax.all_to_all(stacked_factors, "fsdp", split_axis=3, concat_axis=0, tiled=True)
    all_tiles = lax.all_gather(adapter_per_tile, "fsdp", axis=0, tiled=True)
    labels = jnp.arange(adapter_n, dtype=jnp.int32)
    tile_slot = jnp.sum(
        jnp.where(all_tiles[:, None] == labels[None, :], adapter_storage_slot[None, :], 0), axis=1
    )
    tile_factors = jnp.take(factor_cols, tile_slot, axis=0)
    x_cols, g_cols = (
        lax.all_to_all(acts, "fsdp", split_axis=1, concat_axis=0, tiled=True),
        lax.all_to_all(cotangent, "fsdp", split_axis=1, concat_axis=0, tiled=True),
    )
    tiles_in = jnp.stack(
        [
            x_cols.reshape(all_tiles_n, tile_rows, slices),
            g_cols.reshape(all_tiles_n, tile_rows, slices),
        ],
        1,
    )
    partial_low = jnp.einsum(
        "tckd,tcrd->tcrk", tiles_in, tile_factors, preferred_element_type=jnp.float32
    )
    shares = lax.psum_scatter(partial_low, "fsdp", scatter_dimension=0, tiled=True).astype(
        jnp.bfloat16
    )
    lowrank = lax.all_gather(shares, "fsdp", axis=0, tiled=True)
    per_tile = jnp.einsum(
        "tcrk,tckd->tcrd", lowrank[:, ::-1], tiles_in, preferred_element_type=jnp.float32
    ).astype(jnp.bfloat16)
    grad_cols = jnp.einsum(
        "trk,trd->tkd", lowrank[:, 1], tile_factors[:, 0], preferred_element_type=jnp.float32
    )
    grad_cols = grad_cols.astype(jnp.bfloat16).reshape(all_tiles_n * tile_rows, slices)
    grad_x = lax.all_to_all(grad_cols, "fsdp", split_axis=0, concat_axis=1, tiled=True)
    one_hot = (labels[:, None] == tile_slot[None, :]).astype(jnp.bfloat16)
    summed = jnp.einsum(
        "et,tcrd->ecrd", one_hot, per_tile, preferred_element_type=jnp.float32
    ).astype(jnp.bfloat16)
    owned = lax.all_to_all(summed, "fsdp", split_axis=0, concat_axis=3, tiled=True)
    return (grad_x, owned[:, 0], owned[:, 1])


def solution(mesh):
    placed = (
        P(("group", "fsdp"), None),
        P(("group", "fsdp"), None),
        P("fsdp", None, None),
        P("fsdp", None, None),
        P(("group", "fsdp")),
        P(),
    )
    return jax.shard_map(
        shards,
        mesh=mesh,
        in_specs=placed,
        out_specs=(
            P(("group", "fsdp"), None),
            P(("group", "fsdp"), None, None),
            P(("group", "fsdp"), None, None),
        ),
        check_vma=False,
    )
```

profile of v0, /device:TPU:13, one launch (start us, length us, event | category | flops | bytes accessed | tf_op | source)
XLA Modules:
  0.0 327.4 jit_solution(13051593661823213677)
XLA Ops:
  8.2 6.7 %copy.58 = bf16[1,2,16,8192]{2,1,0,3:T(2,128)(2,1)} copy(bf16[1,2,16,8192]{3,2,1,0:T(8,128)(2,1)S(1)} %pad_maximum_fusion.5) | data formatting | bytes 1048576 | tf_op jit(solution)/shard_map/stack | solution.py:19
  15.0 6.4 %reshape.54 = bf16[16,2,8192]{2,1,0:T(2,128)(2,1)} reshape(bf16[8192,1,2,16]{3,2,1,0:T(2,128)(2,1)} %bitcast.46) | data formatting | bytes 1048576
  21.4 6.6 %all-to-all-start = ((bf16[16,2,8192]{2,1,0:T(2,128)(2,1)}), bf16[16,2,8192]{2,1,0:T(2,128)(2,1)S(1)}, u32[]{:S(2)}, u32[]{:S(2)}) async-start(bf16[16,2,8192]{2,1,0:T(2,128)(2,1)} %reshape.54), calls=%async_computation | async-start | bytes 1048576 | tf_op jit(solution)/shard_map/all_to_all | solution.py:20
  28.0 3.2 copy.62
  31.2 2.6 copy.63
  33.8 7.8 %all-to-all-done = bf16[16,2,8192]{2,1,0:T(2,128)(2,1)S(1)} async-done(((bf16[16,2,8192]{2,1,0:T(2,128)(2,1)}), bf16[16,2,8192]{2,1,0:T(2,128)(2,1)S(1)}, u32[]{:S(2)}, u32[]{:S(2)}) %all-to-all-start) | async-done | bytes 524320 | tf_op jit(solution)/shard_map/all_to_all | solution.py:20
  41.5 5.2 %all-to-all-start.1 = ((bf16[128,16,512]{2,0,1:T(8,128)(2,1)}), bf16[128,16,512]{2,0,1:T(8,128)(2,1)}, u32[]{:S(2)}, u32[]{:S(2)}) async-start(bf16[128,16,512]{2,0,1:T(8,128)(2,1)} %copy.63), calls=%async_computation.1 | async-start | bytes 4194304 | tf_op jit(solution)/shard_map/all_to_all | solution.py:28
  46.7 3.2 copy.64
  49.9 2.6 copy.65
  52.5 41.7 %all-to-all-done.1 = bf16[128,16,512]{2,0,1:T(8,128)(2,1)} async-done(((bf16[128,16,512]{2,0,1:T(8,128)(2,1)}), bf16[128,16,512]{2,0,1:T(8,128)(2,1)}, u32[]{:S(2)}, u32[]{:S(2)}) %all-to-all-start.1) | async-done | bytes 2097184 | tf_op jit(solution)/shard_map/all_to_all | solution.py:28
  94.2 4.9 %all-to-all-start.2 = ((bf16[128,16,512]{2,0,1:T(8,128)(2,1)}), bf16[128,16,512]{2,0,1:T(8,128)(2,1)S(1)}, u32[]{:S(2)}, u32[]{:S(2)}) async-start(bf16[128,16,512]{2,0,1:T(8,128)(2,1)} %copy.65), calls=%async_computation.2 | async-start | bytes 4194304 | tf_op jit(solution)/shard_map/all_to_all | solution.py:29
  101.2 43.4 %all-reduce = s32[16]{0:T(128)S(1)} all-reduce(s32[16]{0:T(128)S(1)} %dynamic-update-slice), channel_id=1, replica_groups=mesh['group'=2,'fsdp'=16] {'fsdp'}, use_global_device_ids=true, to_apply=%add | all-reduce | flops 16 | bytes 128
  144.8 4.1 %reshape.55 = bf16[8192,1,2,16]{3,2,1,0:T(2,128)(2,1)} reshape(bf16[16,2,8192]{2,1,0:T(2,128)(2,1)S(1)} %all-to-all-done) | data formatting | bytes 1048576
  148.9 8.9 %copy.60 = bf16[1,2,16,16,512]{4,2,1,3,0:T(8,128)(2,1)S(1)} copy(bf16[1,2,16,16,512]{2,1,4,3,0:T(2,128)(2,1)} %bitcast.47) | data formatting | bytes 1048576 | tf_op jit(solution)/shard_map/all_to_all | solution.py:20
  158.5 3.5 %fusion.1 = f32[16,2,16,128]{3,2,1,0:T(8,128)} fusion(bf16[16,1,128,512]{3,2,1,0:T(8,128)(2,1)S(1)} %bitcast.53, bf16[16,1,128,512]{3,2,1,0:T(8,128)(2,1)} %bitcast.10, bf16[16,2,16,512]{3,2,0,1:T(8,128)(2,1)S(1)} %copy_select_fusion), kind=kOutput, calls=%fused_computation.3 | convolution fusion | flops 69206016 | bytes 4980736 | tf_op jit(solution)/shard_map/tckd,tcrd->tcrk/dot_general | solution.py:38
  162.1 55.2 %reduce-scatter.2.cloned.1.call-done = f32[1,2,16,128]{3,2,1,0:T(8,128)} async-done(((f32[16,2,16,128]{3,2,1,0:T(8,128)}), f32[1,2,16,128]{3,2,1,0:T(8,128)}) %reduce-scatter.2.cloned.1.call-update) | async-done | bytes 16400 | tf_op jit(solution)/shard_map/reduce_scatter | solution.py:41
  218.0 18.1 %all_gather.7 = bf16[16,2,16,128]{3,2,1,0:T(8,128)(2,1)S(1)} all-gather(bf16[1,2,16,128]{3,2,1,0:T(8,128)(2,1)S(1)} %convert_element_type.13), channel_id=1, replica_groups=mesh['group'=2,'fsdp'=16] {'fsdp'}, dimensions={0}, use_global_device_ids=true | all-gather | bytes 139264 | tf_op jit(solution)/shard_map/all_gather | solution.py:44
  236.1 2.3 fusion.2
  240.0 8.2 %all-to-all-start.4 = ((bf16[16,2,16,512]{3,2,1,0:T(8,128)(2,1)}), bf16[16,2,16,512]{3,2,1,0:T(8,128)(2,1)S(1)}, u32[]{:S(2)}, u32[]{:S(2)}) async-start(bf16[16,2,16,512]{3,2,1,0:T(8,128)(2,1)} %copy.70), calls=%async_computation.5 | async-start | bytes 1048576 | tf_op jit(solution)/shard_map/all_to_all | solution.py:57
  250.3 11.5 %all-to-all-done.4 = bf16[16,2,16,512]{3,2,1,0:T(8,128)(2,1)S(1)} async-done(((bf16[16,2,16,512]{3,2,1,0:T(8,128)(2,1)}), bf16[16,2,16,512]{3,2,1,0:T(8,128)(2,1)S(1)}, u32[]{:S(2)}, u32[]{:S(2)}) %all-to-all-start.4) | async-done | bytes 524320 | tf_op jit(solution)/shard_map/all_to_all | solution.py:57
  261.8 4.9 %all-to-all-start.3 = ((bf16[16,128,512]{2,1,0:T(8,128)(2,1)}), bf16[16,128,512]{2,1,0:T(8,128)(2,1)S(1)}, u32[]{:S(2)}, u32[]{:S(2)}) async-start(bf16[16,128,512]{2,1,0:T(8,128)(2,1)} %convolution_convert_fusion), calls=%async_computation.4 | async-start | bytes 4194304 | tf_op jit(solution)/shard_map/all_to_all | solution.py:52
  267.6 46.6 %all-to-all-done.3 = bf16[16,128,512]{2,1,0:T(8,128)(2,1)S(1)} async-done(((bf16[16,128,512]{2,1,0:T(8,128)(2,1)}), bf16[16,128,512]{2,1,0:T(8,128)(2,1)S(1)}, u32[]{:S(2)}, u32[]{:S(2)}) %all-to-all-start.3) | async-done | bytes 2097184 | tf_op jit(solution)/shard_map/all_to_all | solution.py:52
  314.2 2.4 copy.68
  316.5 4.1 %copy.72 = bf16[128,8192]{1,0:T(8,128)(2,1)} copy(bf16[128,8192]{0,1:T(8,128)(2,1)} %bitcast.49) | data formatting | bytes 4194304
  (24 shorter events, 8.5 us)
Async XLA Ops:
  21.4 20.1 %all-to-all-start = ((bf16[16,2,8192]{2,1,0:T(2,128)(2,1)}), bf16[16,2,8192]{2,1,0:T(2,128)(2,1)S(1)}, u32[]{:S(2)}, u32[]{:S(2)}) async-start(bf16[16,2,8192]{2,1,0:T(2,128)(2,1)} %reshape.54), calls=%async_computation | async-start | bytes 1048576 | tf_op jit(solution)/shard_map/all_to_all | solution.py:20
  41.5 52.7 %all-to-all-start.1 = ((bf16[128,16,512]{2,0,1:T(8,128)(2,1)}), bf16[128,16,512]{2,0,1:T(8,128)(2,1)}, u32[]{:S(2)}, u32[]{:S(2)}) async-start(bf16[128,16,512]{2,0,1:T(8,128)(2,1)} %copy.63), calls=%async_computation.1 | async-start | bytes 4194304 | tf_op jit(solution)/shard_map/all_to_all | solution.py:28
  52.5 47.3 %copy-start.1 = (u32[32]{0:T(128)S(1)}, u32[32]{0:T(128)}, u32[]{:S(2)}) copy-start(u32[32]{0:T(128)} %constant.22) | copy-start | bytes 388
  52.5 92.0 %copy-start = (s32[16]{0:T(128)S(1)}, s32[16]{0:T(128)}, u32[]{:S(2)}) copy-start(s32[16]{0:T(128)} %param.11) | copy-start | bytes 196
  94.2 64.3 %all-to-all-start.2 = ((bf16[128,16,512]{2,0,1:T(8,128)(2,1)}), bf16[128,16,512]{2,0,1:T(8,128)(2,1)S(1)}, u32[]{:S(2)}, u32[]{:S(2)}) async-start(bf16[128,16,512]{2,0,1:T(8,128)(2,1)} %copy.65), calls=%async_computation.2 | async-start | bytes 4194304 | tf_op jit(solution)/shard_map/all_to_all | solution.py:29
  99.1 118.2 %reduce-scatter.2.cloned.1.call-start = ((), (), s32[]{:S(2)}) async-start(), calls=%async_computation.6 | async-start | bytes 278528 | tf_op jit(solution)/shard_map/reduce_scatter | solution.py:41
  240.0 21.9 %all-to-all-start.4 = ((bf16[16,2,16,512]{3,2,1,0:T(8,128)(2,1)}), bf16[16,2,16,512]{3,2,1,0:T(8,128)(2,1)S(1)}, u32[]{:S(2)}, u32[]{:S(2)}) async-start(bf16[16,2,16,512]{3,2,1,0:T(8,128)(2,1)} %copy.70), calls=%async_computation.5 | async-start | bytes 1048576 | tf_op jit(solution)/shard_map/all_to_all | solution.py:57
  261.8 52.3 %all-to-all-start.3 = ((bf16[16,128,512]{2,1,0:T(8,128)(2,1)}), bf16[16,128,512]{2,1,0:T(8,128)(2,1)S(1)}, u32[]{:S(2)}, u32[]{:S(2)}) async-start(bf16[16,128,512]{2,1,0:T(8,128)(2,1)} %convolution_convert_fusion), calls=%async_computation.4 | async-start | bytes 4194304 | tf_op jit(solution)/shard_map/all_to_all | solution.py:52
Sparse Core Ops, SparseCore 0:
  162.2 55.0 reduce-scatter.1
where the time goes:
time: 329 us; the launch traced here: 327 us
  waiting for transfers between devices  163 us (50%)
  blocking collectives  61.4 us (19%)
  local copies, waits for them, and re-layouts  48.2 us (15%)
  starting transfers between devices  29.8 us (9%)
  between operations  14.8 us (4%)
  matrix products  8.33 us (3%)
    reduce_scatter x1, waiting for transfers between devices, shards(): lax.psum_scatter(partial_low, 'fsdp', scatter_dimension=0, tiled=True)  55.2 us
    all_to_all x1, waiting for transfers between devices, shards(): lax.all_to_all(grad_cols, 'fsdp', split_axis=0, concat_axis=1, tiled=True)  46.6 us
    unnamed x1, blocking collectives  43.4 us
    all_to_all x1, waiting for transfers between devices, shards(): lax.all_to_all(acts, 'fsdp', split_axis=1, concat_axis=0, tiled=True)  41.7 us
    unnamed x12, local copies, waits for them, and re-layouts  22.4 us
    all_gather x1, blocking collectives, shards(): lowrank = lax.all_gather(shares, 'fsdp', axis=0, tiled=True)  18.1 us
    all_to_all x1, waiting for transfers between devices, shards(): lax.all_to_all(summed, 'fsdp', split_axis=0, concat_axis=3, tiled=True)  11.5 us
    all_to_all x1, local copies, waits for them, and re-layouts, shards(): lax.all_to_all(stacked_factors, 'fsdp', split_axis=3, concat_axis=0, tile...  8.9 us
  transfers between devices with their start and end apart: 6, of which 5 were waited for; matrix products, arithmetic and copies ran while one was open for 9% of the time, Pallas kernels for 0%

commit v1 on v0

v1 whole, which is shorter than its diff:
```python
import functools

import jax
import jax.numpy as jnp
from jax import lax
from jax.experimental import pallas as pl
from jax.experimental.pallas import tpu as pltpu
from jax.sharding import PartitionSpec as P

F32 = jnp.float32
VMEM_LIMIT = 48 * 1024 * 1024


def pack_kernel(down_ref, up_ref, out_ref):
    n, _, w = out_ref.shape
    r = down_ref.shape[1]
    for j in range(n):
        out_ref[j, 0:r, :] = down_ref[0, :, j * w : (j + 1) * w]
        out_ref[j, r : 2 * r, :] = up_ref[0, :, j * w : (j + 1) * w]


def pack(down, up, n):
    _, r, d = down.shape
    return pl.pallas_call(
        pack_kernel,
        out_shape=jax.ShapeDtypeStruct((n, 2 * r, d // n), down.dtype),
        compiler_params=pltpu.CompilerParams(vmem_limit_bytes=VMEM_LIMIT),
    )(down, up)


def unpack_kernel(in_ref, ga_ref, gb_ref):
    n, _, w = in_ref.shape
    r = ga_ref.shape[1]
    for j in range(n):
        ga_ref[0, :, j * w : (j + 1) * w] = in_ref[j, 0:r, :]
        gb_ref[0, :, j * w : (j + 1) * w] = in_ref[j, r : 2 * r, :]


def unpack(blocks):
    n, r2, w = blocks.shape
    out = jax.ShapeDtypeStruct((1, r2 // 2, n * w), blocks.dtype)
    return pl.pallas_call(
        unpack_kernel,
        out_shape=(out, out),
        compiler_params=pltpu.CompilerParams(vmem_limit_bytes=VMEM_LIMIT),
    )(blocks)


def permute_kernel(index_ref, in_ref, out_ref):
    n = out_ref.shape[0]
    for t in range(n):
        out_ref[t] = in_ref[index_ref[t]]


def permute(index, blocks):
    return pl.pallas_call(
        permute_kernel,
        out_shape=jax.ShapeDtypeStruct(blocks.shape, blocks.dtype),
        in_specs=[
            pl.BlockSpec(memory_space=pltpu.SMEM),
            pl.BlockSpec(memory_space=pltpu.VMEM),
        ],
        compiler_params=pltpu.CompilerParams(vmem_limit_bytes=VMEM_LIMIT),
    )(index, blocks)


def grads_kernel(acts_ref, cot_ref, fac_ref, gx_ref, out_ref):
    n, r2, w = fac_ref.shape
    r = r2 // 2
    rows = acts_ref.shape[0]
    dims_nt = (((1,), (1,)), ((), ()))
    low_u = jnp.zeros((r, rows), F32)
    low_h = jnp.zeros((r, rows), F32)
    for j in range(n):
        cols = slice(j * w, (j + 1) * w)
        low_u += lax.dot_general(fac_ref[j, 0:r, :], acts_ref[:, cols], dims_nt, preferred_element_type=F32)
        low_h += lax.dot_general(fac_ref[j, r:r2, :], cot_ref[:, cols], dims_nt, preferred_element_type=F32)
    low_u = low_u.astype(jnp.bfloat16)
    low_h = low_h.astype(jnp.bfloat16)
    for j in range(n):
        cols = slice(j * w, (j + 1) * w)
        out_ref[j, 0:r, :] = jnp.dot(low_h, acts_ref[:, cols], preferred_element_type=F32).astype(jnp.bfloat16)
        out_ref[j, r:r2, :] = jnp.dot(low_u, cot_ref[:, cols], preferred_element_type=F32).astype(jnp.bfloat16)
        gx_ref[:, cols] = lax.dot_general(
            low_h, fac_ref[j, 0:r, :], (((0,), (0,)), ((), ())), preferred_element_type=F32
        ).astype(jnp.bfloat16)


def grads(acts, cot, factors):
    return pl.pallas_call(
        grads_kernel,
        out_shape=(
            jax.ShapeDtypeStruct(acts.shape, acts.dtype),
            jax.ShapeDtypeStruct(factors.shape, factors.dtype),
        ),
        compiler_params=pltpu.CompilerParams(vmem_limit_bytes=VMEM_LIMIT),
    )(acts, cot, factors)


def shards(acts, cotangent, down, up, adapter_per_tile, adapter_storage_slot):
    n = lax.axis_size("fsdp")
    swap = functools.partial(
        lax.all_to_all, axis_name="fsdp", split_axis=0, concat_axis=0, tiled=True
    )
    tile_adapter = lax.all_gather(adapter_per_tile, "fsdp", axis=0, tiled=True)
    labels = jnp.arange(n, dtype=jnp.int32)
    tile_slot = jnp.sum(
        jnp.where(tile_adapter[:, None] == labels[None, :], adapter_storage_slot[None, :], 0),
        axis=1,
    )
    slot_tile = jnp.sum(
        jnp.where(tile_slot[None, :] == labels[:, None], labels[None, :], 0), axis=1
    )
    spread = swap(pack(down, up, n))
    factors = swap(permute(tile_slot, spread))
    grad_x, parts = grads(acts, cotangent, factors)
    owned = swap(permute(slot_tile, swap(parts)))
    grad_a, grad_b = unpack(owned)
    return grad_x, grad_a, grad_b


def solution(mesh):
    placed = (
        P(("group", "fsdp"), None),
        P(("group", "fsdp"), None),
        P("fsdp", None, None),
        P("fsdp", None, None),
        P(("group", "fsdp")),
        P(),
    )
    return jax.shard_map(
        shards,
        mesh=mesh,
        in_specs=placed,
        out_specs=(
            P(("group", "fsdp"), None),
            P(("group", "fsdp"), None, None),
            P(("group", "fsdp"), None, None),
        ),
        check_vma=False,
    )
```

time: 329 us -> 88.1 us (0.27)
  the two profiles are of different devices: /device:TPU:13 before, /device:TPU:0 now
where the time goes in v1:
time: 88.1 us; the launch traced here: 87.6 us
  blocking collectives  50 us (57%)
  waiting for transfers between devices  14.4 us (16%)
  starting transfers between devices  11.6 us (13%)
  Pallas kernels  6.81 us (8%)
  local copies, waits for them, and re-layouts  3.26 us (4%)
  between operations  1.35 us (2%)
    all_to_all x1, blocking collectives, shards(): owned = swap(permute(slot_tile, swap(parts)))  18.4 us
    all_to_all x1, blocking collectives, shards(): factors = swap(permute(tile_slot, spread))  17.8 us
    all_to_all x1, waiting for transfers between devices, shards(): owned = swap(permute(slot_tile, swap(parts)))  14.4 us
    unnamed x1, blocking collectives  13.8 us
    all_to_all x1, starting transfers between devices, shards(): spread = swap(pack(down, up, n))  7.52 us
    all_to_all x1, starting transfers between devices, shards(): owned = swap(permute(slot_tile, swap(parts)))  4.1 us
    pallas_call x1, Pallas kernels, grads(): pl.pallas_call(grads_kernel, out_shape=(jax.ShapeDtypeStruct(acts.shape,...  4 us
    unnamed x15, local copies, waits for them, and re-layouts  3.26 us
  transfers between devices with their start and end apart: 2, of which 1 were waited for; matrix products, arithmetic and copies ran while one was open for 2% of the time, Pallas kernels for 0%

profile of v1, /device:TPU:0, one launch (start us, length us, event | category | flops | bytes accessed | tf_op | source)
XLA Modules:
  0.0 87.6 jit_solution(12797953316483733725)
XLA Ops:
  0.6 0.0 copy-start.5
  0.6 0.0 copy-start.2
  0.7 0.9 %copy-done.2 = bf16[1,16,8192]{2,1,0:T(8,128)(2,1)S(1)} copy-done((bf16[1,16,8192]{2,1,0:T(8,128)(2,1)S(1)}, bf16[1,16,8192]{2,1,0:T(8,128)(2,1)}, u32[]{:S(2)}) %copy-start.2) | copy-done | bytes 262168
  1.6 0.9 %copy-done.3 = bf16[1,16,8192]{2,1,0:T(8,128)(2,1)S(1)} copy-done((bf16[1,16,8192]{2,1,0:T(8,128)(2,1)S(1)}, bf16[1,16,8192]{2,1,0:T(8,128)(2,1)}, u32[]{:S(2)}) %copy-start.3) | copy-done | bytes 262168
  2.6 0.8 shard_map.85
  3.4 7.5 %all-to-all-start = ((bf16[16,32,512]{2,1,0:T(8,128)(2,1)}), bf16[16,32,512]{2,1,0:T(8,128)(2,1)S(1)}, u32[]{:S(2)}, u32[]{:S(2)}) async-start(bf16[16,32,512]{2,1,0:T(8,128)(2,1)} %shard_map.85), calls=%async_computation | async-start | bytes 1048576 | tf_op jit(solution)/shard_map/all_to_all | solution.py:114
  11.6 0.0 copy-done.5
  11.6 0.6 dynamic-slice
  12.2 0.8 dynamic-update-slice
  12.9 13.8 %all-reduce = s32[16]{0:T(128)S(1)} all-reduce(s32[16]{0:T(128)S(1)} %dynamic-update-slice), channel_id=1, replica_groups=mesh['group'=2,'fsdp'=16] {'fsdp'}, use_global_device_ids=true, to_apply=%add | all-reduce | flops 16 | bytes 128
  26.7 0.0 copy-done.4
  26.7 0.2 select_reduce_fusion.1.index_ref
  26.9 0.0 all-to-all-done.in_ref
  26.9 0.0 copy-start.1
  26.9 0.6 shard_map.86
  27.5 17.8 %all_to_all.20.fac_ref = bf16[16,32,512]{2,1,0:T(8,128)(2,1)S(1)} all-to-all(bf16[16,32,512]{2,1,0:T(8,128)(2,1)S(1)} %shard_map.86), channel_id=1, replica_groups=mesh['group'=2,'fsdp'=16] {'fsdp'}, dimensions={0} | all-to-all | bytes 1048576 | tf_op jit(solution)/shard_map/all_to_all | solution.py:115
  45.3 0.0 copy-done.1
  45.3 4.0 %shard_map.87 = (bf16[128,8192]{1,0:T(8,128)(2,1)}, bf16[16,32,512]{2,1,0:T(8,128)(2,1)}) custom-call(bf16[128,8192]{1,0:T(8,128)(2,1)S(1)} %copy-done, bf16[128,8192]{1,0:T(8,128)(2,1)S(1)} %copy-done.1, bf16[16,32,512]{2,1,0:T(8,128)(2,1)S(1)} %all_to_all.20.fac_ref), custom_call_target="tpu_custom_call" | custom-call | tf_op jit(solution)/shard_map/pallas_call | solution.py:90
  49.3 4.1 %all-to-all-start.2 = ((bf16[16,32,512]{2,1,0:T(8,128)(2,1)}), bf16[16,32,512]{2,1,0:T(8,128)(2,1)S(1)}, u32[]{:S(2)}, u32[]{:S(2)}) async-start(bf16[16,32,512]{2,1,0:T(8,128)(2,1)} %get-tuple-element.8), calls=%async_computation.2 | async-start | bytes 1048576 | tf_op jit(solution)/shard_map/all_to_all | solution.py:117
  53.4 0.1 select_reduce_fusion.index_ref
  53.5 14.4 %all-to-all-done.2.in_ref = bf16[16,32,512]{2,1,0:T(8,128)(2,1)S(1)} async-done(((bf16[16,32,512]{2,1,0:T(8,128)(2,1)}), bf16[16,32,512]{2,1,0:T(8,128)(2,1)S(1)}, u32[]{:S(2)}, u32[]{:S(2)}) %all-to-all-start.2) | async-done | bytes 524320 | tf_op jit(solution)/shard_map/all_to_all | solution.py:117
  67.9 0.6 shard_map.88
  68.4 18.4 %all_to_all.21.in_ref = bf16[16,32,512]{2,1,0:T(8,128)(2,1)S(1)} all-to-all(bf16[16,32,512]{2,1,0:T(8,128)(2,1)S(1)} %shard_map.88), channel_id=1, replica_groups=mesh['group'=2,'fsdp'=16] {'fsdp'}, dimensions={0} | all-to-all | bytes 1048576 | tf_op jit(solution)/shard_map/all_to_all | solution.py:117
  86.8 0.8 shard_map.89
  (5 shorter events, 0.0 us)
Async XLA Ops:
  0.6 10.9 %copy-start.5 = (u32[32]{0:T(128)S(1)}, u32[32]{0:T(128)}, u32[]{:S(2)}) copy-start(u32[32]{0:T(128)} %constant.7) | copy-start | bytes 388
  0.6 1.0 %copy-start.2 = (bf16[1,16,8192]{2,1,0:T(8,128)(2,1)S(1)}, bf16[1,16,8192]{2,1,0:T(8,128)(2,1)}, u32[]{:S(2)}) copy-start(bf16[1,16,8192]{2,1,0:T(8,128)(2,1)} %down_ref.1) | copy-start | bytes 786436
  1.6 0.9 %copy-start.3 = (bf16[1,16,8192]{2,1,0:T(8,128)(2,1)S(1)}, bf16[1,16,8192]{2,1,0:T(8,128)(2,1)}, u32[]{:S(2)}) copy-start(bf16[1,16,8192]{2,1,0:T(8,128)(2,1)} %up_ref.1) | copy-start | bytes 786436
  2.6 24.1 %copy-start.4 = (s32[16]{0:T(128)S(1)}, s32[16]{0:T(128)}, u32[]{:S(2)}) copy-start(s32[16]{0:T(128)} %param.11) | copy-start | bytes 196
  2.6 42.7 %copy-start = (bf16[128,8192]{1,0:T(8,128)(2,1)S(1)}, bf16[128,8192]{1,0:T(8,128)(2,1)}, u32[]{:S(2)}) copy-start(bf16[128,8192]{1,0:T(8,128)(2,1)} %acts_ref.1) | copy-start | bytes 6291460
  3.4 23.5 %all-to-all-start = ((bf16[16,32,512]{2,1,0:T(8,128)(2,1)}), bf16[16,32,512]{2,1,0:T(8,128)(2,1)S(1)}, u32[]{:S(2)}, u32[]{:S(2)}) async-start(bf16[16,32,512]{2,1,0:T(8,128)(2,1)} %shard_map.85), calls=%async_computation | async-start | bytes 1048576 | tf_op jit(solution)/shard_map/all_to_all | solution.py:114
  26.9 18.4 %copy-start.1 = (bf16[128,8192]{1,0:T(8,128)(2,1)S(1)}, bf16[128,8192]{1,0:T(8,128)(2,1)}, u32[]{:S(2)}) copy-start(bf16[128,8192]{1,0:T(8,128)(2,1)} %cot_ref.1) | copy-start | bytes 6291460
  49.3 18.6 %all-to-all-start.2 = ((bf16[16,32,512]{2,1,0:T(8,128)(2,1)}), bf16[16,32,512]{2,1,0:T(8,128)(2,1)S(1)}, u32[]{:S(2)}, u32[]{:S(2)}) async-start(bf16[16,32,512]{2,1,0:T(8,128)(2,1)} %get-tuple-element.8), calls=%async_computation.2 | async-start | bytes 1048576 | tf_op jit(solution)/shard_map/all_to_all | solution.py:117

commit v2 on v0

v2 whole, which is shorter than its diff:
```python
import functools

import jax
import jax.numpy as jnp
from jax import lax
from jax.experimental import pallas as pl
from jax.experimental.pallas import tpu as pltpu
from jax.sharding import PartitionSpec as P

F32 = jnp.float32
BF16 = jnp.bfloat16
LANES = 128
ID_ROWS = 16
VMEM = pl.BlockSpec(memory_space=pltpu.VMEM)
SMEM = pl.BlockSpec(memory_space=pltpu.SMEM)
PARAMS = pltpu.CompilerParams(vmem_limit_bytes=48 * 1024 * 1024)


def position():
    me = lax.axis_index("fsdp")
    return me // 2, me % 2


def columns(chunk, w):
    return pl.ds(pl.multiple_of(chunk * w, w), w)


def pack_kernel(m, id_ref, down_ref, up_ref, *outs):
    p, _ = position()
    r, w = down_ref.shape[1], down_ref.shape[2] // m
    mark = jnp.full((ID_ROWS, LANES), id_ref[0].astype(F32), F32).astype(BF16)
    for k in range(m):
        for b in range(w // LANES):
            cols = pl.ds(pl.multiple_of((p ^ k) * w + b * LANES, LANES), LANES)
            outs[k][2 * r * b : 2 * r * b + r, :] = down_ref[0, :, cols]
            outs[k][2 * r * b + r : 2 * r * (b + 1), :] = up_ref[0, :, cols]
        outs[k][2 * r * (w // LANES) :, :] = mark


def stack_kernel(*refs):
    out_ref = refs[-1]
    for k, ref in enumerate(refs[:-1]):
        out_ref[k] = ref[...]


def stack(blocks):
    return pl.pallas_call(
        stack_kernel,
        out_shape=jax.ShapeDtypeStruct((len(blocks), *blocks[0].shape), BF16),
        in_specs=[VMEM] * len(blocks),
        out_specs=VMEM,
        compiler_params=PARAMS,
    )(*blocks)


def deliver_kernel(m, storage_ref, own_ref, other_ref, *outs):
    slots_ref = outs[m]
    p, c = position()
    rows = own_ref.shape[1] - ID_ROWS
    r2 = outs[0].shape[0]

    def slot_of(ref, k):
        label = jnp.max(ref[k, rows:, :].astype(F32)).astype(jnp.int32)
        return storage_ref[label]

    def copy(ref, at, out):
        for b in range(rows // r2):
            out[:, b * LANES : (b + 1) * LANES] = ref[at, b * r2 : (b + 1) * r2, :]

    for k in range(m):
        slot = slot_of(own_ref, k)
        slots_ref[2 * (p ^ k) + c] = slot
        slots_ref[2 * (p ^ k) + 1 - c] = slot_of(other_ref, k)
        at = (slot // 2) ^ p

        @pl.when(slot % 2 == c)
        def _():
            copy(own_ref, at, outs[k])

        @pl.when(slot % 2 != c)
        def _():
            copy(other_ref, at, outs[k])


def grads_kernel(m, acts_ref, cot_ref, *refs):
    factors, gx_ref, outs = refs[:m], refs[m], refs[m + 1 :]
    p, _ = position()
    r2, w = factors[0].shape
    r = r2 // 2
    rows = acts_ref.shape[0]
    dims_nt = (((1,), (1,)), ((), ()))
    low_u = jnp.zeros((r, rows), F32)
    low_h = jnp.zeros((r, rows), F32)
    for k in range(m):
        cols = columns(p ^ k, w)
        low_u += lax.dot_general(factors[k][0:r, :], acts_ref[:, cols], dims_nt, preferred_element_type=F32)
        low_h += lax.dot_general(factors[k][r:r2, :], cot_ref[:, cols], dims_nt, preferred_element_type=F32)
    low_u = low_u.astype(BF16)
    low_h = low_h.astype(BF16)
    for k in range(m):
        cols = columns(p ^ k, w)
        outs[k][0:r, :] = jnp.dot(low_h, acts_ref[:, cols], preferred_element_type=F32).astype(BF16)
        outs[k][r:r2, :] = jnp.dot(low_u, cot_ref[:, cols], preferred_element_type=F32).astype(BF16)
        gx_ref[:, cols] = lax.dot_general(
            low_h, factors[k][0:r, :], (((0,), (0,)), ((), ())), preferred_element_type=F32
        ).astype(BF16)


def collect_kernel(m, slots_ref, own_ref, other_ref, *refs):
    outs, tile_of = refs[:m], refs[m]
    p, c = position()
    for t in range(2 * m):
        tile_of[slots_ref[t]] = t
    for k in range(m):
        tile = tile_of[2 * (p ^ k) + c]
        at = (tile // 2) ^ p

        @pl.when(tile % 2 == c)
        def _():
            outs[k][...] = own_ref[at]

        @pl.when(tile % 2 != c)
        def _():
            outs[k][...] = other_ref[at]


def unpack_kernel(m, *refs):
    ga_ref, gb_ref = refs[m:]
    p, _ = position()
    r2, w = refs[0].shape
    for k in range(m):
        cols = columns(p ^ k, w)
        ga_ref[0, :, cols] = refs[k][0 : r2 // 2, :]
        gb_ref[0, :, cols] = refs[k][r2 // 2 : r2, :]


def shards(acts, cotangent, down, up, adapter_per_tile, adapter_storage_slot):
    n = lax.axis_size("fsdp")
    m = n // 2
    _, r, d = down.shape
    w = d // m

    def exchange(blocks):
        return [blocks[0]] + [
            lax.ppermute(
                blocks[k], "fsdp", [(2 * p + c, 2 * (p ^ k) + c) for p in range(m) for c in range(2)]
            )
            for k in range(1, m)
        ]

    def to_other_core(block):
        return lax.ppermute(block, "fsdp", [(f, f ^ 1) for f in range(n)])

    rows = 2 * r * w // LANES
    flat = jax.ShapeDtypeStruct((rows + ID_ROWS, LANES), BF16)
    wide = jax.ShapeDtypeStruct((2 * r, w), BF16)
    spread = pl.pallas_call(
        functools.partial(pack_kernel, m),
        out_shape=[flat] * m,
        in_specs=[SMEM, VMEM, VMEM],
        out_specs=[VMEM] * m,
        compiler_params=PARAMS,
    )(adapter_per_tile, down, up)
    held = stack(exchange(spread))
    *factors, slots = pl.pallas_call(
        functools.partial(deliver_kernel, m),
        out_shape=[wide] * m + [jax.ShapeDtypeStruct((n,), jnp.int32)],
        in_specs=[SMEM, VMEM, VMEM],
        out_specs=[VMEM] * m + [SMEM],
        compiler_params=PARAMS,
    )(adapter_storage_slot, held, to_other_core(held))
    factors = exchange(factors)
    grad_x, *parts = pl.pallas_call(
        functools.partial(grads_kernel, m),
        out_shape=[jax.ShapeDtypeStruct(acts.shape, BF16)] + [wide] * m,
        in_specs=[VMEM] * (m + 2),
        out_specs=[VMEM] * (m + 1),
        compiler_params=PARAMS,
    )(acts, cotangent, *factors)
    held = stack(exchange(parts))
    owned = pl.pallas_call(
        functools.partial(collect_kernel, m),
        out_shape=[wide] * m,
        in_specs=[SMEM, VMEM, VMEM],
        out_specs=[VMEM] * m,
        scratch_shapes=[pltpu.SMEM((n,), jnp.int32)],
        compiler_params=PARAMS,
    )(slots, held, to_other_core(held))
    grad_a, grad_b = pl.pallas_call(
        functools.partial(unpack_kernel, m),
        out_shape=[jax.ShapeDtypeStruct(down.shape, BF16)] * 2,
        in_specs=[VMEM] * m,
        out_specs=[VMEM] * 2,
        compiler_params=PARAMS,
    )(*exchange(owned))
    return grad_x, grad_a, grad_b


def solution(mesh):
    placed = (
        P(("group", "fsdp"), None),
        P(("group", "fsdp"), None),
        P("fsdp", None, None),
        P("fsdp", None, None),
        P(("group", "fsdp")),
        P(),
    )
    return jax.shard_map(
        shards,
        mesh=mesh,
        in_specs=placed,
        out_specs=(
            P(("group", "fsdp"), None),
            P(("group", "fsdp"), None, None),
            P(("group", "fsdp"), None, None),
        ),
        check_vma=False,
    )
```

time: 329 us -> 89 us (0.27)
  the two profiles are of different devices: /device:TPU:13 before, /device:TPU:0 now
where the time goes in v2:
time: 89 us; the launch traced here: 88.8 us
  starting transfers between devices  48.8 us (55%)
  waiting for transfers between devices  26.5 us (30%)
  Pallas kernels  7.93 us (9%)
  local copies, waits for them, and re-layouts  4.14 us (5%)
  between operations  1.53 us (2%)
    ppermute x28, starting transfers between devices, exchange(): lax.ppermute(blocks[k], 'fsdp', [(2 * p + c, 2 * (p ^ k) + c) for p in ra...  48.6 us
    ppermute x28, waiting for transfers between devices, exchange(): lax.ppermute(blocks[k], 'fsdp', [(2 * p + c, 2 * (p ^ k) + c) for p in ra...  22.6 us
    unnamed x10, local copies, waits for them, and re-layouts  4.14 us
    ppermute x2, waiting for transfers between devices, to_other_core(): return lax.ppermute(block, 'fsdp', [(f, f ^ 1) for f in range(n)])  3.84 us
    pallas_call x1, Pallas kernels, shards(): pl.pallas_call(functools.partial(grads_kernel, m), out_shape=[jax.ShapeDt...  3.82 us
    pallas_call x1, Pallas kernels, shards(): pl.pallas_call(functools.partial(deliver_kernel, m), out_shape=[wide] * m...  2.31 us
  transfers between devices with their start and end apart: 30, of which 10 were waited for; matrix products, arithmetic and copies ran while one was open for 0% of the time, Pallas kernels for 0%

profile of v2, /device:TPU:0, one launch (start us, length us, event | category | flops | bytes accessed | tf_op | source)
XLA Modules:
  0.0 88.8 jit_solution(15031935636412220927)
XLA Ops:
  3.5 3.0 %collective-permute-start = (bf16[272,128]{1,0:T(8,128)(2,1)S(1)}, bf16[272,128]{1,0:T(8,128)(2,1)S(1)}, u32[]{:S(2)}, u32[]{:S(2)}) collective-permute-start(bf16[272,128]{1,0:T(8,128)(2,1)S(1)} %get-tuple-element.40), channel_id=1, source_target_pairs={{0,2},{1,3},{2,0},{3,1},{4,6},{5,7},{6,4},{7,5},{8,10},{9,11},{10,... | collective-permute-start | bytes 208904 | tf_op jit(solution)/shard_map/ppermute | solution.py:145
  8.1 3.0 %collective-permute-start.3 = (bf16[272,128]{1,0:T(8,128)(2,1)S(1)}, bf16[272,128]{1,0:T(8,128)(2,1)S(1)}, u32[]{:S(2)}, u32[]{:S(2)}) collective-permute-start(bf16[272,128]{1,0:T(8,128)(2,1)S(1)} %get-tuple-element.43), channel_id=1, source_target_pairs={{0,8},{1,9},{2,10},{3,11},{4,12},{5,13},{6,14},{7,15},{8,0},{9,1},... | collective-permute-start | bytes 208904 | tf_op jit(solution)/shard_map/ppermute | solution.py:145
  12.4 3.6 %collective-permute-start.5 = (bf16[272,128]{1,0:T(8,128)(2,1)S(1)}, bf16[272,128]{1,0:T(8,128)(2,1)S(1)}, u32[]{:S(2)}, u32[]{:S(2)}) collective-permute-start(bf16[272,128]{1,0:T(8,128)(2,1)S(1)} %get-tuple-element.45), channel_id=1, source_target_pairs={{0,12},{1,13},{2,14},{3,15},{4,8},{5,9},{6,10},{7,11},{8,4},{9,5},... | collective-permute-start | bytes 208904 | tf_op jit(solution)/shard_map/ppermute | solution.py:145
  16.0 5.8 %collective-permute-done.4.refs_5_ = bf16[272,128]{1,0:T(8,128)(2,1)S(1)} collective-permute-done((bf16[272,128]{1,0:T(8,128)(2,1)S(1)}, bf16[272,128]{1,0:T(8,128)(2,1)S(1)}, u32[]{:S(2)}, u32[]{:S(2)}) %collective-permute-start.4) | collective-permute-done | bytes 69664 | tf_op jit(solution)/shard_map/ppermute | solution.py:145
  23.2 1.9 %collective-permute-done.7.other_ref = bf16[8,272,128]{2,1,0:T(8,128)(2,1)S(1)} collective-permute-done((bf16[8,272,128]{2,1,0:T(8,128)(2,1)S(1)}, bf16[8,272,128]{2,1,0:T(8,128)(2,1)S(1)}, u32[]{:S(2)}, u32[]{:S(2)}) %collective-permute-start.7) | collective-permute-done | bytes 557088 | tf_op jit(solution)/shard_map/ppermute | solution.py:152
  25.8 2.3 %shard_map.87 = (bf16[32,1024]{1,0:T(8,128)(2,1)S(1)}, bf16[32,1024]{1,0:T(8,128)(2,1)S(1)}, bf16[32,1024]{1,0:T(8,128)(2,1)S(1)}, bf16[32,1024]{1,0:T(8,128)(2,...) custom-call(s32[16]{0:T(128)S(1)} %copy-done.4, ...), custom_call_target="tpu_custom_call" | custom-call | tf_op jit(solution)/shard_map/pallas_call | solution.py:165
  28.7 2.6 %collective-permute-start.9 = (bf16[32,1024]{1,0:T(8,128)(2,1)S(1)}, bf16[32,1024]{1,0:T(8,128)(2,1)S(1)}, u32[]{:S(2)}, u32[]{:S(2)}) collective-permute-start(bf16[32,1024]{1,0:T(8,128)(2,1)S(1)} %get-tuple-element.49), channel_id=1, source_target_pairs={{0,4},{1,5},{2,6},{3,7},{4,0},{5,1},{6,2},{7,3},{8,12},{9,13},{10,... | collective-permute-start | bytes 196616 | tf_op jit(solution)/shard_map/ppermute | solution.py:145
  32.0 3.1 %collective-permute-start.11 = (bf16[32,1024]{1,0:T(8,128)(2,1)S(1)}, bf16[32,1024]{1,0:T(8,128)(2,1)S(1)}, u32[]{:S(2)}, u32[]{:S(2)}) collective-permute-start(bf16[32,1024]{1,0:T(8,128)(2,1)S(1)} %get-tuple-element.51), channel_id=1, source_target_pairs={{0,8},{1,9},{2,10},{3,11},{4,12},{5,13},{6,14},{7,15},{8,0},{9,1},... | collective-permute-start | bytes 196616 | tf_op jit(solution)/shard_map/ppermute | solution.py:145
  35.1 2.3 %collective-permute-start.13 = (bf16[32,1024]{1,0:T(8,128)(2,1)S(1)}, bf16[32,1024]{1,0:T(8,128)(2,1)S(1)}, u32[]{:S(2)}, u32[]{:S(2)}) collective-permute-start(bf16[32,1024]{1,0:T(8,128)(2,1)S(1)} %get-tuple-element.53), channel_id=1, source_target_pairs={{0,12},{1,13},{2,14},{3,15},{4,8},{5,9},{6,10},{7,11},{8,4},{9,5},... | collective-permute-start | bytes 196616 | tf_op jit(solution)/shard_map/ppermute | solution.py:145
  37.4 2.4 %collective-permute-start.14 = (bf16[32,1024]{1,0:T(8,128)(2,1)S(1)}, bf16[32,1024]{1,0:T(8,128)(2,1)S(1)}, u32[]{:S(2)}, u32[]{:S(2)}) collective-permute-start(bf16[32,1024]{1,0:T(8,128)(2,1)S(1)} %get-tuple-element.54), channel_id=1, source_target_pairs={{0,14},{1,15},{2,12},{3,13},{4,10},{5,11},{6,8},{7,9},{8,6},{9,7},... | collective-permute-start | bytes 196616 | tf_op jit(solution)/shard_map/ppermute | solution.py:145
  39.8 2.5 %collective-permute-done.11.refs_4_ = bf16[32,1024]{1,0:T(8,128)(2,1)S(1)} collective-permute-done((bf16[32,1024]{1,0:T(8,128)(2,1)S(1)}, bf16[32,1024]{1,0:T(8,128)(2,1)S(1)}, u32[]{:S(2)}, u32[]{:S(2)}) %collective-permute-start.11) | collective-permute-done | bytes 65568 | tf_op jit(solution)/shard_map/ppermute | solution.py:145
  42.3 2.6 %collective-permute-done.12.refs_5_ = bf16[32,1024]{1,0:T(8,128)(2,1)S(1)} collective-permute-done((bf16[32,1024]{1,0:T(8,128)(2,1)S(1)}, bf16[32,1024]{1,0:T(8,128)(2,1)S(1)}, u32[]{:S(2)}, u32[]{:S(2)}) %collective-permute-start.12) | collective-permute-done | bytes 65568 | tf_op jit(solution)/shard_map/ppermute | solution.py:145
  46.5 3.8 %shard_map.88 = (bf16[128,8192]{1,0:T(8,128)(2,1)}, bf16[32,1024]{1,0:T(8,128)(2,1)S(1)}, bf16[32,1024]{1,0:T(8,128)(2,1)S(1)}, bf16[32,1024]{1,0:T(8,128)(2,1)S...) custom-call(bf16[128,8192]{1,0:T(8,128)(2,1)S(1)} %copy-done, ...), custom_call_target="tpu_custom_call" | custom-call | tf_op jit(solution)/shard_map/pallas_call | solution.py:173
  51.4 3.0 %collective-permute-start.16 = (bf16[32,1024]{1,0:T(8,128)(2,1)S(1)}, bf16[32,1024]{1,0:T(8,128)(2,1)S(1)}, u32[]{:S(2)}, u32[]{:S(2)}) collective-permute-start(bf16[32,1024]{1,0:T(8,128)(2,1)S(1)} %get-tuple-element.59), channel_id=1, source_target_pairs={{0,4},{1,5},{2,6},{3,7},{4,0},{5,1},{6,2},{7,3},{8,12},{9,13},{10,... | collective-permute-start | bytes 196616 | tf_op jit(solution)/shard_map/ppermute | solution.py:145
  54.9 2.5 %collective-permute-start.18 = (bf16[32,1024]{1,0:T(8,128)(2,1)S(1)}, bf16[32,1024]{1,0:T(8,128)(2,1)S(1)}, u32[]{:S(2)}, u32[]{:S(2)}) collective-permute-start(bf16[32,1024]{1,0:T(8,128)(2,1)S(1)} %get-tuple-element.61), channel_id=1, source_target_pairs={{0,8},{1,9},{2,10},{3,11},{4,12},{5,13},{6,14},{7,15},{8,0},{9,1},... | collective-permute-start | bytes 196616 | tf_op jit(solution)/shard_map/ppermute | solution.py:145
  58.2 2.4 %collective-permute-start.20 = (bf16[32,1024]{1,0:T(8,128)(2,1)S(1)}, bf16[32,1024]{1,0:T(8,128)(2,1)S(1)}, u32[]{:S(2)}, u32[]{:S(2)}) collective-permute-start(bf16[32,1024]{1,0:T(8,128)(2,1)S(1)} %get-tuple-element.63), channel_id=1, source_target_pairs={{0,12},{1,13},{2,14},{3,15},{4,8},{5,9},{6,10},{7,11},{8,4},{9,5},... | collective-permute-start | bytes 196616 | tf_op jit(solution)/shard_map/ppermute | solution.py:145
  60.6 2.0 %collective-permute-start.21 = (bf16[32,1024]{1,0:T(8,128)(2,1)S(1)}, bf16[32,1024]{1,0:T(8,128)(2,1)S(1)}, u32[]{:S(2)}, u32[]{:S(2)}) collective-permute-start(bf16[32,1024]{1,0:T(8,128)(2,1)S(1)} %get-tuple-element.64), channel_id=1, source_target_pairs={{0,14},{1,15},{2,12},{3,13},{4,10},{5,11},{6,8},{7,9},{8,6},{9,7},... | collective-permute-start | bytes 196616 | tf_op jit(solution)/shard_map/ppermute | solution.py:145
  62.6 2.8 %collective-permute-done.18.refs_4_ = bf16[32,1024]{1,0:T(8,128)(2,1)S(1)} collective-permute-done((bf16[32,1024]{1,0:T(8,128)(2,1)S(1)}, bf16[32,1024]{1,0:T(8,128)(2,1)S(1)}, u32[]{:S(2)}, u32[]{:S(2)}) %collective-permute-start.18) | collective-permute-done | bytes 65568 | tf_op jit(solution)/shard_map/ppermute | solution.py:145
  65.4 2.3 %collective-permute-done.19.refs_5_ = bf16[32,1024]{1,0:T(8,128)(2,1)S(1)} collective-permute-done((bf16[32,1024]{1,0:T(8,128)(2,1)S(1)}, bf16[32,1024]{1,0:T(8,128)(2,1)S(1)}, u32[]{:S(2)}, u32[]{:S(2)}) %collective-permute-start.19) | collective-permute-done | bytes 65568 | tf_op jit(solution)/shard_map/ppermute | solution.py:145
  67.8 1.9 %collective-permute-done.22.other_ref = bf16[8,32,1024]{2,1,0:T(8,128)(2,1)S(1)} collective-permute-done((bf16[8,32,1024]{2,1,0:T(8,128)(2,1)S(1)}, bf16[8,32,1024]{2,1,0:T(8,128)(2,1)S(1)}, u32[]{:S(2)}, u32[]{:S(2)}) %collective-permute-start.22) | collective-permute-done | bytes 524320 | tf_op jit(solution)/shard_map/ppermute | solution.py:152
  71.8 2.8 %collective-permute-start.24 = (bf16[32,1024]{1,0:T(8,128)(2,1)S(1)}, bf16[32,1024]{1,0:T(8,128)(2,1)S(1)}, u32[]{:S(2)}, u32[]{:S(2)}) collective-permute-start(bf16[32,1024]{1,0:T(8,128)(2,1)S(1)} %get-tuple-element.67), channel_id=1, source_target_pairs={{0,4},{1,5},{2,6},{3,7},{4,0},{5,1},{6,2},{7,3},{8,12},{9,13},{10,... | collective-permute-start | bytes 196616 | tf_op jit(solution)/shard_map/ppermute | solution.py:145
  74.9 2.5 %collective-permute-start.26 = (bf16[32,1024]{1,0:T(8,128)(2,1)S(1)}, bf16[32,1024]{1,0:T(8,128)(2,1)S(1)}, u32[]{:S(2)}, u32[]{:S(2)}) collective-permute-start(bf16[32,1024]{1,0:T(8,128)(2,1)S(1)} %get-tuple-element.69), channel_id=1, source_target_pairs={{0,8},{1,9},{2,10},{3,11},{4,12},{5,13},{6,14},{7,15},{8,0},{9,1},... | collective-permute-start | bytes 196616 | tf_op jit(solution)/shard_map/ppermute | solution.py:145
  80.2 2.4 %collective-permute-start.29 = (bf16[32,1024]{1,0:T(8,128)(2,1)S(1)}, bf16[32,1024]{1,0:T(8,128)(2,1)S(1)}, u32[]{:S(2)}, u32[]{:S(2)}) collective-permute-start(bf16[32,1024]{1,0:T(8,128)(2,1)S(1)} %get-tuple-element.72), channel_id=1, source_target_pairs={{0,14},{1,15},{2,12},{3,13},{4,10},{5,11},{6,8},{7,9},{8,6},{9,7},... | collective-permute-start | bytes 196616 | tf_op jit(solution)/shard_map/ppermute | solution.py:145
  83.8 4.2 %collective-permute-done.27.refs_5_ = bf16[32,1024]{1,0:T(8,128)(2,1)S(1)} collective-permute-done((bf16[32,1024]{1,0:T(8,128)(2,1)S(1)}, bf16[32,1024]{1,0:T(8,128)(2,1)S(1)}, u32[]{:S(2)}, u32[]{:S(2)}) %collective-permute-start.27) | collective-permute-done | bytes 65568 | tf_op jit(solution)/shard_map/ppermute | solution.py:145
  (53 shorter events, 19.7 us)
Async XLA Ops:
  3.5 8.9 %collective-permute-start = (bf16[272,128]{1,0:T(8,128)(2,1)S(1)}, bf16[272,128]{1,0:T(8,128)(2,1)S(1)}, u32[]{:S(2)}, u32[]{:S(2)}) collective-permute-start(bf16[272,128]{1,0:T(8,128)(2,1)S(1)} %get-tuple-element.40), channel_id=1, source_target_pairs={{0,2},{1,3},{2,0},{3,1},{4,6},{5,7},{6,4},{7,5},{8,10},{9,11},{10,... | collective-permute-start | bytes 208904 | tf_op jit(solution)/shard_map/ppermute | solution.py:145
  6.5 9.5 %collective-permute-start.1 = (bf16[272,128]{1,0:T(8,128)(2,1)S(1)}, bf16[272,128]{1,0:T(8,128)(2,1)S(1)}, u32[]{:S(2)}, u32[]{:S(2)}) collective-permute-start(bf16[272,128]{1,0:T(8,128)(2,1)S(1)} %get-tuple-element.41), channel_id=1, source_target_pairs={{0,4},{1,5},{2,6},{3,7},{4,0},{5,1},{6,2},{7,3},{8,12},{9,13},{10,... | collective-permute-start | bytes 208904 | tf_op jit(solution)/shard_map/ppermute | solution.py:145
  8.1 7.9 %collective-permute-start.2 = (bf16[272,128]{1,0:T(8,128)(2,1)S(1)}, bf16[272,128]{1,0:T(8,128)(2,1)S(1)}, u32[]{:S(2)}, u32[]{:S(2)}) collective-permute-start(bf16[272,128]{1,0:T(8,128)(2,1)S(1)} %get-tuple-element.42), channel_id=1, source_target_pairs={{0,6},{1,7},{2,4},{3,5},{4,2},{5,3},{6,0},{7,1},{8,14},{9,15},{10,... | collective-permute-start | bytes 208904 | tf_op jit(solution)/shard_map/ppermute | solution.py:145
  8.1 7.9 %collective-permute-start.3 = (bf16[272,128]{1,0:T(8,128)(2,1)S(1)}, bf16[272,128]{1,0:T(8,128)(2,1)S(1)}, u32[]{:S(2)}, u32[]{:S(2)}) collective-permute-start(bf16[272,128]{1,0:T(8,128)(2,1)S(1)} %get-tuple-element.43), channel_id=1, source_target_pairs={{0,8},{1,9},{2,10},{3,11},{4,12},{5,13},{6,14},{7,15},{8,0},{9,1},... | collective-permute-start | bytes 208904 | tf_op jit(solution)/shard_map/ppermute | solution.py:145
  11.1 10.7 %collective-permute-start.4 = (bf16[272,128]{1,0:T(8,128)(2,1)S(1)}, bf16[272,128]{1,0:T(8,128)(2,1)S(1)}, u32[]{:S(2)}, u32[]{:S(2)}) collective-permute-start(bf16[272,128]{1,0:T(8,128)(2,1)S(1)} %get-tuple-element.44), channel_id=1, source_target_pairs={{0,10},{1,11},{2,8},{3,9},{4,14},{5,15},{6,12},{7,13},{8,2},{9,3},... | collective-permute-start | bytes 208904 | tf_op jit(solution)/shard_map/ppermute | solution.py:145
  12.4 9.4 %collective-permute-start.5 = (bf16[272,128]{1,0:T(8,128)(2,1)S(1)}, bf16[272,128]{1,0:T(8,128)(2,1)S(1)}, u32[]{:S(2)}, u32[]{:S(2)}) collective-permute-start(bf16[272,128]{1,0:T(8,128)(2,1)S(1)} %get-tuple-element.45), channel_id=1, source_target_pairs={{0,12},{1,13},{2,14},{3,15},{4,8},{5,9},{6,10},{7,11},{8,4},{9,5},... | collective-permute-start | bytes 208904 | tf_op jit(solution)/shard_map/ppermute | solution.py:145
  28.7 8.8 %collective-permute-start.9 = (bf16[32,1024]{1,0:T(8,128)(2,1)S(1)}, bf16[32,1024]{1,0:T(8,128)(2,1)S(1)}, u32[]{:S(2)}, u32[]{:S(2)}) collective-permute-start(bf16[32,1024]{1,0:T(8,128)(2,1)S(1)} %get-tuple-element.49), channel_id=1, source_target_pairs={{0,4},{1,5},{2,6},{3,7},{4,0},{5,1},{6,2},{7,3},{8,12},{9,13},{10,... | collective-permute-start | bytes 196616 | tf_op jit(solution)/shard_map/ppermute | solution.py:145
  31.3 8.5 %collective-permute-start.10 = (bf16[32,1024]{1,0:T(8,128)(2,1)S(1)}, bf16[32,1024]{1,0:T(8,128)(2,1)S(1)}, u32[]{:S(2)}, u32[]{:S(2)}) collective-permute-start(bf16[32,1024]{1,0:T(8,128)(2,1)S(1)} %get-tuple-element.50), channel_id=1, source_target_pairs={{0,6},{1,7},{2,4},{3,5},{4,2},{5,3},{6,0},{7,1},{8,14},{9,15},{10,... | collective-permute-start | bytes 196616 | tf_op jit(solution)/shard_map/ppermute | solution.py:145
  32.0 10.3 %collective-permute-start.11 = (bf16[32,1024]{1,0:T(8,128)(2,1)S(1)}, bf16[32,1024]{1,0:T(8,128)(2,1)S(1)}, u32[]{:S(2)}, u32[]{:S(2)}) collective-permute-start(bf16[32,1024]{1,0:T(8,128)(2,1)S(1)} %get-tuple-element.51), channel_id=1, source_target_pairs={{0,8},{1,9},{2,10},{3,11},{4,12},{5,13},{6,14},{7,15},{8,0},{9,1},... | collective-permute-start | bytes 196616 | tf_op jit(solution)/shard_map/ppermute | solution.py:145
  35.1 9.8 %collective-permute-start.12 = (bf16[32,1024]{1,0:T(8,128)(2,1)S(1)}, bf16[32,1024]{1,0:T(8,128)(2,1)S(1)}, u32[]{:S(2)}, u32[]{:S(2)}) collective-permute-start(bf16[32,1024]{1,0:T(8,128)(2,1)S(1)} %get-tuple-element.52), channel_id=1, source_target_pairs={{0,10},{1,11},{2,8},{3,9},{4,14},{5,15},{6,12},{7,13},{8,2},{9,3},... | collective-permute-start | bytes 196616 | tf_op jit(solution)/shard_map/ppermute | solution.py:145
  35.1 9.8 %collective-permute-start.13 = (bf16[32,1024]{1,0:T(8,128)(2,1)S(1)}, bf16[32,1024]{1,0:T(8,128)(2,1)S(1)}, u32[]{:S(2)}, u32[]{:S(2)}) collective-permute-start(bf16[32,1024]{1,0:T(8,128)(2,1)S(1)} %get-tuple-element.53), channel_id=1, source_target_pairs={{0,12},{1,13},{2,14},{3,15},{4,8},{5,9},{6,10},{7,11},{8,4},{9,5},... | collective-permute-start | bytes 196616 | tf_op jit(solution)/shard_map/ppermute | solution.py:145
  50.3 7.9 %collective-permute-start.15 = (bf16[32,1024]{1,0:T(8,128)(2,1)S(1)}, bf16[32,1024]{1,0:T(8,128)(2,1)S(1)}, u32[]{:S(2)}, u32[]{:S(2)}) collective-permute-start(bf16[32,1024]{1,0:T(8,128)(2,1)S(1)} %get-tuple-element.58), channel_id=1, source_target_pairs={{0,2},{1,3},{2,0},{3,1},{4,6},{5,7},{6,4},{7,5},{8,10},{9,11},{10,... | collective-permute-start | bytes 196616 | tf_op jit(solution)/shard_map/ppermute | solution.py:145
  51.4 9.2 %collective-permute-start.16 = (bf16[32,1024]{1,0:T(8,128)(2,1)S(1)}, bf16[32,1024]{1,0:T(8,128)(2,1)S(1)}, u32[]{:S(2)}, u32[]{:S(2)}) collective-permute-start(bf16[32,1024]{1,0:T(8,128)(2,1)S(1)} %get-tuple-element.59), channel_id=1, source_target_pairs={{0,4},{1,5},{2,6},{3,7},{4,0},{5,1},{6,2},{7,3},{8,12},{9,13},{10,... | collective-permute-start | bytes 196616 | tf_op jit(solution)/shard_map/ppermute | solution.py:145
  54.4 8.2 %collective-permute-start.17 = (bf16[32,1024]{1,0:T(8,128)(2,1)S(1)}, bf16[32,1024]{1,0:T(8,128)(2,1)S(1)}, u32[]{:S(2)}, u32[]{:S(2)}) collective-permute-start(bf16[32,1024]{1,0:T(8,128)(2,1)S(1)} %get-tuple-element.60), channel_id=1, source_target_pairs={{0,6},{1,7},{2,4},{3,5},{4,2},{5,3},{6,0},{7,1},{8,14},{9,15},{10,... | collective-permute-start | bytes 196616 | tf_op jit(solution)/shard_map/ppermute | solution.py:145
  54.9 10.4 %collective-permute-start.18 = (bf16[32,1024]{1,0:T(8,128)(2,1)S(1)}, bf16[32,1024]{1,0:T(8,128)(2,1)S(1)}, u32[]{:S(2)}, u32[]{:S(2)}) collective-permute-start(bf16[32,1024]{1,0:T(8,128)(2,1)S(1)} %get-tuple-element.61), channel_id=1, source_target_pairs={{0,8},{1,9},{2,10},{3,11},{4,12},{5,13},{6,14},{7,15},{8,0},{9,1},... | collective-permute-start | bytes 196616 | tf_op jit(solution)/shard_map/ppermute | solution.py:145
  57.4 10.2 %collective-permute-start.19 = (bf16[32,1024]{1,0:T(8,128)(2,1)S(1)}, bf16[32,1024]{1,0:T(8,128)(2,1)S(1)}, u32[]{:S(2)}, u32[]{:S(2)}) collective-permute-start(bf16[32,1024]{1,0:T(8,128)(2,1)S(1)} %get-tuple-element.62), channel_id=1, source_target_pairs={{0,10},{1,11},{2,8},{3,9},{4,14},{5,15},{6,12},{7,13},{8,2},{9,3},... | collective-permute-start | bytes 196616 | tf_op jit(solution)/shard_map/ppermute | solution.py:145
  58.2 9.4 %collective-permute-start.20 = (bf16[32,1024]{1,0:T(8,128)(2,1)S(1)}, bf16[32,1024]{1,0:T(8,128)(2,1)S(1)}, u32[]{:S(2)}, u32[]{:S(2)}) collective-permute-start(bf16[32,1024]{1,0:T(8,128)(2,1)S(1)} %get-tuple-element.63), channel_id=1, source_target_pairs={{0,12},{1,13},{2,14},{3,15},{4,8},{5,9},{6,10},{7,11},{8,4},{9,5},... | collective-permute-start | bytes 196616 | tf_op jit(solution)/shard_map/ppermute | solution.py:145
  70.4 8.0 %collective-permute-start.23 = (bf16[32,1024]{1,0:T(8,128)(2,1)S(1)}, bf16[32,1024]{1,0:T(8,128)(2,1)S(1)}, u32[]{:S(2)}, u32[]{:S(2)}) collective-permute-start(bf16[32,1024]{1,0:T(8,128)(2,1)S(1)} %get-tuple-element.66), channel_id=1, source_target_pairs={{0,2},{1,3},{2,0},{3,1},{4,6},{5,7},{6,4},{7,5},{8,10},{9,11},{10,... | collective-permute-start | bytes 196616 | tf_op jit(solution)/shard_map/ppermute | solution.py:145
  71.8 8.4 %collective-permute-start.24 = (bf16[32,1024]{1,0:T(8,128)(2,1)S(1)}, bf16[32,1024]{1,0:T(8,128)(2,1)S(1)}, u32[]{:S(2)}, u32[]{:S(2)}) collective-permute-start(bf16[32,1024]{1,0:T(8,128)(2,1)S(1)} %get-tuple-element.67), channel_id=1, source_target_pairs={{0,4},{1,5},{2,6},{3,7},{4,0},{5,1},{6,2},{7,3},{8,12},{9,13},{10,... | collective-permute-start | bytes 196616 | tf_op jit(solution)/shard_map/ppermute | solution.py:145
  74.6 8.0 %collective-permute-start.25 = (bf16[32,1024]{1,0:T(8,128)(2,1)S(1)}, bf16[32,1024]{1,0:T(8,128)(2,1)S(1)}, u32[]{:S(2)}, u32[]{:S(2)}) collective-permute-start(bf16[32,1024]{1,0:T(8,128)(2,1)S(1)} %get-tuple-element.68), channel_id=1, source_target_pairs={{0,6},{1,7},{2,4},{3,5},{4,2},{5,3},{6,0},{7,1},{8,14},{9,15},{10,... | collective-permute-start | bytes 196616 | tf_op jit(solution)/shard_map/ppermute | solution.py:145
  74.9 8.9 %collective-permute-start.26 = (bf16[32,1024]{1,0:T(8,128)(2,1)S(1)}, bf16[32,1024]{1,0:T(8,128)(2,1)S(1)}, u32[]{:S(2)}, u32[]{:S(2)}) collective-permute-start(bf16[32,1024]{1,0:T(8,128)(2,1)S(1)} %get-tuple-element.69), channel_id=1, source_target_pairs={{0,8},{1,9},{2,10},{3,11},{4,12},{5,13},{6,14},{7,15},{8,0},{9,1},... | collective-permute-start | bytes 196616 | tf_op jit(solution)/shard_map/ppermute | solution.py:145
  77.4 10.6 %collective-permute-start.27 = (bf16[32,1024]{1,0:T(8,128)(2,1)S(1)}, bf16[32,1024]{1,0:T(8,128)(2,1)S(1)}, u32[]{:S(2)}, u32[]{:S(2)}) collective-permute-start(bf16[32,1024]{1,0:T(8,128)(2,1)S(1)} %get-tuple-element.70), channel_id=1, source_target_pairs={{0,10},{1,11},{2,8},{3,9},{4,14},{5,15},{6,12},{7,13},{8,2},{9,3},... | collective-permute-start | bytes 196616 | tf_op jit(solution)/shard_map/ppermute | solution.py:145
  78.4 9.6 %collective-permute-start.28 = (bf16[32,1024]{1,0:T(8,128)(2,1)S(1)}, bf16[32,1024]{1,0:T(8,128)(2,1)S(1)}, u32[]{:S(2)}, u32[]{:S(2)}) collective-permute-start(bf16[32,1024]{1,0:T(8,128)(2,1)S(1)} %get-tuple-element.71), channel_id=1, source_target_pairs={{0,12},{1,13},{2,14},{3,15},{4,8},{5,9},{6,10},{7,11},{8,4},{9,5},... | collective-permute-start | bytes 196616 | tf_op jit(solution)/shard_map/ppermute | solution.py:145
  80.2 7.8 %collective-permute-start.29 = (bf16[32,1024]{1,0:T(8,128)(2,1)S(1)}, bf16[32,1024]{1,0:T(8,128)(2,1)S(1)}, u32[]{:S(2)}, u32[]{:S(2)}) collective-permute-start(bf16[32,1024]{1,0:T(8,128)(2,1)S(1)} %get-tuple-element.72), channel_id=1, source_target_pairs={{0,14},{1,15},{2,12},{3,13},{4,10},{5,11},{6,8},{7,9},{8,6},{9,7},... | collective-permute-start | bytes 196616 | tf_op jit(solution)/shard_map/ppermute | solution.py:145
  (11 other events, 81.0 us)

commit v3 on v2

v3 whole, which is shorter than its diff:
```python
import functools

import jax
import jax.numpy as jnp
from jax import lax
from jax.experimental import pallas as pl
from jax.experimental.pallas import tpu as pltpu
from jax.sharding import PartitionSpec as P

F32 = jnp.float32
BF16 = jnp.bfloat16
LANES = 128
ID_ROWS = 16
VMEM = pl.BlockSpec(memory_space=pltpu.VMEM)
HBM = pl.BlockSpec(memory_space=pltpu.HBM)
SMEM = pl.BlockSpec(memory_space=pltpu.SMEM)
PARAMS = pltpu.CompilerParams(vmem_limit_bytes=48 * 1024 * 1024)


def position():
    me = lax.axis_index("fsdp")
    return me // 2, me % 2


def offsets(m):
    return [0, *range(m - 1, 0, -1)]


def columns(chunk, w):
    return pl.ds(pl.multiple_of(chunk * w, w), w)


def pack_kernel(m, id_ref, storage_ref, down_hbm, up_hbm, *refs):
    outs, down_ref, up_ref, sems = refs[:m], *refs[m:]
    p, _ = position()
    loads = [
        pltpu.make_async_copy(down_hbm, down_ref, sems.at[0]),
        pltpu.make_async_copy(up_hbm, up_ref, sems.at[1]),
    ]
    for load in loads:
        load.start()
    for load in loads:
        load.wait()
    r, w = down_ref.shape[1], down_ref.shape[2] // m
    mark = jnp.full((ID_ROWS, LANES), storage_ref[id_ref[0]].astype(F32), F32).astype(BF16)
    for out, k in zip(outs, offsets(m)):
        for b in range(w // LANES):
            cols = pl.ds(pl.multiple_of((p ^ k) * w + b * LANES, LANES), LANES)
            out[2 * r * b : 2 * r * b + r, :] = down_ref[0, :, cols]
            out[2 * r * b + r : 2 * r * (b + 1), :] = up_ref[0, :, cols]
        out[2 * r * (w // LANES) :, :] = mark


def stack_kernel(*refs):
    *blocks, held_ref = refs
    for block, k in zip(blocks, offsets(len(blocks))):
        held_ref[k] = block[...]


def stack(blocks):
    return pl.pallas_call(
        stack_kernel,
        out_shape=jax.ShapeDtypeStruct((len(blocks), *blocks[0].shape), BF16),
        in_specs=[VMEM] * len(blocks),
        out_specs=VMEM,
        compiler_params=PARAMS,
    )(*blocks)


def slot_of(ref, k):
    return ref[k, ref.shape[1] - ID_ROWS :, :].astype(F32)[0, 0].astype(jnp.int32)


def deliver_kernel(m, own_ref, other_ref, *outs):
    p, c = position()
    r2 = outs[0].shape[0]
    blocks = (own_ref.shape[1] - ID_ROWS) // r2
    slots = [slot_of(own_ref, k) for k in offsets(m)]
    for out, slot in zip(outs, slots):
        at, here = (slot // 2) ^ p, slot % 2 == c
        for b in range(blocks):
            rows = slice(b * r2, (b + 1) * r2)
            out[:, b * LANES : (b + 1) * LANES] = jnp.where(
                here, own_ref[at, rows, :], other_ref[at, rows, :]
            )


def inverse_kernel(m, own_ref, other_ref, tile_of):
    p, c = position()
    for ref, core in ((own_ref, c), (other_ref, 1 - c)):
        slots = [slot_of(ref, k) for k in range(m)]
        for k, slot in enumerate(slots):
            tile_of[slot] = 2 * (p ^ k) + core


def grads_kernel(m, acts_ref, cot_ref, *refs):
    factors, low_ref, outs = refs[:m], refs[m], refs[m + 1 :]
    p, _ = position()
    r2, w = factors[0].shape
    r = r2 // 2
    rows = acts_ref.shape[0]
    dims_nt = (((1,), (1,)), ((), ()))
    low_u = jnp.zeros((r, rows), F32)
    low_h = jnp.zeros((r, rows), F32)
    for factor, k in zip(factors, offsets(m)):
        cols = columns(p ^ k, w)
        low_u += lax.dot_general(factor[0:r, :], acts_ref[:, cols], dims_nt, preferred_element_type=F32)
        low_h += lax.dot_general(factor[r:r2, :], cot_ref[:, cols], dims_nt, preferred_element_type=F32)
    low_u = low_u.astype(BF16)
    low_h = low_h.astype(BF16)
    low_ref[...] = low_h
    for out, k in zip(outs, offsets(m)):
        cols = columns(p ^ k, w)
        out[0:r, :] = jnp.dot(low_h, acts_ref[:, cols], preferred_element_type=F32).astype(BF16)
        out[r:r2, :] = jnp.dot(low_u, cot_ref[:, cols], preferred_element_type=F32).astype(BF16)


def inputs_kernel(m, low_ref, *refs):
    factors, gx_ref = refs[:m], refs[m]
    p, _ = position()
    r2, w = factors[0].shape
    for factor, k in zip(factors, offsets(m)):
        gx_ref[:, columns(p ^ k, w)] = lax.dot_general(
            low_ref[...], factor[0 : r2 // 2, :], (((0,), (0,)), ((), ())), preferred_element_type=F32
        ).astype(BF16)


def collect_kernel(m, tile_of, own_ref, other_ref, *outs):
    p, c = position()
    for out, k in zip(outs, offsets(m)):
        tile = tile_of[2 * (p ^ k) + c]
        at, here = (tile // 2) ^ p, tile % 2 == c
        out[...] = jnp.where(here, own_ref[at], other_ref[at])


def unpack_kernel(m, *refs):
    ga_ref, gb_ref = refs[m:]
    p, _ = position()
    r2, w = refs[0].shape
    for block, k in zip(refs, offsets(m)):
        cols = columns(p ^ k, w)
        ga_ref[0, :, cols] = block[0 : r2 // 2, :]
        gb_ref[0, :, cols] = block[r2 // 2 : r2, :]


def shards(acts, cotangent, down, up, adapter_per_tile, adapter_storage_slot):
    n = lax.axis_size("fsdp")
    m = n // 2
    _, r, d = down.shape
    w = d // m

    def exchange(blocks):
        return [blocks[0]] + [
            lax.ppermute(
                block, "fsdp", [(2 * p + c, 2 * (p ^ k) + c) for p in range(m) for c in range(2)]
            )
            for block, k in zip(blocks[1:], offsets(m)[1:])
        ]

    def to_other_core(block):
        return lax.ppermute(block, "fsdp", [(f, f ^ 1) for f in range(n)])

    rows = 2 * r * w // LANES
    flat = jax.ShapeDtypeStruct((rows + ID_ROWS, LANES), BF16)
    wide = jax.ShapeDtypeStruct((2 * r, w), BF16)
    spread = pl.pallas_call(
        functools.partial(pack_kernel, m),
        out_shape=[flat] * m,
        in_specs=[SMEM, SMEM, HBM, HBM],
        out_specs=[VMEM] * m,
        scratch_shapes=[
            pltpu.VMEM(down.shape, BF16),
            pltpu.VMEM(up.shape, BF16),
            pltpu.SemaphoreType.DMA((2,)),
        ],
        compiler_params=PARAMS,
    )(adapter_per_tile, adapter_storage_slot, down, up)
    own = stack(exchange(spread))
    other = to_other_core(own)
    factors = pl.pallas_call(
        functools.partial(deliver_kernel, m),
        out_shape=[wide] * m,
        in_specs=[VMEM, VMEM],
        out_specs=[VMEM] * m,
        compiler_params=PARAMS,
    )(own, other)
    factors = exchange(factors)
    tile_of = pl.pallas_call(
        functools.partial(inverse_kernel, m),
        out_shape=jax.ShapeDtypeStruct((n,), jnp.int32),
        in_specs=[VMEM, VMEM],
        out_specs=SMEM,
        compiler_params=PARAMS,
    )(own, other)
    low, *parts = pl.pallas_call(
        functools.partial(grads_kernel, m),
        out_shape=[jax.ShapeDtypeStruct((r, acts.shape[0]), BF16)] + [wide] * m,
        in_specs=[VMEM] * (m + 2),
        out_specs=[VMEM] * (m + 1),
        compiler_params=PARAMS,
    )(acts, cotangent, *factors)
    parts = exchange(parts)
    grad_x = pl.pallas_call(
        functools.partial(inputs_kernel, m),
        out_shape=jax.ShapeDtypeStruct(acts.shape, BF16),
        in_specs=[VMEM] * (m + 1),
        out_specs=VMEM,
        compiler_params=PARAMS,
        cost_estimate=pl.CostEstimate(
            flops=2 * r * acts.size, bytes_accessed=2 * acts.size, transcendentals=0
        ),
    )(low, *factors)
    own = stack(parts)
    owned = pl.pallas_call(
        functools.partial(collect_kernel, m),
        out_shape=[wide] * m,
        in_specs=[SMEM, VMEM, VMEM],
        out_specs=[VMEM] * m,
        compiler_params=PARAMS,
    )(tile_of, own, to_other_core(own))
    grad_a, grad_b = pl.pallas_call(
        functools.partial(unpack_kernel, m),
        out_shape=[jax.ShapeDtypeStruct(down.shape, BF16)] * 2,
        in_specs=[VMEM] * m,
        out_specs=[VMEM] * 2,
        compiler_params=PARAMS,
    )(*exchange(owned))
    return grad_x, grad_a, grad_b


def solution(mesh):
    placed = (
        P(("group", "fsdp"), None),
        P(("group", "fsdp"), None),
        P("fsdp", None, None),
        P("fsdp", None, None),
        P(("group", "fsdp")),
        P(),
    )
    return jax.shard_map(
        shards,
        mesh=mesh,
        in_specs=placed,
        out_specs=(
            P(("group", "fsdp"), None),
            P(("group", "fsdp"), None, None),
            P(("group", "fsdp"), None, None),
        ),
        check_vma=False,
    )
```

time: 89 us -> 81.2 us (0.912)
  waiting for transfers between devices: 26.5 us -> 15.9 us
  starting transfers between devices: 48.8 us -> 52.4 us
    ppermute x28, waiting for transfers between devices: 22.6 us -> 12.7 us  [exchange(): lax.ppermute(block, 'fsdp', [(2 * p + c, 2 * (p ^ k) + c) for p in range(...]
    ppermute x28, starting transfers between devices: 48.6 us -> 52.2 us  [exchange(): lax.ppermute(block, 'fsdp', [(2 * p + c, 2 * (p ^ k) + c) for p in range(...]
    pallas_call x0 -> x2, Pallas kernels: none -> 2.71 us  [the longest x1 2.05 us: shards(): pl.pallas_call(functools.partial(inputs_kernel, m), out_shape=jax.ShapeDt...]
    pallas_call x1, Pallas kernels: 2.31 us -> 0.22 us  [shards(): pl.pallas_call(functools.partial(deliver_kernel, m), out_shape=[wide] * m...]
    pallas_call x1, Pallas kernels: 3.82 us -> 1.84 us  [shards(): pl.pallas_call(functools.partial(grads_kernel, m), out_shape=[jax.ShapeDt...]
  transfers between devices with their start and end apart: 30 -> 30, of which waited for: 10 -> 16; matrix products, arithmetic and copies ran while one was open for 0% -> 0% of each run, Pallas kernels for 0% -> 3%
where the time goes in v3:
time: 81.2 us; the launch traced here: 81 us
  starting transfers between devices  52.4 us (65%)
  waiting for transfers between devices  15.9 us (20%)
  Pallas kernels  7.05 us (9%)
  local copies, waits for them, and re-layouts  4.14 us (5%)
  between operations  1.54 us (2%)
    ppermute x28, starting transfers between devices, exchange(): lax.ppermute(block, 'fsdp', [(2 * p + c, 2 * (p ^ k) + c) for p in range(...  52.2 us
    ppermute x28, waiting for transfers between devices, exchange(): lax.ppermute(block, 'fsdp', [(2 * p + c, 2 * (p ^ k) + c) for p in range(...  12.7 us
    unnamed x10, local copies, waits for them, and re-layouts  4.14 us
    ppermute x2, waiting for transfers between devices, to_other_core(): return lax.ppermute(block, 'fsdp', [(f, f ^ 1) for f in range(n)])  3.17 us
    pallas_call x1, Pallas kernels, shards(): pl.pallas_call(functools.partial(inputs_kernel, m), out_shape=jax.ShapeDt...  2.05 us
    pallas_call x1, Pallas kernels, shards(): pl.pallas_call(functools.partial(grads_kernel, m), out_shape=[jax.ShapeDt...  1.84 us
  transfers between devices with their start and end apart: 30, of which 16 were waited for; matrix products, arithmetic and copies ran while one was open for 0% of the time, Pallas kernels for 3%

profile of v3, /device:TPU:0, one launch (start us, length us, event | category | flops | bytes accessed | tf_op | source)
XLA Modules:
  0.0 81.0 jit_solution(16296779540403718199)
XLA Ops:
  4.7 6.1 %collective-permute-start = (bf16[272,128]{1,0:T(8,128)(2,1)S(1)}, bf16[272,128]{1,0:T(8,128)(2,1)S(1)}, u32[]{:S(2)}, u32[]{:S(2)}) collective-permute-start(bf16[272,128]{1,0:T(8,128)(2,1)S(1)} %get-tuple-element.39), channel_id=1, source_target_pairs={{0,14},{1,15},{2,12},{3,13},{4,10},{5,11},{6,8},{7,9},{8,6},{9,7},... | collective-permute-start | bytes 208904 | tf_op jit(solution)/shard_map/ppermute | solution.py:154
  11.8 2.0 %collective-permute-start.3 = (bf16[272,128]{1,0:T(8,128)(2,1)S(1)}, bf16[272,128]{1,0:T(8,128)(2,1)S(1)}, u32[]{:S(2)}, u32[]{:S(2)}) collective-permute-start(bf16[272,128]{1,0:T(8,128)(2,1)S(1)} %get-tuple-element.42), channel_id=1, source_target_pairs={{0,8},{1,9},{2,10},{3,11},{4,12},{5,13},{6,14},{7,15},{8,0},{9,1},... | collective-permute-start | bytes 208904 | tf_op jit(solution)/shard_map/ppermute | solution.py:154
  13.8 2.3 %collective-permute-start.4 = (bf16[272,128]{1,0:T(8,128)(2,1)S(1)}, bf16[272,128]{1,0:T(8,128)(2,1)S(1)}, u32[]{:S(2)}, u32[]{:S(2)}) collective-permute-start(bf16[272,128]{1,0:T(8,128)(2,1)S(1)} %get-tuple-element.43), channel_id=1, source_target_pairs={{0,6},{1,7},{2,4},{3,5},{4,2},{5,3},{6,0},{7,1},{8,14},{9,15},{10,... | collective-permute-start | bytes 208904 | tf_op jit(solution)/shard_map/ppermute | solution.py:154
  18.1 3.7 %collective-permute-done.2.refs_3_ = bf16[272,128]{1,0:T(8,128)(2,1)S(1)} collective-permute-done((bf16[272,128]{1,0:T(8,128)(2,1)S(1)}, bf16[272,128]{1,0:T(8,128)(2,1)S(1)}, u32[]{:S(2)}, u32[]{:S(2)}) %collective-permute-start.2) | collective-permute-done | bytes 69664 | tf_op jit(solution)/shard_map/ppermute | solution.py:154
  22.9 1.9 %collective-permute-done.7.other_ref = bf16[8,272,128]{2,1,0:T(8,128)(2,1)S(1)} collective-permute-done((bf16[8,272,128]{2,1,0:T(8,128)(2,1)S(1)}, bf16[8,272,128]{2,1,0:T(8,128)(2,1)S(1)}, u32[]{:S(2)}, u32[]{:S(2)}) %collective-permute-start.7) | collective-permute-done | bytes 557088 | tf_op jit(solution)/shard_map/ppermute | solution.py:161
  25.1 4.4 %collective-permute-start.8 = (bf16[32,1024]{1,0:T(8,128)(2,1)S(1)}, bf16[32,1024]{1,0:T(8,128)(2,1)S(1)}, u32[]{:S(2)}, u32[]{:S(2)}) collective-permute-start(bf16[32,1024]{1,0:T(8,128)(2,1)S(1)} %get-tuple-element.47), channel_id=1, source_target_pairs={{0,14},{1,15},{2,12},{3,13},{4,10},{5,11},{6,8},{7,9},{8,6},{9,7},... | collective-permute-start | bytes 196616 | tf_op jit(solution)/shard_map/ppermute | solution.py:154
  29.5 2.2 %collective-permute-start.10 = (bf16[32,1024]{1,0:T(8,128)(2,1)S(1)}, bf16[32,1024]{1,0:T(8,128)(2,1)S(1)}, u32[]{:S(2)}, u32[]{:S(2)}) collective-permute-start(bf16[32,1024]{1,0:T(8,128)(2,1)S(1)} %get-tuple-element.49), channel_id=1, source_target_pairs={{0,10},{1,11},{2,8},{3,9},{4,14},{5,15},{6,12},{7,13},{8,2},{9,3},... | collective-permute-start | bytes 196616 | tf_op jit(solution)/shard_map/ppermute | solution.py:154
  32.8 2.0 %collective-permute-start.12 = (bf16[32,1024]{1,0:T(8,128)(2,1)S(1)}, bf16[32,1024]{1,0:T(8,128)(2,1)S(1)}, u32[]{:S(2)}, u32[]{:S(2)}) collective-permute-start(bf16[32,1024]{1,0:T(8,128)(2,1)S(1)} %get-tuple-element.51), channel_id=1, source_target_pairs={{0,6},{1,7},{2,4},{3,5},{4,2},{5,3},{6,0},{7,1},{8,14},{9,15},{10,... | collective-permute-start | bytes 196616 | tf_op jit(solution)/shard_map/ppermute | solution.py:154
  34.8 1.8 %collective-permute-start.13 = (bf16[32,1024]{1,0:T(8,128)(2,1)S(1)}, bf16[32,1024]{1,0:T(8,128)(2,1)S(1)}, u32[]{:S(2)}, u32[]{:S(2)}) collective-permute-start(bf16[32,1024]{1,0:T(8,128)(2,1)S(1)} %get-tuple-element.52), channel_id=1, source_target_pairs={{0,4},{1,5},{2,6},{3,7},{4,0},{5,1},{6,2},{7,3},{8,12},{9,13},{10,... | collective-permute-start | bytes 196616 | tf_op jit(solution)/shard_map/ppermute | solution.py:154
  36.6 1.9 %collective-permute-start.14 = (bf16[32,1024]{1,0:T(8,128)(2,1)S(1)}, bf16[32,1024]{1,0:T(8,128)(2,1)S(1)}, u32[]{:S(2)}, u32[]{:S(2)}) collective-permute-start(bf16[32,1024]{1,0:T(8,128)(2,1)S(1)} %get-tuple-element.53), channel_id=1, source_target_pairs={{0,2},{1,3},{2,0},{3,1},{4,6},{5,7},{6,4},{7,5},{8,10},{9,11},{10,... | collective-permute-start | bytes 196616 | tf_op jit(solution)/shard_map/ppermute | solution.py:154
  38.5 2.0 %collective-permute-done.10.refs_3_ = bf16[32,1024]{1,0:T(8,128)(2,1)S(1)} collective-permute-done((bf16[32,1024]{1,0:T(8,128)(2,1)S(1)}, bf16[32,1024]{1,0:T(8,128)(2,1)S(1)}, u32[]{:S(2)}, u32[]{:S(2)}) %collective-permute-start.10) | collective-permute-done | bytes 65568 | tf_op jit(solution)/shard_map/ppermute | solution.py:154
  41.4 1.6 %copy-done.1 = bf16[128,8192]{1,0:T(8,128)(2,1)S(1)} copy-done((bf16[128,8192]{1,0:T(8,128)(2,1)S(1)}, bf16[128,8192]{1,0:T(8,128)(2,1)}, u32[]{:S(2)}) %copy-start.1) | copy-done | bytes 2097176
  42.9 1.8 %shard_map.88 = (bf16[16,128]{1,0:T(8,128)(2,1)S(1)}, bf16[32,1024]{1,0:T(8,128)(2,1)S(1)}, bf16[32,1024]{1,0:T(8,128)(2,1)S(1)}, bf16[32,1024]{1,0:T(8,128)(2,1...) custom-call(bf16[128,8192]{1,0:T(8,128)(2,1)S(1)} %copy-done, ...), custom_call_target="tpu_custom_call" | custom-call | tf_op jit(solution)/shard_map/pallas_call | solution.py:195
  44.8 4.6 %collective-permute-start.15 = (bf16[32,1024]{1,0:T(8,128)(2,1)S(1)}, bf16[32,1024]{1,0:T(8,128)(2,1)S(1)}, u32[]{:S(2)}, u32[]{:S(2)}) collective-permute-start(bf16[32,1024]{1,0:T(8,128)(2,1)S(1)} %get-tuple-element.56), channel_id=1, source_target_pairs={{0,14},{1,15},{2,12},{3,13},{4,10},{5,11},{6,8},{7,9},{8,6},{9,7},... | collective-permute-start | bytes 196616 | tf_op jit(solution)/shard_map/ppermute | solution.py:154
  49.5 1.8 %collective-permute-start.17 = (bf16[32,1024]{1,0:T(8,128)(2,1)S(1)}, bf16[32,1024]{1,0:T(8,128)(2,1)S(1)}, u32[]{:S(2)}, u32[]{:S(2)}) collective-permute-start(bf16[32,1024]{1,0:T(8,128)(2,1)S(1)} %get-tuple-element.58), channel_id=1, source_target_pairs={{0,10},{1,11},{2,8},{3,9},{4,14},{5,15},{6,12},{7,13},{8,2},{9,3},... | collective-permute-start | bytes 196616 | tf_op jit(solution)/shard_map/ppermute | solution.py:154
  51.3 1.7 %collective-permute-start.18 = (bf16[32,1024]{1,0:T(8,128)(2,1)S(1)}, bf16[32,1024]{1,0:T(8,128)(2,1)S(1)}, u32[]{:S(2)}, u32[]{:S(2)}) collective-permute-start(bf16[32,1024]{1,0:T(8,128)(2,1)S(1)} %get-tuple-element.59), channel_id=1, source_target_pairs={{0,8},{1,9},{2,10},{3,11},{4,12},{5,13},{6,14},{7,15},{8,0},{9,1},... | collective-permute-start | bytes 196616 | tf_op jit(solution)/shard_map/ppermute | solution.py:154
  53.1 1.6 %collective-permute-start.19 = (bf16[32,1024]{1,0:T(8,128)(2,1)S(1)}, bf16[32,1024]{1,0:T(8,128)(2,1)S(1)}, u32[]{:S(2)}, u32[]{:S(2)}) collective-permute-start(bf16[32,1024]{1,0:T(8,128)(2,1)S(1)} %get-tuple-element.60), channel_id=1, source_target_pairs={{0,6},{1,7},{2,4},{3,5},{4,2},{5,3},{6,0},{7,1},{8,14},{9,15},{10,... | collective-permute-start | bytes 196616 | tf_op jit(solution)/shard_map/ppermute | solution.py:154
  55.8 1.6 %collective-permute-start.21 = (bf16[32,1024]{1,0:T(8,128)(2,1)S(1)}, bf16[32,1024]{1,0:T(8,128)(2,1)S(1)}, u32[]{:S(2)}, u32[]{:S(2)}) collective-permute-start(bf16[32,1024]{1,0:T(8,128)(2,1)S(1)} %get-tuple-element.62), channel_id=1, source_target_pairs={{0,2},{1,3},{2,0},{3,1},{4,6},{5,7},{6,4},{7,5},{8,10},{9,11},{10,... | collective-permute-start | bytes 196616 | tf_op jit(solution)/shard_map/ppermute | solution.py:154
  57.4 2.6 %collective-permute-done.17.refs_3_ = bf16[32,1024]{1,0:T(8,128)(2,1)S(1)} collective-permute-done((bf16[32,1024]{1,0:T(8,128)(2,1)S(1)}, bf16[32,1024]{1,0:T(8,128)(2,1)S(1)}, u32[]{:S(2)}, u32[]{:S(2)}) %collective-permute-start.17) | collective-permute-done | bytes 65568 | tf_op jit(solution)/shard_map/ppermute | solution.py:154
  63.1 4.1 %collective-permute-start.23 = (bf16[32,1024]{1,0:T(8,128)(2,1)S(1)}, bf16[32,1024]{1,0:T(8,128)(2,1)S(1)}, u32[]{:S(2)}, u32[]{:S(2)}) collective-permute-start(bf16[32,1024]{1,0:T(8,128)(2,1)S(1)} %get-tuple-element.64), channel_id=1, source_target_pairs={{0,14},{1,15},{2,12},{3,13},{4,10},{5,11},{6,8},{7,9},{8,6},{9,7},... | collective-permute-start | bytes 196616 | tf_op jit(solution)/shard_map/ppermute | solution.py:154
  67.7 2.0 %collective-permute-start.25 = (bf16[32,1024]{1,0:T(8,128)(2,1)S(1)}, bf16[32,1024]{1,0:T(8,128)(2,1)S(1)}, u32[]{:S(2)}, u32[]{:S(2)}) collective-permute-start(bf16[32,1024]{1,0:T(8,128)(2,1)S(1)} %get-tuple-element.66), channel_id=1, source_target_pairs={{0,10},{1,11},{2,8},{3,9},{4,14},{5,15},{6,12},{7,13},{8,2},{9,3},... | collective-permute-start | bytes 196616 | tf_op jit(solution)/shard_map/ppermute | solution.py:154
  69.6 1.5 %collective-permute-start.26 = (bf16[32,1024]{1,0:T(8,128)(2,1)S(1)}, bf16[32,1024]{1,0:T(8,128)(2,1)S(1)}, u32[]{:S(2)}, u32[]{:S(2)}) collective-permute-start(bf16[32,1024]{1,0:T(8,128)(2,1)S(1)} %get-tuple-element.67), channel_id=1, source_target_pairs={{0,8},{1,9},{2,10},{3,11},{4,12},{5,13},{6,14},{7,15},{8,0},{9,1},... | collective-permute-start | bytes 196616 | tf_op jit(solution)/shard_map/ppermute | solution.py:154
  72.6 3.3 %collective-permute-start.28 = (bf16[32,1024]{1,0:T(8,128)(2,1)S(1)}, bf16[32,1024]{1,0:T(8,128)(2,1)S(1)}, u32[]{:S(2)}, u32[]{:S(2)}) collective-permute-start(bf16[32,1024]{1,0:T(8,128)(2,1)S(1)} %get-tuple-element.69), channel_id=1, source_target_pairs={{0,4},{1,5},{2,6},{3,7},{4,0},{5,1},{6,2},{7,3},{8,12},{9,13},{10,... | collective-permute-start | bytes 196616 | tf_op jit(solution)/shard_map/ppermute | solution.py:154
  76.3 2.0 %shard_map.89 = bf16[128,8192]{1,0:T(8,128)(2,1)} custom-call(bf16[16,128]{1,0:T(8,128)(2,1)S(1)} %get-tuple-element.54.low_ref, bf16[32,1024]{1,0:T(8,128)(2,1)S(1)} %get-tuple-element.46.refs_0_, bf16[32,1024]{1,0:T(8,128)(2,1)S(1)} %collective-permute-done.8.refs_1_, bf16[32,1024]{1,0:T(8,128)(2,1)S(1)} %collective-permute-done.9.refs_2_, ...), custom_call_target="tpu_custom_call" | custom-call | flops 33554432 | bytes 2097152 | tf_op jit(solution)/shard_map/pallas_call | solution.py:203
  (55 shorter events, 18.9 us)
Async XLA Ops:
  4.7 11.4 %collective-permute-start = (bf16[272,128]{1,0:T(8,128)(2,1)S(1)}, bf16[272,128]{1,0:T(8,128)(2,1)S(1)}, u32[]{:S(2)}, u32[]{:S(2)}) collective-permute-start(bf16[272,128]{1,0:T(8,128)(2,1)S(1)} %get-tuple-element.39), channel_id=1, source_target_pairs={{0,14},{1,15},{2,12},{3,13},{4,10},{5,11},{6,8},{7,9},{8,6},{9,7},... | collective-permute-start | bytes 208904 | tf_op jit(solution)/shard_map/ppermute | solution.py:154
  10.8 6.7 %collective-permute-start.1 = (bf16[272,128]{1,0:T(8,128)(2,1)S(1)}, bf16[272,128]{1,0:T(8,128)(2,1)S(1)}, u32[]{:S(2)}, u32[]{:S(2)}) collective-permute-start(bf16[272,128]{1,0:T(8,128)(2,1)S(1)} %get-tuple-element.40), channel_id=1, source_target_pairs={{0,12},{1,13},{2,14},{3,15},{4,8},{5,9},{6,10},{7,11},{8,4},{9,5},... | collective-permute-start | bytes 208904 | tf_op jit(solution)/shard_map/ppermute | solution.py:154
  11.0 10.7 %collective-permute-start.2 = (bf16[272,128]{1,0:T(8,128)(2,1)S(1)}, bf16[272,128]{1,0:T(8,128)(2,1)S(1)}, u32[]{:S(2)}, u32[]{:S(2)}) collective-permute-start(bf16[272,128]{1,0:T(8,128)(2,1)S(1)} %get-tuple-element.41), channel_id=1, source_target_pairs={{0,10},{1,11},{2,8},{3,9},{4,14},{5,15},{6,12},{7,13},{8,2},{9,3},... | collective-permute-start | bytes 208904 | tf_op jit(solution)/shard_map/ppermute | solution.py:154
  11.8 11.0 %collective-permute-start.3 = (bf16[272,128]{1,0:T(8,128)(2,1)S(1)}, bf16[272,128]{1,0:T(8,128)(2,1)S(1)}, u32[]{:S(2)}, u32[]{:S(2)}) collective-permute-start(bf16[272,128]{1,0:T(8,128)(2,1)S(1)} %get-tuple-element.42), channel_id=1, source_target_pairs={{0,8},{1,9},{2,10},{3,11},{4,12},{5,13},{6,14},{7,15},{8,0},{9,1},... | collective-permute-start | bytes 208904 | tf_op jit(solution)/shard_map/ppermute | solution.py:154
  13.8 8.9 %collective-permute-start.4 = (bf16[272,128]{1,0:T(8,128)(2,1)S(1)}, bf16[272,128]{1,0:T(8,128)(2,1)S(1)}, u32[]{:S(2)}, u32[]{:S(2)}) collective-permute-start(bf16[272,128]{1,0:T(8,128)(2,1)S(1)} %get-tuple-element.43), channel_id=1, source_target_pairs={{0,6},{1,7},{2,4},{3,5},{4,2},{5,3},{6,0},{7,1},{8,14},{9,15},{10,... | collective-permute-start | bytes 208904 | tf_op jit(solution)/shard_map/ppermute | solution.py:154
  16.1 6.7 %collective-permute-start.5 = (bf16[272,128]{1,0:T(8,128)(2,1)S(1)}, bf16[272,128]{1,0:T(8,128)(2,1)S(1)}, u32[]{:S(2)}, u32[]{:S(2)}) collective-permute-start(bf16[272,128]{1,0:T(8,128)(2,1)S(1)} %get-tuple-element.44), channel_id=1, source_target_pairs={{0,4},{1,5},{2,6},{3,7},{4,0},{5,1},{6,2},{7,3},{8,12},{9,13},{10,... | collective-permute-start | bytes 208904 | tf_op jit(solution)/shard_map/ppermute | solution.py:154
  25.1 9.7 %collective-permute-start.8 = (bf16[32,1024]{1,0:T(8,128)(2,1)S(1)}, bf16[32,1024]{1,0:T(8,128)(2,1)S(1)}, u32[]{:S(2)}, u32[]{:S(2)}) collective-permute-start(bf16[32,1024]{1,0:T(8,128)(2,1)S(1)} %get-tuple-element.47), channel_id=1, source_target_pairs={{0,14},{1,15},{2,12},{3,13},{4,10},{5,11},{6,8},{7,9},{8,6},{9,7},... | collective-permute-start | bytes 196616 | tf_op jit(solution)/shard_map/ppermute | solution.py:154
  29.5 7.1 %collective-permute-start.9 = (bf16[32,1024]{1,0:T(8,128)(2,1)S(1)}, bf16[32,1024]{1,0:T(8,128)(2,1)S(1)}, u32[]{:S(2)}, u32[]{:S(2)}) collective-permute-start(bf16[32,1024]{1,0:T(8,128)(2,1)S(1)} %get-tuple-element.48), channel_id=1, source_target_pairs={{0,12},{1,13},{2,14},{3,15},{4,8},{5,9},{6,10},{7,11},{8,4},{9,5},... | collective-permute-start | bytes 196616 | tf_op jit(solution)/shard_map/ppermute | solution.py:154
  29.5 11.0 %collective-permute-start.10 = (bf16[32,1024]{1,0:T(8,128)(2,1)S(1)}, bf16[32,1024]{1,0:T(8,128)(2,1)S(1)}, u32[]{:S(2)}, u32[]{:S(2)}) collective-permute-start(bf16[32,1024]{1,0:T(8,128)(2,1)S(1)} %get-tuple-element.49), channel_id=1, source_target_pairs={{0,10},{1,11},{2,8},{3,9},{4,14},{5,15},{6,12},{7,13},{8,2},{9,3},... | collective-permute-start | bytes 196616 | tf_op jit(solution)/shard_map/ppermute | solution.py:154
  31.7 9.4 %collective-permute-start.11 = (bf16[32,1024]{1,0:T(8,128)(2,1)S(1)}, bf16[32,1024]{1,0:T(8,128)(2,1)S(1)}, u32[]{:S(2)}, u32[]{:S(2)}) collective-permute-start(bf16[32,1024]{1,0:T(8,128)(2,1)S(1)} %get-tuple-element.50), channel_id=1, source_target_pairs={{0,8},{1,9},{2,10},{3,11},{4,12},{5,13},{6,14},{7,15},{8,0},{9,1},... | collective-permute-start | bytes 196616 | tf_op jit(solution)/shard_map/ppermute | solution.py:154
  32.8 8.3 %collective-permute-start.12 = (bf16[32,1024]{1,0:T(8,128)(2,1)S(1)}, bf16[32,1024]{1,0:T(8,128)(2,1)S(1)}, u32[]{:S(2)}, u32[]{:S(2)}) collective-permute-start(bf16[32,1024]{1,0:T(8,128)(2,1)S(1)} %get-tuple-element.51), channel_id=1, source_target_pairs={{0,6},{1,7},{2,4},{3,5},{4,2},{5,3},{6,0},{7,1},{8,14},{9,15},{10,... | collective-permute-start | bytes 196616 | tf_op jit(solution)/shard_map/ppermute | solution.py:154
  34.8 6.5 %collective-permute-start.13 = (bf16[32,1024]{1,0:T(8,128)(2,1)S(1)}, bf16[32,1024]{1,0:T(8,128)(2,1)S(1)}, u32[]{:S(2)}, u32[]{:S(2)}) collective-permute-start(bf16[32,1024]{1,0:T(8,128)(2,1)S(1)} %get-tuple-element.52), channel_id=1, source_target_pairs={{0,4},{1,5},{2,6},{3,7},{4,0},{5,1},{6,2},{7,3},{8,12},{9,13},{10,... | collective-permute-start | bytes 196616 | tf_op jit(solution)/shard_map/ppermute | solution.py:154
  44.8 9.9 %collective-permute-start.15 = (bf16[32,1024]{1,0:T(8,128)(2,1)S(1)}, bf16[32,1024]{1,0:T(8,128)(2,1)S(1)}, u32[]{:S(2)}, u32[]{:S(2)}) collective-permute-start(bf16[32,1024]{1,0:T(8,128)(2,1)S(1)} %get-tuple-element.56), channel_id=1, source_target_pairs={{0,14},{1,15},{2,12},{3,13},{4,10},{5,11},{6,8},{7,9},{8,6},{9,7},... | collective-permute-start | bytes 196616 | tf_op jit(solution)/shard_map/ppermute | solution.py:154
  49.3 6.4 %collective-permute-start.16 = (bf16[32,1024]{1,0:T(8,128)(2,1)S(1)}, bf16[32,1024]{1,0:T(8,128)(2,1)S(1)}, u32[]{:S(2)}, u32[]{:S(2)}) collective-permute-start(bf16[32,1024]{1,0:T(8,128)(2,1)S(1)} %get-tuple-element.57), channel_id=1, source_target_pairs={{0,12},{1,13},{2,14},{3,15},{4,8},{5,9},{6,10},{7,11},{8,4},{9,5},... | collective-permute-start | bytes 196616 | tf_op jit(solution)/shard_map/ppermute | solution.py:154
  49.5 10.5 %collective-permute-start.17 = (bf16[32,1024]{1,0:T(8,128)(2,1)S(1)}, bf16[32,1024]{1,0:T(8,128)(2,1)S(1)}, u32[]{:S(2)}, u32[]{:S(2)}) collective-permute-start(bf16[32,1024]{1,0:T(8,128)(2,1)S(1)} %get-tuple-element.58), channel_id=1, source_target_pairs={{0,10},{1,11},{2,8},{3,9},{4,14},{5,15},{6,12},{7,13},{8,2},{9,3},... | collective-permute-start | bytes 196616 | tf_op jit(solution)/shard_map/ppermute | solution.py:154
  51.3 8.9 %collective-permute-start.18 = (bf16[32,1024]{1,0:T(8,128)(2,1)S(1)}, bf16[32,1024]{1,0:T(8,128)(2,1)S(1)}, u32[]{:S(2)}, u32[]{:S(2)}) collective-permute-start(bf16[32,1024]{1,0:T(8,128)(2,1)S(1)} %get-tuple-element.59), channel_id=1, source_target_pairs={{0,8},{1,9},{2,10},{3,11},{4,12},{5,13},{6,14},{7,15},{8,0},{9,1},... | collective-permute-start | bytes 196616 | tf_op jit(solution)/shard_map/ppermute | solution.py:154
  53.1 7.1 %collective-permute-start.19 = (bf16[32,1024]{1,0:T(8,128)(2,1)S(1)}, bf16[32,1024]{1,0:T(8,128)(2,1)S(1)}, u32[]{:S(2)}, u32[]{:S(2)}) collective-permute-start(bf16[32,1024]{1,0:T(8,128)(2,1)S(1)} %get-tuple-element.60), channel_id=1, source_target_pairs={{0,6},{1,7},{2,4},{3,5},{4,2},{5,3},{6,0},{7,1},{8,14},{9,15},{10,... | collective-permute-start | bytes 196616 | tf_op jit(solution)/shard_map/ppermute | solution.py:154
  54.6 5.8 %collective-permute-start.20 = (bf16[32,1024]{1,0:T(8,128)(2,1)S(1)}, bf16[32,1024]{1,0:T(8,128)(2,1)S(1)}, u32[]{:S(2)}, u32[]{:S(2)}) collective-permute-start(bf16[32,1024]{1,0:T(8,128)(2,1)S(1)} %get-tuple-element.61), channel_id=1, source_target_pairs={{0,4},{1,5},{2,6},{3,7},{4,0},{5,1},{6,2},{7,3},{8,12},{9,13},{10,... | collective-permute-start | bytes 196616 | tf_op jit(solution)/shard_map/ppermute | solution.py:154
  63.1 9.5 %collective-permute-start.23 = (bf16[32,1024]{1,0:T(8,128)(2,1)S(1)}, bf16[32,1024]{1,0:T(8,128)(2,1)S(1)}, u32[]{:S(2)}, u32[]{:S(2)}) collective-permute-start(bf16[32,1024]{1,0:T(8,128)(2,1)S(1)} %get-tuple-element.64), channel_id=1, source_target_pairs={{0,14},{1,15},{2,12},{3,13},{4,10},{5,11},{6,8},{7,9},{8,6},{9,7},... | collective-permute-start | bytes 196616 | tf_op jit(solution)/shard_map/ppermute | solution.py:154
  67.2 8.7 %collective-permute-start.24 = (bf16[32,1024]{1,0:T(8,128)(2,1)S(1)}, bf16[32,1024]{1,0:T(8,128)(2,1)S(1)}, u32[]{:S(2)}, u32[]{:S(2)}) collective-permute-start(bf16[32,1024]{1,0:T(8,128)(2,1)S(1)} %get-tuple-element.65), channel_id=1, source_target_pairs={{0,12},{1,13},{2,14},{3,15},{4,8},{5,9},{6,10},{7,11},{8,4},{9,5},... | collective-permute-start | bytes 196616 | tf_op jit(solution)/shard_map/ppermute | solution.py:154
  67.7 10.9 %collective-permute-start.25 = (bf16[32,1024]{1,0:T(8,128)(2,1)S(1)}, bf16[32,1024]{1,0:T(8,128)(2,1)S(1)}, u32[]{:S(2)}, u32[]{:S(2)}) collective-permute-start(bf16[32,1024]{1,0:T(8,128)(2,1)S(1)} %get-tuple-element.66), channel_id=1, source_target_pairs={{0,10},{1,11},{2,8},{3,9},{4,14},{5,15},{6,12},{7,13},{8,2},{9,3},... | collective-permute-start | bytes 196616 | tf_op jit(solution)/shard_map/ppermute | solution.py:154
  69.6 9.5 %collective-permute-start.26 = (bf16[32,1024]{1,0:T(8,128)(2,1)S(1)}, bf16[32,1024]{1,0:T(8,128)(2,1)S(1)}, u32[]{:S(2)}, u32[]{:S(2)}) collective-permute-start(bf16[32,1024]{1,0:T(8,128)(2,1)S(1)} %get-tuple-element.67), channel_id=1, source_target_pairs={{0,8},{1,9},{2,10},{3,11},{4,12},{5,13},{6,14},{7,15},{8,0},{9,1},... | collective-permute-start | bytes 196616 | tf_op jit(solution)/shard_map/ppermute | solution.py:154
  71.2 7.9 %collective-permute-start.27 = (bf16[32,1024]{1,0:T(8,128)(2,1)S(1)}, bf16[32,1024]{1,0:T(8,128)(2,1)S(1)}, u32[]{:S(2)}, u32[]{:S(2)}) collective-permute-start(bf16[32,1024]{1,0:T(8,128)(2,1)S(1)} %get-tuple-element.68), channel_id=1, source_target_pairs={{0,6},{1,7},{2,4},{3,5},{4,2},{5,3},{6,0},{7,1},{8,14},{9,15},{10,... | collective-permute-start | bytes 196616 | tf_op jit(solution)/shard_map/ppermute | solution.py:154
  72.6 6.8 %collective-permute-start.28 = (bf16[32,1024]{1,0:T(8,128)(2,1)S(1)}, bf16[32,1024]{1,0:T(8,128)(2,1)S(1)}, u32[]{:S(2)}, u32[]{:S(2)}) collective-permute-start(bf16[32,1024]{1,0:T(8,128)(2,1)S(1)} %get-tuple-element.69), channel_id=1, source_target_pairs={{0,4},{1,5},{2,6},{3,7},{4,0},{5,1},{6,2},{7,3},{8,12},{9,13},{10,... | collective-permute-start | bytes 196616 | tf_op jit(solution)/shard_map/ppermute | solution.py:154
  (11 other events, 67.8 us)

commit v4 on v0

v4 whole, which is shorter than its diff:
```python
import jax
import jax.numpy as jnp
from jax import lax
from jax.experimental import pallas as pl
from jax.experimental.pallas import tpu as pltpu
from jax.sharding import PartitionSpec as P

F32 = jnp.float32
BF16 = jnp.bfloat16
LANES = 128
ID_ROWS = 16
VMEM = pl.BlockSpec(memory_space=pltpu.VMEM)
HBM = pl.BlockSpec(memory_space=pltpu.HBM)
SMEM = pl.BlockSpec(memory_space=pltpu.SMEM)
PARAMS = pltpu.CompilerParams(vmem_limit_bytes=48 * 1024 * 1024)


def position():
    me = lax.axis_index("fsdp")
    return me // 2, me % 2


def pack_kernel(id_ref, storage_ref, down_hbm, up_hbm, out_ref, down_ref, up_ref, sems):
    m = out_ref.shape[0]
    loads = [
        pltpu.make_async_copy(down_hbm, down_ref, sems.at[0]),
        pltpu.make_async_copy(up_hbm, up_ref, sems.at[1]),
    ]
    for load in loads:
        load.start()
    for load in loads:
        load.wait()
    r, blocks = down_ref.shape[1], down_ref.shape[2] // m // LANES
    mark = jnp.full((ID_ROWS, LANES), storage_ref[id_ref[0]].astype(F32), F32).astype(BF16)
    for j in range(m):
        for b in range(blocks):
            cols = slice((j * blocks + b) * LANES, (j * blocks + b + 1) * LANES)
            out_ref[j, 2 * r * b : 2 * r * b + r, :] = down_ref[0, :, cols]
            out_ref[j, 2 * r * b + r : 2 * r * (b + 1), :] = up_ref[0, :, cols]
        out_ref[j, 2 * r * blocks :, :] = mark


def slot_of(ref, j):
    return ref[j, ref.shape[1] - ID_ROWS :, :].astype(F32)[0, 0].astype(jnp.int32)


def deliver_kernel(own_ref, other_ref, out_ref):
    _, c = position()
    m, r2, _ = out_ref.shape
    blocks = (own_ref.shape[1] - ID_ROWS) // r2
    slots = [slot_of(own_ref, j) for j in range(m)]
    for j, slot in enumerate(slots):
        at, here = slot // 2, slot % 2 == c
        for b in range(blocks):
            rows = slice(b * r2, (b + 1) * r2)
            out_ref[j, :, b * LANES : (b + 1) * LANES] = jnp.where(
                here, own_ref[at, rows, :], other_ref[at, rows, :]
            )


def inverse_kernel(own_ref, other_ref, tile_of):
    _, c = position()
    m = own_ref.shape[0]
    for ref, core in ((own_ref, c), (other_ref, 1 - c)):
        slots = [slot_of(ref, j) for j in range(m)]
        for j, slot in enumerate(slots):
            tile_of[slot] = 2 * j + core


def grads_kernel(acts_ref, cot_ref, factors_ref, low_ref, out_ref):
    m, r2, w = factors_ref.shape
    r = r2 // 2
    rows = acts_ref.shape[0]
    dims_nt = (((1,), (1,)), ((), ()))
    low_u = jnp.zeros((r, rows), F32)
    low_h = jnp.zeros((r, rows), F32)
    for j in range(m):
        cols = slice(j * w, (j + 1) * w)
        low_u += lax.dot_general(factors_ref[j, 0:r, :], acts_ref[:, cols], dims_nt, preferred_element_type=F32)
        low_h += lax.dot_general(factors_ref[j, r:r2, :], cot_ref[:, cols], dims_nt, preferred_element_type=F32)
    low_u = low_u.astype(BF16)
    low_h = low_h.astype(BF16)
    low_ref[...] = low_h
    for j in range(m):
        cols = slice(j * w, (j + 1) * w)
        out_ref[j, 0:r, :] = jnp.dot(low_h, acts_ref[:, cols], preferred_element_type=F32).astype(BF16)
        out_ref[j, r:r2, :] = jnp.dot(low_u, cot_ref[:, cols], preferred_element_type=F32).astype(BF16)


def inputs_kernel(low_ref, factors_ref, gx_ref):
    m, r2, w = factors_ref.shape
    for j in range(m):
        gx_ref[:, j * w : (j + 1) * w] = lax.dot_general(
            low_ref[...], factors_ref[j, 0 : r2 // 2, :], (((0,), (0,)), ((), ())), preferred_element_type=F32
        ).astype(BF16)


def collect_kernel(tile_of, own_ref, other_ref, out_ref):
    _, c = position()
    for j in range(out_ref.shape[0]):
        tile = tile_of[2 * j + c]
        out_ref[j] = jnp.where(tile % 2 == c, own_ref[tile // 2], other_ref[tile // 2])


def unpack_kernel(in_ref, ga_ref, gb_ref):
    m, r2, w = in_ref.shape
    for j in range(m):
        ga_ref[0, :, j * w : (j + 1) * w] = in_ref[j, 0 : r2 // 2, :]
        gb_ref[0, :, j * w : (j + 1) * w] = in_ref[j, r2 // 2 : r2, :]


def call(kernel, out_shape, in_specs, out_specs, **options):
    return pl.pallas_call(
        kernel,
        out_shape=out_shape,
        in_specs=in_specs,
        out_specs=out_specs,
        compiler_params=PARAMS,
        **options,
    )


def shards(acts, cotangent, down, up, adapter_per_tile, adapter_storage_slot):
    n = lax.axis_size("fsdp")
    m = n // 2
    _, r, d = down.shape
    w = d // m
    cores = [[2 * p + c for p in range(m)] for c in range(2)]

    def exchange(blocks):
        return lax.all_to_all(
            blocks, "fsdp", split_axis=0, concat_axis=0, tiled=True, axis_index_groups=cores
        )

    def to_other_core(block):
        return lax.ppermute(block, "fsdp", [(f, f ^ 1) for f in range(n)])

    flat = jax.ShapeDtypeStruct((m, 2 * r * w // LANES + ID_ROWS, LANES), BF16)
    wide = jax.ShapeDtypeStruct((m, 2 * r, w), BF16)
    low = jax.ShapeDtypeStruct((r, acts.shape[0]), BF16)
    own = exchange(
        call(
            pack_kernel,
            flat,
            [SMEM, SMEM, HBM, HBM],
            VMEM,
            scratch_shapes=[
                pltpu.VMEM(down.shape, BF16),
                pltpu.VMEM(up.shape, BF16),
                pltpu.SemaphoreType.DMA((2,)),
            ],
        )(adapter_per_tile, adapter_storage_slot, down, up)
    )
    other = to_other_core(own)
    factors = exchange(call(deliver_kernel, wide, [VMEM] * 2, VMEM)(own, other))
    tile_of = call(inverse_kernel, jax.ShapeDtypeStruct((n,), jnp.int32), [VMEM] * 2, SMEM)(own, other)
    low, parts = call(grads_kernel, (low, wide), [VMEM] * 3, [VMEM] * 2)(acts, cotangent, factors)
    own = exchange(parts)
    grad_x = call(
        inputs_kernel,
        jax.ShapeDtypeStruct(acts.shape, BF16),
        [VMEM] * 2,
        VMEM,
        cost_estimate=pl.CostEstimate(
            flops=2 * r * acts.size, bytes_accessed=2 * acts.size, transcendentals=0
        ),
    )(low, factors)
    owned = call(collect_kernel, wide, [SMEM, VMEM, VMEM], VMEM)(tile_of, own, to_other_core(own))
    grad_a, grad_b = call(
        unpack_kernel, [jax.ShapeDtypeStruct(down.shape, BF16)] * 2, [VMEM], [VMEM] * 2
    )(exchange(owned))
    return grad_x, grad_a, grad_b


def solution(mesh):
    placed = (
        P(("group", "fsdp"), None),
        P(("group", "fsdp"), None),
        P("fsdp", None, None),
        P("fsdp", None, None),
        P(("group", "fsdp")),
        P(),
    )
    return jax.shard_map(
        shards,
        mesh=mesh,
        in_specs=placed,
        out_specs=(
            P(("group", "fsdp"), None),
            P(("group", "fsdp"), None, None),
            P(("group", "fsdp"), None, None),
        ),
        check_vma=False,
    )
```

time: 329 us -> 89.9 us (0.27)
  the two profiles are of different devices: /device:TPU:13 before, /device:TPU:0 now
where the time goes in v4:
time: 89.9 us; the launch traced here: 89.5 us
  blocking collectives  58.3 us (65%)
  waiting for transfers between devices  16 us (18%)
  Pallas kernels  7.68 us (9%)
  starting transfers between devices  3.64 us (4%)
  local copies, waits for them, and re-layouts  2.56 us (3%)
  between operations  1.33 us (1%)
    all_to_all x3, blocking collectives, exchange(): lax.all_to_all(blocks, 'fsdp', split_axis=0, concat_axis=0, tiled=True, a...  58.3 us
    all_to_all x1, waiting for transfers between devices, exchange(): lax.all_to_all(blocks, 'fsdp', split_axis=0, concat_axis=0, tiled=True, a...  12.8 us
    all_to_all x1, starting transfers between devices, exchange(): lax.all_to_all(blocks, 'fsdp', split_axis=0, concat_axis=0, tiled=True, a...  3.64 us
    ppermute x2, waiting for transfers between devices, to_other_core(): return lax.ppermute(block, 'fsdp', [(f, f ^ 1) for f in range(n)])  3.19 us
    unnamed x10, local copies, waits for them, and re-layouts  2.56 us
    pallas_call x1, Pallas kernels, shards(): call(inputs_kernel, jax.ShapeDtypeStruct(acts.shape, BF16), [VMEM] * 2, V...  2.05 us
    pallas_call x1, Pallas kernels, shards(): call(grads_kernel, (low, wide), [VMEM] * 3, [VMEM] * 2)  1.82 us
  transfers between devices with their start and end apart: 3, of which 3 were waited for; matrix products, arithmetic and copies ran while one was open for 0% of the time, Pallas kernels for 3%

profile of v4, /device:TPU:0, one launch (start us, length us, event | category | flops | bytes accessed | tf_op | source)
XLA Modules:
  0.0 89.5 jit_solution(16369841703308474453)
XLA Ops:
  1.3 0.0 copy-start.2
  1.3 0.9 %copy-done.2 = bf16[1,16,8192]{2,1,0:T(8,128)(2,1)S(1)} copy-done((bf16[1,16,8192]{2,1,0:T(8,128)(2,1)S(1)}, bf16[1,16,8192]{2,1,0:T(8,128)(2,1)}, u32[]{:S(2)}) %copy-start.2) | copy-done | bytes 262168
  2.2 0.0 copy-start.3
  2.2 0.9 %copy-done.3 = bf16[1,16,8192]{2,1,0:T(8,128)(2,1)S(1)} copy-done((bf16[1,16,8192]{2,1,0:T(8,128)(2,1)S(1)}, bf16[1,16,8192]{2,1,0:T(8,128)(2,1)}, u32[]{:S(2)}) %copy-start.3) | copy-done | bytes 262168
  3.2 0.7 copy-done.4
  3.8 0.7 shard_map.85
  4.5 0.0 copy-start
  4.5 23.2 %all_to_all.20.own_ref = bf16[8,272,128]{2,1,0:T(8,128)(2,1)S(1)} all-to-all(bf16[8,272,128]{2,1,0:T(8,128)(2,1)S(1)} %shard_map.85), channel_id=1, replica_groups={{0,2,4,6,8,10,12,14},{1,3,5,7,9,11,13,15},{16,18,20,22,24,26,28,30},{17..., dimensions={0} | all-to-all | bytes 1114112 | tf_op jit(solution)/shard_map/all_to_all | solution.py:131
  27.8 0.0 collective-permute-start
  27.8 2.0 %collective-permute-done.other_ref = bf16[8,272,128]{2,1,0:T(8,128)(2,1)S(1)} collective-permute-done((bf16[8,272,128]{2,1,0:T(8,128)(2,1)S(1)}, bf16[8,272,128]{2,1,0:T(8,128)(2,1)S(1)}, u32[]{:S(2)}, u32[]{:S(2)}) %collective-permute-start) | collective-permute-done | bytes 557088 | tf_op jit(solution)/shard_map/ppermute | solution.py:136
  29.7 0.2 shard_map.86
  29.9 17.5 %all_to_all.21.factors_ref = bf16[8,32,1024]{2,1,0:T(8,128)(2,1)S(1)} all-to-all(bf16[8,32,1024]{2,1,0:T(8,128)(2,1)S(1)} %shard_map.86), channel_id=1, replica_groups={{0,2,4,6,8,10,12,14},{1,3,5,7,9,11,13,15},{16,18,20,22,24,26,28,30},{17..., dimensions={0} | all-to-all | bytes 1048576 | tf_op jit(solution)/shard_map/all_to_all | solution.py:131
  47.4 0.0 copy-done.1
  47.4 0.0 copy-done
  47.4 1.8 %shard_map.87 = (bf16[16,128]{1,0:T(8,128)(2,1)S(1)}, bf16[8,32,1024]{2,1,0:T(8,128)(2,1)S(1)}) custom-call(bf16[128,8192]{1,0:T(8,128)(2,1)S(1)} %copy-done, bf16[128,8192]{1,0:T(8,128)(2,1)S(1)} %copy-done.1, bf16[8,32,1024]{2,1,0:T(8,128)(2,1)S(1)} %all_to_all.21.factors_ref), custom_call_target="tpu_custom_call" | custom-call | tf_op jit(solution)/shard_map/pallas_call | solution.py:157
  49.2 17.6 %all_to_all.22.own_ref = bf16[8,32,1024]{2,1,0:T(8,128)(2,1)S(1)} all-to-all(bf16[8,32,1024]{2,1,0:T(8,128)(2,1)S(1)} %get-tuple-element.8), channel_id=1, replica_groups={{0,2,4,6,8,10,12,14},{1,3,5,7,9,11,13,15},{16,18,20,22,24,26,28,30},{17..., dimensions={0} | all-to-all | bytes 1048576 | tf_op jit(solution)/shard_map/all_to_all | solution.py:131
  66.9 0.0 collective-permute-start.1
  66.9 0.7 shard_map.89.tile_of
  67.5 1.2 %collective-permute-done.1.other_ref = bf16[8,32,1024]{2,1,0:T(8,128)(2,1)S(1)} collective-permute-done((bf16[8,32,1024]{2,1,0:T(8,128)(2,1)S(1)}, bf16[8,32,1024]{2,1,0:T(8,128)(2,1)S(1)}, u32[]{:S(2)}, u32[]{:S(2)}) %collective-permute-start.1) | collective-permute-done | bytes 524320 | tf_op jit(solution)/shard_map/ppermute | solution.py:136
  68.8 1.4 %shard_map.90 = bf16[8,32,1024]{2,1,0:T(8,128)(2,1)} custom-call(s32[16]{0:T(128)S(1)} %shard_map.89.tile_of, bf16[8,32,1024]{2,1,0:T(8,128)(2,1)S(1)} %all_to_all.22.own_ref, bf16[8,32,1024]{2,1,0:T(8,128)(2,1)S(1)} %collective-permute-done.1.other_ref), custom_call_target="tpu_custom_call" | custom-call | tf_op jit(solution)/shard_map/pallas_call | solution.py:168
  70.2 3.6 %all-to-all-start.3 = ((bf16[8,32,1024]{2,1,0:T(8,128)(2,1)}), bf16[8,32,1024]{2,1,0:T(8,128)(2,1)S(1)}, u32[]{:S(2)}, u32[]{:S(2)}) async-start(bf16[8,32,1024]{2,1,0:T(8,128)(2,1)} %shard_map.90), calls=%async_computation.3 | async-start | bytes 1048576 | tf_op jit(solution)/shard_map/all_to_all | solution.py:131
  73.8 2.1 %shard_map.88 = bf16[128,8192]{1,0:T(8,128)(2,1)} custom-call(bf16[16,128]{1,0:T(8,128)(2,1)S(1)} %get-tuple-element.7.low_ref, bf16[8,32,1024]{2,1,0:T(8,128)(2,1)S(1)} %all_to_all.21.factors_ref), custom_call_target="tpu_custom_call" | custom-call | flops 33554432 | bytes 2097152 | tf_op jit(solution)/shard_map/pallas_call | solution.py:159
  75.9 12.8 %all-to-all-done.3.in_ref = bf16[8,32,1024]{2,1,0:T(8,128)(2,1)S(1)} async-done(((bf16[8,32,1024]{2,1,0:T(8,128)(2,1)}), bf16[8,32,1024]{2,1,0:T(8,128)(2,1)S(1)}, u32[]{:S(2)}, u32[]{:S(2)}) %all-to-all-start.3) | async-done | bytes 524320 | tf_op jit(solution)/shard_map/all_to_all | solution.py:131
  88.7 0.8 shard_map.91
  (2 shorter events, 0.0 us)
Async XLA Ops:
  1.3 1.0 %copy-start.2 = (bf16[1,16,8192]{2,1,0:T(8,128)(2,1)S(1)}, bf16[1,16,8192]{2,1,0:T(8,128)(2,1)}, u32[]{:S(2)}) copy-start(bf16[1,16,8192]{2,1,0:T(8,128)(2,1)} %down_hbm.1) | copy-start | bytes 786436
  2.2 0.9 %copy-start.3 = (bf16[1,16,8192]{2,1,0:T(8,128)(2,1)S(1)}, bf16[1,16,8192]{2,1,0:T(8,128)(2,1)}, u32[]{:S(2)}) copy-start(bf16[1,16,8192]{2,1,0:T(8,128)(2,1)} %up_hbm.1) | copy-start | bytes 786436
  3.2 0.7 copy-start.4
  3.8 43.6 %copy-start.1 = (bf16[128,8192]{1,0:T(8,128)(2,1)S(1)}, bf16[128,8192]{1,0:T(8,128)(2,1)}, u32[]{:S(2)}) copy-start(bf16[128,8192]{1,0:T(8,128)(2,1)} %cot_ref.1) | copy-start | bytes 6291460
  4.5 42.9 %copy-start = (bf16[128,8192]{1,0:T(8,128)(2,1)S(1)}, bf16[128,8192]{1,0:T(8,128)(2,1)}, u32[]{:S(2)}) copy-start(bf16[128,8192]{1,0:T(8,128)(2,1)} %acts_ref.1) | copy-start | bytes 6291460
  27.8 2.0 %collective-permute-start = (bf16[8,272,128]{2,1,0:T(8,128)(2,1)S(1)}, bf16[8,272,128]{2,1,0:T(8,128)(2,1)S(1)}, u32[]{:S(2)}, u32[]{:S(2)}) collective-permute-start(bf16[8,272,128]{2,1,0:T(8,128)(2,1)S(1)} %all_to_all.20.own_ref), channel_id=1, source_target_pairs={{0,1},{1,0},{2,3},{3,2},{4,5},{5,4},{6,7},{7,6},{8,9},{9,8},{10,11... | collective-permute-start | bytes 1671176 | tf_op jit(solution)/shard_map/ppermute | solution.py:136
  66.9 1.9 %collective-permute-start.1 = (bf16[8,32,1024]{2,1,0:T(8,128)(2,1)S(1)}, bf16[8,32,1024]{2,1,0:T(8,128)(2,1)S(1)}, u32[]{:S(2)}, u32[]{:S(2)}) collective-permute-start(bf16[8,32,1024]{2,1,0:T(8,128)(2,1)S(1)} %all_to_all.22.own_ref), channel_id=1, source_target_pairs={{0,1},{1,0},{2,3},{3,2},{4,5},{5,4},{6,7},{7,6},{8,9},{9,8},{10,11... | collective-permute-start | bytes 1572872 | tf_op jit(solution)/shard_map/ppermute | solution.py:136
  70.2 18.5 %all-to-all-start.3 = ((bf16[8,32,1024]{2,1,0:T(8,128)(2,1)}), bf16[8,32,1024]{2,1,0:T(8,128)(2,1)S(1)}, u32[]{:S(2)}, u32[]{:S(2)}) async-start(bf16[8,32,1024]{2,1,0:T(8,128)(2,1)} %shard_map.90), calls=%async_computation.3 | async-start | bytes 1048576 | tf_op jit(solution)/shard_map/all_to_all | solution.py:131

commit v5 on v3

--- a/solution.py
+++ b/solution.py
@@ -14,7 +14,8 @@
 VMEM = pl.BlockSpec(memory_space=pltpu.VMEM)
 HBM = pl.BlockSpec(memory_space=pltpu.HBM)
 SMEM = pl.BlockSpec(memory_space=pltpu.SMEM)
-PARAMS = pltpu.CompilerParams(vmem_limit_bytes=48 * 1024 * 1024)
+PARAMS = pltpu.CompilerParams(vmem_limit_bytes=32 * 1024 * 1024)
+ALONE = pltpu.CompilerParams(vmem_limit_bytes=60 * 1024 * 1024)
 
 
 def position():
@@ -22,8 +23,13 @@
     return me // 2, me % 2
 
 
+def halves(m):
+    return [*range(m // 2)], [*range(m - 1, m // 2 - 1, -1)]
+
+
 def offsets(m):
-    return [0, *range(m - 1, 0, -1)]
+    near, far = halves(m)
+    return near[:1] + far[:2] + near[1:2] + far[2:] + near[2:]
 
 
 def columns(chunk, w):
@@ -53,8 +59,8 @@
 
 def stack_kernel(*refs):
     *blocks, held_ref = refs
-    for block, k in zip(blocks, offsets(len(blocks))):
-        held_ref[k] = block[...]
+    for at, block in enumerate(blocks):
+        held_ref[at] = block[...]
 
 
 def stack(blocks):
@@ -67,33 +73,47 @@
     )(*blocks)
 
 
-def slot_of(ref, k):
-    return ref[k, ref.shape[1] - ID_ROWS :, :].astype(F32)[0, 0].astype(jnp.int32)
-
-
-def deliver_kernel(m, own_ref, other_ref, *outs):
-    p, c = position()
+def pick(held, chip, here, rows):
+    own_near, own_far, other_near, other_far = held
+    h = own_near.shape[0]
+    k = chip ^ position()[0]
+    near, u, v = k < h, lax.rem(k, h), h - 1 - lax.rem(k, h)
+    own = jnp.where(near, own_near[u, rows, :], own_far[v, rows, :])
+    other = jnp.where(near, other_near[u, rows, :], other_far[v, rows, :])
+    return jnp.where(here, own, other)
+
+
+def slot_of(near, far, k):
+    h = near.shape[0]
+    ref, at = (near, k) if k < h else (far, 2 * h - 1 - k)
+    return ref[at, ref.shape[1] - ID_ROWS :, :].astype(F32)[0, 0].astype(jnp.int32)
+
+
+def deliver_kernel(m, *refs):
+    held, outs = refs[:4], refs[4:]
+    _, c = position()
     r2 = outs[0].shape[0]
-    blocks = (own_ref.shape[1] - ID_ROWS) // r2
-    slots = [slot_of(own_ref, k) for k in offsets(m)]
+    blocks = (held[0].shape[1] - ID_ROWS) // r2
+    slots = [slot_of(*held[:2], k) for k in offsets(m)]
     for out, slot in zip(outs, slots):
-        at, here = (slot // 2) ^ p, slot % 2 == c
         for b in range(blocks):
             rows = slice(b * r2, (b + 1) * r2)
-            out[:, b * LANES : (b + 1) * LANES] = jnp.where(
-                here, own_ref[at, rows, :], other_ref[at, rows, :]
-            )
-
-
-def inverse_kernel(m, own_ref, other_ref, tile_of):
+            out[:, b * LANES : (b + 1) * LANES] = pick(held, slot // 2, slot % 2 == c, rows)
+
+
+def inverse_kernel(m, own_near, own_far, other_near, other_far, tile_of):
     p, c = position()
-    for ref, core in ((own_ref, c), (other_ref, 1 - c)):
-        slots = [slot_of(ref, k) for k in range(m)]
+    for near, far, core in ((own_near, own_far, c), (other_near, other_far, 1 - c)):
+        slots = [slot_of(near, far, k) for k in range(m)]
         for k, slot in enumerate(slots):
             tile_of[slot] = 2 * (p ^ k) + core
 
 
-def grads_kernel(m, acts_ref, cot_ref, *refs):
+def touch_kernel(_, token_ref):
+    token_ref[...] = jnp.zeros_like(token_ref)
+
+
+def grads_kernel(m, _, acts_ref, cot_ref, *refs):
     factors, low_ref, outs = refs[:m], refs[m], refs[m + 1 :]
     p, _ = position()
     r2, w = factors[0].shape
@@ -125,12 +145,12 @@
         ).astype(BF16)
 
 
-def collect_kernel(m, tile_of, own_ref, other_ref, *outs):
+def collect_kernel(m, tile_of, *refs):
+    held, outs = refs[:4], refs[4:]
     p, c = position()
     for out, k in zip(outs, offsets(m)):
         tile = tile_of[2 * (p ^ k) + c]
-        at, here = (tile // 2) ^ p, tile % 2 == c
-        out[...] = jnp.where(here, own_ref[at], other_ref[at])
+        out[...] = pick(held, tile // 2, tile % 2 == c, slice(None))
 
 
 def unpack_kernel(m, *refs):
@@ -157,8 +177,10 @@
             for block, k in zip(blocks[1:], offsets(m)[1:])
         ]
 
-    def to_other_core(block):
-        return lax.ppermute(block, "fsdp", [(f, f ^ 1) for f in range(n)])
+    def gather(blocks):
+        by_offset = dict(zip(offsets(m), blocks))
+        own = [stack([by_offset[k] for k in half]) for half in halves(m)]
+        return own + [lax.ppermute(half, "fsdp", [(f, f ^ 1) for f in range(n)]) for half in own]
 
     rows = 2 * r * w // LANES
     flat = jax.ShapeDtypeStruct((rows + ID_ROWS, LANES), BF16)
@@ -173,32 +195,39 @@
             pltpu.VMEM(up.shape, BF16),
             pltpu.SemaphoreType.DMA((2,)),
         ],
-        compiler_params=PARAMS,
+        compiler_params=ALONE,
     )(adapter_per_tile, adapter_storage_slot, down, up)
-    own = stack(exchange(spread))
-    other = to_other_core(own)
+    token = pl.pallas_call(
+        touch_kernel,
+        out_shape=jax.ShapeDtypeStruct((8, LANES), F32),
+        in_specs=[VMEM],
+        out_specs=VMEM,
+        compiler_params=PARAMS,
+    )(cotangent)
+    first = stack(spread[:1])[0]
+    held = gather(exchange([first, *spread[1:]]))
     factors = pl.pallas_call(
         functools.partial(deliver_kernel, m),
         out_shape=[wide] * m,
-        in_specs=[VMEM, VMEM],
+        in_specs=[VMEM] * 4,
         out_specs=[VMEM] * m,
         compiler_params=PARAMS,
-    )(own, other)
+    )(*held)
     factors = exchange(factors)
     tile_of = pl.pallas_call(
         functools.partial(inverse_kernel, m),
         out_shape=jax.ShapeDtypeStruct((n,), jnp.int32),
-        in_specs=[VMEM, VMEM],
+        in_specs=[VMEM] * 4,
         out_specs=SMEM,
         compiler_params=PARAMS,
-    )(own, other)
+    )(*held)
     low, *parts = pl.pallas_call(
         functools.partial(grads_kernel, m),
         out_shape=[jax.ShapeDtypeStruct((r, acts.shape[0]), BF16)] + [wide] * m,
-        in_specs=[VMEM] * (m + 2),
+        in_specs=[VMEM] * (m + 3),
         out_specs=[VMEM] * (m + 1),
         compiler_params=PARAMS,
-    )(acts, cotangent, *factors)
+    )(token, acts, cotangent, *factors)
     parts = exchange(parts)
     grad_x = pl.pallas_call(
         functools.partial(inputs_kernel, m),
@@ -210,14 +239,13 @@
             flops=2 * r * acts.size, bytes_accessed=2 * acts.size, transcendentals=0
         ),
     )(low, *factors)
-    own = stack(parts)
     owned = pl.pallas_call(
         functools.partial(collect_kernel, m),
         out_shape=[wide] * m,
-        in_specs=[SMEM, VMEM, VMEM],
+        in_specs=[SMEM] + [VMEM] * 4,
         out_specs=[VMEM] * m,
         compiler_params=PARAMS,
-    )(tile_of, own, to_other_core(own))
+    )(tile_of, *gather(parts))
     grad_a, grad_b = pl.pallas_call(
         functools.partial(unpack_kernel, m),
         out_shape=[jax.ShapeDtypeStruct(down.shape, BF16)] * 2,

time: 81.2 us -> 82.6 us (1.017)
  starting transfers between devices: 52.4 us -> 58.4 us
  waiting for transfers between devices: 15.9 us -> 12.4 us
  local copies, waits for them, and re-layouts: 4.14 us -> 0.89 us
  Pallas kernels: 7.05 us -> 9.15 us
    ppermute x28, starting transfers between devices: 52.2 us -> 58.1 us  [exchange(): lax.ppermute(block, 'fsdp', [(2 * p + c, 2 * (p ^ k) + c) for p in range(...]
    unnamed x10 -> x6, local copies, waits for them, and re-layouts: 4.14 us -> 0.89 us
    ppermute x28, waiting for transfers between devices: 12.7 us -> 9.97 us  [exchange(): lax.ppermute(block, 'fsdp', [(2 * p + c, 2 * (p ^ k) + c) for p in range(...]
    pallas_call x1, Pallas kernels: 0.75 us -> 2.64 us  [shards(): pl.pallas_call(functools.partial(pack_kernel, m), out_shape=[flat] * m, i...]
    ppermute x2 -> x4, waiting for transfers between devices: 3.17 us -> 2.39 us  [gather(): lax.ppermute(half, 'fsdp', [(f, f ^ 1) for f in range(n)])]
  transfers between devices with their start and end apart: 30 -> 32, of which waited for: 16 -> 14; matrix products, arithmetic and copies ran while one was open for 0% -> 0% of each run, Pallas kernels for 3% -> 3%
where the time goes in v5:
time: 82.6 us; the launch traced here: 82.4 us
  starting transfers between devices  58.4 us (71%)
  waiting for transfers between devices  12.4 us (15%)
  Pallas kernels  9.15 us (11%)
  between operations  1.59 us (2%)
  local copies, waits for them, and re-layouts  0.89 us (1%)
    ppermute x28, starting transfers between devices, exchange(): lax.ppermute(block, 'fsdp', [(2 * p + c, 2 * (p ^ k) + c) for p in range(...  58.1 us
    ppermute x28, waiting for transfers between devices, exchange(): lax.ppermute(block, 'fsdp', [(2 * p + c, 2 * (p ^ k) + c) for p in range(...  9.97 us
    pallas_call x1, Pallas kernels, shards(): pl.pallas_call(functools.partial(pack_kernel, m), out_shape=[flat] * m, i...  2.64 us
    ppermute x4, waiting for transfers between devices, gather(): lax.ppermute(half, 'fsdp', [(f, f ^ 1) for f in range(n)])  2.39 us
    pallas_call x1, Pallas kernels, shards(): pl.pallas_call(functools.partial(inputs_kernel, m), out_shape=jax.ShapeDt...  2.05 us
    pallas_call x1, Pallas kernels, shards(): pl.pallas_call(functools.partial(grads_kernel, m), out_shape=[jax.ShapeDt...  1.84 us
  transfers between devices with their start and end apart: 32, of which 14 were waited for; matrix products, arithmetic and copies ran while one was open for 0% of the time, Pallas kernels for 3%

profile of v5, /device:TPU:0, one launch (start us, length us, event | category | flops | bytes accessed | tf_op | source)
XLA Modules:
  0.0 82.4 jit_solution(11965072872929759029)
XLA Ops:
  1.4 2.6 %shard_map.86 = (bf16[272,128]{1,0:T(8,128)(2,1)}, bf16[272,128]{1,0:T(8,128)(2,1)}, bf16[272,128]{1,0:T(8,128)(2,1)}, bf16[272,128]{1,0:T(8,128)(2,1)}, bf16[27...) custom-call(s32[1]{0:T(128)S(6)} %copy.9.id_ref, ...), custom_call_target="tpu_custom_call" | custom-call | tf_op jit(solution)/shard_map/pallas_call | solution.py:188
  4.1 6.1 %collective-permute-start.3 = (bf16[272,128]{1,0:T(8,128)(2,1)}, bf16[272,128]{1,0:T(8,128)(2,1)S(1)}, u32[]{:S(2)}, u32[]{:S(2)}) collective-permute-start(bf16[272,128]{1,0:T(8,128)(2,1)} %get-tuple-element.42), channel_id=1, source_target_pairs={{0,14},{1,15},{2,12},{3,13},{4,10},{5,11},{6,8},{7,9},{8,6},{9,7},... | collective-permute-start | bytes 208904 | tf_op jit(solution)/shard_map/ppermute | solution.py:174
  10.8 1.8 %collective-permute-start.5 = (bf16[272,128]{1,0:T(8,128)(2,1)}, bf16[272,128]{1,0:T(8,128)(2,1)S(1)}, u32[]{:S(2)}, u32[]{:S(2)}) collective-permute-start(bf16[272,128]{1,0:T(8,128)(2,1)} %get-tuple-element.44), channel_id=1, source_target_pairs={{0,10},{1,11},{2,8},{3,9},{4,14},{5,15},{6,12},{7,13},{8,2},{9,3},... | collective-permute-start | bytes 208904 | tf_op jit(solution)/shard_map/ppermute | solution.py:174
  12.6 2.1 %collective-permute-start.6 = (bf16[272,128]{1,0:T(8,128)(2,1)}, bf16[272,128]{1,0:T(8,128)(2,1)S(1)}, u32[]{:S(2)}, u32[]{:S(2)}) collective-permute-start(bf16[272,128]{1,0:T(8,128)(2,1)} %get-tuple-element.45), channel_id=1, source_target_pairs={{0,8},{1,9},{2,10},{3,11},{4,12},{5,13},{6,14},{7,15},{8,0},{9,1},... | collective-permute-start | bytes 208904 | tf_op jit(solution)/shard_map/ppermute | solution.py:174
  14.8 2.6 %collective-permute-start.1 = (bf16[272,128]{1,0:T(8,128)(2,1)}, bf16[272,128]{1,0:T(8,128)(2,1)S(1)}, u32[]{:S(2)}, u32[]{:S(2)}) collective-permute-start(bf16[272,128]{1,0:T(8,128)(2,1)} %get-tuple-element.40), channel_id=1, source_target_pairs={{0,4},{1,5},{2,6},{3,7},{4,0},{5,1},{6,2},{7,3},{8,12},{9,13},{10,... | collective-permute-start | bytes 208904 | tf_op jit(solution)/shard_map/ppermute | solution.py:174
  17.4 2.2 %collective-permute-start.2 = (bf16[272,128]{1,0:T(8,128)(2,1)}, bf16[272,128]{1,0:T(8,128)(2,1)S(1)}, u32[]{:S(2)}, u32[]{:S(2)}) collective-permute-start(bf16[272,128]{1,0:T(8,128)(2,1)} %get-tuple-element.41), channel_id=1, source_target_pairs={{0,6},{1,7},{2,4},{3,5},{4,2},{5,3},{6,0},{7,1},{8,14},{9,15},{10,... | collective-permute-start | bytes 208904 | tf_op jit(solution)/shard_map/ppermute | solution.py:174
  23.9 1.4 %collective-permute-done.7.refs_2_.other_near = bf16[4,272,128]{2,1,0:T(8,128)(2,1)S(1)} collective-permute-done((bf16[4,272,128]{2,1,0:T(8,128)(2,1)S(1)}, bf16[4,272,128]{2,1,0:T(8,128)(2,1)S(1)}, u32[]{:S(2)}, u32[]{:S(2)}) %collective-permute-start.7) | collective-permute-done | bytes 278560 | tf_op jit(solution)/shard_map/ppermute | solution.py:183
  25.6 3.6 %collective-permute-start.9 = (bf16[32,1024]{1,0:T(8,128)(2,1)S(1)}, bf16[32,1024]{1,0:T(8,128)(2,1)S(1)}, u32[]{:S(2)}, u32[]{:S(2)}) collective-permute-start(bf16[32,1024]{1,0:T(8,128)(2,1)S(1)} %get-tuple-element.47), channel_id=1, source_target_pairs={{0,14},{1,15},{2,12},{3,13},{4,10},{5,11},{6,8},{7,9},{8,6},{9,7},... | collective-permute-start | bytes 196616 | tf_op jit(solution)/shard_map/ppermute | solution.py:174
  31.0 1.6 %collective-permute-start.12 = (bf16[32,1024]{1,0:T(8,128)(2,1)S(1)}, bf16[32,1024]{1,0:T(8,128)(2,1)S(1)}, u32[]{:S(2)}, u32[]{:S(2)}) collective-permute-start(bf16[32,1024]{1,0:T(8,128)(2,1)S(1)} %get-tuple-element.50), channel_id=1, source_target_pairs={{0,10},{1,11},{2,8},{3,9},{4,14},{5,15},{6,12},{7,13},{8,2},{9,3},... | collective-permute-start | bytes 196616 | tf_op jit(solution)/shard_map/ppermute | solution.py:174
  32.5 1.5 %collective-permute-start.13 = (bf16[32,1024]{1,0:T(8,128)(2,1)S(1)}, bf16[32,1024]{1,0:T(8,128)(2,1)S(1)}, u32[]{:S(2)}, u32[]{:S(2)}) collective-permute-start(bf16[32,1024]{1,0:T(8,128)(2,1)S(1)} %get-tuple-element.51), channel_id=1, source_target_pairs={{0,8},{1,9},{2,10},{3,11},{4,12},{5,13},{6,14},{7,15},{8,0},{9,1},... | collective-permute-start | bytes 196616 | tf_op jit(solution)/shard_map/ppermute | solution.py:174
  34.1 2.8 %collective-permute-start.14 = (bf16[32,1024]{1,0:T(8,128)(2,1)S(1)}, bf16[32,1024]{1,0:T(8,128)(2,1)S(1)}, u32[]{:S(2)}, u32[]{:S(2)}) collective-permute-start(bf16[32,1024]{1,0:T(8,128)(2,1)S(1)} %get-tuple-element.52), channel_id=1, source_target_pairs={{0,4},{1,5},{2,6},{3,7},{4,0},{5,1},{6,2},{7,3},{8,12},{9,13},{10,... | collective-permute-start | bytes 196616 | tf_op jit(solution)/shard_map/ppermute | solution.py:174
  36.9 2.5 %collective-permute-start.15 = (bf16[32,1024]{1,0:T(8,128)(2,1)S(1)}, bf16[32,1024]{1,0:T(8,128)(2,1)S(1)}, u32[]{:S(2)}, u32[]{:S(2)}) collective-permute-start(bf16[32,1024]{1,0:T(8,128)(2,1)S(1)} %get-tuple-element.53), channel_id=1, source_target_pairs={{0,6},{1,7},{2,4},{3,5},{4,2},{5,3},{6,0},{7,1},{8,14},{9,15},{10,... | collective-permute-start | bytes 196616 | tf_op jit(solution)/shard_map/ppermute | solution.py:174
  39.4 1.3 %collective-permute-done.12.refs_4_ = bf16[32,1024]{1,0:T(8,128)(2,1)S(1)} collective-permute-done((bf16[32,1024]{1,0:T(8,128)(2,1)S(1)}, bf16[32,1024]{1,0:T(8,128)(2,1)S(1)}, u32[]{:S(2)}, u32[]{:S(2)}) %collective-permute-start.12) | collective-permute-done | bytes 65568 | tf_op jit(solution)/shard_map/ppermute | solution.py:174
  43.0 1.8 %shard_map.91 = (bf16[16,128]{1,0:T(8,128)(2,1)S(1)}, bf16[32,1024]{1,0:T(8,128)(2,1)S(1)}, bf16[32,1024]{1,0:T(8,128)(2,1)S(1)}, bf16[32,1024]{1,0:T(8,128)(2,1...) custom-call(f32[8,128]{1,0:T(8,128)S(1)} %shard_map.85._, ...), custom_call_target="tpu_custom_call" | custom-call | tf_op jit(solution)/shard_map/pallas_call | solution.py:224
  44.8 4.4 %collective-permute-start.19 = (bf16[32,1024]{1,0:T(8,128)(2,1)S(1)}, bf16[32,1024]{1,0:T(8,128)(2,1)S(1)}, u32[]{:S(2)}, u32[]{:S(2)}) collective-permute-start(bf16[32,1024]{1,0:T(8,128)(2,1)S(1)} %get-tuple-element.59), channel_id=1, source_target_pairs={{0,14},{1,15},{2,12},{3,13},{4,10},{5,11},{6,8},{7,9},{8,6},{9,7},... | collective-permute-start | bytes 196616 | tf_op jit(solution)/shard_map/ppermute | solution.py:174
  50.3 1.5 %collective-permute-start.21 = (bf16[32,1024]{1,0:T(8,128)(2,1)S(1)}, bf16[32,1024]{1,0:T(8,128)(2,1)S(1)}, u32[]{:S(2)}, u32[]{:S(2)}) collective-permute-start(bf16[32,1024]{1,0:T(8,128)(2,1)S(1)} %get-tuple-element.61), channel_id=1, source_target_pairs={{0,10},{1,11},{2,8},{3,9},{4,14},{5,15},{6,12},{7,13},{8,2},{9,3},... | collective-permute-start | bytes 196616 | tf_op jit(solution)/shard_map/ppermute | solution.py:174
  51.9 1.9 %collective-permute-start.22 = (bf16[32,1024]{1,0:T(8,128)(2,1)S(1)}, bf16[32,1024]{1,0:T(8,128)(2,1)S(1)}, u32[]{:S(2)}, u32[]{:S(2)}) collective-permute-start(bf16[32,1024]{1,0:T(8,128)(2,1)S(1)} %get-tuple-element.62), channel_id=1, source_target_pairs={{0,8},{1,9},{2,10},{3,11},{4,12},{5,13},{6,14},{7,15},{8,0},{9,1},... | collective-permute-start | bytes 196616 | tf_op jit(solution)/shard_map/ppermute | solution.py:174
  53.7 2.0 %collective-permute-start.17 = (bf16[32,1024]{1,0:T(8,128)(2,1)S(1)}, bf16[32,1024]{1,0:T(8,128)(2,1)S(1)}, u32[]{:S(2)}, u32[]{:S(2)}) collective-permute-start(bf16[32,1024]{1,0:T(8,128)(2,1)S(1)} %get-tuple-element.57), channel_id=1, source_target_pairs={{0,4},{1,5},{2,6},{3,7},{4,0},{5,1},{6,2},{7,3},{8,12},{9,13},{10,... | collective-permute-start | bytes 196616 | tf_op jit(solution)/shard_map/ppermute | solution.py:174
  55.8 2.9 %collective-permute-start.18 = (bf16[32,1024]{1,0:T(8,128)(2,1)S(1)}, bf16[32,1024]{1,0:T(8,128)(2,1)S(1)}, u32[]{:S(2)}, u32[]{:S(2)}) collective-permute-start(bf16[32,1024]{1,0:T(8,128)(2,1)S(1)} %get-tuple-element.58), channel_id=1, source_target_pairs={{0,6},{1,7},{2,4},{3,5},{4,2},{5,3},{6,0},{7,1},{8,14},{9,15},{10,... | collective-permute-start | bytes 196616 | tf_op jit(solution)/shard_map/ppermute | solution.py:174
  63.4 4.3 %collective-permute-start.25 = (bf16[32,1024]{1,0:T(8,128)(2,1)S(1)}, bf16[32,1024]{1,0:T(8,128)(2,1)S(1)}, u32[]{:S(2)}, u32[]{:S(2)}) collective-permute-start(bf16[32,1024]{1,0:T(8,128)(2,1)S(1)} %get-tuple-element.64), channel_id=1, source_target_pairs={{0,14},{1,15},{2,12},{3,13},{4,10},{5,11},{6,8},{7,9},{8,6},{9,7},... | collective-permute-start | bytes 196616 | tf_op jit(solution)/shard_map/ppermute | solution.py:174
  69.1 2.7 %collective-permute-start.28 = (bf16[32,1024]{1,0:T(8,128)(2,1)S(1)}, bf16[32,1024]{1,0:T(8,128)(2,1)S(1)}, u32[]{:S(2)}, u32[]{:S(2)}) collective-permute-start(bf16[32,1024]{1,0:T(8,128)(2,1)S(1)} %get-tuple-element.67), channel_id=1, source_target_pairs={{0,10},{1,11},{2,8},{3,9},{4,14},{5,15},{6,12},{7,13},{8,2},{9,3},... | collective-permute-start | bytes 196616 | tf_op jit(solution)/shard_map/ppermute | solution.py:174
  72.3 3.3 %collective-permute-start.30 = (bf16[32,1024]{1,0:T(8,128)(2,1)S(1)}, bf16[32,1024]{1,0:T(8,128)(2,1)S(1)}, u32[]{:S(2)}, u32[]{:S(2)}) collective-permute-start(bf16[32,1024]{1,0:T(8,128)(2,1)S(1)} %get-tuple-element.69), channel_id=1, source_target_pairs={{0,4},{1,5},{2,6},{3,7},{4,0},{5,1},{6,2},{7,3},{8,12},{9,13},{10,... | collective-permute-start | bytes 196616 | tf_op jit(solution)/shard_map/ppermute | solution.py:174
  75.6 2.8 %collective-permute-start.31 = (bf16[32,1024]{1,0:T(8,128)(2,1)S(1)}, bf16[32,1024]{1,0:T(8,128)(2,1)S(1)}, u32[]{:S(2)}, u32[]{:S(2)}) collective-permute-start(bf16[32,1024]{1,0:T(8,128)(2,1)S(1)} %get-tuple-element.70), channel_id=1, source_target_pairs={{0,6},{1,7},{2,4},{3,5},{4,2},{5,3},{6,0},{7,1},{8,14},{9,15},{10,... | collective-permute-start | bytes 196616 | tf_op jit(solution)/shard_map/ppermute | solution.py:174
  78.4 2.1 %shard_map.92 = bf16[128,8192]{1,0:T(8,128)(2,1)} custom-call(bf16[16,128]{1,0:T(8,128)(2,1)S(1)} %get-tuple-element.54.low_ref, bf16[32,1024]{1,0:T(8,128)(2,1)S(1)} %get-tuple-element.46.refs_0_, bf16[32,1024]{1,0:T(8,128)(2,1)S(1)} %collective-permute-done.9.refs_1_, bf16[32,1024]{1,0:T(8,128)(2,1)S(1)} %collective-permute-done.10.refs_2_, ...), custom_call_target="tpu_custom_call" | custom-call | flops 33554432 | bytes 2097152 | tf_op jit(solution)/shard_map/pallas_call | solution.py:232
  (59 shorter events, 18.8 us)
Async XLA Ops:
  4.1 10.7 %collective-permute-start.3 = (bf16[272,128]{1,0:T(8,128)(2,1)}, bf16[272,128]{1,0:T(8,128)(2,1)S(1)}, u32[]{:S(2)}, u32[]{:S(2)}) collective-permute-start(bf16[272,128]{1,0:T(8,128)(2,1)} %get-tuple-element.42), channel_id=1, source_target_pairs={{0,14},{1,15},{2,12},{3,13},{4,10},{5,11},{6,8},{7,9},{8,6},{9,7},... | collective-permute-start | bytes 208904 | tf_op jit(solution)/shard_map/ppermute | solution.py:174
  10.2 7.3 %collective-permute-start.4 = (bf16[272,128]{1,0:T(8,128)(2,1)}, bf16[272,128]{1,0:T(8,128)(2,1)S(1)}, u32[]{:S(2)}, u32[]{:S(2)}) collective-permute-start(bf16[272,128]{1,0:T(8,128)(2,1)} %get-tuple-element.43), channel_id=1, source_target_pairs={{0,12},{1,13},{2,14},{3,15},{4,8},{5,9},{6,10},{7,11},{8,4},{9,5},... | collective-permute-start | bytes 208904 | tf_op jit(solution)/shard_map/ppermute | solution.py:174
  10.4 12.0 %collective-permute-start = (bf16[272,128]{1,0:T(8,128)(2,1)}, bf16[272,128]{1,0:T(8,128)(2,1)S(1)}, u32[]{:S(2)}, u32[]{:S(2)}) collective-permute-start(bf16[272,128]{1,0:T(8,128)(2,1)} %get-tuple-element.39), channel_id=1, source_target_pairs={{0,2},{1,3},{2,0},{3,1},{4,6},{5,7},{6,4},{7,5},{8,10},{9,11},{10,... | collective-permute-start | bytes 208904 | tf_op jit(solution)/shard_map/ppermute | solution.py:174
  10.8 10.1 %collective-permute-start.5 = (bf16[272,128]{1,0:T(8,128)(2,1)}, bf16[272,128]{1,0:T(8,128)(2,1)S(1)}, u32[]{:S(2)}, u32[]{:S(2)}) collective-permute-start(bf16[272,128]{1,0:T(8,128)(2,1)} %get-tuple-element.44), channel_id=1, source_target_pairs={{0,10},{1,11},{2,8},{3,9},{4,14},{5,15},{6,12},{7,13},{8,2},{9,3},... | collective-permute-start | bytes 208904 | tf_op jit(solution)/shard_map/ppermute | solution.py:174
  12.6 9.6 %collective-permute-start.6 = (bf16[272,128]{1,0:T(8,128)(2,1)}, bf16[272,128]{1,0:T(8,128)(2,1)S(1)}, u32[]{:S(2)}, u32[]{:S(2)}) collective-permute-start(bf16[272,128]{1,0:T(8,128)(2,1)} %get-tuple-element.45), channel_id=1, source_target_pairs={{0,8},{1,9},{2,10},{3,11},{4,12},{5,13},{6,14},{7,15},{8,0},{9,1},... | collective-permute-start | bytes 208904 | tf_op jit(solution)/shard_map/ppermute | solution.py:174
  14.8 7.6 %collective-permute-start.1 = (bf16[272,128]{1,0:T(8,128)(2,1)}, bf16[272,128]{1,0:T(8,128)(2,1)S(1)}, u32[]{:S(2)}, u32[]{:S(2)}) collective-permute-start(bf16[272,128]{1,0:T(8,128)(2,1)} %get-tuple-element.40), channel_id=1, source_target_pairs={{0,4},{1,5},{2,6},{3,7},{4,0},{5,1},{6,2},{7,3},{8,12},{9,13},{10,... | collective-permute-start | bytes 208904 | tf_op jit(solution)/shard_map/ppermute | solution.py:174
  25.6 8.5 %collective-permute-start.9 = (bf16[32,1024]{1,0:T(8,128)(2,1)S(1)}, bf16[32,1024]{1,0:T(8,128)(2,1)S(1)}, u32[]{:S(2)}, u32[]{:S(2)}) collective-permute-start(bf16[32,1024]{1,0:T(8,128)(2,1)S(1)} %get-tuple-element.47), channel_id=1, source_target_pairs={{0,14},{1,15},{2,12},{3,13},{4,10},{5,11},{6,8},{7,9},{8,6},{9,7},... | collective-permute-start | bytes 196616 | tf_op jit(solution)/shard_map/ppermute | solution.py:174
  29.2 7.7 %collective-permute-start.10 = (bf16[32,1024]{1,0:T(8,128)(2,1)S(1)}, bf16[32,1024]{1,0:T(8,128)(2,1)S(1)}, u32[]{:S(2)}, u32[]{:S(2)}) collective-permute-start(bf16[32,1024]{1,0:T(8,128)(2,1)S(1)} %get-tuple-element.48), channel_id=1, source_target_pairs={{0,12},{1,13},{2,14},{3,15},{4,8},{5,9},{6,10},{7,11},{8,4},{9,5},... | collective-permute-start | bytes 196616 | tf_op jit(solution)/shard_map/ppermute | solution.py:174
  29.7 9.7 %collective-permute-start.11 = (bf16[32,1024]{1,0:T(8,128)(2,1)S(1)}, bf16[32,1024]{1,0:T(8,128)(2,1)S(1)}, u32[]{:S(2)}, u32[]{:S(2)}) collective-permute-start(bf16[32,1024]{1,0:T(8,128)(2,1)S(1)} %get-tuple-element.49), channel_id=1, source_target_pairs={{0,2},{1,3},{2,0},{3,1},{4,6},{5,7},{6,4},{7,5},{8,10},{9,11},{10,... | collective-permute-start | bytes 196616 | tf_op jit(solution)/shard_map/ppermute | solution.py:174
  31.0 9.8 %collective-permute-start.12 = (bf16[32,1024]{1,0:T(8,128)(2,1)S(1)}, bf16[32,1024]{1,0:T(8,128)(2,1)S(1)}, u32[]{:S(2)}, u32[]{:S(2)}) collective-permute-start(bf16[32,1024]{1,0:T(8,128)(2,1)S(1)} %get-tuple-element.50), channel_id=1, source_target_pairs={{0,10},{1,11},{2,8},{3,9},{4,14},{5,15},{6,12},{7,13},{8,2},{9,3},... | collective-permute-start | bytes 196616 | tf_op jit(solution)/shard_map/ppermute | solution.py:174
  32.5 8.9 %collective-permute-start.13 = (bf16[32,1024]{1,0:T(8,128)(2,1)S(1)}, bf16[32,1024]{1,0:T(8,128)(2,1)S(1)}, u32[]{:S(2)}, u32[]{:S(2)}) collective-permute-start(bf16[32,1024]{1,0:T(8,128)(2,1)S(1)} %get-tuple-element.51), channel_id=1, source_target_pairs={{0,8},{1,9},{2,10},{3,11},{4,12},{5,13},{6,14},{7,15},{8,0},{9,1},... | collective-permute-start | bytes 196616 | tf_op jit(solution)/shard_map/ppermute | solution.py:174
  34.1 7.9 %collective-permute-start.14 = (bf16[32,1024]{1,0:T(8,128)(2,1)S(1)}, bf16[32,1024]{1,0:T(8,128)(2,1)S(1)}, u32[]{:S(2)}, u32[]{:S(2)}) collective-permute-start(bf16[32,1024]{1,0:T(8,128)(2,1)S(1)} %get-tuple-element.52), channel_id=1, source_target_pairs={{0,4},{1,5},{2,6},{3,7},{4,0},{5,1},{6,2},{7,3},{8,12},{9,13},{10,... | collective-permute-start | bytes 196616 | tf_op jit(solution)/shard_map/ppermute | solution.py:174
  44.8 8.9 %collective-permute-start.19 = (bf16[32,1024]{1,0:T(8,128)(2,1)S(1)}, bf16[32,1024]{1,0:T(8,128)(2,1)S(1)}, u32[]{:S(2)}, u32[]{:S(2)}) collective-permute-start(bf16[32,1024]{1,0:T(8,128)(2,1)S(1)} %get-tuple-element.59), channel_id=1, source_target_pairs={{0,14},{1,15},{2,12},{3,13},{4,10},{5,11},{6,8},{7,9},{8,6},{9,7},... | collective-permute-start | bytes 196616 | tf_op jit(solution)/shard_map/ppermute | solution.py:174
  49.2 6.5 %collective-permute-start.20 = (bf16[32,1024]{1,0:T(8,128)(2,1)S(1)}, bf16[32,1024]{1,0:T(8,128)(2,1)S(1)}, u32[]{:S(2)}, u32[]{:S(2)}) collective-permute-start(bf16[32,1024]{1,0:T(8,128)(2,1)S(1)} %get-tuple-element.60), channel_id=1, source_target_pairs={{0,12},{1,13},{2,14},{3,15},{4,8},{5,9},{6,10},{7,11},{8,4},{9,5},... | collective-permute-start | bytes 196616 | tf_op jit(solution)/shard_map/ppermute | solution.py:174
  49.4 10.7 %collective-permute-start.16 = (bf16[32,1024]{1,0:T(8,128)(2,1)S(1)}, bf16[32,1024]{1,0:T(8,128)(2,1)S(1)}, u32[]{:S(2)}, u32[]{:S(2)}) collective-permute-start(bf16[32,1024]{1,0:T(8,128)(2,1)S(1)} %get-tuple-element.56), channel_id=1, source_target_pairs={{0,2},{1,3},{2,0},{3,1},{4,6},{5,7},{6,4},{7,5},{8,10},{9,11},{10,... | collective-permute-start | bytes 196616 | tf_op jit(solution)/shard_map/ppermute | solution.py:174
  50.3 8.5 %collective-permute-start.21 = (bf16[32,1024]{1,0:T(8,128)(2,1)S(1)}, bf16[32,1024]{1,0:T(8,128)(2,1)S(1)}, u32[]{:S(2)}, u32[]{:S(2)}) collective-permute-start(bf16[32,1024]{1,0:T(8,128)(2,1)S(1)} %get-tuple-element.61), channel_id=1, source_target_pairs={{0,10},{1,11},{2,8},{3,9},{4,14},{5,15},{6,12},{7,13},{8,2},{9,3},... | collective-permute-start | bytes 196616 | tf_op jit(solution)/shard_map/ppermute | solution.py:174
  51.9 8.0 %collective-permute-start.22 = (bf16[32,1024]{1,0:T(8,128)(2,1)S(1)}, bf16[32,1024]{1,0:T(8,128)(2,1)S(1)}, u32[]{:S(2)}, u32[]{:S(2)}) collective-permute-start(bf16[32,1024]{1,0:T(8,128)(2,1)S(1)} %get-tuple-element.62), channel_id=1, source_target_pairs={{0,8},{1,9},{2,10},{3,11},{4,12},{5,13},{6,14},{7,15},{8,0},{9,1},... | collective-permute-start | bytes 196616 | tf_op jit(solution)/shard_map/ppermute | solution.py:174
  53.7 6.3 %collective-permute-start.17 = (bf16[32,1024]{1,0:T(8,128)(2,1)S(1)}, bf16[32,1024]{1,0:T(8,128)(2,1)S(1)}, u32[]{:S(2)}, u32[]{:S(2)}) collective-permute-start(bf16[32,1024]{1,0:T(8,128)(2,1)S(1)} %get-tuple-element.57), channel_id=1, source_target_pairs={{0,4},{1,5},{2,6},{3,7},{4,0},{5,1},{6,2},{7,3},{8,12},{9,13},{10,... | collective-permute-start | bytes 196616 | tf_op jit(solution)/shard_map/ppermute | solution.py:174
  63.4 8.9 %collective-permute-start.25 = (bf16[32,1024]{1,0:T(8,128)(2,1)S(1)}, bf16[32,1024]{1,0:T(8,128)(2,1)S(1)}, u32[]{:S(2)}, u32[]{:S(2)}) collective-permute-start(bf16[32,1024]{1,0:T(8,128)(2,1)S(1)} %get-tuple-element.64), channel_id=1, source_target_pairs={{0,14},{1,15},{2,12},{3,13},{4,10},{5,11},{6,8},{7,9},{8,6},{9,7},... | collective-permute-start | bytes 196616 | tf_op jit(solution)/shard_map/ppermute | solution.py:174
  67.7 7.8 %collective-permute-start.26 = (bf16[32,1024]{1,0:T(8,128)(2,1)S(1)}, bf16[32,1024]{1,0:T(8,128)(2,1)S(1)}, u32[]{:S(2)}, u32[]{:S(2)}) collective-permute-start(bf16[32,1024]{1,0:T(8,128)(2,1)S(1)} %get-tuple-element.65), channel_id=1, source_target_pairs={{0,12},{1,13},{2,14},{3,15},{4,8},{5,9},{6,10},{7,11},{8,4},{9,5},... | collective-permute-start | bytes 196616 | tf_op jit(solution)/shard_map/ppermute | solution.py:174
  67.9 12.6 %collective-permute-start.27 = (bf16[32,1024]{1,0:T(8,128)(2,1)S(1)}, bf16[32,1024]{1,0:T(8,128)(2,1)S(1)}, u32[]{:S(2)}, u32[]{:S(2)}) collective-permute-start(bf16[32,1024]{1,0:T(8,128)(2,1)S(1)} %get-tuple-element.66), channel_id=1, source_target_pairs={{0,2},{1,3},{2,0},{3,1},{4,6},{5,7},{6,4},{7,5},{8,10},{9,11},{10,... | collective-permute-start | bytes 196616 | tf_op jit(solution)/shard_map/ppermute | solution.py:174
  69.1 11.4 %collective-permute-start.28 = (bf16[32,1024]{1,0:T(8,128)(2,1)S(1)}, bf16[32,1024]{1,0:T(8,128)(2,1)S(1)}, u32[]{:S(2)}, u32[]{:S(2)}) collective-permute-start(bf16[32,1024]{1,0:T(8,128)(2,1)S(1)} %get-tuple-element.67), channel_id=1, source_target_pairs={{0,10},{1,11},{2,8},{3,9},{4,14},{5,15},{6,12},{7,13},{8,2},{9,3},... | collective-permute-start | bytes 196616 | tf_op jit(solution)/shard_map/ppermute | solution.py:174
  71.8 8.7 %collective-permute-start.29 = (bf16[32,1024]{1,0:T(8,128)(2,1)S(1)}, bf16[32,1024]{1,0:T(8,128)(2,1)S(1)}, u32[]{:S(2)}, u32[]{:S(2)}) collective-permute-start(bf16[32,1024]{1,0:T(8,128)(2,1)S(1)} %get-tuple-element.68), channel_id=1, source_target_pairs={{0,8},{1,9},{2,10},{3,11},{4,12},{5,13},{6,14},{7,15},{8,0},{9,1},... | collective-permute-start | bytes 196616 | tf_op jit(solution)/shard_map/ppermute | solution.py:174
  72.3 8.2 %collective-permute-start.30 = (bf16[32,1024]{1,0:T(8,128)(2,1)S(1)}, bf16[32,1024]{1,0:T(8,128)(2,1)S(1)}, u32[]{:S(2)}, u32[]{:S(2)}) collective-permute-start(bf16[32,1024]{1,0:T(8,128)(2,1)S(1)} %get-tuple-element.69), channel_id=1, source_target_pairs={{0,4},{1,5},{2,6},{3,7},{4,0},{5,1},{6,2},{7,3},{8,12},{9,13},{10,... | collective-permute-start | bytes 196616 | tf_op jit(solution)/shard_map/ppermute | solution.py:174
  (11 other events, 92.5 us)

commit v6 on v0

v6 whole, which is shorter than its diff:
```python
import functools

import jax
import jax.numpy as jnp
from jax import lax
from jax.experimental import pallas as pl
from jax.experimental.pallas import tpu as pltpu
from jax.sharding import PartitionSpec as P

F32 = jnp.float32
BF16 = jnp.bfloat16
LANES = 128
ID_ROWS = 16
VMEM = pl.BlockSpec(memory_space=pltpu.VMEM)
HBM = pl.BlockSpec(memory_space=pltpu.HBM)
SMEM = pl.BlockSpec(memory_space=pltpu.SMEM)
PARAMS = pltpu.CompilerParams(vmem_limit_bytes=32 * 1024 * 1024)
ALONE = pltpu.CompilerParams(vmem_limit_bytes=60 * 1024 * 1024)


def position():
    me = lax.axis_index("fsdp")
    return me // 2, me % 2


def far_offsets(m):
    return range(m - 1, m // 2 - 1, -1)


def chips(m):
    p, _ = position()
    h = m // 2
    return [p // h * h + q for q in range(h)] + [p ^ k for k in far_offsets(m)]


def blocks(near, far):
    return [near.at[q] for q in range(near.shape[0])] + list(far)


def columns(chip, w, first=0, size=None):
    size = size or w
    return pl.ds(pl.multiple_of(chip * w + first, LANES), size)


def pack_kernel(m, id_ref, storage_ref, down_hbm, up_hbm, near_hbm, *refs):
    far_hbm, (down_ref, up_ref, out_ref, load_sems, store_sems) = refs[: m // 2], refs[m // 2 :]
    r, w = down_ref.shape[0], down_ref.shape[1] // m
    order = [*zip(range(m), chips(m), blocks(near_hbm, far_hbm))]
    order = order[m // 2 :] + order[: m // 2]
    loads = []
    for i, chip, _ in order:
        cols = columns(chip, w)
        loads.append(
            [
                pltpu.make_async_copy(src.at[0, :, cols], dst.at[:, i * w : (i + 1) * w], sem)
                for src, dst, sem in (
                    (down_hbm, down_ref, load_sems.at[0, i]),
                    (up_hbm, up_ref, load_sems.at[1, i]),
                )
            ]
        )
        for load in loads[-1]:
            load.start()
    mark = jnp.full((ID_ROWS, LANES), storage_ref[id_ref[0]].astype(F32), F32).astype(BF16)
    stores = []
    for (i, _, dst), pair in zip(order, loads):
        for load in pair:
            load.wait()
        for b in range(w // LANES):
            cols = slice(i * w + b * LANES, i * w + (b + 1) * LANES)
            out_ref[i, 2 * r * b : 2 * r * b + r, :] = down_ref[:, cols]
            out_ref[i, 2 * r * b + r : 2 * r * (b + 1), :] = up_ref[:, cols]
        out_ref[i, 2 * r * (w // LANES) :, :] = mark
        stores.append(pltpu.make_async_copy(out_ref.at[i], dst, store_sems.at[i]))
        stores[-1].start()
    for store in stores:
        store.wait()


def stack_kernel(*refs):
    *parts, out_ref = refs
    for i, part in enumerate(parts):
        out_ref[i] = part[...]


def slot_of(block):
    mark = block[block.shape[0] - ID_ROWS :, :]
    return mark.astype(F32)[0, 0].astype(jnp.int32)


def pick(held, chip, here, rows, cols):
    own_near, own_far, other_near, other_far = held
    h = own_near.shape[0]
    p, _ = position()
    is_near, u, v = chip // h == p // h, chip % h, 2 * h - 1 - (chip ^ p)
    u, v = jnp.where(is_near, u, 0), jnp.where(is_near, 0, v)
    own = jnp.where(is_near, own_near[u, rows, cols], own_far[v, rows, cols])
    other = jnp.where(is_near, other_near[u, rows, cols], other_far[v, rows, cols])
    return jnp.where(here, own, other)


def deliver_kernel(m, own_near, own_far, other_near, other_far, near_ref, *far):
    _, c = position()
    outs = blocks(near_ref, far)
    r2, w = outs[0].shape
    slots = [slot_of(block) for block in blocks(own_near, blocks(own_far, ()))]
    for out, slot in zip(outs, slots):
        for b in range(w // LANES):
            out[:, b * LANES : (b + 1) * LANES] = pick(
                (own_near, own_far, other_near, other_far),
                slot // 2,
                slot % 2 == c,
                slice(b * r2, (b + 1) * r2),
                slice(None),
            )


def inverse_kernel(m, own_near, own_far, other_near, other_far, tile_of):
    _, c = position()
    for near, far, core in ((own_near, own_far, c), (other_near, other_far, 1 - c)):
        slots = [slot_of(block) for block in blocks(near, blocks(far, ()))]
        for chip, slot in zip(chips(m), slots):
            tile_of[slot] = 2 * chip + core


def touch_kernel(after, array, token_ref):
    token_ref[...] = jnp.zeros_like(token_ref)


def grads_kernel(m, _, acts_ref, cot_ref, near_in, *refs):
    far_in, low_ref, near_out, far_out = refs[: m // 2], refs[m // 2], refs[m // 2 + 1], refs[m // 2 + 2 :]
    r2, w = near_in.shape[1:]
    r = r2 // 2
    rows = acts_ref.shape[0]
    dims_nt = (((1,), (1,)), ((), ()))
    low_u = jnp.zeros((r, rows), F32)
    low_h = jnp.zeros((r, rows), F32)
    for chip, factor in zip(chips(m), blocks(near_in, far_in)):
        cols = columns(chip, w)
        low_u += lax.dot_general(factor[0:r, :], acts_ref[:, cols], dims_nt, preferred_element_type=F32)
        low_h += lax.dot_general(factor[r:r2, :], cot_ref[:, cols], dims_nt, preferred_element_type=F32)
    low_u = low_u.astype(BF16)
    low_h = low_h.astype(BF16)
    low_ref[...] = low_h
    for chip, out in zip(chips(m), blocks(near_out, far_out)):
        cols = columns(chip, w)
        out[0:r, :] = jnp.dot(low_h, acts_ref[:, cols], preferred_element_type=F32).astype(BF16)
        out[r:r2, :] = jnp.dot(low_u, cot_ref[:, cols], preferred_element_type=F32).astype(BF16)


def inputs_kernel(m, _, low_ref, near_ref, *refs):
    far, gx_ref = refs[: m // 2], refs[m // 2]
    r2, w = near_ref.shape[1:]
    for chip, factor in zip(chips(m), blocks(near_ref, far)):
        gx_ref[:, columns(chip, w)] = lax.dot_general(
            low_ref[...], factor[0 : r2 // 2, :], (((0,), (0,)), ((), ())), preferred_element_type=F32
        ).astype(BF16)


def collect_kernel(m, tile_of, own_near, own_far, other_near, other_far, near_ref, *far):
    _, c = position()
    w = near_ref.shape[2]
    for chip, out in zip(chips(m), blocks(near_ref, far)):
        tile = tile_of[2 * chip + c]
        for b in range(w // LANES):
            cols = slice(b * LANES, (b + 1) * LANES)
            out[:, cols] = pick(
                (own_near, own_far, other_near, other_far), tile // 2, tile % 2 == c, slice(None), cols
            )


def unpack_kernel(m, near_ref, *refs):
    far, (ga_hbm, gb_hbm, sems) = refs[: m // 2], refs[m // 2 :]
    r2, w = near_ref.shape[1:]
    stores = []
    for i, (chip, block) in enumerate(zip(chips(m), blocks(near_ref, far))):
        for j, out in enumerate((ga_hbm, gb_hbm)):
            rows = pl.ds(j * (r2 // 2), r2 // 2)
            stores.append(
                pltpu.make_async_copy(block.at[rows, :], out.at[0, :, columns(chip, w)], sems.at[j, i])
            )
            stores[-1].start()
    for store in stores:
        store.wait()


def call(kernel, out_shape, in_specs, out_specs, params=PARAMS, **options):
    return pl.pallas_call(
        kernel,
        out_shape=out_shape,
        in_specs=in_specs,
        out_specs=out_specs,
        compiler_params=params,
        **options,
    )


def shards(acts, cotangent, down, up, adapter_per_tile, adapter_storage_slot):
    n = lax.axis_size("fsdp")
    m = n // 2
    h = m // 2
    _, r, d = down.shape
    w = d // m

    def exchange(near, *far):
        pairs = [
            [(2 * p + c, 2 * (p ^ k) + c) for p in range(m) for c in range(2)] for k in far_offsets(m)
        ]
        far = [lax.ppermute(block, "fsdp", pair) for block, pair in zip(far, pairs)]
        groups = [[2 * (s * h + q) + c for q in range(h)] for s in range(2) for c in range(2)]
        near = lax.all_to_all(
            near, "fsdp", split_axis=0, concat_axis=0, tiled=True, axis_index_groups=groups
        )
        return near, *far

    def gather(near, *far):
        stacked = jax.ShapeDtypeStruct((h, *far[0].shape), BF16)
        own = [near, call(stack_kernel, stacked, [VMEM] * h, VMEM)(*far)]
        return own + [lax.ppermute(half, "fsdp", [(f, f ^ 1) for f in range(n)]) for half in own]

    def shapes(rows, cols):
        one = jax.ShapeDtypeStruct((rows, cols), BF16)
        return [jax.ShapeDtypeStruct((h, rows, cols), BF16)] + [one] * h

    flat = shapes(2 * r * w // LANES + ID_ROWS, LANES)
    wide = shapes(2 * r, w)
    spread = call(
        functools.partial(pack_kernel, m),
        flat,
        [SMEM, SMEM, HBM, HBM],
        [HBM] * (h + 1),
        ALONE,
        scratch_shapes=[
            pltpu.VMEM((r, d), BF16),
            pltpu.VMEM((r, d), BF16),
            pltpu.VMEM((m, *flat[1].shape), BF16),
            pltpu.SemaphoreType.DMA((2, m)),
            pltpu.SemaphoreType.DMA((m,)),
        ],
    )(adapter_per_tile, adapter_storage_slot, down, up)
    held = gather(*exchange(*spread))
    factors = call(functools.partial(deliver_kernel, m), wide, [VMEM] * 4, [VMEM] * (h + 1))(*held)
    token = call(touch_kernel, jax.ShapeDtypeStruct((8, LANES), F32), [VMEM] * 2, VMEM)(
        factors[-1], cotangent
    )
    factors = exchange(*factors)
    tile_of = call(
        functools.partial(inverse_kernel, m), jax.ShapeDtypeStruct((n,), jnp.int32), [VMEM] * 4, SMEM
    )(*held)
    low, *parts = call(
        functools.partial(grads_kernel, m),
        [jax.ShapeDtypeStruct((r, acts.shape[0]), BF16)] + wide,
        [VMEM] * (h + 4),
        [VMEM] * (h + 2),
    )(token, acts, cotangent, *factors)
    parts = exchange(*parts)
    owned = call(functools.partial(collect_kernel, m), wide, [SMEM] + [VMEM] * 4, [VMEM] * (h + 1))(
        tile_of, *gather(*parts)
    )
    grad_x = call(
        functools.partial(inputs_kernel, m),
        jax.ShapeDtypeStruct(acts.shape, BF16),
        [VMEM] * (h + 3),
        VMEM,
        cost_estimate=pl.CostEstimate(
            flops=2 * r * acts.size, bytes_accessed=2 * acts.size, transcendentals=0
        ),
    )(owned[-1], low, *factors)
    grad_a, grad_b = call(
        functools.partial(unpack_kernel, m),
        [jax.ShapeDtypeStruct(down.shape, BF16)] * 2,
        [VMEM] * (h + 1),
        [HBM] * 2,
        scratch_shapes=[pltpu.SemaphoreType.DMA((2, m))],
    )(*exchange(*owned))
    return grad_x, grad_a, grad_b


def solution(mesh):
    placed = (
        P(("group", "fsdp"), None),
        P(("group", "fsdp"), None),
        P("fsdp", None, None),
        P("fsdp", None, None),
        P(("group", "fsdp")),
        P(),
    )
    return jax.shard_map(
        shards,
        mesh=mesh,
        in_specs=placed,
        out_specs=(
            P(("group", "fsdp"), None),
            P(("group", "fsdp"), None, None),
            P(("group", "fsdp"), None, None),
        ),
        check_vma=False,
    )
```

time: 329 us -> 104 us (0.32)
  the two profiles are of different devices: /device:TPU:13 before, /device:TPU:0 now
where the time goes in v6:
time: 104 us; the launch traced here: 103 us
  starting transfers between devices  47.7 us (46%)
  waiting for transfers between devices  31.4 us (30%)
  local copies, waits for them, and re-layouts  12.7 us (12%)
  Pallas kernels  9.97 us (10%)
  between operations  1.58 us (2%)
    ppermute x16, starting transfers between devices, exchange(): far = [lax.ppermute(block, 'fsdp', pair) for block, pair in zip(far, pairs)]  31 us
    ppermute x16, waiting for transfers between devices, exchange(): far = [lax.ppermute(block, 'fsdp', pair) for block, pair in zip(far, pairs)]  29.2 us
    all_to_all x4, starting transfers between devices, exchange(): lax.all_to_all(near, 'fsdp', split_axis=0, concat_axis=0, tiled=True, axi...  15.6 us
    unnamed x44, local copies, waits for them, and re-layouts  12.7 us
    pallas_call x1, Pallas kernels, shards(): call(functools.partial(pack_kernel, m), flat, [SMEM, SMEM, HBM, HBM], [HB...  2.53 us
    ppermute x4, waiting for transfers between devices, gather(): lax.ppermute(half, 'fsdp', [(f, f ^ 1) for f in range(n)])  2.17 us
  transfers between devices with their start and end apart: 24, of which 17 were waited for; matrix products, arithmetic and copies ran while one was open for 0% of the time, Pallas kernels for 3%

profile of v6, /device:TPU:0, one launch (start us, length us, event | category | flops | bytes accessed | tf_op | source)
XLA Modules:
  0.0 103.3 jit_solution(5293791351309007260)
XLA Ops:
  1.4 2.5 %shard_map.85 = (bf16[4,272,128]{2,1,0:T(8,128)(2,1)}, bf16[272,128]{1,0:T(8,128)(2,1)}, bf16[272,128]{1,0:T(8,128)(2,1)}, bf16[272,128]{1,0:T(8,128)(2,1)}, bf16[272,128]{1,0:T(8,128)(2,1)}) custom-call(s32[1]{0:T(128)S(6)} %copy.9.id_ref, s32[16]{0:T(128)} %storage_ref.1, bf16[1,16,8192]{2,1,0:T(8,128)(2,1)} %down_hbm.1, bf16[1,16,8192]{2,1,0:T(8,128)(2,1)} %up_hbm.1), custom_call_target="tpu_custom_call" | custom-call | tf_op jit(solution)/shard_map/pallas_call | solution.py:227
  4.0 5.3 %all-to-all-start = ((bf16[4,272,128]{2,1,0:T(8,128)(2,1)}), bf16[4,272,128]{2,1,0:T(8,128)(2,1)S(1)}, u32[]{:S(2)}, u32[]{:S(2)}) async-start(bf16[4,272,128]{2,1,0:T(8,128)(2,1)} %get-tuple-element.26), calls=%async_computation | async-start | bytes 557056 | tf_op jit(solution)/shard_map/all_to_all | solution.py:211
  9.2 4.9 %collective-permute-start = (bf16[272,128]{1,0:T(8,128)(2,1)}, bf16[272,128]{1,0:T(8,128)(2,1)S(1)}, u32[]{:S(2)}, u32[]{:S(2)}) collective-permute-start(bf16[272,128]{1,0:T(8,128)(2,1)} %get-tuple-element.27), channel_id=1, source_target_pairs={{0,14},{1,15},{2,12},{3,13},{4,10},{5,11},{6,8},{7,9},{8,6},{9,7},... | collective-permute-start | bytes 208904 | tf_op jit(solution)/shard_map/ppermute | solution.py:209
  14.8 2.4 %collective-permute-start.3 = (bf16[272,128]{1,0:T(8,128)(2,1)}, bf16[272,128]{1,0:T(8,128)(2,1)S(1)}, u32[]{:S(2)}, u32[]{:S(2)}) collective-permute-start(bf16[272,128]{1,0:T(8,128)(2,1)} %get-tuple-element.30), channel_id=1, source_target_pairs={{0,8},{1,9},{2,10},{3,11},{4,12},{5,13},{6,14},{7,15},{8,0},{9,1},... | collective-permute-start | bytes 208904 | tf_op jit(solution)/shard_map/ppermute | solution.py:209
  17.1 3.1 %collective-permute-done.refs_0_ = bf16[272,128]{1,0:T(8,128)(2,1)S(1)} collective-permute-done((bf16[272,128]{1,0:T(8,128)(2,1)}, bf16[272,128]{1,0:T(8,128)(2,1)S(1)}, u32[]{:S(2)}, u32[]{:S(2)}) %collective-permute-start) | collective-permute-done | bytes 69664 | tf_op jit(solution)/shard_map/ppermute | solution.py:209
  20.9 4.2 %collective-permute-done.2.refs_2_ = bf16[272,128]{1,0:T(8,128)(2,1)S(1)} collective-permute-done((bf16[272,128]{1,0:T(8,128)(2,1)}, bf16[272,128]{1,0:T(8,128)(2,1)S(1)}, u32[]{:S(2)}, u32[]{:S(2)}) %collective-permute-start.2) | collective-permute-done | bytes 69664 | tf_op jit(solution)/shard_map/ppermute | solution.py:209
  31.3 3.4 %all-to-all-start.1 = ((bf16[4,32,1024]{2,1,0:T(8,128)(2,1)}), bf16[4,32,1024]{2,1,0:T(8,128)(2,1)S(1)}, u32[]{:S(2)}, u32[]{:S(2)}) async-start(bf16[4,32,1024]{2,1,0:T(8,128)(2,1)} %copy-done.12), calls=%async_computation.1 | async-start | bytes 524288 | tf_op jit(solution)/shard_map/all_to_all | solution.py:211
  34.7 3.1 %collective-permute-start.6 = (bf16[32,1024]{1,0:T(8,128)(2,1)}, bf16[32,1024]{1,0:T(8,128)(2,1)S(1)}, u32[]{:S(2)}, u32[]{:S(2)}) collective-permute-start(bf16[32,1024]{1,0:T(8,128)(2,1)} %copy-done.21), channel_id=1, source_target_pairs={{0,14},{1,15},{2,12},{3,13},{4,10},{5,11},{6,8},{7,9},{8,6},{9,7},... | collective-permute-start | bytes 196616 | tf_op jit(solution)/shard_map/ppermute | solution.py:209
  37.8 2.2 %collective-permute-start.7 = (bf16[32,1024]{1,0:T(8,128)(2,1)}, bf16[32,1024]{1,0:T(8,128)(2,1)S(1)}, u32[]{:S(2)}, u32[]{:S(2)}) collective-permute-start(bf16[32,1024]{1,0:T(8,128)(2,1)} %copy-done.19), channel_id=1, source_target_pairs={{0,12},{1,13},{2,14},{3,15},{4,8},{5,9},{6,10},{7,11},{8,4},{9,5},... | collective-permute-start | bytes 196616 | tf_op jit(solution)/shard_map/ppermute | solution.py:209
  40.0 2.5 %collective-permute-start.9 = (bf16[32,1024]{1,0:T(8,128)(2,1)}, bf16[32,1024]{1,0:T(8,128)(2,1)S(1)}, u32[]{:S(2)}, u32[]{:S(2)}) collective-permute-start(bf16[32,1024]{1,0:T(8,128)(2,1)} %copy-done.13), channel_id=1, source_target_pairs={{0,8},{1,9},{2,10},{3,11},{4,12},{5,13},{6,14},{7,15},{8,0},{9,1},... | collective-permute-start | bytes 196616 | tf_op jit(solution)/shard_map/ppermute | solution.py:209
  45.1 5.1 %collective-permute-done.8.refs_2_ = bf16[32,1024]{1,0:T(8,128)(2,1)S(1)} collective-permute-done((bf16[32,1024]{1,0:T(8,128)(2,1)}, bf16[32,1024]{1,0:T(8,128)(2,1)S(1)}, u32[]{:S(2)}, u32[]{:S(2)}) %collective-permute-start.8) | collective-permute-done | bytes 65568 | tf_op jit(solution)/shard_map/ppermute | solution.py:209
  51.6 1.6 %copy-done.1 = bf16[128,8192]{1,0:T(8,128)(2,1)S(1)} copy-done((bf16[128,8192]{1,0:T(8,128)(2,1)S(1)}, bf16[128,8192]{1,0:T(8,128)(2,1)}, u32[]{:S(2)}) %copy-start.1) | copy-done | bytes 2097176
  55.7 1.8 %shard_map.90 = (bf16[16,128]{1,0:T(8,128)(2,1)S(1)}, bf16[4,32,1024]{2,1,0:T(8,128)(2,1)S(1)}, bf16[32,1024]{1,0:T(8,128)(2,1)S(1)}, bf16[32,1024]{1,0:T(8,128)...) custom-call(f32[8,128]{1,0:T(8,128)S(1)} %shard_map.89._, bf16[128,8192]{1,0:T(8,128)(2,1)S(1)} %copy-done.1, ...), custom_call_target="tpu_custom_call" | custom-call | tf_op jit(solution)/shard_map/pallas_call | solution.py:250
  60.7 3.5 %all-to-all-start.2 = ((bf16[4,32,1024]{2,1,0:T(8,128)(2,1)}), bf16[4,32,1024]{2,1,0:T(8,128)(2,1)S(1)}, u32[]{:S(2)}, u32[]{:S(2)}) async-start(bf16[4,32,1024]{2,1,0:T(8,128)(2,1)} %copy-done.11), calls=%async_computation.2 | async-start | bytes 524288 | tf_op jit(solution)/shard_map/all_to_all | solution.py:211
  64.3 2.5 %collective-permute-start.10 = (bf16[32,1024]{1,0:T(8,128)(2,1)}, bf16[32,1024]{1,0:T(8,128)(2,1)S(1)}, u32[]{:S(2)}, u32[]{:S(2)}) collective-permute-start(bf16[32,1024]{1,0:T(8,128)(2,1)} %copy-done.20), channel_id=1, source_target_pairs={{0,14},{1,15},{2,12},{3,13},{4,10},{5,11},{6,8},{7,9},{8,6},{9,7},... | collective-permute-start | bytes 196616 | tf_op jit(solution)/shard_map/ppermute | solution.py:209
  66.8 2.7 %collective-permute-start.11 = (bf16[32,1024]{1,0:T(8,128)(2,1)}, bf16[32,1024]{1,0:T(8,128)(2,1)S(1)}, u32[]{:S(2)}, u32[]{:S(2)}) collective-permute-start(bf16[32,1024]{1,0:T(8,128)(2,1)} %copy-done.18), channel_id=1, source_target_pairs={{0,12},{1,13},{2,14},{3,15},{4,8},{5,9},{6,10},{7,11},{8,4},{9,5},... | collective-permute-start | bytes 196616 | tf_op jit(solution)/shard_map/ppermute | solution.py:209
  69.5 2.5 %collective-permute-start.13 = (bf16[32,1024]{1,0:T(8,128)(2,1)}, bf16[32,1024]{1,0:T(8,128)(2,1)S(1)}, u32[]{:S(2)}, u32[]{:S(2)}) collective-permute-start(bf16[32,1024]{1,0:T(8,128)(2,1)} %copy-done.15), channel_id=1, source_target_pairs={{0,8},{1,9},{2,10},{3,11},{4,12},{5,13},{6,14},{7,15},{8,0},{9,1},... | collective-permute-start | bytes 196616 | tf_op jit(solution)/shard_map/ppermute | solution.py:209
  73.5 5.3 %collective-permute-done.12.refs_2_ = bf16[32,1024]{1,0:T(8,128)(2,1)S(1)} collective-permute-done((bf16[32,1024]{1,0:T(8,128)(2,1)}, bf16[32,1024]{1,0:T(8,128)(2,1)S(1)}, u32[]{:S(2)}, u32[]{:S(2)}) %collective-permute-start.12) | collective-permute-done | bytes 65568 | tf_op jit(solution)/shard_map/ppermute | solution.py:209
  83.0 3.4 %all-to-all-start.3 = ((bf16[4,32,1024]{2,1,0:T(8,128)(2,1)}), bf16[4,32,1024]{2,1,0:T(8,128)(2,1)S(1)}, u32[]{:S(2)}, u32[]{:S(2)}) async-start(bf16[4,32,1024]{2,1,0:T(8,128)(2,1)} %get-tuple-element.43), calls=%async_computation.3 | async-start | bytes 524288 | tf_op jit(solution)/shard_map/all_to_all | solution.py:211
  86.4 2.7 %collective-permute-start.16 = (bf16[32,1024]{1,0:T(8,128)(2,1)S(1)}, bf16[32,1024]{1,0:T(8,128)(2,1)S(1)}, u32[]{:S(2)}, u32[]{:S(2)}) collective-permute-start(bf16[32,1024]{1,0:T(8,128)(2,1)S(1)} %get-tuple-element.44), channel_id=1, source_target_pairs={{0,14},{1,15},{2,12},{3,13},{4,10},{5,11},{6,8},{7,9},{8,6},{9,7},... | collective-permute-start | bytes 196616 | tf_op jit(solution)/shard_map/ppermute | solution.py:209
  89.1 2.6 %collective-permute-start.17 = (bf16[32,1024]{1,0:T(8,128)(2,1)S(1)}, bf16[32,1024]{1,0:T(8,128)(2,1)S(1)}, u32[]{:S(2)}, u32[]{:S(2)}) collective-permute-start(bf16[32,1024]{1,0:T(8,128)(2,1)S(1)} %get-tuple-element.45), channel_id=1, source_target_pairs={{0,12},{1,13},{2,14},{3,15},{4,8},{5,9},{6,10},{7,11},{8,4},{9,5},... | collective-permute-start | bytes 196616 | tf_op jit(solution)/shard_map/ppermute | solution.py:209
  91.7 2.5 %collective-permute-start.19 = (bf16[32,1024]{1,0:T(8,128)(2,1)S(1)}, bf16[32,1024]{1,0:T(8,128)(2,1)S(1)}, u32[]{:S(2)}, u32[]{:S(2)}) collective-permute-start(bf16[32,1024]{1,0:T(8,128)(2,1)S(1)} %get-tuple-element.41._), channel_id=1, source_target_pairs={{0,8},{1,9},{2,10},{3,11},{4,12},{5,13},{6,14},{7,15},{8,0},{9,1},... | collective-permute-start | bytes 196616 | tf_op jit(solution)/shard_map/ppermute | solution.py:209
  94.1 2.0 %shard_map.93 = bf16[128,8192]{1,0:T(8,128)(2,1)} custom-call(bf16[32,1024]{1,0:T(8,128)(2,1)S(1)} %get-tuple-element.41._, bf16[16,128]{1,0:T(8,128)(2,1)S(1)} %get-tuple-element.42.low_ref, bf16[4,32,1024]{2,1,0:T(8,128)(2,1)S(1)} %all-to-all-done.1.near_in.near_ref, bf16[32,1024]{1,0:T(8,128)(2,1)S(1)} %collective-permute-done.6.refs_0_, ...), custom_call_target="tpu_custom_call" | custom-call | flops 33554432 | bytes 2097152 | tf_op jit(solution)/shard_map/pallas_call | solution.py:260
  96.2 5.5 %collective-permute-done.18.refs_2_ = bf16[32,1024]{1,0:T(8,128)(2,1)S(1)} collective-permute-done((bf16[32,1024]{1,0:T(8,128)(2,1)S(1)}, bf16[32,1024]{1,0:T(8,128)(2,1)S(1)}, u32[]{:S(2)}, u32[]{:S(2)}) %collective-permute-start.18) | collective-permute-done | bytes 65568 | tf_op jit(solution)/shard_map/ppermute | solution.py:209
  (78 shorter events, 24.4 us)
Async XLA Ops:
  4.0 22.4 %all-to-all-start = ((bf16[4,272,128]{2,1,0:T(8,128)(2,1)}), bf16[4,272,128]{2,1,0:T(8,128)(2,1)S(1)}, u32[]{:S(2)}, u32[]{:S(2)}) async-start(bf16[4,272,128]{2,1,0:T(8,128)(2,1)} %get-tuple-element.26), calls=%async_computation | async-start | bytes 557056 | tf_op jit(solution)/shard_map/all_to_all | solution.py:211
  9.2 11.0 %collective-permute-start = (bf16[272,128]{1,0:T(8,128)(2,1)}, bf16[272,128]{1,0:T(8,128)(2,1)S(1)}, u32[]{:S(2)}, u32[]{:S(2)}) collective-permute-start(bf16[272,128]{1,0:T(8,128)(2,1)} %get-tuple-element.27), channel_id=1, source_target_pairs={{0,14},{1,15},{2,12},{3,13},{4,10},{5,11},{6,8},{7,9},{8,6},{9,7},... | collective-permute-start | bytes 208904 | tf_op jit(solution)/shard_map/ppermute | solution.py:209
  14.2 6.8 %collective-permute-start.1 = (bf16[272,128]{1,0:T(8,128)(2,1)}, bf16[272,128]{1,0:T(8,128)(2,1)S(1)}, u32[]{:S(2)}, u32[]{:S(2)}) collective-permute-start(bf16[272,128]{1,0:T(8,128)(2,1)} %get-tuple-element.28), channel_id=1, source_target_pairs={{0,12},{1,13},{2,14},{3,15},{4,8},{5,9},{6,10},{7,11},{8,4},{9,5},... | collective-permute-start | bytes 208904 | tf_op jit(solution)/shard_map/ppermute | solution.py:209
  14.5 10.6 %collective-permute-start.2 = (bf16[272,128]{1,0:T(8,128)(2,1)}, bf16[272,128]{1,0:T(8,128)(2,1)S(1)}, u32[]{:S(2)}, u32[]{:S(2)}) collective-permute-start(bf16[272,128]{1,0:T(8,128)(2,1)} %get-tuple-element.29), channel_id=1, source_target_pairs={{0,10},{1,11},{2,8},{3,9},{4,14},{5,15},{6,12},{7,13},{8,2},{9,3},... | collective-permute-start | bytes 208904 | tf_op jit(solution)/shard_map/ppermute | solution.py:209
  14.8 11.5 %collective-permute-start.3 = (bf16[272,128]{1,0:T(8,128)(2,1)}, bf16[272,128]{1,0:T(8,128)(2,1)S(1)}, u32[]{:S(2)}, u32[]{:S(2)}) collective-permute-start(bf16[272,128]{1,0:T(8,128)(2,1)} %get-tuple-element.30), channel_id=1, source_target_pairs={{0,8},{1,9},{2,10},{3,11},{4,12},{5,13},{6,14},{7,15},{8,0},{9,1},... | collective-permute-start | bytes 208904 | tf_op jit(solution)/shard_map/ppermute | solution.py:209
  26.3 1.6 %collective-permute-start.5 = (bf16[4,272,128]{2,1,0:T(8,128)(2,1)S(1)}, bf16[4,272,128]{2,1,0:T(8,128)(2,1)S(1)}, u32[]{:S(2)}, u32[]{:S(2)}) collective-permute-start(bf16[4,272,128]{2,1,0:T(8,128)(2,1)S(1)} %shard_map.86.own_far), channel_id=1, source_target_pairs={{0,1},{1,0},{2,3},{3,2},{4,5},{5,4},{6,7},{7,6},{8,9},{9,8},{10,11... | collective-permute-start | bytes 835592 | tf_op jit(solution)/shard_map/ppermute | solution.py:219
  26.4 1.9 %collective-permute-start.4 = (bf16[4,272,128]{2,1,0:T(8,128)(2,1)S(1)}, bf16[4,272,128]{2,1,0:T(8,128)(2,1)S(1)}, u32[]{:S(2)}, u32[]{:S(2)}) collective-permute-start(bf16[4,272,128]{2,1,0:T(8,128)(2,1)S(1)} %all-to-all-done.own_near), channel_id=1, source_target_pairs={{0,1},{1,0},{2,3},{3,2},{4,5},{5,4},{6,7},{7,6},{8,9},{9,8},{10,11... | collective-permute-start | bytes 835592 | tf_op jit(solution)/shard_map/ppermute | solution.py:219
  31.3 20.3 %all-to-all-start.1 = ((bf16[4,32,1024]{2,1,0:T(8,128)(2,1)}), bf16[4,32,1024]{2,1,0:T(8,128)(2,1)S(1)}, u32[]{:S(2)}, u32[]{:S(2)}) async-start(bf16[4,32,1024]{2,1,0:T(8,128)(2,1)} %copy-done.12), calls=%async_computation.1 | async-start | bytes 524288 | tf_op jit(solution)/shard_map/all_to_all | solution.py:211
  34.7 8.6 %collective-permute-start.6 = (bf16[32,1024]{1,0:T(8,128)(2,1)}, bf16[32,1024]{1,0:T(8,128)(2,1)S(1)}, u32[]{:S(2)}, u32[]{:S(2)}) collective-permute-start(bf16[32,1024]{1,0:T(8,128)(2,1)} %copy-done.21), channel_id=1, source_target_pairs={{0,14},{1,15},{2,12},{3,13},{4,10},{5,11},{6,8},{7,9},{8,6},{9,7},... | collective-permute-start | bytes 196616 | tf_op jit(solution)/shard_map/ppermute | solution.py:209
  37.8 6.7 %collective-permute-start.7 = (bf16[32,1024]{1,0:T(8,128)(2,1)}, bf16[32,1024]{1,0:T(8,128)(2,1)S(1)}, u32[]{:S(2)}, u32[]{:S(2)}) collective-permute-start(bf16[32,1024]{1,0:T(8,128)(2,1)} %copy-done.19), channel_id=1, source_target_pairs={{0,12},{1,13},{2,14},{3,15},{4,8},{5,9},{6,10},{7,11},{8,4},{9,5},... | collective-permute-start | bytes 196616 | tf_op jit(solution)/shard_map/ppermute | solution.py:209
  40.0 10.3 %collective-permute-start.8 = (bf16[32,1024]{1,0:T(8,128)(2,1)}, bf16[32,1024]{1,0:T(8,128)(2,1)S(1)}, u32[]{:S(2)}, u32[]{:S(2)}) collective-permute-start(bf16[32,1024]{1,0:T(8,128)(2,1)} %copy-done.17), channel_id=1, source_target_pairs={{0,10},{1,11},{2,8},{3,9},{4,14},{5,15},{6,12},{7,13},{8,2},{9,3},... | collective-permute-start | bytes 196616 | tf_op jit(solution)/shard_map/ppermute | solution.py:209
  40.0 11.0 %collective-permute-start.9 = (bf16[32,1024]{1,0:T(8,128)(2,1)}, bf16[32,1024]{1,0:T(8,128)(2,1)S(1)}, u32[]{:S(2)}, u32[]{:S(2)}) collective-permute-start(bf16[32,1024]{1,0:T(8,128)(2,1)} %copy-done.13), channel_id=1, source_target_pairs={{0,8},{1,9},{2,10},{3,11},{4,12},{5,13},{6,14},{7,15},{8,0},{9,1},... | collective-permute-start | bytes 196616 | tf_op jit(solution)/shard_map/ppermute | solution.py:209
  60.7 18.8 %all-to-all-start.2 = ((bf16[4,32,1024]{2,1,0:T(8,128)(2,1)}), bf16[4,32,1024]{2,1,0:T(8,128)(2,1)S(1)}, u32[]{:S(2)}, u32[]{:S(2)}) async-start(bf16[4,32,1024]{2,1,0:T(8,128)(2,1)} %copy-done.11), calls=%async_computation.2 | async-start | bytes 524288 | tf_op jit(solution)/shard_map/all_to_all | solution.py:211
  64.3 8.1 %collective-permute-start.10 = (bf16[32,1024]{1,0:T(8,128)(2,1)}, bf16[32,1024]{1,0:T(8,128)(2,1)S(1)}, u32[]{:S(2)}, u32[]{:S(2)}) collective-permute-start(bf16[32,1024]{1,0:T(8,128)(2,1)} %copy-done.20), channel_id=1, source_target_pairs={{0,14},{1,15},{2,12},{3,13},{4,10},{5,11},{6,8},{7,9},{8,6},{9,7},... | collective-permute-start | bytes 196616 | tf_op jit(solution)/shard_map/ppermute | solution.py:209
  66.8 6.7 %collective-permute-start.11 = (bf16[32,1024]{1,0:T(8,128)(2,1)}, bf16[32,1024]{1,0:T(8,128)(2,1)S(1)}, u32[]{:S(2)}, u32[]{:S(2)}) collective-permute-start(bf16[32,1024]{1,0:T(8,128)(2,1)} %copy-done.18), channel_id=1, source_target_pairs={{0,12},{1,13},{2,14},{3,15},{4,8},{5,9},{6,10},{7,11},{8,4},{9,5},... | collective-permute-start | bytes 196616 | tf_op jit(solution)/shard_map/ppermute | solution.py:209
  69.5 9.3 %collective-permute-start.12 = (bf16[32,1024]{1,0:T(8,128)(2,1)}, bf16[32,1024]{1,0:T(8,128)(2,1)S(1)}, u32[]{:S(2)}, u32[]{:S(2)}) collective-permute-start(bf16[32,1024]{1,0:T(8,128)(2,1)} %copy-done.16), channel_id=1, source_target_pairs={{0,10},{1,11},{2,8},{3,9},{4,14},{5,15},{6,12},{7,13},{8,2},{9,3},... | collective-permute-start | bytes 196616 | tf_op jit(solution)/shard_map/ppermute | solution.py:209
  69.5 9.9 %collective-permute-start.13 = (bf16[32,1024]{1,0:T(8,128)(2,1)}, bf16[32,1024]{1,0:T(8,128)(2,1)S(1)}, u32[]{:S(2)}, u32[]{:S(2)}) collective-permute-start(bf16[32,1024]{1,0:T(8,128)(2,1)} %copy-done.15), channel_id=1, source_target_pairs={{0,8},{1,9},{2,10},{3,11},{4,12},{5,13},{6,14},{7,15},{8,0},{9,1},... | collective-permute-start | bytes 196616 | tf_op jit(solution)/shard_map/ppermute | solution.py:209
  79.4 1.6 %collective-permute-start.15 = (bf16[4,32,1024]{2,1,0:T(8,128)(2,1)S(1)}, bf16[4,32,1024]{2,1,0:T(8,128)(2,1)S(1)}, u32[]{:S(2)}, u32[]{:S(2)}) collective-permute-start(bf16[4,32,1024]{2,1,0:T(8,128)(2,1)S(1)} %shard_map.91.own_far), channel_id=1, source_target_pairs={{0,1},{1,0},{2,3},{3,2},{4,5},{5,4},{6,7},{7,6},{8,9},{9,8},{10,11... | collective-permute-start | bytes 786440 | tf_op jit(solution)/shard_map/ppermute | solution.py:219
  79.5 1.9 %collective-permute-start.14 = (bf16[4,32,1024]{2,1,0:T(8,128)(2,1)S(1)}, bf16[4,32,1024]{2,1,0:T(8,128)(2,1)S(1)}, u32[]{:S(2)}, u32[]{:S(2)}) collective-permute-start(bf16[4,32,1024]{2,1,0:T(8,128)(2,1)S(1)} %all-to-all-done.2.own_near), channel_id=1, source_target_pairs={{0,1},{1,0},{2,3},{3,2},{4,5},{5,4},{6,7},{7,6},{8,9},{9,8},{10,11... | collective-permute-start | bytes 786440 | tf_op jit(solution)/shard_map/ppermute | solution.py:219
  83.0 19.4 %all-to-all-start.3 = ((bf16[4,32,1024]{2,1,0:T(8,128)(2,1)}), bf16[4,32,1024]{2,1,0:T(8,128)(2,1)S(1)}, u32[]{:S(2)}, u32[]{:S(2)}) async-start(bf16[4,32,1024]{2,1,0:T(8,128)(2,1)} %get-tuple-element.43), calls=%async_computation.3 | async-start | bytes 524288 | tf_op jit(solution)/shard_map/all_to_all | solution.py:211
  86.4 9.8 %collective-permute-start.16 = (bf16[32,1024]{1,0:T(8,128)(2,1)S(1)}, bf16[32,1024]{1,0:T(8,128)(2,1)S(1)}, u32[]{:S(2)}, u32[]{:S(2)}) collective-permute-start(bf16[32,1024]{1,0:T(8,128)(2,1)S(1)} %get-tuple-element.44), channel_id=1, source_target_pairs={{0,14},{1,15},{2,12},{3,13},{4,10},{5,11},{6,8},{7,9},{8,6},{9,7},... | collective-permute-start | bytes 196616 | tf_op jit(solution)/shard_map/ppermute | solution.py:209
  89.1 7.1 %collective-permute-start.17 = (bf16[32,1024]{1,0:T(8,128)(2,1)S(1)}, bf16[32,1024]{1,0:T(8,128)(2,1)S(1)}, u32[]{:S(2)}, u32[]{:S(2)}) collective-permute-start(bf16[32,1024]{1,0:T(8,128)(2,1)S(1)} %get-tuple-element.45), channel_id=1, source_target_pairs={{0,12},{1,13},{2,14},{3,15},{4,8},{5,9},{6,10},{7,11},{8,4},{9,5},... | collective-permute-start | bytes 196616 | tf_op jit(solution)/shard_map/ppermute | solution.py:209
  91.7 10.1 %collective-permute-start.18 = (bf16[32,1024]{1,0:T(8,128)(2,1)S(1)}, bf16[32,1024]{1,0:T(8,128)(2,1)S(1)}, u32[]{:S(2)}, u32[]{:S(2)}) collective-permute-start(bf16[32,1024]{1,0:T(8,128)(2,1)S(1)} %get-tuple-element.46), channel_id=1, source_target_pairs={{0,10},{1,11},{2,8},{3,9},{4,14},{5,15},{6,12},{7,13},{8,2},{9,3},... | collective-permute-start | bytes 196616 | tf_op jit(solution)/shard_map/ppermute | solution.py:209
  91.7 10.8 %collective-permute-start.19 = (bf16[32,1024]{1,0:T(8,128)(2,1)S(1)}, bf16[32,1024]{1,0:T(8,128)(2,1)S(1)}, u32[]{:S(2)}, u32[]{:S(2)}) collective-permute-start(bf16[32,1024]{1,0:T(8,128)(2,1)S(1)} %get-tuple-element.41._), channel_id=1, source_target_pairs={{0,8},{1,9},{2,10},{3,11},{4,12},{5,13},{6,14},{7,15},{8,0},{9,1},... | collective-permute-start | bytes 196616 | tf_op jit(solution)/shard_map/ppermute | solution.py:209
  (22 other events, 158.1 us)

commit v7 on v5

--- a/solution.py
+++ b/solution.py
@@ -23,13 +23,12 @@
     return me // 2, me % 2
 
 
-def halves(m):
-    return [*range(m // 2)], [*range(m - 1, m // 2 - 1, -1)]
-
-
 def offsets(m):
-    near, far = halves(m)
-    return near[:1] + far[:2] + near[1:2] + far[2:] + near[2:]
+    return [0, 1, *range(m - 1, m // 2 - 1, -1), *range(2, m // 2)]
+
+
+def rank(k, m):
+    return jnp.where(k < 2, k, jnp.where(k < m // 2, m // 2 + k, m + 1 - k))
 
 
 def columns(chunk, w):
@@ -37,24 +36,39 @@
 
 
 def pack_kernel(m, id_ref, storage_ref, down_hbm, up_hbm, *refs):
-    outs, down_ref, up_ref, sems = refs[:m], *refs[m:]
-    p, _ = position()
-    loads = [
-        pltpu.make_async_copy(down_hbm, down_ref, sems.at[0]),
-        pltpu.make_async_copy(up_hbm, up_ref, sems.at[1]),
-    ]
-    for load in loads:
-        load.start()
-    for load in loads:
-        load.wait()
-    r, w = down_ref.shape[1], down_ref.shape[2] // m
+    outs, (down_ref, up_ref, out_ref, load_sems, store_sems) = refs[:m], refs[m:]
+    p, _ = position()
+    r, w = down_ref.shape[0], down_ref.shape[1] // m
+    order = [*zip(range(m), offsets(m), outs)]
+    order = order[1:] + order[:1]
+    loads = []
+    for i, k, _ in order:
+        cols = columns(p ^ k, w)
+        loads.append(
+            [
+                pltpu.make_async_copy(src.at[0, :, cols], dst.at[:, i * w : (i + 1) * w], sem)
+                for src, dst, sem in (
+                    (down_hbm, down_ref, load_sems.at[0, i]),
+                    (up_hbm, up_ref, load_sems.at[1, i]),
+                )
+            ]
+        )
+        for load in loads[-1]:
+            load.start()
     mark = jnp.full((ID_ROWS, LANES), storage_ref[id_ref[0]].astype(F32), F32).astype(BF16)
-    for out, k in zip(outs, offsets(m)):
+    stores = []
+    for (i, _, dst), pair in zip(order, loads):
+        for load in pair:
+            load.wait()
         for b in range(w // LANES):
-            cols = pl.ds(pl.multiple_of((p ^ k) * w + b * LANES, LANES), LANES)
-            out[2 * r * b : 2 * r * b + r, :] = down_ref[0, :, cols]
-            out[2 * r * b + r : 2 * r * (b + 1), :] = up_ref[0, :, cols]
-        out[2 * r * (w // LANES) :, :] = mark
+            cols = slice(i * w + b * LANES, i * w + (b + 1) * LANES)
+            out_ref[i, 2 * r * b : 2 * r * b + r, :] = down_ref[:, cols]
+            out_ref[i, 2 * r * b + r : 2 * r * (b + 1), :] = up_ref[:, cols]
+        out_ref[i, 2 * r * (w // LANES) :, :] = mark
+        stores.append(pltpu.make_async_copy(out_ref.at[i], dst, store_sems.at[i]))
+        stores[-1].start()
+    for store in stores:
+        store.wait()
 
 
 def stack_kernel(*refs):
@@ -74,19 +88,22 @@
 
 
 def pick(held, chip, here, rows):
-    own_near, own_far, other_near, other_far = held
-    h = own_near.shape[0]
-    k = chip ^ position()[0]
-    near, u, v = k < h, lax.rem(k, h), h - 1 - lax.rem(k, h)
-    own = jnp.where(near, own_near[u, rows, :], own_far[v, rows, :])
-    other = jnp.where(near, other_near[u, rows, :], other_far[v, rows, :])
+    own_a, own_b, other_a, other_b = held
+    h = own_a.shape[0]
+    at = rank(chip ^ position()[0], 2 * h)
+    in_a, at = at < h, lax.rem(at, h)
+    own = jnp.where(in_a, own_a[at, rows, :], own_b[at, rows, :])
+    other = jnp.where(in_a, other_a[at, rows, :], other_b[at, rows, :])
     return jnp.where(here, own, other)
 
 
-def slot_of(near, far, k):
-    h = near.shape[0]
-    ref, at = (near, k) if k < h else (far, 2 * h - 1 - k)
-    return ref[at, ref.shape[1] - ID_ROWS :, :].astype(F32)[0, 0].astype(jnp.int32)
+def marks(*halves):
+    h, rows, _ = halves[0].shape
+    return [
+        half[at, rows - ID_ROWS :, :].astype(F32)[0, 0].astype(jnp.int32)
+        for half in halves
+        for at in range(h)
+    ]
 
 
 def deliver_kernel(m, *refs):
@@ -94,22 +111,20 @@
     _, c = position()
     r2 = outs[0].shape[0]
     blocks = (held[0].shape[1] - ID_ROWS) // r2
-    slots = [slot_of(*held[:2], k) for k in offsets(m)]
-    for out, slot in zip(outs, slots):
+    for out, slot in zip(outs, marks(*held[:2])):
         for b in range(blocks):
             rows = slice(b * r2, (b + 1) * r2)
             out[:, b * LANES : (b + 1) * LANES] = pick(held, slot // 2, slot % 2 == c, rows)
 
 
-def inverse_kernel(m, own_near, own_far, other_near, other_far, tile_of):
+def inverse_kernel(m, own_a, own_b, other_a, other_b, tile_of):
     p, c = position()
-    for near, far, core in ((own_near, own_far, c), (other_near, other_far, 1 - c)):
-        slots = [slot_of(near, far, k) for k in range(m)]
-        for k, slot in enumerate(slots):
+    for slots, core in ((marks(own_a, own_b), c), (marks(other_a, other_b), 1 - c)):
+        for k, slot in zip(offsets(m), slots):
             tile_of[slot] = 2 * (p ^ k) + core
 
 
-def touch_kernel(_, token_ref):
+def touch_kernel(after, array, token_ref):
     token_ref[...] = jnp.zeros_like(token_ref)
 
 
@@ -135,7 +150,7 @@
         out[r:r2, :] = jnp.dot(low_u, cot_ref[:, cols], preferred_element_type=F32).astype(BF16)
 
 
-def inputs_kernel(m, low_ref, *refs):
+def inputs_kernel(m, _, low_ref, *refs):
     factors, gx_ref = refs[:m], refs[m]
     p, _ = position()
     r2, w = factors[0].shape
@@ -178,8 +193,7 @@
         ]
 
     def gather(blocks):
-        by_offset = dict(zip(offsets(m), blocks))
-        own = [stack([by_offset[k] for k in half]) for half in halves(m)]
+        own = [stack(blocks[: m // 2]), stack(blocks[m // 2 :])]
         return own + [lax.ppermute(half, "fsdp", [(f, f ^ 1) for f in range(n)]) for half in own]
 
     rows = 2 * r * w // LANES
@@ -189,23 +203,17 @@
         functools.partial(pack_kernel, m),
         out_shape=[flat] * m,
         in_specs=[SMEM, SMEM, HBM, HBM],
-        out_specs=[VMEM] * m,
+        out_specs=[HBM] * m,
         scratch_shapes=[
-            pltpu.VMEM(down.shape, BF16),
-            pltpu.VMEM(up.shape, BF16),
-            pltpu.SemaphoreType.DMA((2,)),
+            pltpu.VMEM((r, d), BF16),
+            pltpu.VMEM((r, d), BF16),
+            pltpu.VMEM((m, *flat.shape), BF16),
+            pltpu.SemaphoreType.DMA((2, m)),
+            pltpu.SemaphoreType.DMA((m,)),
         ],
         compiler_params=ALONE,
     )(adapter_per_tile, adapter_storage_slot, down, up)
-    token = pl.pallas_call(
-        touch_kernel,
-        out_shape=jax.ShapeDtypeStruct((8, LANES), F32),
-        in_specs=[VMEM],
-        out_specs=VMEM,
-        compiler_params=PARAMS,
-    )(cotangent)
-    first = stack(spread[:1])[0]
-    held = gather(exchange([first, *spread[1:]]))
+    held = gather(exchange(spread))
     factors = pl.pallas_call(
         functools.partial(deliver_kernel, m),
         out_shape=[wide] * m,
@@ -213,6 +221,13 @@
         out_specs=[VMEM] * m,
         compiler_params=PARAMS,
     )(*held)
+    token = pl.pallas_call(
+        touch_kernel,
+        out_shape=jax.ShapeDtypeStruct((8, LANES), F32),
+        in_specs=[VMEM, VMEM],
+        out_specs=VMEM,
+        compiler_params=PARAMS,
+    )(factors[-1], cotangent)
     factors = exchange(factors)
     tile_of = pl.pallas_call(
         functools.partial(inverse_kernel, m),
@@ -229,16 +244,6 @@
         compiler_params=PARAMS,
     )(token, acts, cotangent, *factors)
     parts = exchange(parts)
-    grad_x = pl.pallas_call(
-        functools.partial(inputs_kernel, m),
-        out_shape=jax.ShapeDtypeStruct(acts.shape, BF16),
-        in_specs=[VMEM] * (m + 1),
-        out_specs=VMEM,
-        compiler_params=PARAMS,
-        cost_estimate=pl.CostEstimate(
-            flops=2 * r * acts.size, bytes_accessed=2 * acts.size, transcendentals=0
-        ),
-    )(low, *factors)
     owned = pl.pallas_call(
         functools.partial(collect_kernel, m),
         out_shape=[wide] * m,
@@ -246,6 +251,16 @@
         out_specs=[VMEM] * m,
         compiler_params=PARAMS,
     )(tile_of, *gather(parts))
+    grad_x = pl.pallas_call(
+        functools.partial(inputs_kernel, m),
+        out_shape=jax.ShapeDtypeStruct(acts.shape, BF16),
+        in_specs=[VMEM] * (m + 2),
+        out_specs=VMEM,
+        compiler_params=PARAMS,
+        cost_estimate=pl.CostEstimate(
+            flops=2 * r * acts.size, bytes_accessed=2 * acts.size, transcendentals=0
+        ),
+    )(owned[-1], low, *factors)
     grad_a, grad_b = pl.pallas_call(
         functools.partial(unpack_kernel, m),
         out_shape=[jax.ShapeDtypeStruct(down.shape, BF16)] * 2,

time: 82.6 us -> 80 us (0.969)
  starting transfers between devices: 58.4 us -> 49.8 us
  waiting for transfers between devices: 12.4 us -> 18.3 us
    ppermute x28, starting transfers between devices: 58.1 us -> 49.5 us  [exchange(): lax.ppermute(block, 'fsdp', [(2 * p + c, 2 * (p ^ k) + c) for p in range(...]
    ppermute x28, waiting for transfers between devices: 9.97 us -> 16 us  [exchange(): lax.ppermute(block, 'fsdp', [(2 * p + c, 2 * (p ^ k) + c) for p in range(...]
  transfers between devices with their start and end apart: 32 -> 32, of which waited for: 14 -> 13; matrix products, arithmetic and copies ran while one was open for 0% -> 0% of each run, Pallas kernels for 3% -> 4%
where the time goes in v7:
time: 80 us; the launch traced here: 79.7 us
  starting transfers between devices  49.8 us (62%)
  waiting for transfers between devices  18.3 us (23%)
  Pallas kernels  9.07 us (11%)
  between operations  1.55 us (2%)
  local copies, waits for them, and re-layouts  0.89 us (1%)
    ppermute x28, starting transfers between devices, exchange(): lax.ppermute(block, 'fsdp', [(2 * p + c, 2 * (p ^ k) + c) for p in range(...  49.5 us
    ppermute x28, waiting for transfers between devices, exchange(): lax.ppermute(block, 'fsdp', [(2 * p + c, 2 * (p ^ k) + c) for p in range(...  16 us
    pallas_call x1, Pallas kernels, shards(): pl.pallas_call(functools.partial(pack_kernel, m), out_shape=[flat] * m, i...  2.54 us
    ppermute x4, waiting for transfers between devices, gather(): lax.ppermute(half, 'fsdp', [(f, f ^ 1) for f in range(n)])  2.38 us
    pallas_call x1, Pallas kernels, shards(): pl.pallas_call(functools.partial(inputs_kernel, m), out_shape=jax.ShapeDt...  2.05 us
    pallas_call x1, Pallas kernels, shards(): pl.pallas_call(functools.partial(grads_kernel, m), out_shape=[jax.ShapeDt...  1.84 us
  transfers between devices with their start and end apart: 32, of which 13 were waited for; matrix products, arithmetic and copies ran while one was open for 0% of the time, Pallas kernels for 4%

profile of v7, /device:TPU:0, one launch (start us, length us, event | category | flops | bytes accessed | tf_op | source)
XLA Modules:
  0.0 79.7 jit_solution(10749237379577900842)
XLA Ops:
  1.4 2.5 %shard_map.85 = (bf16[272,128]{1,0:T(8,128)(2,1)}, bf16[272,128]{1,0:T(8,128)(2,1)}, bf16[272,128]{1,0:T(8,128)(2,1)}, bf16[272,128]{1,0:T(8,128)(2,1)}, bf16[27...) custom-call(s32[1]{0:T(128)S(6)} %copy.9.id_ref, ...), custom_call_target="tpu_custom_call" | custom-call | tf_op jit(solution)/shard_map/pallas_call | solution.py:202
  4.0 3.0 %collective-permute-start = (bf16[272,128]{1,0:T(8,128)(2,1)}, bf16[272,128]{1,0:T(8,128)(2,1)S(1)}, u32[]{:S(2)}, u32[]{:S(2)}) collective-permute-start(bf16[272,128]{1,0:T(8,128)(2,1)} %get-tuple-element.39), channel_id=1, source_target_pairs={{0,2},{1,3},{2,0},{3,1},{4,6},{5,7},{6,4},{7,5},{8,10},{9,11},{10,... | collective-permute-start | bytes 208904 | tf_op jit(solution)/shard_map/ppermute | solution.py:189
  7.0 3.5 %collective-permute-start.1 = (bf16[272,128]{1,0:T(8,128)(2,1)}, bf16[272,128]{1,0:T(8,128)(2,1)S(1)}, u32[]{:S(2)}, u32[]{:S(2)}) collective-permute-start(bf16[272,128]{1,0:T(8,128)(2,1)} %get-tuple-element.40), channel_id=1, source_target_pairs={{0,14},{1,15},{2,12},{3,13},{4,10},{5,11},{6,8},{7,9},{8,6},{9,7},... | collective-permute-start | bytes 208904 | tf_op jit(solution)/shard_map/ppermute | solution.py:189
  10.6 1.9 %collective-permute-start.3 = (bf16[272,128]{1,0:T(8,128)(2,1)}, bf16[272,128]{1,0:T(8,128)(2,1)S(1)}, u32[]{:S(2)}, u32[]{:S(2)}) collective-permute-start(bf16[272,128]{1,0:T(8,128)(2,1)} %get-tuple-element.42), channel_id=1, source_target_pairs={{0,10},{1,11},{2,8},{3,9},{4,14},{5,15},{6,12},{7,13},{8,2},{9,3},... | collective-permute-start | bytes 208904 | tf_op jit(solution)/shard_map/ppermute | solution.py:189
  12.5 2.1 %collective-permute-start.4 = (bf16[272,128]{1,0:T(8,128)(2,1)}, bf16[272,128]{1,0:T(8,128)(2,1)S(1)}, u32[]{:S(2)}, u32[]{:S(2)}) collective-permute-start(bf16[272,128]{1,0:T(8,128)(2,1)} %get-tuple-element.43), channel_id=1, source_target_pairs={{0,8},{1,9},{2,10},{3,11},{4,12},{5,13},{6,14},{7,15},{8,0},{9,1},... | collective-permute-start | bytes 208904 | tf_op jit(solution)/shard_map/ppermute | solution.py:189
  15.9 2.1 %collective-permute-start.6 = (bf16[272,128]{1,0:T(8,128)(2,1)}, bf16[272,128]{1,0:T(8,128)(2,1)S(1)}, u32[]{:S(2)}, u32[]{:S(2)}) collective-permute-start(bf16[272,128]{1,0:T(8,128)(2,1)} %get-tuple-element.45), channel_id=1, source_target_pairs={{0,6},{1,7},{2,4},{3,5},{4,2},{5,3},{6,0},{7,1},{8,14},{9,15},{10,... | collective-permute-start | bytes 208904 | tf_op jit(solution)/shard_map/ppermute | solution.py:189
  19.0 3.7 %collective-permute-done.3.refs_0_ = bf16[272,128]{1,0:T(8,128)(2,1)S(1)} collective-permute-done((bf16[272,128]{1,0:T(8,128)(2,1)}, bf16[272,128]{1,0:T(8,128)(2,1)S(1)}, u32[]{:S(2)}, u32[]{:S(2)}) %collective-permute-start.3) | collective-permute-done | bytes 69664 | tf_op jit(solution)/shard_map/ppermute | solution.py:189
  23.7 1.5 %collective-permute-done.8.other_b.refs_3_ = bf16[4,272,128]{2,1,0:T(8,128)(2,1)S(1)} collective-permute-done((bf16[4,272,128]{2,1,0:T(8,128)(2,1)S(1)}, bf16[4,272,128]{2,1,0:T(8,128)(2,1)S(1)}, u32[]{:S(2)}, u32[]{:S(2)}) %collective-permute-start.8) | collective-permute-done | bytes 278560 | tf_op jit(solution)/shard_map/ppermute | solution.py:197
  26.3 3.6 %collective-permute-start.10 = (bf16[32,1024]{1,0:T(8,128)(2,1)S(1)}, bf16[32,1024]{1,0:T(8,128)(2,1)S(1)}, u32[]{:S(2)}, u32[]{:S(2)}) collective-permute-start(bf16[32,1024]{1,0:T(8,128)(2,1)S(1)} %get-tuple-element.49), channel_id=1, source_target_pairs={{0,14},{1,15},{2,12},{3,13},{4,10},{5,11},{6,8},{7,9},{8,6},{9,7},... | collective-permute-start | bytes 196616 | tf_op jit(solution)/shard_map/ppermute | solution.py:189
  31.4 2.5 %collective-permute-start.13 = (bf16[32,1024]{1,0:T(8,128)(2,1)S(1)}, bf16[32,1024]{1,0:T(8,128)(2,1)S(1)}, u32[]{:S(2)}, u32[]{:S(2)}) collective-permute-start(bf16[32,1024]{1,0:T(8,128)(2,1)S(1)} %get-tuple-element.52), channel_id=1, source_target_pairs={{0,8},{1,9},{2,10},{3,11},{4,12},{5,13},{6,14},{7,15},{8,0},{9,1},... | collective-permute-start | bytes 196616 | tf_op jit(solution)/shard_map/ppermute | solution.py:189
  34.7 2.0 %collective-permute-start.15 = (bf16[32,1024]{1,0:T(8,128)(2,1)S(1)}, bf16[32,1024]{1,0:T(8,128)(2,1)S(1)}, u32[]{:S(2)}, u32[]{:S(2)}) collective-permute-start(bf16[32,1024]{1,0:T(8,128)(2,1)S(1)} %get-tuple-element.46.after), channel_id=1, source_target_pairs={{0,6},{1,7},{2,4},{3,5},{4,2},{5,3},{6,0},{7,1},{8,14},{9,15},{10,... | collective-permute-start | bytes 196616 | tf_op jit(solution)/shard_map/ppermute | solution.py:189
  36.8 2.7 %collective-permute-done.12.refs_4_ = bf16[32,1024]{1,0:T(8,128)(2,1)S(1)} collective-permute-done((bf16[32,1024]{1,0:T(8,128)(2,1)S(1)}, bf16[32,1024]{1,0:T(8,128)(2,1)S(1)}, u32[]{:S(2)}, u32[]{:S(2)}) %collective-permute-start.12) | collective-permute-done | bytes 65568 | tf_op jit(solution)/shard_map/ppermute | solution.py:189
  39.5 1.7 %collective-permute-done.13.refs_5_ = bf16[32,1024]{1,0:T(8,128)(2,1)S(1)} collective-permute-done((bf16[32,1024]{1,0:T(8,128)(2,1)S(1)}, bf16[32,1024]{1,0:T(8,128)(2,1)S(1)}, u32[]{:S(2)}, u32[]{:S(2)}) %collective-permute-start.13) | collective-permute-done | bytes 65568 | tf_op jit(solution)/shard_map/ppermute | solution.py:189
  42.0 1.8 %shard_map.91 = (bf16[16,128]{1,0:T(8,128)(2,1)S(1)}, bf16[32,1024]{1,0:T(8,128)(2,1)S(1)}, bf16[32,1024]{1,0:T(8,128)(2,1)S(1)}, bf16[32,1024]{1,0:T(8,128)(2,1...) custom-call(f32[8,128]{1,0:T(8,128)S(1)} %shard_map.90._, ...), custom_call_target="tpu_custom_call" | custom-call | tf_op jit(solution)/shard_map/pallas_call | solution.py:239
  45.0 3.2 %collective-permute-start.17 = (bf16[32,1024]{1,0:T(8,128)(2,1)S(1)}, bf16[32,1024]{1,0:T(8,128)(2,1)S(1)}, u32[]{:S(2)}, u32[]{:S(2)}) collective-permute-start(bf16[32,1024]{1,0:T(8,128)(2,1)S(1)} %get-tuple-element.56), channel_id=1, source_target_pairs={{0,14},{1,15},{2,12},{3,13},{4,10},{5,11},{6,8},{7,9},{8,6},{9,7},... | collective-permute-start | bytes 196616 | tf_op jit(solution)/shard_map/ppermute | solution.py:189
  49.2 1.5 %collective-permute-start.19 = (bf16[32,1024]{1,0:T(8,128)(2,1)S(1)}, bf16[32,1024]{1,0:T(8,128)(2,1)S(1)}, u32[]{:S(2)}, u32[]{:S(2)}) collective-permute-start(bf16[32,1024]{1,0:T(8,128)(2,1)S(1)} %get-tuple-element.58), channel_id=1, source_target_pairs={{0,10},{1,11},{2,8},{3,9},{4,14},{5,15},{6,12},{7,13},{8,2},{9,3},... | collective-permute-start | bytes 196616 | tf_op jit(solution)/shard_map/ppermute | solution.py:189
  50.7 2.0 %collective-permute-start.20 = (bf16[32,1024]{1,0:T(8,128)(2,1)S(1)}, bf16[32,1024]{1,0:T(8,128)(2,1)S(1)}, u32[]{:S(2)}, u32[]{:S(2)}) collective-permute-start(bf16[32,1024]{1,0:T(8,128)(2,1)S(1)} %get-tuple-element.59), channel_id=1, source_target_pairs={{0,8},{1,9},{2,10},{3,11},{4,12},{5,13},{6,14},{7,15},{8,0},{9,1},... | collective-permute-start | bytes 196616 | tf_op jit(solution)/shard_map/ppermute | solution.py:189
  53.1 1.9 %collective-permute-start.22 = (bf16[32,1024]{1,0:T(8,128)(2,1)S(1)}, bf16[32,1024]{1,0:T(8,128)(2,1)S(1)}, u32[]{:S(2)}, u32[]{:S(2)}) collective-permute-start(bf16[32,1024]{1,0:T(8,128)(2,1)S(1)} %get-tuple-element.61), channel_id=1, source_target_pairs={{0,6},{1,7},{2,4},{3,5},{4,2},{5,3},{6,0},{7,1},{8,14},{9,15},{10,... | collective-permute-start | bytes 196616 | tf_op jit(solution)/shard_map/ppermute | solution.py:189
  55.2 3.2 %collective-permute-done.19.refs_0_ = bf16[32,1024]{1,0:T(8,128)(2,1)S(1)} collective-permute-done((bf16[32,1024]{1,0:T(8,128)(2,1)S(1)}, bf16[32,1024]{1,0:T(8,128)(2,1)S(1)}, u32[]{:S(2)}, u32[]{:S(2)}) %collective-permute-start.19) | collective-permute-done | bytes 65568 | tf_op jit(solution)/shard_map/ppermute | solution.py:189
  63.1 3.4 %collective-permute-start.26 = (bf16[32,1024]{1,0:T(8,128)(2,1)S(1)}, bf16[32,1024]{1,0:T(8,128)(2,1)S(1)}, u32[]{:S(2)}, u32[]{:S(2)}) collective-permute-start(bf16[32,1024]{1,0:T(8,128)(2,1)S(1)} %get-tuple-element.66), channel_id=1, source_target_pairs={{0,14},{1,15},{2,12},{3,13},{4,10},{5,11},{6,8},{7,9},{8,6},{9,7},... | collective-permute-start | bytes 196616 | tf_op jit(solution)/shard_map/ppermute | solution.py:189
  67.3 1.4 %collective-permute-start.28 = (bf16[32,1024]{1,0:T(8,128)(2,1)S(1)}, bf16[32,1024]{1,0:T(8,128)(2,1)S(1)}, u32[]{:S(2)}, u32[]{:S(2)}) collective-permute-start(bf16[32,1024]{1,0:T(8,128)(2,1)S(1)} %get-tuple-element.68), channel_id=1, source_target_pairs={{0,10},{1,11},{2,8},{3,9},{4,14},{5,15},{6,12},{7,13},{8,2},{9,3},... | collective-permute-start | bytes 196616 | tf_op jit(solution)/shard_map/ppermute | solution.py:189
  68.7 2.0 %collective-permute-start.29 = (bf16[32,1024]{1,0:T(8,128)(2,1)S(1)}, bf16[32,1024]{1,0:T(8,128)(2,1)S(1)}, u32[]{:S(2)}, u32[]{:S(2)}) collective-permute-start(bf16[32,1024]{1,0:T(8,128)(2,1)S(1)} %get-tuple-element.69), channel_id=1, source_target_pairs={{0,8},{1,9},{2,10},{3,11},{4,12},{5,13},{6,14},{7,15},{8,0},{9,1},... | collective-permute-start | bytes 196616 | tf_op jit(solution)/shard_map/ppermute | solution.py:189
  71.4 3.6 %collective-permute-start.31 = (bf16[32,1024]{1,0:T(8,128)(2,1)S(1)}, bf16[32,1024]{1,0:T(8,128)(2,1)S(1)}, u32[]{:S(2)}, u32[]{:S(2)}) collective-permute-start(bf16[32,1024]{1,0:T(8,128)(2,1)S(1)} %get-tuple-element.62._), channel_id=1, source_target_pairs={{0,6},{1,7},{2,4},{3,5},{4,2},{5,3},{6,0},{7,1},{8,14},{9,15},{10,... | collective-permute-start | bytes 196616 | tf_op jit(solution)/shard_map/ppermute | solution.py:189
  75.1 2.1 %shard_map.95 = bf16[128,8192]{1,0:T(8,128)(2,1)} custom-call(bf16[32,1024]{1,0:T(8,128)(2,1)S(1)} %get-tuple-element.62._, bf16[16,128]{1,0:T(8,128)(2,1)S(1)} %get-tuple-element.63.low_ref, bf16[32,1024]{1,0:T(8,128)(2,1)S(1)} %get-tuple-element.47.refs_0_, bf16[32,1024]{1,0:T(8,128)(2,1)S(1)} %collective-permute-done.9.refs_1_, ...), custom_call_target="tpu_custom_call" | custom-call | flops 33554432 | bytes 2097152 | tf_op jit(solution)/shard_map/pallas_call | solution.py:254
  (58 shorter events, 18.9 us)
Async XLA Ops:
  4.0 10.7 %collective-permute-start = (bf16[272,128]{1,0:T(8,128)(2,1)}, bf16[272,128]{1,0:T(8,128)(2,1)S(1)}, u32[]{:S(2)}, u32[]{:S(2)}) collective-permute-start(bf16[272,128]{1,0:T(8,128)(2,1)} %get-tuple-element.39), channel_id=1, source_target_pairs={{0,2},{1,3},{2,0},{3,1},{4,6},{5,7},{6,4},{7,5},{8,10},{9,11},{10,... | collective-permute-start | bytes 208904 | tf_op jit(solution)/shard_map/ppermute | solution.py:189
  7.0 8.9 %collective-permute-start.1 = (bf16[272,128]{1,0:T(8,128)(2,1)}, bf16[272,128]{1,0:T(8,128)(2,1)S(1)}, u32[]{:S(2)}, u32[]{:S(2)}) collective-permute-start(bf16[272,128]{1,0:T(8,128)(2,1)} %get-tuple-element.40), channel_id=1, source_target_pairs={{0,14},{1,15},{2,12},{3,13},{4,10},{5,11},{6,8},{7,9},{8,6},{9,7},... | collective-permute-start | bytes 208904 | tf_op jit(solution)/shard_map/ppermute | solution.py:189
  10.6 7.4 %collective-permute-start.2 = (bf16[272,128]{1,0:T(8,128)(2,1)}, bf16[272,128]{1,0:T(8,128)(2,1)S(1)}, u32[]{:S(2)}, u32[]{:S(2)}) collective-permute-start(bf16[272,128]{1,0:T(8,128)(2,1)} %get-tuple-element.41), channel_id=1, source_target_pairs={{0,12},{1,13},{2,14},{3,15},{4,8},{5,9},{6,10},{7,11},{8,4},{9,5},... | collective-permute-start | bytes 208904 | tf_op jit(solution)/shard_map/ppermute | solution.py:189
  10.6 12.0 %collective-permute-start.3 = (bf16[272,128]{1,0:T(8,128)(2,1)}, bf16[272,128]{1,0:T(8,128)(2,1)S(1)}, u32[]{:S(2)}, u32[]{:S(2)}) collective-permute-start(bf16[272,128]{1,0:T(8,128)(2,1)} %get-tuple-element.42), channel_id=1, source_target_pairs={{0,10},{1,11},{2,8},{3,9},{4,14},{5,15},{6,12},{7,13},{8,2},{9,3},... | collective-permute-start | bytes 208904 | tf_op jit(solution)/shard_map/ppermute | solution.py:189
  12.5 10.1 %collective-permute-start.4 = (bf16[272,128]{1,0:T(8,128)(2,1)}, bf16[272,128]{1,0:T(8,128)(2,1)S(1)}, u32[]{:S(2)}, u32[]{:S(2)}) collective-permute-start(bf16[272,128]{1,0:T(8,128)(2,1)} %get-tuple-element.43), channel_id=1, source_target_pairs={{0,8},{1,9},{2,10},{3,11},{4,12},{5,13},{6,14},{7,15},{8,0},{9,1},... | collective-permute-start | bytes 208904 | tf_op jit(solution)/shard_map/ppermute | solution.py:189
  14.7 8.0 %collective-permute-start.5 = (bf16[272,128]{1,0:T(8,128)(2,1)}, bf16[272,128]{1,0:T(8,128)(2,1)S(1)}, u32[]{:S(2)}, u32[]{:S(2)}) collective-permute-start(bf16[272,128]{1,0:T(8,128)(2,1)} %get-tuple-element.44), channel_id=1, source_target_pairs={{0,4},{1,5},{2,6},{3,7},{4,0},{5,1},{6,2},{7,3},{8,12},{9,13},{10,... | collective-permute-start | bytes 208904 | tf_op jit(solution)/shard_map/ppermute | solution.py:189
  15.9 7.6 %collective-permute-start.6 = (bf16[272,128]{1,0:T(8,128)(2,1)}, bf16[272,128]{1,0:T(8,128)(2,1)S(1)}, u32[]{:S(2)}, u32[]{:S(2)}) collective-permute-start(bf16[272,128]{1,0:T(8,128)(2,1)} %get-tuple-element.45), channel_id=1, source_target_pairs={{0,6},{1,7},{2,4},{3,5},{4,2},{5,3},{6,0},{7,1},{8,14},{9,15},{10,... | collective-permute-start | bytes 208904 | tf_op jit(solution)/shard_map/ppermute | solution.py:189
  25.5 8.4 %collective-permute-start.9 = (bf16[32,1024]{1,0:T(8,128)(2,1)S(1)}, bf16[32,1024]{1,0:T(8,128)(2,1)S(1)}, u32[]{:S(2)}, u32[]{:S(2)}) collective-permute-start(bf16[32,1024]{1,0:T(8,128)(2,1)S(1)} %get-tuple-element.48), channel_id=1, source_target_pairs={{0,2},{1,3},{2,0},{3,1},{4,6},{5,7},{6,4},{7,5},{8,10},{9,11},{10,... | collective-permute-start | bytes 196616 | tf_op jit(solution)/shard_map/ppermute | solution.py:189
  26.3 8.4 %collective-permute-start.10 = (bf16[32,1024]{1,0:T(8,128)(2,1)S(1)}, bf16[32,1024]{1,0:T(8,128)(2,1)S(1)}, u32[]{:S(2)}, u32[]{:S(2)}) collective-permute-start(bf16[32,1024]{1,0:T(8,128)(2,1)S(1)} %get-tuple-element.49), channel_id=1, source_target_pairs={{0,14},{1,15},{2,12},{3,13},{4,10},{5,11},{6,8},{7,9},{8,6},{9,7},... | collective-permute-start | bytes 196616 | tf_op jit(solution)/shard_map/ppermute | solution.py:189
  30.9 8.6 %collective-permute-start.12 = (bf16[32,1024]{1,0:T(8,128)(2,1)S(1)}, bf16[32,1024]{1,0:T(8,128)(2,1)S(1)}, u32[]{:S(2)}, u32[]{:S(2)}) collective-permute-start(bf16[32,1024]{1,0:T(8,128)(2,1)S(1)} %get-tuple-element.51), channel_id=1, source_target_pairs={{0,10},{1,11},{2,8},{3,9},{4,14},{5,15},{6,12},{7,13},{8,2},{9,3},... | collective-permute-start | bytes 196616 | tf_op jit(solution)/shard_map/ppermute | solution.py:189
  31.4 9.7 %collective-permute-start.13 = (bf16[32,1024]{1,0:T(8,128)(2,1)S(1)}, bf16[32,1024]{1,0:T(8,128)(2,1)S(1)}, u32[]{:S(2)}, u32[]{:S(2)}) collective-permute-start(bf16[32,1024]{1,0:T(8,128)(2,1)S(1)} %get-tuple-element.52), channel_id=1, source_target_pairs={{0,8},{1,9},{2,10},{3,11},{4,12},{5,13},{6,14},{7,15},{8,0},{9,1},... | collective-permute-start | bytes 196616 | tf_op jit(solution)/shard_map/ppermute | solution.py:189
  34.0 7.2 %collective-permute-start.14 = (bf16[32,1024]{1,0:T(8,128)(2,1)S(1)}, bf16[32,1024]{1,0:T(8,128)(2,1)S(1)}, u32[]{:S(2)}, u32[]{:S(2)}) collective-permute-start(bf16[32,1024]{1,0:T(8,128)(2,1)S(1)} %get-tuple-element.53), channel_id=1, source_target_pairs={{0,4},{1,5},{2,6},{3,7},{4,0},{5,1},{6,2},{7,3},{8,12},{9,13},{10,... | collective-permute-start | bytes 196616 | tf_op jit(solution)/shard_map/ppermute | solution.py:189
  34.7 7.3 %collective-permute-start.15 = (bf16[32,1024]{1,0:T(8,128)(2,1)S(1)}, bf16[32,1024]{1,0:T(8,128)(2,1)S(1)}, u32[]{:S(2)}, u32[]{:S(2)}) collective-permute-start(bf16[32,1024]{1,0:T(8,128)(2,1)S(1)} %get-tuple-element.46.after), channel_id=1, source_target_pairs={{0,6},{1,7},{2,4},{3,5},{4,2},{5,3},{6,0},{7,1},{8,14},{9,15},{10,... | collective-permute-start | bytes 196616 | tf_op jit(solution)/shard_map/ppermute | solution.py:189
  43.9 8.8 %collective-permute-start.16 = (bf16[32,1024]{1,0:T(8,128)(2,1)S(1)}, bf16[32,1024]{1,0:T(8,128)(2,1)S(1)}, u32[]{:S(2)}, u32[]{:S(2)}) collective-permute-start(bf16[32,1024]{1,0:T(8,128)(2,1)S(1)} %get-tuple-element.55), channel_id=1, source_target_pairs={{0,2},{1,3},{2,0},{3,1},{4,6},{5,7},{6,4},{7,5},{8,10},{9,11},{10,... | collective-permute-start | bytes 196616 | tf_op jit(solution)/shard_map/ppermute | solution.py:189
  45.0 8.1 %collective-permute-start.17 = (bf16[32,1024]{1,0:T(8,128)(2,1)S(1)}, bf16[32,1024]{1,0:T(8,128)(2,1)S(1)}, u32[]{:S(2)}, u32[]{:S(2)}) collective-permute-start(bf16[32,1024]{1,0:T(8,128)(2,1)S(1)} %get-tuple-element.56), channel_id=1, source_target_pairs={{0,14},{1,15},{2,12},{3,13},{4,10},{5,11},{6,8},{7,9},{8,6},{9,7},... | collective-permute-start | bytes 196616 | tf_op jit(solution)/shard_map/ppermute | solution.py:189
  49.2 9.2 %collective-permute-start.19 = (bf16[32,1024]{1,0:T(8,128)(2,1)S(1)}, bf16[32,1024]{1,0:T(8,128)(2,1)S(1)}, u32[]{:S(2)}, u32[]{:S(2)}) collective-permute-start(bf16[32,1024]{1,0:T(8,128)(2,1)S(1)} %get-tuple-element.58), channel_id=1, source_target_pairs={{0,10},{1,11},{2,8},{3,9},{4,14},{5,15},{6,12},{7,13},{8,2},{9,3},... | collective-permute-start | bytes 196616 | tf_op jit(solution)/shard_map/ppermute | solution.py:189
  50.7 8.0 %collective-permute-start.20 = (bf16[32,1024]{1,0:T(8,128)(2,1)S(1)}, bf16[32,1024]{1,0:T(8,128)(2,1)S(1)}, u32[]{:S(2)}, u32[]{:S(2)}) collective-permute-start(bf16[32,1024]{1,0:T(8,128)(2,1)S(1)} %get-tuple-element.59), channel_id=1, source_target_pairs={{0,8},{1,9},{2,10},{3,11},{4,12},{5,13},{6,14},{7,15},{8,0},{9,1},... | collective-permute-start | bytes 196616 | tf_op jit(solution)/shard_map/ppermute | solution.py:189
  61.9 8.8 %collective-permute-start.25 = (bf16[32,1024]{1,0:T(8,128)(2,1)S(1)}, bf16[32,1024]{1,0:T(8,128)(2,1)S(1)}, u32[]{:S(2)}, u32[]{:S(2)}) collective-permute-start(bf16[32,1024]{1,0:T(8,128)(2,1)S(1)} %get-tuple-element.65), channel_id=1, source_target_pairs={{0,2},{1,3},{2,0},{3,1},{4,6},{5,7},{6,4},{7,5},{8,10},{9,11},{10,... | collective-permute-start | bytes 196616 | tf_op jit(solution)/shard_map/ppermute | solution.py:189
  63.1 8.4 %collective-permute-start.26 = (bf16[32,1024]{1,0:T(8,128)(2,1)S(1)}, bf16[32,1024]{1,0:T(8,128)(2,1)S(1)}, u32[]{:S(2)}, u32[]{:S(2)}) collective-permute-start(bf16[32,1024]{1,0:T(8,128)(2,1)S(1)} %get-tuple-element.66), channel_id=1, source_target_pairs={{0,14},{1,15},{2,12},{3,13},{4,10},{5,11},{6,8},{7,9},{8,6},{9,7},... | collective-permute-start | bytes 196616 | tf_op jit(solution)/shard_map/ppermute | solution.py:189
  66.5 10.6 %collective-permute-start.27 = (bf16[32,1024]{1,0:T(8,128)(2,1)S(1)}, bf16[32,1024]{1,0:T(8,128)(2,1)S(1)}, u32[]{:S(2)}, u32[]{:S(2)}) collective-permute-start(bf16[32,1024]{1,0:T(8,128)(2,1)S(1)} %get-tuple-element.67), channel_id=1, source_target_pairs={{0,12},{1,13},{2,14},{3,15},{4,8},{5,9},{6,10},{7,11},{8,4},{9,5},... | collective-permute-start | bytes 196616 | tf_op jit(solution)/shard_map/ppermute | solution.py:189
  67.3 10.0 %collective-permute-start.28 = (bf16[32,1024]{1,0:T(8,128)(2,1)S(1)}, bf16[32,1024]{1,0:T(8,128)(2,1)S(1)}, u32[]{:S(2)}, u32[]{:S(2)}) collective-permute-start(bf16[32,1024]{1,0:T(8,128)(2,1)S(1)} %get-tuple-element.68), channel_id=1, source_target_pairs={{0,10},{1,11},{2,8},{3,9},{4,14},{5,15},{6,12},{7,13},{8,2},{9,3},... | collective-permute-start | bytes 196616 | tf_op jit(solution)/shard_map/ppermute | solution.py:189
  68.7 9.1 %collective-permute-start.29 = (bf16[32,1024]{1,0:T(8,128)(2,1)S(1)}, bf16[32,1024]{1,0:T(8,128)(2,1)S(1)}, u32[]{:S(2)}, u32[]{:S(2)}) collective-permute-start(bf16[32,1024]{1,0:T(8,128)(2,1)S(1)} %get-tuple-element.69), channel_id=1, source_target_pairs={{0,8},{1,9},{2,10},{3,11},{4,12},{5,13},{6,14},{7,15},{8,0},{9,1},... | collective-permute-start | bytes 196616 | tf_op jit(solution)/shard_map/ppermute | solution.py:189
  70.7 7.1 %collective-permute-start.30 = (bf16[32,1024]{1,0:T(8,128)(2,1)S(1)}, bf16[32,1024]{1,0:T(8,128)(2,1)S(1)}, u32[]{:S(2)}, u32[]{:S(2)}) collective-permute-start(bf16[32,1024]{1,0:T(8,128)(2,1)S(1)} %get-tuple-element.70), channel_id=1, source_target_pairs={{0,4},{1,5},{2,6},{3,7},{4,0},{5,1},{6,2},{7,3},{8,12},{9,13},{10,... | collective-permute-start | bytes 196616 | tf_op jit(solution)/shard_map/ppermute | solution.py:189
  71.4 7.4 %collective-permute-start.31 = (bf16[32,1024]{1,0:T(8,128)(2,1)S(1)}, bf16[32,1024]{1,0:T(8,128)(2,1)S(1)}, u32[]{:S(2)}, u32[]{:S(2)}) collective-permute-start(bf16[32,1024]{1,0:T(8,128)(2,1)S(1)} %get-tuple-element.62._), channel_id=1, source_target_pairs={{0,6},{1,7},{2,4},{3,5},{4,2},{5,3},{6,0},{7,1},{8,14},{9,15},{10,... | collective-permute-start | bytes 196616 | tf_op jit(solution)/shard_map/ppermute | solution.py:189
  (11 other events, 99.4 us)

commit v8 on v7

v8 whole, which is shorter than its diff:
```python
import functools

import jax
import jax.numpy as jnp
from jax import lax
from jax.experimental import pallas as pl
from jax.experimental.pallas import tpu as pltpu
from jax.sharding import PartitionSpec as P

F32 = jnp.float32
BF16 = jnp.bfloat16
LANES = 128
ID_ROWS = 16
VMEM = pl.BlockSpec(memory_space=pltpu.VMEM)
HBM = pl.BlockSpec(memory_space=pltpu.HBM)
SMEM = pl.BlockSpec(memory_space=pltpu.SMEM)
PARAMS = pltpu.CompilerParams(vmem_limit_bytes=32 * 1024 * 1024)
ALONE = pltpu.CompilerParams(vmem_limit_bytes=60 * 1024 * 1024)


def position():
    me = lax.axis_index("fsdp")
    return me // 2, me % 2


def offsets(m):
    return [0, 1, *range(m - 1, m // 2 - 1, -1), *range(2, m // 2)]


def rank(k, m):
    return jnp.where(k < 2, k, jnp.where(k < m // 2, m // 2 + k, m + 1 - k))


def deliveries(groups, h):
    pairs = [(x, k) for x in range(groups) for k in range(h)]
    return sorted(pairs, key=lambda pair: (pair[0].bit_count() + pair[1].bit_count(), pair))


def share(groups, h, x, k):
    return (lax.axis_index("group") ^ x) * h + (lax.rem(position()[0], h) ^ k)


def columns(chunk, w):
    return pl.ds(pl.multiple_of(chunk * w, w), w)


def pack_kernel(groups, h, id_ref, storage_ref, down_hbm, up_hbm, *refs):
    outs, (down_ref, up_ref, out_ref, load_sems, store_sems) = refs[:h], refs[h:]
    r, w = down_ref.shape[0], down_ref.shape[1] // h
    loads = []
    for k in range(h):
        cols = columns(share(groups, h, 0, k), w)
        loads.append(
            [
                pltpu.make_async_copy(src.at[0, :, cols], dst.at[:, k * w : (k + 1) * w], sem)
                for src, dst, sem in (
                    (down_hbm, down_ref, load_sems.at[0, k]),
                    (up_hbm, up_ref, load_sems.at[1, k]),
                )
            ]
        )
        for load in loads[-1]:
            load.start()
    mark = jnp.full((ID_ROWS, LANES), storage_ref[id_ref[0]].astype(F32), F32).astype(BF16)
    stores = []
    for k, (dst, pair) in enumerate(zip(outs, loads)):
        for load in pair:
            load.wait()
        for b in range(w // LANES):
            cols = slice(k * w + b * LANES, k * w + (b + 1) * LANES)
            out_ref[k, 2 * r * b : 2 * r * b + r, :] = down_ref[:, cols]
            out_ref[k, 2 * r * b + r : 2 * r * (b + 1), :] = up_ref[:, cols]
        out_ref[k, 2 * r * (w // LANES) :, :] = mark
        stores.append(pltpu.make_async_copy(out_ref.at[k], dst, store_sems.at[k]))
        stores[-1].start()
    for store in stores:
        store.wait()


def stack_kernel(h, *refs):
    held_ref = refs[-1]
    for at, block in enumerate(refs[:h]):
        held_ref[at] = block[...]


def near_kernel(*refs):
    *blocks, held_ref, marks_ref = refs
    for at, block in enumerate(blocks):
        held_ref[at] = block[...]
        marks_ref[at] = block[block.shape[0] - ID_ROWS :, :]


def pick(held, at, here, rows):
    own_a, own_b, other_a, other_b = held
    h = own_a.shape[0]
    in_a, at = at < h, lax.rem(at, h)
    own = jnp.where(in_a, own_a[at, rows, :], own_b[at, rows, :])
    other = jnp.where(in_a, other_a[at, rows, :], other_b[at, rows, :])
    return jnp.where(here, own, other)


def slots_of(held_ref):
    h, rows, _ = held_ref.shape
    return [
        held_ref[at, rows - ID_ROWS :, :].astype(F32)[0, 0].astype(jnp.int32) for at in range(h)
    ]


def deliver_kernel(groups, *refs):
    held, marks, outs = refs[:4], refs[4 : groups + 3], refs[groups + 3 :]
    p, c = position()
    h = held[0].shape[0]
    r2, w = outs[0].shape
    slots = [slots_of(held[0])] + [slots_of(mark) for mark in marks]
    for out, (x, k) in zip(outs, deliveries(groups, h)):
        slot = slots[x][k]
        for b in range(w // LANES):
            rows = slice(b * r2, (b + 1) * r2)
            out[:, b * LANES : (b + 1) * LANES] = pick(held, (slot // 2) ^ p, slot % 2 == c, rows)


def inverse_kernel(own_a, own_b, other_a, other_b, tile_of):
    p, c = position()
    for near, far, core in ((own_a, own_b, c), (other_a, other_b, 1 - c)):
        for k, slot in enumerate(slots_of(near) + slots_of(far)):
            tile_of[slot] = 2 * (p ^ k) + core


def touch_kernel(after, array, token_ref):
    token_ref[...] = jnp.zeros_like(token_ref)


def grads_kernel(m, groups, _, acts_ref, cot_ref, *refs):
    ways = deliveries(groups, m // 2)
    factors, low_ref, outs = refs[: len(ways)], refs[len(ways)], refs[len(ways) + 1 :]
    p, _ = position()
    r2, w = factors[0].shape
    r = r2 // 2
    rows = acts_ref.shape[0]
    dims_nt = (((1,), (1,)), ((), ()))
    low_u = jnp.zeros((r, rows), F32)
    low_h = jnp.zeros((r, rows), F32)
    for (x, k), factor in zip(ways, factors):
        cols = columns(share(groups, m // 2, x, k), w)
        low_u += lax.dot_general(factor[0:r, :], acts_ref[:, cols], dims_nt, preferred_element_type=F32)
        low_h += lax.dot_general(factor[r:r2, :], cot_ref[:, cols], dims_nt, preferred_element_type=F32)
    low_u = low_u.astype(BF16)
    low_h = low_h.astype(BF16)
    low_ref[...] = low_h
    for k, out in zip(offsets(m), outs):
        cols = columns(p ^ k, out.shape[1])
        out[0:r, :] = jnp.dot(low_h, acts_ref[:, cols], preferred_element_type=F32).astype(BF16)
        out[r:r2, :] = jnp.dot(low_u, cot_ref[:, cols], preferred_element_type=F32).astype(BF16)


def inputs_kernel(m, groups, _, low_ref, *refs):
    *factors, gx_ref = refs
    for (x, k), factor in zip(deliveries(groups, m // 2), factors):
        r2, w = factor.shape
        gx_ref[:, columns(share(groups, m // 2, x, k), w)] = lax.dot_general(
            low_ref[...], factor[0 : r2 // 2, :], (((0,), (0,)), ((), ())), preferred_element_type=F32
        ).astype(BF16)


def collect_kernel(m, tile_of, *refs):
    held, outs = refs[:4], refs[4:]
    p, c = position()
    for out, k in zip(outs, offsets(m)):
        tile = tile_of[2 * (p ^ k) + c]
        out[...] = pick(held, rank((tile // 2) ^ p, m), tile % 2 == c, slice(None))


def unpack_kernel(m, *refs):
    ga_ref, gb_ref = refs[m:]
    p, _ = position()
    r2, w = refs[0].shape
    for block, k in zip(refs, offsets(m)):
        cols = columns(p ^ k, w)
        ga_ref[0, :, cols] = block[0 : r2 // 2, :]
        gb_ref[0, :, cols] = block[r2 // 2 : r2, :]


def call(kernel, out_shape, in_specs, out_specs, params=PARAMS, **options):
    return pl.pallas_call(
        kernel,
        out_shape=out_shape,
        in_specs=in_specs,
        out_specs=out_specs,
        compiler_params=params,
        **options,
    )


def bf16(*shape):
    return jax.ShapeDtypeStruct(shape, BF16)


def shards(acts, cotangent, down, up, adapter_per_tile, adapter_storage_slot):
    groups, n = lax.axis_size("group"), lax.axis_size("fsdp")
    m, h = n // 2, n // 4
    _, r, d = down.shape

    def to_chip(k, block):
        pairs = [(2 * p + c, 2 * (p ^ k) + c) for p in range(m) for c in range(2)]
        return lax.ppermute(block, "fsdp", pairs)

    def to_device(x, k, block):
        pairs = [
            (g * n + 2 * p + c, (g ^ x) * n + 2 * (p ^ k) + c)
            for g in range(groups)
            for p in range(m)
            for c in range(2)
        ]
        return lax.ppermute(block, ("group", "fsdp"), pairs)

    def exchange(blocks):
        return [blocks[0]] + [to_chip(k, block) for block, k in zip(blocks[1:], offsets(m)[1:])]

    def with_other_core(*own):
        return [*own, *(lax.ppermute(half, "fsdp", [(f, f ^ 1) for f in range(n)]) for half in own)]

    def stack(blocks, *after):
        count = len(blocks) + len(after)
        return call(
            functools.partial(stack_kernel, h), bf16(h, *blocks[0].shape), [VMEM] * count, VMEM
        )(*blocks, *after)

    ways = deliveries(groups, h)
    w = d // len(ways)
    flat = bf16(2 * r * w // LANES + ID_ROWS, LANES)
    spread = call(
        functools.partial(pack_kernel, groups, h),
        [flat] * h,
        [SMEM, SMEM, HBM, HBM],
        [HBM] * h,
        ALONE,
        scratch_shapes=[
            pltpu.VMEM((r, h * w), BF16),
            pltpu.VMEM((r, h * w), BF16),
            pltpu.VMEM((h, *flat.shape), BF16),
            pltpu.SemaphoreType.DMA((2, h)),
            pltpu.SemaphoreType.DMA((h,)),
        ],
    )(adapter_per_tile, adapter_storage_slot, down, up)
    near = [spread[0]] + [to_chip(k, spread[k]) for k in range(1, h)]
    far = [to_chip(h, block) for block in near]
    near, marks = call(
        near_kernel, [bf16(h, *flat.shape), bf16(h, ID_ROWS, LANES)], [VMEM] * h, [VMEM] * 2
    )(*near)
    marks = [to_device(x, 0, marks) for x in range(1, groups)]
    held = with_other_core(near, stack(far, *marks))
    factors = call(
        functools.partial(deliver_kernel, groups),
        [bf16(2 * r, w)] * len(ways),
        [VMEM] * (groups + 3),
        [VMEM] * len(ways),
    )(*held, *marks)
    token = call(touch_kernel, jax.ShapeDtypeStruct((8, LANES), F32), [VMEM] * 2, VMEM)(
        factors[-1], cotangent
    )
    factors = [factors[0]] + [
        to_device(x, k, block) for (x, k), block in zip(ways[1:], factors[1:])
    ]
    tile_of = call(inverse_kernel, jax.ShapeDtypeStruct((n,), jnp.int32), [VMEM] * 4, SMEM)(*held)

    wide = bf16(2 * r, d // m)
    low, *parts = call(
        functools.partial(grads_kernel, m, groups),
        [bf16(r, acts.shape[0])] + [wide] * m,
        [VMEM] * (len(ways) + 3),
        [VMEM] * (m + 1),
    )(token, acts, cotangent, *factors)
    parts = exchange(parts)
    owned = call(functools.partial(collect_kernel, m), [wide] * m, [SMEM] + [VMEM] * 4, [VMEM] * m)(
        tile_of, *with_other_core(stack(parts[:h]), stack(parts[h:]))
    )
    grad_x = call(
        functools.partial(inputs_kernel, m, groups),
        bf16(*acts.shape),
        [VMEM] * (len(ways) + 2),
        VMEM,
        cost_estimate=pl.CostEstimate(
            flops=2 * r * acts.size, bytes_accessed=2 * acts.size, transcendentals=0
        ),
    )(owned[-1], low, *factors)
    grad_a, grad_b = call(
        functools.partial(unpack_kernel, m), [bf16(*down.shape)] * 2, [VMEM] * m, [VMEM] * 2
    )(*exchange(owned))
    return grad_x, grad_a, grad_b


def solution(mesh):
    placed = (
        P(("group", "fsdp"), None),
        P(("group", "fsdp"), None),
        P("fsdp", None, None),
        P("fsdp", None, None),
        P(("group", "fsdp")),
        P(),
    )
    return jax.shard_map(
        shards,
        mesh=mesh,
        in_specs=placed,
        out_specs=(
            P(("group", "fsdp"), None),
            P(("group", "fsdp"), None, None),
            P(("group", "fsdp"), None, None),
        ),
        check_vma=False,
    )
```

time: 80 us -> 79 us (0.988)
  waiting for transfers between devices: 18.3 us -> 16.6 us
  starting transfers between devices: 49.8 us -> 50.8 us
    ppermute x32 -> x33, waiting for transfers between devices: 18.3 us -> 16.6 us  [the longest x21 7.8 us: to_chip(): return lax.ppermute(block, 'fsdp', pairs)]
    ppermute x32 -> x33, starting transfers between devices: 49.8 us -> 50.8 us  [the longest x21 39.7 us: to_chip(): return lax.ppermute(block, 'fsdp', pairs)]
  transfers between devices with their start and end apart: 32 -> 33, of which waited for: 13 -> 15; matrix products, arithmetic and copies ran while one was open for 0% -> 0% of each run, Pallas kernels for 4% -> 4%
where the time goes in v8:
time: 79 us; the launch traced here: 78.7 us
  starting transfers between devices  50.8 us (64%)
  waiting for transfers between devices  16.6 us (21%)
  Pallas kernels  8.82 us (11%)
  between operations  1.56 us (2%)
  local copies, waits for them, and re-layouts  0.89 us (1%)
    ppermute x21, starting transfers between devices, to_chip(): return lax.ppermute(block, 'fsdp', pairs)  39.7 us
    ppermute x8, starting transfers between devices, to_device(): return lax.ppermute(block, ('group', 'fsdp'), pairs)  11 us
    ppermute x21, waiting for transfers between devices, to_chip(): return lax.ppermute(block, 'fsdp', pairs)  7.8 us
    ppermute x8, waiting for transfers between devices, to_device(): return lax.ppermute(block, ('group', 'fsdp'), pairs)  6.42 us
    ppermute x4, waiting for transfers between devices, with_other_core(): lax.ppermute(half, 'fsdp', [(f, f ^ 1) for f in range(n)])  2.38 us
    pallas_call x1, Pallas kernels, shards(): call(functools.partial(pack_kernel, groups, h), [flat] * h, [SMEM, SMEM,...  2.3 us
    pallas_call x1, Pallas kernels, shards(): call(functools.partial(inputs_kernel, m, groups), bf16(*acts.shape), [VME...  2.05 us
    pallas_call x1, Pallas kernels, shards(): call(functools.partial(grads_kernel, m, groups), [bf16(r, acts.shape[0])]...  1.83 us
  transfers between devices with their start and end apart: 33, of which 15 were waited for; matrix products, arithmetic and copies ran while one was open for 0% of the time, Pallas kernels for 4%

profile of v8, /device:TPU:0, one launch (start us, length us, event | category | flops | bytes accessed | tf_op | source)
XLA Modules:
  0.0 78.7 jit_solution(7977283462554458865)
XLA Ops:
  1.4 2.3 %shard_map.85 = (bf16[272,128]{1,0:T(8,128)(2,1)}, bf16[272,128]{1,0:T(8,128)(2,1)}, bf16[272,128]{1,0:T(8,128)(2,1)}, bf16[272,128]{1,0:T(8,128)(2,1)}) custom-call(s32[1]{0:T(128)S(6)} %copy.9.id_ref, s32[16]{0:T(128)} %storage_ref.1, bf16[1,16,8192]{2,1,0:T(8,128)(2,1)} %down_hbm.1, bf16[1,16,8192]{2,1,0:T(8,128)(2,1)} %up_hbm.1), custom_call_target="tpu_custom_call" | custom-call | tf_op jit(solution)/shard_map/pallas_call | solution.py:231
  3.8 3.0 %collective-permute-start = (bf16[272,128]{1,0:T(8,128)(2,1)}, bf16[272,128]{1,0:T(8,128)(2,1)S(1)}, u32[]{:S(2)}, u32[]{:S(2)}) collective-permute-start(bf16[272,128]{1,0:T(8,128)(2,1)} %get-tuple-element.37), channel_id=1, source_target_pairs={{0,2},{1,3},{2,0},{3,1},{4,6},{5,7},{6,4},{7,5},{8,10},{9,11},{10,... | collective-permute-start | bytes 208904 | tf_op jit(solution)/shard_map/ppermute | solution.py:205
  6.8 1.6 %collective-permute-start.1 = (bf16[272,128]{1,0:T(8,128)(2,1)}, bf16[272,128]{1,0:T(8,128)(2,1)S(1)}, u32[]{:S(2)}, u32[]{:S(2)}) collective-permute-start(bf16[272,128]{1,0:T(8,128)(2,1)} %get-tuple-element.38), channel_id=1, source_target_pairs={{0,4},{1,5},{2,6},{3,7},{4,0},{5,1},{6,2},{7,3},{8,12},{9,13},{10,... | collective-permute-start | bytes 208904 | tf_op jit(solution)/shard_map/ppermute | solution.py:205
  8.4 3.0 %collective-permute-start.3 = (bf16[272,128]{1,0:T(8,128)(2,1)}, bf16[272,128]{1,0:T(8,128)(2,1)S(1)}, u32[]{:S(2)}, u32[]{:S(2)}) collective-permute-start(bf16[272,128]{1,0:T(8,128)(2,1)} %get-tuple-element.36.refs_0_), channel_id=1, source_target_pairs={{0,8},{1,9},{2,10},{3,11},{4,12},{5,13},{6,14},{7,15},{8,0},{9,1},... | collective-permute-start | bytes 208904 | tf_op jit(solution)/shard_map/ppermute | solution.py:205
  12.6 2.0 %collective-permute-start.5 = (bf16[272,128]{1,0:T(8,128)(2,1)S(1)}, bf16[272,128]{1,0:T(8,128)(2,1)S(1)}, u32[]{:S(2)}, u32[]{:S(2)}) collective-permute-start(bf16[272,128]{1,0:T(8,128)(2,1)S(1)} %collective-permute-done.1.refs_2_), channel_id=1, source_target_pairs={{0,8},{1,9},{2,10},{3,11},{4,12},{5,13},{6,14},{7,15},{8,0},{9,1},... | collective-permute-start | bytes 208904 | tf_op jit(solution)/shard_map/ppermute | solution.py:205
  14.6 2.1 %collective-permute-start.6 = (bf16[272,128]{1,0:T(8,128)(2,1)S(1)}, bf16[272,128]{1,0:T(8,128)(2,1)S(1)}, u32[]{:S(2)}, u32[]{:S(2)}) collective-permute-start(bf16[272,128]{1,0:T(8,128)(2,1)S(1)} %collective-permute-done.2.refs_3_), channel_id=1, source_target_pairs={{0,8},{1,9},{2,10},{3,11},{4,12},{5,13},{6,14},{7,15},{8,0},{9,1},... | collective-permute-start | bytes 208904 | tf_op jit(solution)/shard_map/ppermute | solution.py:205
  17.6 1.6 %collective-permute-start.7 = (bf16[4,16,128]{2,1,0:T(8,128)(2,1)S(1)}, bf16[4,16,128]{2,1,0:T(8,128)(2,1)S(1)}, u32[]{:S(2)}, u32[]{:S(2)}) collective-permute-start(bf16[4,16,128]{2,1,0:T(8,128)(2,1)S(1)} %get-tuple-element.41), channel_id=1, source_target_pairs={{0,16},{1,17},{2,18},{3,19},{4,20},{5,21},{6,22},{7,23},{8,24},{9,... | collective-permute-start | bytes 49160 | tf_op jit(solution)/shard_map/ppermute | solution.py:214
  19.2 2.2 %collective-permute-done.7.refs_4_ = bf16[4,16,128]{2,1,0:T(8,128)(2,1)S(1)} collective-permute-done((bf16[4,16,128]{2,1,0:T(8,128)(2,1)S(1)}, bf16[4,16,128]{2,1,0:T(8,128)(2,1)S(1)}, u32[]{:S(2)}, u32[]{:S(2)}) %collective-permute-start.7) | collective-permute-done | bytes 16416 | tf_op jit(solution)/shard_map/ppermute | solution.py:214
  22.2 1.4 %collective-permute-done.5.refs_2_ = bf16[272,128]{1,0:T(8,128)(2,1)S(1)} collective-permute-done((bf16[272,128]{1,0:T(8,128)(2,1)S(1)}, bf16[272,128]{1,0:T(8,128)(2,1)S(1)}, u32[]{:S(2)}, u32[]{:S(2)}) %collective-permute-start.5) | collective-permute-done | bytes 69664 | tf_op jit(solution)/shard_map/ppermute | solution.py:205
  24.4 1.5 %collective-permute-done.9.other_b.refs_3_ = bf16[4,272,128]{2,1,0:T(8,128)(2,1)S(1)} collective-permute-done((bf16[4,272,128]{2,1,0:T(8,128)(2,1)S(1)}, bf16[4,272,128]{2,1,0:T(8,128)(2,1)S(1)}, u32[]{:S(2)}, u32[]{:S(2)}) %collective-permute-start.9) | collective-permute-done | bytes 278560 | tf_op jit(solution)/shard_map/ppermute | solution.py:220
  26.3 1.6 %collective-permute-start.10 = (bf16[32,1024]{1,0:T(8,128)(2,1)S(1)}, bf16[32,1024]{1,0:T(8,128)(2,1)S(1)}, u32[]{:S(2)}, u32[]{:S(2)}) collective-permute-start(bf16[32,1024]{1,0:T(8,128)(2,1)S(1)} %get-tuple-element.44), channel_id=1, source_target_pairs={{0,2},{1,3},{2,0},{3,1},{4,6},{5,7},{6,4},{7,5},{8,10},{9,11},{10,... | collective-permute-start | bytes 196616 | tf_op jit(solution)/shard_map/ppermute | solution.py:214
  27.9 1.5 %collective-permute-start.12 = (bf16[32,1024]{1,0:T(8,128)(2,1)S(1)}, bf16[32,1024]{1,0:T(8,128)(2,1)S(1)}, u32[]{:S(2)}, u32[]{:S(2)}) collective-permute-start(bf16[32,1024]{1,0:T(8,128)(2,1)S(1)} %get-tuple-element.46), channel_id=1, source_target_pairs={{0,16},{1,17},{2,18},{3,19},{4,20},{5,21},{6,22},{7,23},{8,24},{9,... | collective-permute-start | bytes 196616 | tf_op jit(solution)/shard_map/ppermute | solution.py:214
  29.4 2.2 %collective-permute-start.13 = (bf16[32,1024]{1,0:T(8,128)(2,1)S(1)}, bf16[32,1024]{1,0:T(8,128)(2,1)S(1)}, u32[]{:S(2)}, u32[]{:S(2)}) collective-permute-start(bf16[32,1024]{1,0:T(8,128)(2,1)S(1)} %get-tuple-element.47), channel_id=1, source_target_pairs={{0,6},{1,7},{2,4},{3,5},{4,2},{5,3},{6,0},{7,1},{8,14},{9,15},{10,... | collective-permute-start | bytes 196616 | tf_op jit(solution)/shard_map/ppermute | solution.py:214
  33.8 1.9 %collective-permute-start.16 = (bf16[32,1024]{1,0:T(8,128)(2,1)S(1)}, bf16[32,1024]{1,0:T(8,128)(2,1)S(1)}, u32[]{:S(2)}, u32[]{:S(2)}) collective-permute-start(bf16[32,1024]{1,0:T(8,128)(2,1)S(1)} %get-tuple-element.42.after), channel_id=1, source_target_pairs={{0,22},{1,23},{2,20},{3,21},{4,18},{5,19},{6,16},{7,17},{8,30},{9,... | collective-permute-start | bytes 196616 | tf_op jit(solution)/shard_map/ppermute | solution.py:214
  38.0 1.8 %collective-permute-done.16.refs_7_ = bf16[32,1024]{1,0:T(8,128)(2,1)S(1)} collective-permute-done((bf16[32,1024]{1,0:T(8,128)(2,1)S(1)}, bf16[32,1024]{1,0:T(8,128)(2,1)S(1)}, u32[]{:S(2)}, u32[]{:S(2)}) %collective-permute-start.16) | collective-permute-done | bytes 65568 | tf_op jit(solution)/shard_map/ppermute | solution.py:214
  39.9 1.8 %shard_map.91 = (bf16[16,128]{1,0:T(8,128)(2,1)S(1)}, bf16[32,1024]{1,0:T(8,128)(2,1)S(1)}, bf16[32,1024]{1,0:T(8,128)(2,1)S(1)}, bf16[32,1024]{1,0:T(8,128)(2,1...) custom-call(f32[8,128]{1,0:T(8,128)S(1)} %shard_map.90._, ...), custom_call_target="tpu_custom_call" | custom-call | tf_op jit(solution)/shard_map/pallas_call | solution.py:267
  42.5 3.2 %collective-permute-start.18 = (bf16[32,1024]{1,0:T(8,128)(2,1)S(1)}, bf16[32,1024]{1,0:T(8,128)(2,1)S(1)}, u32[]{:S(2)}, u32[]{:S(2)}) collective-permute-start(bf16[32,1024]{1,0:T(8,128)(2,1)S(1)} %get-tuple-element.52), channel_id=1, source_target_pairs={{0,14},{1,15},{2,12},{3,13},{4,10},{5,11},{6,8},{7,9},{8,6},{9,7},... | collective-permute-start | bytes 196616 | tf_op jit(solution)/shard_map/ppermute | solution.py:205
  48.4 1.8 %collective-permute-start.21 = (bf16[32,1024]{1,0:T(8,128)(2,1)S(1)}, bf16[32,1024]{1,0:T(8,128)(2,1)S(1)}, u32[]{:S(2)}, u32[]{:S(2)}) collective-permute-start(bf16[32,1024]{1,0:T(8,128)(2,1)S(1)} %get-tuple-element.55), channel_id=1, source_target_pairs={{0,8},{1,9},{2,10},{3,11},{4,12},{5,13},{6,14},{7,15},{8,0},{9,1},... | collective-permute-start | bytes 196616 | tf_op jit(solution)/shard_map/ppermute | solution.py:205
  50.4 4.6 %collective-permute-start.23 = (bf16[32,1024]{1,0:T(8,128)(2,1)S(1)}, bf16[32,1024]{1,0:T(8,128)(2,1)S(1)}, u32[]{:S(2)}, u32[]{:S(2)}) collective-permute-start(bf16[32,1024]{1,0:T(8,128)(2,1)S(1)} %get-tuple-element.57), channel_id=1, source_target_pairs={{0,6},{1,7},{2,4},{3,5},{4,2},{5,3},{6,0},{7,1},{8,14},{9,15},{10,... | collective-permute-start | bytes 196616 | tf_op jit(solution)/shard_map/ppermute | solution.py:205
  60.8 3.0 %collective-permute-start.27 = (bf16[32,1024]{1,0:T(8,128)(2,1)S(1)}, bf16[32,1024]{1,0:T(8,128)(2,1)S(1)}, u32[]{:S(2)}, u32[]{:S(2)}) collective-permute-start(bf16[32,1024]{1,0:T(8,128)(2,1)S(1)} %get-tuple-element.62), channel_id=1, source_target_pairs={{0,14},{1,15},{2,12},{3,13},{4,10},{5,11},{6,8},{7,9},{8,6},{9,7},... | collective-permute-start | bytes 196616 | tf_op jit(solution)/shard_map/ppermute | solution.py:205
  66.2 2.3 %collective-permute-start.30 = (bf16[32,1024]{1,0:T(8,128)(2,1)S(1)}, bf16[32,1024]{1,0:T(8,128)(2,1)S(1)}, u32[]{:S(2)}, u32[]{:S(2)}) collective-permute-start(bf16[32,1024]{1,0:T(8,128)(2,1)S(1)} %get-tuple-element.65), channel_id=1, source_target_pairs={{0,8},{1,9},{2,10},{3,11},{4,12},{5,13},{6,14},{7,15},{8,0},{9,1},... | collective-permute-start | bytes 196616 | tf_op jit(solution)/shard_map/ppermute | solution.py:205
  69.0 4.3 %collective-permute-start.32 = (bf16[32,1024]{1,0:T(8,128)(2,1)S(1)}, bf16[32,1024]{1,0:T(8,128)(2,1)S(1)}, u32[]{:S(2)}, u32[]{:S(2)}) collective-permute-start(bf16[32,1024]{1,0:T(8,128)(2,1)S(1)} %get-tuple-element.58._), channel_id=1, source_target_pairs={{0,6},{1,7},{2,4},{3,5},{4,2},{5,3},{6,0},{7,1},{8,14},{9,15},{10,... | collective-permute-start | bytes 196616 | tf_op jit(solution)/shard_map/ppermute | solution.py:205
  73.3 2.1 %shard_map.95 = bf16[128,8192]{1,0:T(8,128)(2,1)} custom-call(bf16[32,1024]{1,0:T(8,128)(2,1)S(1)} %get-tuple-element.58._, bf16[16,128]{1,0:T(8,128)(2,1)S(1)} %get-tuple-element.59.low_ref, bf16[32,1024]{1,0:T(8,128)(2,1)S(1)} %get-tuple-element.43.refs_0_, bf16[32,1024]{1,0:T(8,128)(2,1)S(1)} %collective-permute-done.10.refs_1_, ...), custom_call_target="tpu_custom_call" | custom-call | flops 33554432 | bytes 2097152 | tf_op jit(solution)/shard_map/pallas_call | solution.py:277
  76.3 1.6 %collective-permute-done.32.refs_7_ = bf16[32,1024]{1,0:T(8,128)(2,1)S(1)} collective-permute-done((bf16[32,1024]{1,0:T(8,128)(2,1)S(1)}, bf16[32,1024]{1,0:T(8,128)(2,1)S(1)}, u32[]{:S(2)}, u32[]{:S(2)}) %collective-permute-start.32) | collective-permute-done | bytes 65568 | tf_op jit(solution)/shard_map/ppermute | solution.py:205
  (60 shorter events, 22.8 us)
Async XLA Ops:
  3.8 7.6 %collective-permute-start = (bf16[272,128]{1,0:T(8,128)(2,1)}, bf16[272,128]{1,0:T(8,128)(2,1)S(1)}, u32[]{:S(2)}, u32[]{:S(2)}) collective-permute-start(bf16[272,128]{1,0:T(8,128)(2,1)} %get-tuple-element.37), channel_id=1, source_target_pairs={{0,2},{1,3},{2,0},{3,1},{4,6},{5,7},{6,4},{7,5},{8,10},{9,11},{10,... | collective-permute-start | bytes 208904 | tf_op jit(solution)/shard_map/ppermute | solution.py:205
  8.4 6.3 %collective-permute-start.2 = (bf16[272,128]{1,0:T(8,128)(2,1)}, bf16[272,128]{1,0:T(8,128)(2,1)S(1)}, u32[]{:S(2)}, u32[]{:S(2)}) collective-permute-start(bf16[272,128]{1,0:T(8,128)(2,1)} %get-tuple-element.39), channel_id=1, source_target_pairs={{0,6},{1,7},{2,4},{3,5},{4,2},{5,3},{6,0},{7,1},{8,14},{9,15},{10,... | collective-permute-start | bytes 208904 | tf_op jit(solution)/shard_map/ppermute | solution.py:205
  8.4 10.8 %collective-permute-start.3 = (bf16[272,128]{1,0:T(8,128)(2,1)}, bf16[272,128]{1,0:T(8,128)(2,1)S(1)}, u32[]{:S(2)}, u32[]{:S(2)}) collective-permute-start(bf16[272,128]{1,0:T(8,128)(2,1)} %get-tuple-element.36.refs_0_), channel_id=1, source_target_pairs={{0,8},{1,9},{2,10},{3,11},{4,12},{5,13},{6,14},{7,15},{8,0},{9,1},... | collective-permute-start | bytes 208904 | tf_op jit(solution)/shard_map/ppermute | solution.py:205
  11.3 10.8 %collective-permute-start.4 = (bf16[272,128]{1,0:T(8,128)(2,1)S(1)}, bf16[272,128]{1,0:T(8,128)(2,1)S(1)}, u32[]{:S(2)}, u32[]{:S(2)}) collective-permute-start(bf16[272,128]{1,0:T(8,128)(2,1)S(1)} %collective-permute-done.refs_1_), channel_id=1, source_target_pairs={{0,8},{1,9},{2,10},{3,11},{4,12},{5,13},{6,14},{7,15},{8,0},{9,1},... | collective-permute-start | bytes 208904 | tf_op jit(solution)/shard_map/ppermute | solution.py:205
  12.6 10.9 %collective-permute-start.5 = (bf16[272,128]{1,0:T(8,128)(2,1)S(1)}, bf16[272,128]{1,0:T(8,128)(2,1)S(1)}, u32[]{:S(2)}, u32[]{:S(2)}) collective-permute-start(bf16[272,128]{1,0:T(8,128)(2,1)S(1)} %collective-permute-done.1.refs_2_), channel_id=1, source_target_pairs={{0,8},{1,9},{2,10},{3,11},{4,12},{5,13},{6,14},{7,15},{8,0},{9,1},... | collective-permute-start | bytes 208904 | tf_op jit(solution)/shard_map/ppermute | solution.py:205
  14.6 9.6 %collective-permute-start.6 = (bf16[272,128]{1,0:T(8,128)(2,1)S(1)}, bf16[272,128]{1,0:T(8,128)(2,1)S(1)}, u32[]{:S(2)}, u32[]{:S(2)}) collective-permute-start(bf16[272,128]{1,0:T(8,128)(2,1)S(1)} %collective-permute-done.2.refs_3_), channel_id=1, source_target_pairs={{0,8},{1,9},{2,10},{3,11},{4,12},{5,13},{6,14},{7,15},{8,0},{9,1},... | collective-permute-start | bytes 208904 | tf_op jit(solution)/shard_map/ppermute | solution.py:205
  26.3 6.6 %collective-permute-start.10 = (bf16[32,1024]{1,0:T(8,128)(2,1)S(1)}, bf16[32,1024]{1,0:T(8,128)(2,1)S(1)}, u32[]{:S(2)}, u32[]{:S(2)}) collective-permute-start(bf16[32,1024]{1,0:T(8,128)(2,1)S(1)} %get-tuple-element.44), channel_id=1, source_target_pairs={{0,2},{1,3},{2,0},{3,1},{4,6},{5,7},{6,4},{7,5},{8,10},{9,11},{10,... | collective-permute-start | bytes 196616 | tf_op jit(solution)/shard_map/ppermute | solution.py:214
  27.9 7.8 %collective-permute-start.12 = (bf16[32,1024]{1,0:T(8,128)(2,1)S(1)}, bf16[32,1024]{1,0:T(8,128)(2,1)S(1)}, u32[]{:S(2)}, u32[]{:S(2)}) collective-permute-start(bf16[32,1024]{1,0:T(8,128)(2,1)S(1)} %get-tuple-element.46), channel_id=1, source_target_pairs={{0,16},{1,17},{2,18},{3,19},{4,20},{5,21},{6,22},{7,23},{8,24},{9,... | collective-permute-start | bytes 196616 | tf_op jit(solution)/shard_map/ppermute | solution.py:214
  29.4 6.3 %collective-permute-start.13 = (bf16[32,1024]{1,0:T(8,128)(2,1)S(1)}, bf16[32,1024]{1,0:T(8,128)(2,1)S(1)}, u32[]{:S(2)}, u32[]{:S(2)}) collective-permute-start(bf16[32,1024]{1,0:T(8,128)(2,1)S(1)} %get-tuple-element.47), channel_id=1, source_target_pairs={{0,6},{1,7},{2,4},{3,5},{4,2},{5,3},{6,0},{7,1},{8,14},{9,15},{10,... | collective-permute-start | bytes 196616 | tf_op jit(solution)/shard_map/ppermute | solution.py:214
  33.8 6.1 %collective-permute-start.16 = (bf16[32,1024]{1,0:T(8,128)(2,1)S(1)}, bf16[32,1024]{1,0:T(8,128)(2,1)S(1)}, u32[]{:S(2)}, u32[]{:S(2)}) collective-permute-start(bf16[32,1024]{1,0:T(8,128)(2,1)S(1)} %get-tuple-element.42.after), channel_id=1, source_target_pairs={{0,22},{1,23},{2,20},{3,21},{4,18},{5,19},{6,16},{7,17},{8,30},{9,... | collective-permute-start | bytes 196616 | tf_op jit(solution)/shard_map/ppermute | solution.py:214
  41.7 8.5 %collective-permute-start.17 = (bf16[32,1024]{1,0:T(8,128)(2,1)S(1)}, bf16[32,1024]{1,0:T(8,128)(2,1)S(1)}, u32[]{:S(2)}, u32[]{:S(2)}) collective-permute-start(bf16[32,1024]{1,0:T(8,128)(2,1)S(1)} %get-tuple-element.51), channel_id=1, source_target_pairs={{0,2},{1,3},{2,0},{3,1},{4,6},{5,7},{6,4},{7,5},{8,10},{9,11},{10,... | collective-permute-start | bytes 196616 | tf_op jit(solution)/shard_map/ppermute | solution.py:205
  42.5 7.9 %collective-permute-start.18 = (bf16[32,1024]{1,0:T(8,128)(2,1)S(1)}, bf16[32,1024]{1,0:T(8,128)(2,1)S(1)}, u32[]{:S(2)}, u32[]{:S(2)}) collective-permute-start(bf16[32,1024]{1,0:T(8,128)(2,1)S(1)} %get-tuple-element.52), channel_id=1, source_target_pairs={{0,14},{1,15},{2,12},{3,13},{4,10},{5,11},{6,8},{7,9},{8,6},{9,7},... | collective-permute-start | bytes 196616 | tf_op jit(solution)/shard_map/ppermute | solution.py:205
  45.8 9.2 %collective-permute-start.19 = (bf16[32,1024]{1,0:T(8,128)(2,1)S(1)}, bf16[32,1024]{1,0:T(8,128)(2,1)S(1)}, u32[]{:S(2)}, u32[]{:S(2)}) collective-permute-start(bf16[32,1024]{1,0:T(8,128)(2,1)S(1)} %get-tuple-element.53), channel_id=1, source_target_pairs={{0,12},{1,13},{2,14},{3,15},{4,8},{5,9},{6,10},{7,11},{8,4},{9,5},... | collective-permute-start | bytes 196616 | tf_op jit(solution)/shard_map/ppermute | solution.py:205
  47.0 8.8 %collective-permute-start.20 = (bf16[32,1024]{1,0:T(8,128)(2,1)S(1)}, bf16[32,1024]{1,0:T(8,128)(2,1)S(1)}, u32[]{:S(2)}, u32[]{:S(2)}) collective-permute-start(bf16[32,1024]{1,0:T(8,128)(2,1)S(1)} %get-tuple-element.54), channel_id=1, source_target_pairs={{0,10},{1,11},{2,8},{3,9},{4,14},{5,15},{6,12},{7,13},{8,2},{9,3},... | collective-permute-start | bytes 196616 | tf_op jit(solution)/shard_map/ppermute | solution.py:205
  48.4 8.5 %collective-permute-start.21 = (bf16[32,1024]{1,0:T(8,128)(2,1)S(1)}, bf16[32,1024]{1,0:T(8,128)(2,1)S(1)}, u32[]{:S(2)}, u32[]{:S(2)}) collective-permute-start(bf16[32,1024]{1,0:T(8,128)(2,1)S(1)} %get-tuple-element.55), channel_id=1, source_target_pairs={{0,8},{1,9},{2,10},{3,11},{4,12},{5,13},{6,14},{7,15},{8,0},{9,1},... | collective-permute-start | bytes 196616 | tf_op jit(solution)/shard_map/ppermute | solution.py:205
  50.2 6.6 %collective-permute-start.22 = (bf16[32,1024]{1,0:T(8,128)(2,1)S(1)}, bf16[32,1024]{1,0:T(8,128)(2,1)S(1)}, u32[]{:S(2)}, u32[]{:S(2)}) collective-permute-start(bf16[32,1024]{1,0:T(8,128)(2,1)S(1)} %get-tuple-element.56), channel_id=1, source_target_pairs={{0,4},{1,5},{2,6},{3,7},{4,0},{5,1},{6,2},{7,3},{8,12},{9,13},{10,... | collective-permute-start | bytes 196616 | tf_op jit(solution)/shard_map/ppermute | solution.py:205
  50.4 6.8 %collective-permute-start.23 = (bf16[32,1024]{1,0:T(8,128)(2,1)S(1)}, bf16[32,1024]{1,0:T(8,128)(2,1)S(1)}, u32[]{:S(2)}, u32[]{:S(2)}) collective-permute-start(bf16[32,1024]{1,0:T(8,128)(2,1)S(1)} %get-tuple-element.57), channel_id=1, source_target_pairs={{0,6},{1,7},{2,4},{3,5},{4,2},{5,3},{6,0},{7,1},{8,14},{9,15},{10,... | collective-permute-start | bytes 196616 | tf_op jit(solution)/shard_map/ppermute | solution.py:205
  59.6 8.9 %collective-permute-start.26 = (bf16[32,1024]{1,0:T(8,128)(2,1)S(1)}, bf16[32,1024]{1,0:T(8,128)(2,1)S(1)}, u32[]{:S(2)}, u32[]{:S(2)}) collective-permute-start(bf16[32,1024]{1,0:T(8,128)(2,1)S(1)} %get-tuple-element.61), channel_id=1, source_target_pairs={{0,2},{1,3},{2,0},{3,1},{4,6},{5,7},{6,4},{7,5},{8,10},{9,11},{10,... | collective-permute-start | bytes 196616 | tf_op jit(solution)/shard_map/ppermute | solution.py:205
  60.8 8.2 %collective-permute-start.27 = (bf16[32,1024]{1,0:T(8,128)(2,1)S(1)}, bf16[32,1024]{1,0:T(8,128)(2,1)S(1)}, u32[]{:S(2)}, u32[]{:S(2)}) collective-permute-start(bf16[32,1024]{1,0:T(8,128)(2,1)S(1)} %get-tuple-element.62), channel_id=1, source_target_pairs={{0,14},{1,15},{2,12},{3,13},{4,10},{5,11},{6,8},{7,9},{8,6},{9,7},... | collective-permute-start | bytes 196616 | tf_op jit(solution)/shard_map/ppermute | solution.py:205
  63.8 11.5 %collective-permute-start.28 = (bf16[32,1024]{1,0:T(8,128)(2,1)S(1)}, bf16[32,1024]{1,0:T(8,128)(2,1)S(1)}, u32[]{:S(2)}, u32[]{:S(2)}) collective-permute-start(bf16[32,1024]{1,0:T(8,128)(2,1)S(1)} %get-tuple-element.63), channel_id=1, source_target_pairs={{0,12},{1,13},{2,14},{3,15},{4,8},{5,9},{6,10},{7,11},{8,4},{9,5},... | collective-permute-start | bytes 196616 | tf_op jit(solution)/shard_map/ppermute | solution.py:205
  65.0 11.3 %collective-permute-start.29 = (bf16[32,1024]{1,0:T(8,128)(2,1)S(1)}, bf16[32,1024]{1,0:T(8,128)(2,1)S(1)}, u32[]{:S(2)}, u32[]{:S(2)}) collective-permute-start(bf16[32,1024]{1,0:T(8,128)(2,1)S(1)} %get-tuple-element.64), channel_id=1, source_target_pairs={{0,10},{1,11},{2,8},{3,9},{4,14},{5,15},{6,12},{7,13},{8,2},{9,3},... | collective-permute-start | bytes 196616 | tf_op jit(solution)/shard_map/ppermute | solution.py:205
  66.2 10.1 %collective-permute-start.30 = (bf16[32,1024]{1,0:T(8,128)(2,1)S(1)}, bf16[32,1024]{1,0:T(8,128)(2,1)S(1)}, u32[]{:S(2)}, u32[]{:S(2)}) collective-permute-start(bf16[32,1024]{1,0:T(8,128)(2,1)S(1)} %get-tuple-element.65), channel_id=1, source_target_pairs={{0,8},{1,9},{2,10},{3,11},{4,12},{5,13},{6,14},{7,15},{8,0},{9,1},... | collective-permute-start | bytes 196616 | tf_op jit(solution)/shard_map/ppermute | solution.py:205
  68.5 7.8 %collective-permute-start.31 = (bf16[32,1024]{1,0:T(8,128)(2,1)S(1)}, bf16[32,1024]{1,0:T(8,128)(2,1)S(1)}, u32[]{:S(2)}, u32[]{:S(2)}) collective-permute-start(bf16[32,1024]{1,0:T(8,128)(2,1)S(1)} %get-tuple-element.66), channel_id=1, source_target_pairs={{0,4},{1,5},{2,6},{3,7},{4,0},{5,1},{6,2},{7,3},{8,12},{9,13},{10,... | collective-permute-start | bytes 196616 | tf_op jit(solution)/shard_map/ppermute | solution.py:205
  69.0 8.9 %collective-permute-start.32 = (bf16[32,1024]{1,0:T(8,128)(2,1)S(1)}, bf16[32,1024]{1,0:T(8,128)(2,1)S(1)}, u32[]{:S(2)}, u32[]{:S(2)}) collective-permute-start(bf16[32,1024]{1,0:T(8,128)(2,1)S(1)} %get-tuple-element.58._), channel_id=1, source_target_pairs={{0,6},{1,7},{2,4},{3,5},{4,2},{5,3},{6,0},{7,1},{8,14},{9,15},{10,... | collective-permute-start | bytes 196616 | tf_op jit(solution)/shard_map/ppermute | solution.py:205
  (12 other events, 109.3 us)

commit v9 on v8

--- a/solution.py
+++ b/solution.py
@@ -33,7 +33,8 @@
 
 def deliveries(groups, h):
     pairs = [(x, k) for x in range(groups) for k in range(h)]
-    return sorted(pairs, key=lambda pair: (pair[0].bit_count() + pair[1].bit_count(), pair))
+    far = sorted(pairs[1:], key=lambda pair: (-pair[0].bit_count() - pair[1].bit_count(), pair))
+    return pairs[:1] + far
 
 
 def share(groups, h, x, k):
@@ -47,6 +48,7 @@
 def pack_kernel(groups, h, id_ref, storage_ref, down_hbm, up_hbm, *refs):
     outs, (down_ref, up_ref, out_ref, load_sems, store_sems) = refs[:h], refs[h:]
     r, w = down_ref.shape[0], down_ref.shape[1] // h
+    first = outs[0].shape[0]
     loads = []
     for k in range(h):
         cols = columns(share(groups, h, 0, k), w)
@@ -63,7 +65,7 @@
             load.start()
     mark = jnp.full((ID_ROWS, LANES), storage_ref[id_ref[0]].astype(F32), F32).astype(BF16)
     stores = []
-    for k, (dst, pair) in enumerate(zip(outs, loads)):
+    for k, pair in enumerate(loads):
         for load in pair:
             load.wait()
         for b in range(w // LANES):
@@ -71,22 +73,34 @@
             out_ref[k, 2 * r * b : 2 * r * b + r, :] = down_ref[:, cols]
             out_ref[k, 2 * r * b + r : 2 * r * (b + 1), :] = up_ref[:, cols]
         out_ref[k, 2 * r * (w // LANES) :, :] = mark
-        stores.append(pltpu.make_async_copy(out_ref.at[k], dst, store_sems.at[k]))
-        stores[-1].start()
+        dsts = [outs[0].at[k]] * (k < first) + [outs[k]] * (k > 0)
+        for i, dst in enumerate(dsts):
+            stores.append(pltpu.make_async_copy(out_ref.at[k], dst, store_sems.at[i, k]))
+            stores[-1].start()
     for store in stores:
         store.wait()
 
 
+def block_of(ref):
+    return ref[0] if len(ref.shape) == 3 else ref[...]
+
+
 def stack_kernel(h, *refs):
     held_ref = refs[-1]
-    for at, block in enumerate(refs[:h]):
-        held_ref[at] = block[...]
+    for at, ref in enumerate(refs[:h]):
+        held_ref[at] = block_of(ref)
+
+
+def split_kernel(array_ref, *outs):
+    for at, out in enumerate(outs):
+        out[...] = array_ref[at + 1]
 
 
 def near_kernel(*refs):
     *blocks, held_ref, marks_ref = refs
-    for at, block in enumerate(blocks):
-        held_ref[at] = block[...]
+    for at, ref in enumerate(blocks):
+        block = block_of(ref)
+        held_ref[at] = block
         marks_ref[at] = block[block.shape[0] - ID_ROWS :, :]
 
 
@@ -222,7 +236,7 @@
     def stack(blocks, *after):
         count = len(blocks) + len(after)
         return call(
-            functools.partial(stack_kernel, h), bf16(h, *blocks[0].shape), [VMEM] * count, VMEM
+            functools.partial(stack_kernel, h), bf16(h, *blocks[-1].shape), [VMEM] * count, VMEM
         )(*blocks, *after)
 
     ways = deliveries(groups, h)
@@ -230,7 +244,7 @@
     flat = bf16(2 * r * w // LANES + ID_ROWS, LANES)
     spread = call(
         functools.partial(pack_kernel, groups, h),
-        [flat] * h,
+        [bf16(h // 2, *flat.shape)] + [flat] * (h - 1),
         [SMEM, SMEM, HBM, HBM],
         [HBM] * h,
         ALONE,
@@ -239,11 +253,14 @@
             pltpu.VMEM((r, h * w), BF16),
             pltpu.VMEM((h, *flat.shape), BF16),
             pltpu.SemaphoreType.DMA((2, h)),
-            pltpu.SemaphoreType.DMA((h,)),
+            pltpu.SemaphoreType.DMA((2, h)),
         ],
     )(adapter_per_tile, adapter_storage_slot, down, up)
+    crossed = to_chip(h, spread[0])
     near = [spread[0]] + [to_chip(k, spread[k]) for k in range(1, h)]
-    far = [to_chip(h, block) for block in near]
+    handed = call(split_kernel, [flat] * (h // 2 - 1), [VMEM], [VMEM] * (h // 2 - 1))(crossed)
+    far = [crossed] + [to_chip(k + 1, block) for k, block in enumerate(handed)]
+    far += [to_chip(h, block) for block in near[h // 2 :]]
     near, marks = call(
         near_kernel, [bf16(h, *flat.shape), bf16(h, ID_ROWS, LANES)], [VMEM] * h, [VMEM] * 2
     )(*near)

time: 79 us -> 77.7 us (0.984)
  waiting for transfers between devices: 16.6 us -> 15.2 us
    ppermute x8, waiting for transfers between devices: 6.42 us -> 4.47 us  [to_device(): return lax.ppermute(block, ('group', 'fsdp'), pairs)]
    ppermute x8, starting transfers between devices: 11 us -> 12.5 us  [to_device(): return lax.ppermute(block, ('group', 'fsdp'), pairs)]
    ppermute x21, starting transfers between devices: 39.7 us -> 38.2 us  [to_chip(): return lax.ppermute(block, 'fsdp', pairs)]
    pallas_call x4 -> x5, Pallas kernels: 2.35 us -> 2.4 us  [the longest x1 2.34 us: shards(): call(functools.partial(pack_kernel, groups, h), [bf16(h // 2, *flat.shape...]
  transfers between devices with their start and end apart: 33 -> 33, of which waited for: 15 -> 12; matrix products, arithmetic and copies ran while one was open for 0% -> 0% of each run, Pallas kernels for 4% -> 4%
where the time goes in v9:
time: 77.7 us; the launch traced here: 77.4 us
  starting transfers between devices  50.9 us (66%)
  waiting for transfers between devices  15.2 us (20%)
  Pallas kernels  8.87 us (11%)
  between operations  1.57 us (2%)
  local copies, waits for them, and re-layouts  0.92 us (1%)
    ppermute x21, starting transfers between devices, to_chip(): return lax.ppermute(block, 'fsdp', pairs)  38.2 us
    ppermute x8, starting transfers between devices, to_device(): return lax.ppermute(block, ('group', 'fsdp'), pairs)  12.5 us
    ppermute x21, waiting for transfers between devices, to_chip(): return lax.ppermute(block, 'fsdp', pairs)  8.33 us
    ppermute x8, waiting for transfers between devices, to_device(): return lax.ppermute(block, ('group', 'fsdp'), pairs)  4.47 us
    ppermute x4, waiting for transfers between devices, with_other_core(): lax.ppermute(half, 'fsdp', [(f, f ^ 1) for f in range(n)])  2.38 us
    pallas_call x1, Pallas kernels, shards(): call(functools.partial(pack_kernel, groups, h), [bf16(h // 2, *flat.shape...  2.34 us
    pallas_call x1, Pallas kernels, shards(): call(functools.partial(inputs_kernel, m, groups), bf16(*acts.shape), [VME...  2.05 us
    pallas_call x1, Pallas kernels, shards(): call(functools.partial(grads_kernel, m, groups), [bf16(r, acts.shape[0])]...  1.83 us
  transfers between devices with their start and end apart: 33, of which 12 were waited for; matrix products, arithmetic and copies ran while one was open for 0% of the time, Pallas kernels for 4%

profile of v9, /device:TPU:0, one launch (start us, length us, event | category | flops | bytes accessed | tf_op | source)
XLA Modules:
  0.0 77.4 jit_solution(6971083304848439421)
XLA Ops:
  1.4 2.3 %shard_map.85 = (bf16[2,272,128]{2,1,0:T(8,128)(2,1)}, bf16[272,128]{1,0:T(8,128)(2,1)}, bf16[272,128]{1,0:T(8,128)(2,1)}, bf16[272,128]{1,0:T(8,128)(2,1)}) custom-call(s32[1]{0:T(128)S(6)} %copy.9.id_ref, s32[16]{0:T(128)} %storage_ref.1, bf16[1,16,8192]{2,1,0:T(8,128)(2,1)} %down_hbm.1, bf16[1,16,8192]{2,1,0:T(8,128)(2,1)} %up_hbm.1), custom_call_target="tpu_custom_call" | custom-call | tf_op jit(solution)/shard_map/pallas_call | solution.py:245
  3.8 4.1 %collective-permute-start.3 = (bf16[2,272,128]{2,1,0:T(8,128)(2,1)}, bf16[2,272,128]{2,1,0:T(8,128)(2,1)S(1)}, u32[]{:S(2)}, u32[]{:S(2)}) collective-permute-start(bf16[2,272,128]{2,1,0:T(8,128)(2,1)} %get-tuple-element.36.refs_0_), channel_id=1, source_target_pairs={{0,8},{1,9},{2,10},{3,11},{4,12},{5,13},{6,14},{7,15},{8,0},{9,1},... | collective-permute-start | bytes 417800 | tf_op jit(solution)/shard_map/ppermute | solution.py:219
  7.9 1.6 %collective-permute-start.1 = (bf16[272,128]{1,0:T(8,128)(2,1)}, bf16[272,128]{1,0:T(8,128)(2,1)S(1)}, u32[]{:S(2)}, u32[]{:S(2)}) collective-permute-start(bf16[272,128]{1,0:T(8,128)(2,1)} %get-tuple-element.38), channel_id=1, source_target_pairs={{0,4},{1,5},{2,6},{3,7},{4,0},{5,1},{6,2},{7,3},{8,12},{9,13},{10,... | collective-permute-start | bytes 208904 | tf_op jit(solution)/shard_map/ppermute | solution.py:219
  11.4 2.0 %collective-permute-done.1.refs_2_ = bf16[272,128]{1,0:T(8,128)(2,1)S(1)} collective-permute-done((bf16[272,128]{1,0:T(8,128)(2,1)}, bf16[272,128]{1,0:T(8,128)(2,1)S(1)}, u32[]{:S(2)}, u32[]{:S(2)}) %collective-permute-start.1) | collective-permute-done | bytes 69664 | tf_op jit(solution)/shard_map/ppermute | solution.py:219
  13.4 2.3 %collective-permute-start.5 = (bf16[272,128]{1,0:T(8,128)(2,1)S(1)}, bf16[272,128]{1,0:T(8,128)(2,1)S(1)}, u32[]{:S(2)}, u32[]{:S(2)}) collective-permute-start(bf16[272,128]{1,0:T(8,128)(2,1)S(1)} %collective-permute-done.1.refs_2_), channel_id=1, source_target_pairs={{0,8},{1,9},{2,10},{3,11},{4,12},{5,13},{6,14},{7,15},{8,0},{9,1},... | collective-permute-start | bytes 208904 | tf_op jit(solution)/shard_map/ppermute | solution.py:219
  15.7 1.6 %collective-permute-done.2.refs_3_ = bf16[272,128]{1,0:T(8,128)(2,1)S(1)} collective-permute-done((bf16[272,128]{1,0:T(8,128)(2,1)}, bf16[272,128]{1,0:T(8,128)(2,1)S(1)}, u32[]{:S(2)}, u32[]{:S(2)}) %collective-permute-start.2) | collective-permute-done | bytes 69664 | tf_op jit(solution)/shard_map/ppermute | solution.py:219
  19.5 1.6 %collective-permute-start.7 = (bf16[4,16,128]{2,1,0:T(8,128)(2,1)S(1)}, bf16[4,16,128]{2,1,0:T(8,128)(2,1)S(1)}, u32[]{:S(2)}, u32[]{:S(2)}) collective-permute-start(bf16[4,16,128]{2,1,0:T(8,128)(2,1)S(1)} %get-tuple-element.41), channel_id=1, source_target_pairs={{0,16},{1,17},{2,18},{3,19},{4,20},{5,21},{6,22},{7,23},{8,24},{9,... | collective-permute-start | bytes 49160 | tf_op jit(solution)/shard_map/ppermute | solution.py:228
  21.1 2.2 %collective-permute-done.7.refs_4_ = bf16[4,16,128]{2,1,0:T(8,128)(2,1)S(1)} collective-permute-done((bf16[4,16,128]{2,1,0:T(8,128)(2,1)S(1)}, bf16[4,16,128]{2,1,0:T(8,128)(2,1)S(1)}, u32[]{:S(2)}, u32[]{:S(2)}) %collective-permute-start.7) | collective-permute-done | bytes 16416 | tf_op jit(solution)/shard_map/ppermute | solution.py:228
  23.4 1.5 %collective-permute-done.9.other_b.refs_3_ = bf16[4,272,128]{2,1,0:T(8,128)(2,1)S(1)} collective-permute-done((bf16[4,272,128]{2,1,0:T(8,128)(2,1)S(1)}, bf16[4,272,128]{2,1,0:T(8,128)(2,1)S(1)}, u32[]{:S(2)}, u32[]{:S(2)}) %collective-permute-start.9) | collective-permute-done | bytes 278560 | tf_op jit(solution)/shard_map/ppermute | solution.py:234
  25.3 2.7 %collective-permute-start.10 = (bf16[32,1024]{1,0:T(8,128)(2,1)S(1)}, bf16[32,1024]{1,0:T(8,128)(2,1)S(1)}, u32[]{:S(2)}, u32[]{:S(2)}) collective-permute-start(bf16[32,1024]{1,0:T(8,128)(2,1)S(1)} %get-tuple-element.44), channel_id=1, source_target_pairs={{0,22},{1,23},{2,20},{3,21},{4,18},{5,19},{6,16},{7,17},{8,30},{9,... | collective-permute-start | bytes 196616 | tf_op jit(solution)/shard_map/ppermute | solution.py:228
  30.1 2.3 %collective-permute-start.13 = (bf16[32,1024]{1,0:T(8,128)(2,1)S(1)}, bf16[32,1024]{1,0:T(8,128)(2,1)S(1)}, u32[]{:S(2)}, u32[]{:S(2)}) collective-permute-start(bf16[32,1024]{1,0:T(8,128)(2,1)S(1)} %get-tuple-element.47), channel_id=1, source_target_pairs={{0,20},{1,21},{2,22},{3,23},{4,16},{5,17},{6,18},{7,19},{8,28},{9,... | collective-permute-start | bytes 196616 | tf_op jit(solution)/shard_map/ppermute | solution.py:228
  32.4 1.5 %collective-permute-start.14 = (bf16[32,1024]{1,0:T(8,128)(2,1)S(1)}, bf16[32,1024]{1,0:T(8,128)(2,1)S(1)}, u32[]{:S(2)}, u32[]{:S(2)}) collective-permute-start(bf16[32,1024]{1,0:T(8,128)(2,1)S(1)} %get-tuple-element.48), channel_id=1, source_target_pairs={{0,2},{1,3},{2,0},{3,1},{4,6},{5,7},{6,4},{7,5},{8,10},{9,11},{10,... | collective-permute-start | bytes 196616 | tf_op jit(solution)/shard_map/ppermute | solution.py:228
  34.2 2.1 %collective-permute-start.16 = (bf16[32,1024]{1,0:T(8,128)(2,1)S(1)}, bf16[32,1024]{1,0:T(8,128)(2,1)S(1)}, u32[]{:S(2)}, u32[]{:S(2)}) collective-permute-start(bf16[32,1024]{1,0:T(8,128)(2,1)S(1)} %get-tuple-element.42.after), channel_id=1, source_target_pairs={{0,16},{1,17},{2,18},{3,19},{4,20},{5,21},{6,22},{7,23},{8,24},{9,... | collective-permute-start | bytes 196616 | tf_op jit(solution)/shard_map/ppermute | solution.py:228
  36.7 1.5 %collective-permute-done.15.refs_6_ = bf16[32,1024]{1,0:T(8,128)(2,1)S(1)} collective-permute-done((bf16[32,1024]{1,0:T(8,128)(2,1)S(1)}, bf16[32,1024]{1,0:T(8,128)(2,1)S(1)}, u32[]{:S(2)}, u32[]{:S(2)}) %collective-permute-start.15) | collective-permute-done | bytes 65568 | tf_op jit(solution)/shard_map/ppermute | solution.py:228
  38.5 1.8 %shard_map.92 = (bf16[16,128]{1,0:T(8,128)(2,1)S(1)}, bf16[32,1024]{1,0:T(8,128)(2,1)S(1)}, bf16[32,1024]{1,0:T(8,128)(2,1)S(1)}, bf16[32,1024]{1,0:T(8,128)(2,1...) custom-call(f32[8,128]{1,0:T(8,128)S(1)} %shard_map.91._, ...), custom_call_target="tpu_custom_call" | custom-call | tf_op jit(solution)/shard_map/pallas_call | solution.py:284
  41.3 3.3 %collective-permute-start.18 = (bf16[32,1024]{1,0:T(8,128)(2,1)S(1)}, bf16[32,1024]{1,0:T(8,128)(2,1)S(1)}, u32[]{:S(2)}, u32[]{:S(2)}) collective-permute-start(bf16[32,1024]{1,0:T(8,128)(2,1)S(1)} %get-tuple-element.52), channel_id=1, source_target_pairs={{0,14},{1,15},{2,12},{3,13},{4,10},{5,11},{6,8},{7,9},{8,6},{9,7},... | collective-permute-start | bytes 196616 | tf_op jit(solution)/shard_map/ppermute | solution.py:219
  47.1 1.9 %collective-permute-start.21 = (bf16[32,1024]{1,0:T(8,128)(2,1)S(1)}, bf16[32,1024]{1,0:T(8,128)(2,1)S(1)}, u32[]{:S(2)}, u32[]{:S(2)}) collective-permute-start(bf16[32,1024]{1,0:T(8,128)(2,1)S(1)} %get-tuple-element.55), channel_id=1, source_target_pairs={{0,8},{1,9},{2,10},{3,11},{4,12},{5,13},{6,14},{7,15},{8,0},{9,1},... | collective-permute-start | bytes 196616 | tf_op jit(solution)/shard_map/ppermute | solution.py:219
  49.2 4.5 %collective-permute-start.23 = (bf16[32,1024]{1,0:T(8,128)(2,1)S(1)}, bf16[32,1024]{1,0:T(8,128)(2,1)S(1)}, u32[]{:S(2)}, u32[]{:S(2)}) collective-permute-start(bf16[32,1024]{1,0:T(8,128)(2,1)S(1)} %get-tuple-element.57), channel_id=1, source_target_pairs={{0,6},{1,7},{2,4},{3,5},{4,2},{5,3},{6,0},{7,1},{8,14},{9,15},{10,... | collective-permute-start | bytes 196616 | tf_op jit(solution)/shard_map/ppermute | solution.py:219
  53.9 1.6 %collective-permute-done.21.refs_1_ = bf16[32,1024]{1,0:T(8,128)(2,1)S(1)} collective-permute-done((bf16[32,1024]{1,0:T(8,128)(2,1)S(1)}, bf16[32,1024]{1,0:T(8,128)(2,1)S(1)}, u32[]{:S(2)}, u32[]{:S(2)}) %collective-permute-start.21) | collective-permute-done | bytes 65568 | tf_op jit(solution)/shard_map/ppermute | solution.py:219
  59.6 3.0 %collective-permute-start.27 = (bf16[32,1024]{1,0:T(8,128)(2,1)S(1)}, bf16[32,1024]{1,0:T(8,128)(2,1)S(1)}, u32[]{:S(2)}, u32[]{:S(2)}) collective-permute-start(bf16[32,1024]{1,0:T(8,128)(2,1)S(1)} %get-tuple-element.62), channel_id=1, source_target_pairs={{0,14},{1,15},{2,12},{3,13},{4,10},{5,11},{6,8},{7,9},{8,6},{9,7},... | collective-permute-start | bytes 196616 | tf_op jit(solution)/shard_map/ppermute | solution.py:219
  64.2 3.0 %collective-permute-start.30 = (bf16[32,1024]{1,0:T(8,128)(2,1)S(1)}, bf16[32,1024]{1,0:T(8,128)(2,1)S(1)}, u32[]{:S(2)}, u32[]{:S(2)}) collective-permute-start(bf16[32,1024]{1,0:T(8,128)(2,1)S(1)} %get-tuple-element.65), channel_id=1, source_target_pairs={{0,8},{1,9},{2,10},{3,11},{4,12},{5,13},{6,14},{7,15},{8,0},{9,1},... | collective-permute-start | bytes 196616 | tf_op jit(solution)/shard_map/ppermute | solution.py:219
  67.7 4.3 %collective-permute-start.32 = (bf16[32,1024]{1,0:T(8,128)(2,1)S(1)}, bf16[32,1024]{1,0:T(8,128)(2,1)S(1)}, u32[]{:S(2)}, u32[]{:S(2)}) collective-permute-start(bf16[32,1024]{1,0:T(8,128)(2,1)S(1)} %get-tuple-element.58._), channel_id=1, source_target_pairs={{0,6},{1,7},{2,4},{3,5},{4,2},{5,3},{6,0},{7,1},{8,14},{9,15},{10,... | collective-permute-start | bytes 196616 | tf_op jit(solution)/shard_map/ppermute | solution.py:219
  72.0 2.1 %shard_map.96 = bf16[128,8192]{1,0:T(8,128)(2,1)} custom-call(bf16[32,1024]{1,0:T(8,128)(2,1)S(1)} %get-tuple-element.58._, bf16[16,128]{1,0:T(8,128)(2,1)S(1)} %get-tuple-element.59.low_ref, bf16[32,1024]{1,0:T(8,128)(2,1)S(1)} %get-tuple-element.43.refs_0_, bf16[32,1024]{1,0:T(8,128)(2,1)S(1)} %collective-permute-done.10.refs_1_, ...), custom_call_target="tpu_custom_call" | custom-call | flops 33554432 | bytes 2097152 | tf_op jit(solution)/shard_map/pallas_call | solution.py:294
  75.0 1.6 %collective-permute-done.32.refs_7_ = bf16[32,1024]{1,0:T(8,128)(2,1)S(1)} collective-permute-done((bf16[32,1024]{1,0:T(8,128)(2,1)S(1)}, bf16[32,1024]{1,0:T(8,128)(2,1)S(1)}, u32[]{:S(2)}, u32[]{:S(2)}) %collective-permute-start.32) | collective-permute-done | bytes 65568 | tf_op jit(solution)/shard_map/ppermute | solution.py:219
  (61 shorter events, 19.4 us)
Async XLA Ops:
  3.8 13.6 %collective-permute-start.3 = (bf16[2,272,128]{2,1,0:T(8,128)(2,1)}, bf16[2,272,128]{2,1,0:T(8,128)(2,1)S(1)}, u32[]{:S(2)}, u32[]{:S(2)}) collective-permute-start(bf16[2,272,128]{2,1,0:T(8,128)(2,1)} %get-tuple-element.36.refs_0_), channel_id=1, source_target_pairs={{0,8},{1,9},{2,10},{3,11},{4,12},{5,13},{6,14},{7,15},{8,0},{9,1},... | collective-permute-start | bytes 417800 | tf_op jit(solution)/shard_map/ppermute | solution.py:219
  9.5 7.8 %collective-permute-start.2 = (bf16[272,128]{1,0:T(8,128)(2,1)}, bf16[272,128]{1,0:T(8,128)(2,1)S(1)}, u32[]{:S(2)}, u32[]{:S(2)}) collective-permute-start(bf16[272,128]{1,0:T(8,128)(2,1)} %get-tuple-element.39), channel_id=1, source_target_pairs={{0,6},{1,7},{2,4},{3,5},{4,2},{5,3},{6,0},{7,1},{8,14},{9,15},{10,... | collective-permute-start | bytes 208904 | tf_op jit(solution)/shard_map/ppermute | solution.py:219
  10.9 7.7 %collective-permute-start = (bf16[272,128]{1,0:T(8,128)(2,1)}, bf16[272,128]{1,0:T(8,128)(2,1)S(1)}, u32[]{:S(2)}, u32[]{:S(2)}) collective-permute-start(bf16[272,128]{1,0:T(8,128)(2,1)} %get-tuple-element.37), channel_id=1, source_target_pairs={{0,2},{1,3},{2,0},{3,1},{4,6},{5,7},{6,4},{7,5},{8,10},{9,11},{10,... | collective-permute-start | bytes 208904 | tf_op jit(solution)/shard_map/ppermute | solution.py:219
  13.4 9.9 %collective-permute-start.5 = (bf16[272,128]{1,0:T(8,128)(2,1)S(1)}, bf16[272,128]{1,0:T(8,128)(2,1)S(1)}, u32[]{:S(2)}, u32[]{:S(2)}) collective-permute-start(bf16[272,128]{1,0:T(8,128)(2,1)S(1)} %collective-permute-done.1.refs_2_), channel_id=1, source_target_pairs={{0,8},{1,9},{2,10},{3,11},{4,12},{5,13},{6,14},{7,15},{8,0},{9,1},... | collective-permute-start | bytes 208904 | tf_op jit(solution)/shard_map/ppermute | solution.py:219
  17.3 6.0 %collective-permute-start.6 = (bf16[272,128]{1,0:T(8,128)(2,1)S(1)}, bf16[272,128]{1,0:T(8,128)(2,1)S(1)}, u32[]{:S(2)}, u32[]{:S(2)}) collective-permute-start(bf16[272,128]{1,0:T(8,128)(2,1)S(1)} %collective-permute-done.2.refs_3_), channel_id=1, source_target_pairs={{0,8},{1,9},{2,10},{3,11},{4,12},{5,13},{6,14},{7,15},{8,0},{9,1},... | collective-permute-start | bytes 208904 | tf_op jit(solution)/shard_map/ppermute | solution.py:219
  17.4 5.9 %collective-permute-start.4 = (bf16[272,128]{1,0:T(8,128)(2,1)S(1)}, bf16[272,128]{1,0:T(8,128)(2,1)S(1)}, u32[]{:S(2)}, u32[]{:S(2)}) collective-permute-start(bf16[272,128]{1,0:T(8,128)(2,1)S(1)} %shard_map.87), channel_id=1, source_target_pairs={{0,2},{1,3},{2,0},{3,1},{4,6},{5,7},{6,4},{7,5},{8,10},{9,11},{10,... | collective-permute-start | bytes 208904 | tf_op jit(solution)/shard_map/ppermute | solution.py:219
  25.3 8.6 %collective-permute-start.10 = (bf16[32,1024]{1,0:T(8,128)(2,1)S(1)}, bf16[32,1024]{1,0:T(8,128)(2,1)S(1)}, u32[]{:S(2)}, u32[]{:S(2)}) collective-permute-start(bf16[32,1024]{1,0:T(8,128)(2,1)S(1)} %get-tuple-element.44), channel_id=1, source_target_pairs={{0,22},{1,23},{2,20},{3,21},{4,18},{5,19},{6,16},{7,17},{8,30},{9,... | collective-permute-start | bytes 196616 | tf_op jit(solution)/shard_map/ppermute | solution.py:228
  28.0 6.2 %collective-permute-start.11 = (bf16[32,1024]{1,0:T(8,128)(2,1)S(1)}, bf16[32,1024]{1,0:T(8,128)(2,1)S(1)}, u32[]{:S(2)}, u32[]{:S(2)}) collective-permute-start(bf16[32,1024]{1,0:T(8,128)(2,1)S(1)} %get-tuple-element.45), channel_id=1, source_target_pairs={{0,6},{1,7},{2,4},{3,5},{4,2},{5,3},{6,0},{7,1},{8,14},{9,15},{10,... | collective-permute-start | bytes 196616 | tf_op jit(solution)/shard_map/ppermute | solution.py:228
  29.2 7.0 %collective-permute-start.12 = (bf16[32,1024]{1,0:T(8,128)(2,1)S(1)}, bf16[32,1024]{1,0:T(8,128)(2,1)S(1)}, u32[]{:S(2)}, u32[]{:S(2)}) collective-permute-start(bf16[32,1024]{1,0:T(8,128)(2,1)S(1)} %get-tuple-element.46), channel_id=1, source_target_pairs={{0,18},{1,19},{2,16},{3,17},{4,22},{5,23},{6,20},{7,21},{8,26},{9,... | collective-permute-start | bytes 196616 | tf_op jit(solution)/shard_map/ppermute | solution.py:228
  30.1 6.2 %collective-permute-start.13 = (bf16[32,1024]{1,0:T(8,128)(2,1)S(1)}, bf16[32,1024]{1,0:T(8,128)(2,1)S(1)}, u32[]{:S(2)}, u32[]{:S(2)}) collective-permute-start(bf16[32,1024]{1,0:T(8,128)(2,1)S(1)} %get-tuple-element.47), channel_id=1, source_target_pairs={{0,20},{1,21},{2,22},{3,23},{4,16},{5,17},{6,18},{7,19},{8,28},{9,... | collective-permute-start | bytes 196616 | tf_op jit(solution)/shard_map/ppermute | solution.py:228
  40.4 8.6 %collective-permute-start.17 = (bf16[32,1024]{1,0:T(8,128)(2,1)S(1)}, bf16[32,1024]{1,0:T(8,128)(2,1)S(1)}, u32[]{:S(2)}, u32[]{:S(2)}) collective-permute-start(bf16[32,1024]{1,0:T(8,128)(2,1)S(1)} %get-tuple-element.51), channel_id=1, source_target_pairs={{0,2},{1,3},{2,0},{3,1},{4,6},{5,7},{6,4},{7,5},{8,10},{9,11},{10,... | collective-permute-start | bytes 196616 | tf_op jit(solution)/shard_map/ppermute | solution.py:219
  41.3 7.9 %collective-permute-start.18 = (bf16[32,1024]{1,0:T(8,128)(2,1)S(1)}, bf16[32,1024]{1,0:T(8,128)(2,1)S(1)}, u32[]{:S(2)}, u32[]{:S(2)}) collective-permute-start(bf16[32,1024]{1,0:T(8,128)(2,1)S(1)} %get-tuple-element.52), channel_id=1, source_target_pairs={{0,14},{1,15},{2,12},{3,13},{4,10},{5,11},{6,8},{7,9},{8,6},{9,7},... | collective-permute-start | bytes 196616 | tf_op jit(solution)/shard_map/ppermute | solution.py:219
  44.6 9.1 %collective-permute-start.19 = (bf16[32,1024]{1,0:T(8,128)(2,1)S(1)}, bf16[32,1024]{1,0:T(8,128)(2,1)S(1)}, u32[]{:S(2)}, u32[]{:S(2)}) collective-permute-start(bf16[32,1024]{1,0:T(8,128)(2,1)S(1)} %get-tuple-element.53), channel_id=1, source_target_pairs={{0,12},{1,13},{2,14},{3,15},{4,8},{5,9},{6,10},{7,11},{8,4},{9,5},... | collective-permute-start | bytes 196616 | tf_op jit(solution)/shard_map/ppermute | solution.py:219
  45.7 8.2 %collective-permute-start.20 = (bf16[32,1024]{1,0:T(8,128)(2,1)S(1)}, bf16[32,1024]{1,0:T(8,128)(2,1)S(1)}, u32[]{:S(2)}, u32[]{:S(2)}) collective-permute-start(bf16[32,1024]{1,0:T(8,128)(2,1)S(1)} %get-tuple-element.54), channel_id=1, source_target_pairs={{0,10},{1,11},{2,8},{3,9},{4,14},{5,15},{6,12},{7,13},{8,2},{9,3},... | collective-permute-start | bytes 196616 | tf_op jit(solution)/shard_map/ppermute | solution.py:219
  47.1 8.5 %collective-permute-start.21 = (bf16[32,1024]{1,0:T(8,128)(2,1)S(1)}, bf16[32,1024]{1,0:T(8,128)(2,1)S(1)}, u32[]{:S(2)}, u32[]{:S(2)}) collective-permute-start(bf16[32,1024]{1,0:T(8,128)(2,1)S(1)} %get-tuple-element.55), channel_id=1, source_target_pairs={{0,8},{1,9},{2,10},{3,11},{4,12},{5,13},{6,14},{7,15},{8,0},{9,1},... | collective-permute-start | bytes 196616 | tf_op jit(solution)/shard_map/ppermute | solution.py:219
  49.0 6.5 %collective-permute-start.22 = (bf16[32,1024]{1,0:T(8,128)(2,1)S(1)}, bf16[32,1024]{1,0:T(8,128)(2,1)S(1)}, u32[]{:S(2)}, u32[]{:S(2)}) collective-permute-start(bf16[32,1024]{1,0:T(8,128)(2,1)S(1)} %get-tuple-element.56), channel_id=1, source_target_pairs={{0,4},{1,5},{2,6},{3,7},{4,0},{5,1},{6,2},{7,3},{8,12},{9,13},{10,... | collective-permute-start | bytes 196616 | tf_op jit(solution)/shard_map/ppermute | solution.py:219
  49.2 6.8 %collective-permute-start.23 = (bf16[32,1024]{1,0:T(8,128)(2,1)S(1)}, bf16[32,1024]{1,0:T(8,128)(2,1)S(1)}, u32[]{:S(2)}, u32[]{:S(2)}) collective-permute-start(bf16[32,1024]{1,0:T(8,128)(2,1)S(1)} %get-tuple-element.57), channel_id=1, source_target_pairs={{0,6},{1,7},{2,4},{3,5},{4,2},{5,3},{6,0},{7,1},{8,14},{9,15},{10,... | collective-permute-start | bytes 196616 | tf_op jit(solution)/shard_map/ppermute | solution.py:219
  58.3 8.9 %collective-permute-start.26 = (bf16[32,1024]{1,0:T(8,128)(2,1)S(1)}, bf16[32,1024]{1,0:T(8,128)(2,1)S(1)}, u32[]{:S(2)}, u32[]{:S(2)}) collective-permute-start(bf16[32,1024]{1,0:T(8,128)(2,1)S(1)} %get-tuple-element.61), channel_id=1, source_target_pairs={{0,2},{1,3},{2,0},{3,1},{4,6},{5,7},{6,4},{7,5},{8,10},{9,11},{10,... | collective-permute-start | bytes 196616 | tf_op jit(solution)/shard_map/ppermute | solution.py:219
  59.6 8.1 %collective-permute-start.27 = (bf16[32,1024]{1,0:T(8,128)(2,1)S(1)}, bf16[32,1024]{1,0:T(8,128)(2,1)S(1)}, u32[]{:S(2)}, u32[]{:S(2)}) collective-permute-start(bf16[32,1024]{1,0:T(8,128)(2,1)S(1)} %get-tuple-element.62), channel_id=1, source_target_pairs={{0,14},{1,15},{2,12},{3,13},{4,10},{5,11},{6,8},{7,9},{8,6},{9,7},... | collective-permute-start | bytes 196616 | tf_op jit(solution)/shard_map/ppermute | solution.py:219
  62.6 11.5 %collective-permute-start.28 = (bf16[32,1024]{1,0:T(8,128)(2,1)S(1)}, bf16[32,1024]{1,0:T(8,128)(2,1)S(1)}, u32[]{:S(2)}, u32[]{:S(2)}) collective-permute-start(bf16[32,1024]{1,0:T(8,128)(2,1)S(1)} %get-tuple-element.63), channel_id=1, source_target_pairs={{0,12},{1,13},{2,14},{3,15},{4,8},{5,9},{6,10},{7,11},{8,4},{9,5},... | collective-permute-start | bytes 196616 | tf_op jit(solution)/shard_map/ppermute | solution.py:219
  63.7 11.3 %collective-permute-start.29 = (bf16[32,1024]{1,0:T(8,128)(2,1)S(1)}, bf16[32,1024]{1,0:T(8,128)(2,1)S(1)}, u32[]{:S(2)}, u32[]{:S(2)}) collective-permute-start(bf16[32,1024]{1,0:T(8,128)(2,1)S(1)} %get-tuple-element.64), channel_id=1, source_target_pairs={{0,10},{1,11},{2,8},{3,9},{4,14},{5,15},{6,12},{7,13},{8,2},{9,3},... | collective-permute-start | bytes 196616 | tf_op jit(solution)/shard_map/ppermute | solution.py:219
  64.2 10.8 %collective-permute-start.30 = (bf16[32,1024]{1,0:T(8,128)(2,1)S(1)}, bf16[32,1024]{1,0:T(8,128)(2,1)S(1)}, u32[]{:S(2)}, u32[]{:S(2)}) collective-permute-start(bf16[32,1024]{1,0:T(8,128)(2,1)S(1)} %get-tuple-element.65), channel_id=1, source_target_pairs={{0,8},{1,9},{2,10},{3,11},{4,12},{5,13},{6,14},{7,15},{8,0},{9,1},... | collective-permute-start | bytes 196616 | tf_op jit(solution)/shard_map/ppermute | solution.py:219
  67.3 7.7 %collective-permute-start.31 = (bf16[32,1024]{1,0:T(8,128)(2,1)S(1)}, bf16[32,1024]{1,0:T(8,128)(2,1)S(1)}, u32[]{:S(2)}, u32[]{:S(2)}) collective-permute-start(bf16[32,1024]{1,0:T(8,128)(2,1)S(1)} %get-tuple-element.66), channel_id=1, source_target_pairs={{0,4},{1,5},{2,6},{3,7},{4,0},{5,1},{6,2},{7,3},{8,12},{9,13},{10,... | collective-permute-start | bytes 196616 | tf_op jit(solution)/shard_map/ppermute | solution.py:219
  67.7 8.9 %collective-permute-start.32 = (bf16[32,1024]{1,0:T(8,128)(2,1)S(1)}, bf16[32,1024]{1,0:T(8,128)(2,1)S(1)}, u32[]{:S(2)}, u32[]{:S(2)}) collective-permute-start(bf16[32,1024]{1,0:T(8,128)(2,1)S(1)} %get-tuple-element.58._), channel_id=1, source_target_pairs={{0,6},{1,7},{2,4},{3,5},{4,2},{5,3},{6,0},{7,1},{8,14},{9,15},{10,... | collective-permute-start | bytes 196616 | tf_op jit(solution)/shard_map/ppermute | solution.py:219
  (12 other events, 88.4 us)

commit v10 on v9

--- a/solution.py
+++ b/solution.py
@@ -24,11 +24,14 @@
 
 
 def offsets(m):
-    return [0, 1, *range(m - 1, m // 2 - 1, -1), *range(2, m // 2)]
+    near, far = [*range(1, m // 2)], [*range(m - 1, m // 2 - 1, -1)]
+    return [0, far[0], near[0], far[1], near[1], *far[2:], *near[2:]]
 
 
 def rank(k, m):
-    return jnp.where(k < 2, k, jnp.where(k < m // 2, m // 2 + k, m + 1 - k))
+    near = jnp.where(k < 3, 2 * k, m // 2 + k)
+    far = jnp.where(k > m - 3, 2 * (m - 1 - k) + 1, m + 2 - k)
+    return jnp.where(k < m // 2, near, far)
 
 
 def deliveries(groups, h):
@@ -46,7 +49,7 @@
 
 
 def pack_kernel(groups, h, id_ref, storage_ref, down_hbm, up_hbm, *refs):
-    outs, (down_ref, up_ref, out_ref, load_sems, store_sems) = refs[:h], refs[h:]
+    outs, (down_ref, up_ref, out_ref, load_sems, store_sems) = refs[: h + 1], refs[h + 1 :]
     r, w = down_ref.shape[0], down_ref.shape[1] // h
     first = outs[0].shape[0]
     loads = []
@@ -73,7 +76,7 @@
             out_ref[k, 2 * r * b : 2 * r * b + r, :] = down_ref[:, cols]
             out_ref[k, 2 * r * b + r : 2 * r * (b + 1), :] = up_ref[:, cols]
         out_ref[k, 2 * r * (w // LANES) :, :] = mark
-        dsts = [outs[0].at[k]] * (k < first) + [outs[k]] * (k > 0)
+        dsts = [outs[k + 1]] + ([outs[0].at[k - 1]] if 0 < k <= first else [])
         for i, dst in enumerate(dsts):
             stores.append(pltpu.make_async_copy(out_ref.at[k], dst, store_sems.at[i, k]))
             stores[-1].start()
@@ -81,25 +84,21 @@
         store.wait()
 
 
-def block_of(ref):
-    return ref[0] if len(ref.shape) == 3 else ref[...]
-
-
 def stack_kernel(h, *refs):
     held_ref = refs[-1]
     for at, ref in enumerate(refs[:h]):
-        held_ref[at] = block_of(ref)
+        held_ref[at] = ref[...]
 
 
 def split_kernel(array_ref, *outs):
     for at, out in enumerate(outs):
-        out[...] = array_ref[at + 1]
+        out[...] = array_ref[at]
 
 
 def near_kernel(*refs):
     *blocks, held_ref, marks_ref = refs
     for at, ref in enumerate(blocks):
-        block = block_of(ref)
+        block = ref[...]
         held_ref[at] = block
         marks_ref[at] = block[block.shape[0] - ID_ROWS :, :]
 
@@ -242,11 +241,11 @@
     ways = deliveries(groups, h)
     w = d // len(ways)
     flat = bf16(2 * r * w // LANES + ID_ROWS, LANES)
-    spread = call(
+    first, *spread = call(
         functools.partial(pack_kernel, groups, h),
-        [bf16(h // 2, *flat.shape)] + [flat] * (h - 1),
+        [bf16(h // 2, *flat.shape)] + [flat] * h,
         [SMEM, SMEM, HBM, HBM],
-        [HBM] * h,
+        [HBM] * (h + 1),
         ALONE,
         scratch_shapes=[
             pltpu.VMEM((r, h * w), BF16),
@@ -256,11 +255,11 @@
             pltpu.SemaphoreType.DMA((2, h)),
         ],
     )(adapter_per_tile, adapter_storage_slot, down, up)
-    crossed = to_chip(h, spread[0])
+    first = to_chip(h, first)
     near = [spread[0]] + [to_chip(k, spread[k]) for k in range(1, h)]
-    handed = call(split_kernel, [flat] * (h // 2 - 1), [VMEM], [VMEM] * (h // 2 - 1))(crossed)
-    far = [crossed] + [to_chip(k + 1, block) for k, block in enumerate(handed)]
-    far += [to_chip(h, block) for block in near[h // 2 :]]
+    handed = call(split_kernel, [flat] * (h // 2), [VMEM], [VMEM] * (h // 2))(first)
+    far = [to_chip(h, near[0])] + [to_chip(k + 1, block) for k, block in enumerate(handed)]
+    far += [to_chip(h, block) for block in near[h // 2 + 1 :]]
     near, marks = call(
         near_kernel, [bf16(h, *flat.shape), bf16(h, ID_ROWS, LANES)], [VMEM] * h, [VMEM] * 2
     )(*near)

time: 77.7 us -> 74.7 us (0.961)
  starting transfers between devices: 50.9 us -> 46.3 us
  waiting for transfers between devices: 15.2 us -> 16.7 us
    ppermute x21 -> x22, starting transfers between devices: 38.2 us -> 35.1 us  [to_chip(): return lax.ppermute(block, 'fsdp', pairs)]
    ppermute x8, waiting for transfers between devices: 4.47 us -> 6.69 us  [to_device(): return lax.ppermute(block, ('group', 'fsdp'), pairs)]
    ppermute x8, starting transfers between devices: 12.5 us -> 11 us  [to_device(): return lax.ppermute(block, ('group', 'fsdp'), pairs)]
    ppermute x21 -> x22, waiting for transfers between devices: 8.33 us -> 7.64 us  [to_chip(): return lax.ppermute(block, 'fsdp', pairs)]
  transfers between devices with their start and end apart: 33 -> 34, of which waited for: 12 -> 12; matrix products, arithmetic and copies ran while one was open for 0% -> 0% of each run, Pallas kernels for 4% -> 4%
where the time goes in v10:
time: 74.7 us; the launch traced here: 74.4 us
  starting transfers between devices  46.3 us (62%)
  waiting for transfers between devices  16.7 us (22%)
  Pallas kernels  8.9 us (12%)
  between operations  1.58 us (2%)
  local copies, waits for them, and re-layouts  0.89 us (1%)
    ppermute x22, starting transfers between devices, to_chip(): return lax.ppermute(block, 'fsdp', pairs)  35.1 us
    ppermute x8, starting transfers between devices, to_device(): return lax.ppermute(block, ('group', 'fsdp'), pairs)  11 us
    ppermute x22, waiting for transfers between devices, to_chip(): return lax.ppermute(block, 'fsdp', pairs)  7.64 us
    ppermute x8, waiting for transfers between devices, to_device(): return lax.ppermute(block, ('group', 'fsdp'), pairs)  6.69 us
    ppermute x4, waiting for transfers between devices, with_other_core(): lax.ppermute(half, 'fsdp', [(f, f ^ 1) for f in range(n)])  2.38 us
    pallas_call x1, Pallas kernels, shards(): call(functools.partial(pack_kernel, groups, h), [bf16(h // 2, *flat.shape...  2.37 us
    pallas_call x1, Pallas kernels, shards(): call(functools.partial(inputs_kernel, m, groups), bf16(*acts.shape), [VME...  2.05 us
    pallas_call x1, Pallas kernels, shards(): call(functools.partial(grads_kernel, m, groups), [bf16(r, acts.shape[0])]...  1.83 us
  transfers between devices with their start and end apart: 34, of which 12 were waited for; matrix products, arithmetic and copies ran while one was open for 0% of the time, Pallas kernels for 4%

profile of v10, /device:TPU:0, one launch (start us, length us, event | category | flops | bytes accessed | tf_op | source)
XLA Modules:
  0.0 74.4 jit_solution(7089781874523650625)
XLA Ops:
  1.4 2.4 %shard_map.85 = (bf16[2,272,128]{2,1,0:T(8,128)(2,1)}, bf16[272,128]{1,0:T(8,128)(2,1)}, bf16[272,128]{1,0:T(8,128)(2,1)}, bf16[272,128]{1,0:T(8,128)(2,1)}, bf16[272,128]{1,0:T(8,128)(2,1)}) custom-call(s32[1]{0:T(128)S(6)} %copy.9.id_ref, s32[16]{0:T(128)} %storage_ref.1, bf16[1,16,8192]{2,1,0:T(8,128)(2,1)} %down_hbm.1, bf16[1,16,8192]{2,1,0:T(8,128)(2,1)} %up_hbm.1), custom_call_target="tpu_custom_call" | custom-call | tf_op jit(solution)/shard_map/pallas_call | solution.py:244
  3.8 4.1 %collective-permute-start.4 = (bf16[2,272,128]{2,1,0:T(8,128)(2,1)}, bf16[2,272,128]{2,1,0:T(8,128)(2,1)S(1)}, u32[]{:S(2)}, u32[]{:S(2)}) collective-permute-start(bf16[2,272,128]{2,1,0:T(8,128)(2,1)} %get-tuple-element.44), channel_id=1, source_target_pairs={{0,8},{1,9},{2,10},{3,11},{4,12},{5,13},{6,14},{7,15},{8,0},{9,1},... | collective-permute-start | bytes 417800 | tf_op jit(solution)/shard_map/ppermute | solution.py:218
  7.9 2.5 %collective-permute-start.2 = (bf16[272,128]{1,0:T(8,128)(2,1)}, bf16[272,128]{1,0:T(8,128)(2,1)S(1)}, u32[]{:S(2)}, u32[]{:S(2)}) collective-permute-start(bf16[272,128]{1,0:T(8,128)(2,1)} %get-tuple-element.42), channel_id=1, source_target_pairs={{0,6},{1,7},{2,4},{3,5},{4,2},{5,3},{6,0},{7,1},{8,14},{9,15},{10,... | collective-permute-start | bytes 208904 | tf_op jit(solution)/shard_map/ppermute | solution.py:218
  11.5 2.4 %collective-permute-done.2.refs_3_ = bf16[272,128]{1,0:T(8,128)(2,1)S(1)} collective-permute-done((bf16[272,128]{1,0:T(8,128)(2,1)}, bf16[272,128]{1,0:T(8,128)(2,1)S(1)}, u32[]{:S(2)}, u32[]{:S(2)}) %collective-permute-start.2) | collective-permute-done | bytes 69664 | tf_op jit(solution)/shard_map/ppermute | solution.py:218
  13.9 3.1 %collective-permute-start.7 = (bf16[272,128]{1,0:T(8,128)(2,1)S(1)}, bf16[272,128]{1,0:T(8,128)(2,1)S(1)}, u32[]{:S(2)}, u32[]{:S(2)}) collective-permute-start(bf16[272,128]{1,0:T(8,128)(2,1)S(1)} %collective-permute-done.2.refs_3_), channel_id=1, source_target_pairs={{0,8},{1,9},{2,10},{3,11},{4,12},{5,13},{6,14},{7,15},{8,0},{9,1},... | collective-permute-start | bytes 208904 | tf_op jit(solution)/shard_map/ppermute | solution.py:218
  16.9 1.7 %collective-permute-start.5 = (bf16[272,128]{1,0:T(8,128)(2,1)S(1)}, bf16[272,128]{1,0:T(8,128)(2,1)S(1)}, u32[]{:S(2)}, u32[]{:S(2)}) collective-permute-start(bf16[272,128]{1,0:T(8,128)(2,1)S(1)} %get-tuple-element.45), channel_id=1, source_target_pairs={{0,2},{1,3},{2,0},{3,1},{4,6},{5,7},{6,4},{7,5},{8,10},{9,11},{10,... | collective-permute-start | bytes 208904 | tf_op jit(solution)/shard_map/ppermute | solution.py:218
  20.7 2.7 %collective-permute-done.8.refs_4_ = bf16[4,16,128]{2,1,0:T(8,128)(2,1)S(1)} collective-permute-done((bf16[4,16,128]{2,1,0:T(8,128)(2,1)S(1)}, bf16[4,16,128]{2,1,0:T(8,128)(2,1)S(1)}, u32[]{:S(2)}, u32[]{:S(2)}) %collective-permute-start.8) | collective-permute-done | bytes 16416 | tf_op jit(solution)/shard_map/ppermute | solution.py:227
  23.5 1.5 %collective-permute-done.10.other_b.refs_3_ = bf16[4,272,128]{2,1,0:T(8,128)(2,1)S(1)} collective-permute-done((bf16[4,272,128]{2,1,0:T(8,128)(2,1)S(1)}, bf16[4,272,128]{2,1,0:T(8,128)(2,1)S(1)}, u32[]{:S(2)}, u32[]{:S(2)}) %collective-permute-start.10) | collective-permute-done | bytes 278560 | tf_op jit(solution)/shard_map/ppermute | solution.py:233
  25.4 2.8 %collective-permute-start.11 = (bf16[32,1024]{1,0:T(8,128)(2,1)S(1)}, bf16[32,1024]{1,0:T(8,128)(2,1)S(1)}, u32[]{:S(2)}, u32[]{:S(2)}) collective-permute-start(bf16[32,1024]{1,0:T(8,128)(2,1)S(1)} %get-tuple-element.50), channel_id=1, source_target_pairs={{0,22},{1,23},{2,20},{3,21},{4,18},{5,19},{6,16},{7,17},{8,30},{9,... | collective-permute-start | bytes 196616 | tf_op jit(solution)/shard_map/ppermute | solution.py:227
  30.0 2.6 %collective-permute-start.14 = (bf16[32,1024]{1,0:T(8,128)(2,1)S(1)}, bf16[32,1024]{1,0:T(8,128)(2,1)S(1)}, u32[]{:S(2)}, u32[]{:S(2)}) collective-permute-start(bf16[32,1024]{1,0:T(8,128)(2,1)S(1)} %get-tuple-element.53), channel_id=1, source_target_pairs={{0,20},{1,21},{2,22},{3,23},{4,16},{5,17},{6,18},{7,19},{8,28},{9,... | collective-permute-start | bytes 196616 | tf_op jit(solution)/shard_map/ppermute | solution.py:227
  33.6 1.4 %collective-permute-start.16 = (bf16[32,1024]{1,0:T(8,128)(2,1)S(1)}, bf16[32,1024]{1,0:T(8,128)(2,1)S(1)}, u32[]{:S(2)}, u32[]{:S(2)}) collective-permute-start(bf16[32,1024]{1,0:T(8,128)(2,1)S(1)} %get-tuple-element.55), channel_id=1, source_target_pairs={{0,4},{1,5},{2,6},{3,7},{4,0},{5,1},{6,2},{7,3},{8,12},{9,13},{10,... | collective-permute-start | bytes 196616 | tf_op jit(solution)/shard_map/ppermute | solution.py:227
  35.3 1.5 %collective-permute-done.15.refs_5_ = bf16[32,1024]{1,0:T(8,128)(2,1)S(1)} collective-permute-done((bf16[32,1024]{1,0:T(8,128)(2,1)S(1)}, bf16[32,1024]{1,0:T(8,128)(2,1)S(1)}, u32[]{:S(2)}, u32[]{:S(2)}) %collective-permute-start.15) | collective-permute-done | bytes 65568 | tf_op jit(solution)/shard_map/ppermute | solution.py:227
  37.9 1.4 %collective-permute-done.17.refs_7_ = bf16[32,1024]{1,0:T(8,128)(2,1)S(1)} collective-permute-done((bf16[32,1024]{1,0:T(8,128)(2,1)S(1)}, bf16[32,1024]{1,0:T(8,128)(2,1)S(1)}, u32[]{:S(2)}, u32[]{:S(2)}) %collective-permute-start.17) | collective-permute-done | bytes 65568 | tf_op jit(solution)/shard_map/ppermute | solution.py:227
  39.3 1.8 %shard_map.92 = (bf16[16,128]{1,0:T(8,128)(2,1)S(1)}, bf16[32,1024]{1,0:T(8,128)(2,1)S(1)}, bf16[32,1024]{1,0:T(8,128)(2,1)S(1)}, bf16[32,1024]{1,0:T(8,128)(2,1...) custom-call(f32[8,128]{1,0:T(8,128)S(1)} %shard_map.91._, ...), custom_call_target="tpu_custom_call" | custom-call | tf_op jit(solution)/shard_map/pallas_call | solution.py:283
  41.1 2.9 %collective-permute-start.18 = (bf16[32,1024]{1,0:T(8,128)(2,1)S(1)}, bf16[32,1024]{1,0:T(8,128)(2,1)S(1)}, u32[]{:S(2)}, u32[]{:S(2)}) collective-permute-start(bf16[32,1024]{1,0:T(8,128)(2,1)S(1)} %get-tuple-element.57), channel_id=1, source_target_pairs={{0,14},{1,15},{2,12},{3,13},{4,10},{5,11},{6,8},{7,9},{8,6},{9,7},... | collective-permute-start | bytes 196616 | tf_op jit(solution)/shard_map/ppermute | solution.py:218
  44.0 1.5 %collective-permute-start.19 = (bf16[32,1024]{1,0:T(8,128)(2,1)S(1)}, bf16[32,1024]{1,0:T(8,128)(2,1)S(1)}, u32[]{:S(2)}, u32[]{:S(2)}) collective-permute-start(bf16[32,1024]{1,0:T(8,128)(2,1)S(1)} %get-tuple-element.58), channel_id=1, source_target_pairs={{0,2},{1,3},{2,0},{3,1},{4,6},{5,7},{6,4},{7,5},{8,10},{9,11},{10,... | collective-permute-start | bytes 196616 | tf_op jit(solution)/shard_map/ppermute | solution.py:218
  46.5 3.4 %collective-permute-start.22 = (bf16[32,1024]{1,0:T(8,128)(2,1)S(1)}, bf16[32,1024]{1,0:T(8,128)(2,1)S(1)}, u32[]{:S(2)}, u32[]{:S(2)}) collective-permute-start(bf16[32,1024]{1,0:T(8,128)(2,1)S(1)} %get-tuple-element.61), channel_id=1, source_target_pairs={{0,10},{1,11},{2,8},{3,9},{4,14},{5,15},{6,12},{7,13},{8,2},{9,3},... | collective-permute-start | bytes 196616 | tf_op jit(solution)/shard_map/ppermute | solution.py:218
  50.0 2.4 %collective-permute-start.24 = (bf16[32,1024]{1,0:T(8,128)(2,1)S(1)}, bf16[32,1024]{1,0:T(8,128)(2,1)S(1)}, u32[]{:S(2)}, u32[]{:S(2)}) collective-permute-start(bf16[32,1024]{1,0:T(8,128)(2,1)S(1)} %get-tuple-element.63), channel_id=1, source_target_pairs={{0,6},{1,7},{2,4},{3,5},{4,2},{5,3},{6,0},{7,1},{8,14},{9,15},{10,... | collective-permute-start | bytes 196616 | tf_op jit(solution)/shard_map/ppermute | solution.py:218
  57.7 3.7 %collective-permute-start.27 = (bf16[32,1024]{1,0:T(8,128)(2,1)S(1)}, bf16[32,1024]{1,0:T(8,128)(2,1)S(1)}, u32[]{:S(2)}, u32[]{:S(2)}) collective-permute-start(bf16[32,1024]{1,0:T(8,128)(2,1)S(1)} %get-tuple-element.67), channel_id=1, source_target_pairs={{0,14},{1,15},{2,12},{3,13},{4,10},{5,11},{6,8},{7,9},{8,6},{9,7},... | collective-permute-start | bytes 196616 | tf_op jit(solution)/shard_map/ppermute | solution.py:218
  61.4 1.6 %collective-permute-start.29 = (bf16[32,1024]{1,0:T(8,128)(2,1)S(1)}, bf16[32,1024]{1,0:T(8,128)(2,1)S(1)}, u32[]{:S(2)}, u32[]{:S(2)}) collective-permute-start(bf16[32,1024]{1,0:T(8,128)(2,1)S(1)} %get-tuple-element.69), channel_id=1, source_target_pairs={{0,12},{1,13},{2,14},{3,15},{4,8},{5,9},{6,10},{7,11},{8,4},{9,5},... | collective-permute-start | bytes 196616 | tf_op jit(solution)/shard_map/ppermute | solution.py:218
  63.0 4.2 %collective-permute-start.31 = (bf16[32,1024]{1,0:T(8,128)(2,1)S(1)}, bf16[32,1024]{1,0:T(8,128)(2,1)S(1)}, u32[]{:S(2)}, u32[]{:S(2)}) collective-permute-start(bf16[32,1024]{1,0:T(8,128)(2,1)S(1)} %get-tuple-element.71), channel_id=1, source_target_pairs={{0,10},{1,11},{2,8},{3,9},{4,14},{5,15},{6,12},{7,13},{8,2},{9,3},... | collective-permute-start | bytes 196616 | tf_op jit(solution)/shard_map/ppermute | solution.py:218
  67.4 1.7 %collective-permute-start.33 = (bf16[32,1024]{1,0:T(8,128)(2,1)S(1)}, bf16[32,1024]{1,0:T(8,128)(2,1)S(1)}, u32[]{:S(2)}, u32[]{:S(2)}) collective-permute-start(bf16[32,1024]{1,0:T(8,128)(2,1)S(1)} %get-tuple-element.64._), channel_id=1, source_target_pairs={{0,6},{1,7},{2,4},{3,5},{4,2},{5,3},{6,0},{7,1},{8,14},{9,15},{10,... | collective-permute-start | bytes 196616 | tf_op jit(solution)/shard_map/ppermute | solution.py:218
  69.1 2.0 %shard_map.96 = bf16[128,8192]{1,0:T(8,128)(2,1)} custom-call(bf16[32,1024]{1,0:T(8,128)(2,1)S(1)} %get-tuple-element.64._, bf16[16,128]{1,0:T(8,128)(2,1)S(1)} %get-tuple-element.65.low_ref, bf16[32,1024]{1,0:T(8,128)(2,1)S(1)} %get-tuple-element.49.refs_0_, bf16[32,1024]{1,0:T(8,128)(2,1)S(1)} %collective-permute-done.11.refs_1_, ...), custom_call_target="tpu_custom_call" | custom-call | flops 33554432 | bytes 2097152 | tf_op jit(solution)/shard_map/pallas_call | solution.py:293
  71.2 2.1 %collective-permute-done.31.refs_5_ = bf16[32,1024]{1,0:T(8,128)(2,1)S(1)} collective-permute-done((bf16[32,1024]{1,0:T(8,128)(2,1)S(1)}, bf16[32,1024]{1,0:T(8,128)(2,1)S(1)}, u32[]{:S(2)}, u32[]{:S(2)}) %collective-permute-start.31) | collective-permute-done | bytes 65568 | tf_op jit(solution)/shard_map/ppermute | solution.py:218
  (63 shorter events, 15.3 us)
Async XLA Ops:
  3.8 13.1 %collective-permute-start.4 = (bf16[2,272,128]{2,1,0:T(8,128)(2,1)}, bf16[2,272,128]{2,1,0:T(8,128)(2,1)S(1)}, u32[]{:S(2)}, u32[]{:S(2)}) collective-permute-start(bf16[2,272,128]{2,1,0:T(8,128)(2,1)} %get-tuple-element.44), channel_id=1, source_target_pairs={{0,8},{1,9},{2,10},{3,11},{4,12},{5,13},{6,14},{7,15},{8,0},{9,1},... | collective-permute-start | bytes 417800 | tf_op jit(solution)/shard_map/ppermute | solution.py:218
  7.9 5.9 %collective-permute-start.2 = (bf16[272,128]{1,0:T(8,128)(2,1)}, bf16[272,128]{1,0:T(8,128)(2,1)S(1)}, u32[]{:S(2)}, u32[]{:S(2)}) collective-permute-start(bf16[272,128]{1,0:T(8,128)(2,1)} %get-tuple-element.42), channel_id=1, source_target_pairs={{0,6},{1,7},{2,4},{3,5},{4,2},{5,3},{6,0},{7,1},{8,14},{9,15},{10,... | collective-permute-start | bytes 208904 | tf_op jit(solution)/shard_map/ppermute | solution.py:218
  10.4 8.2 %collective-permute-start = (bf16[272,128]{1,0:T(8,128)(2,1)}, bf16[272,128]{1,0:T(8,128)(2,1)S(1)}, u32[]{:S(2)}, u32[]{:S(2)}) collective-permute-start(bf16[272,128]{1,0:T(8,128)(2,1)} %get-tuple-element.40), channel_id=1, source_target_pairs={{0,2},{1,3},{2,0},{3,1},{4,6},{5,7},{6,4},{7,5},{8,10},{9,11},{10,... | collective-permute-start | bytes 208904 | tf_op jit(solution)/shard_map/ppermute | solution.py:218
  11.0 7.7 %collective-permute-start.1 = (bf16[272,128]{1,0:T(8,128)(2,1)}, bf16[272,128]{1,0:T(8,128)(2,1)S(1)}, u32[]{:S(2)}, u32[]{:S(2)}) collective-permute-start(bf16[272,128]{1,0:T(8,128)(2,1)} %get-tuple-element.41), channel_id=1, source_target_pairs={{0,4},{1,5},{2,6},{3,7},{4,0},{5,1},{6,2},{7,3},{8,12},{9,13},{10,... | collective-permute-start | bytes 208904 | tf_op jit(solution)/shard_map/ppermute | solution.py:218
  11.4 9.3 %collective-permute-start.3 = (bf16[272,128]{1,0:T(8,128)(2,1)}, bf16[272,128]{1,0:T(8,128)(2,1)S(1)}, u32[]{:S(2)}, u32[]{:S(2)}) collective-permute-start(bf16[272,128]{1,0:T(8,128)(2,1)} %get-tuple-element.39.refs_0_), channel_id=1, source_target_pairs={{0,8},{1,9},{2,10},{3,11},{4,12},{5,13},{6,14},{7,15},{8,0},{9,1},... | collective-permute-start | bytes 208904 | tf_op jit(solution)/shard_map/ppermute | solution.py:218
  13.9 9.5 %collective-permute-start.7 = (bf16[272,128]{1,0:T(8,128)(2,1)S(1)}, bf16[272,128]{1,0:T(8,128)(2,1)S(1)}, u32[]{:S(2)}, u32[]{:S(2)}) collective-permute-start(bf16[272,128]{1,0:T(8,128)(2,1)S(1)} %collective-permute-done.2.refs_3_), channel_id=1, source_target_pairs={{0,8},{1,9},{2,10},{3,11},{4,12},{5,13},{6,14},{7,15},{8,0},{9,1},... | collective-permute-start | bytes 208904 | tf_op jit(solution)/shard_map/ppermute | solution.py:218
  16.9 6.5 %collective-permute-start.5 = (bf16[272,128]{1,0:T(8,128)(2,1)S(1)}, bf16[272,128]{1,0:T(8,128)(2,1)S(1)}, u32[]{:S(2)}, u32[]{:S(2)}) collective-permute-start(bf16[272,128]{1,0:T(8,128)(2,1)S(1)} %get-tuple-element.45), channel_id=1, source_target_pairs={{0,2},{1,3},{2,0},{3,1},{4,6},{5,7},{6,4},{7,5},{8,10},{9,11},{10,... | collective-permute-start | bytes 208904 | tf_op jit(solution)/shard_map/ppermute | solution.py:218
  25.4 8.2 %collective-permute-start.11 = (bf16[32,1024]{1,0:T(8,128)(2,1)S(1)}, bf16[32,1024]{1,0:T(8,128)(2,1)S(1)}, u32[]{:S(2)}, u32[]{:S(2)}) collective-permute-start(bf16[32,1024]{1,0:T(8,128)(2,1)S(1)} %get-tuple-element.50), channel_id=1, source_target_pairs={{0,22},{1,23},{2,20},{3,21},{4,18},{5,19},{6,16},{7,17},{8,30},{9,... | collective-permute-start | bytes 196616 | tf_op jit(solution)/shard_map/ppermute | solution.py:227
  28.2 6.8 %collective-permute-start.12 = (bf16[32,1024]{1,0:T(8,128)(2,1)S(1)}, bf16[32,1024]{1,0:T(8,128)(2,1)S(1)}, u32[]{:S(2)}, u32[]{:S(2)}) collective-permute-start(bf16[32,1024]{1,0:T(8,128)(2,1)S(1)} %get-tuple-element.51), channel_id=1, source_target_pairs={{0,6},{1,7},{2,4},{3,5},{4,2},{5,3},{6,0},{7,1},{8,14},{9,15},{10,... | collective-permute-start | bytes 196616 | tf_op jit(solution)/shard_map/ppermute | solution.py:227
  28.8 6.5 %collective-permute-start.13 = (bf16[32,1024]{1,0:T(8,128)(2,1)S(1)}, bf16[32,1024]{1,0:T(8,128)(2,1)S(1)}, u32[]{:S(2)}, u32[]{:S(2)}) collective-permute-start(bf16[32,1024]{1,0:T(8,128)(2,1)S(1)} %get-tuple-element.52), channel_id=1, source_target_pairs={{0,18},{1,19},{2,16},{3,17},{4,22},{5,23},{6,20},{7,21},{8,26},{9,... | collective-permute-start | bytes 196616 | tf_op jit(solution)/shard_map/ppermute | solution.py:227
  30.0 5.4 %collective-permute-start.14 = (bf16[32,1024]{1,0:T(8,128)(2,1)S(1)}, bf16[32,1024]{1,0:T(8,128)(2,1)S(1)}, u32[]{:S(2)}, u32[]{:S(2)}) collective-permute-start(bf16[32,1024]{1,0:T(8,128)(2,1)S(1)} %get-tuple-element.53), channel_id=1, source_target_pairs={{0,20},{1,21},{2,22},{3,23},{4,16},{5,17},{6,18},{7,19},{8,28},{9,... | collective-permute-start | bytes 196616 | tf_op jit(solution)/shard_map/ppermute | solution.py:227
  41.1 8.8 %collective-permute-start.18 = (bf16[32,1024]{1,0:T(8,128)(2,1)S(1)}, bf16[32,1024]{1,0:T(8,128)(2,1)S(1)}, u32[]{:S(2)}, u32[]{:S(2)}) collective-permute-start(bf16[32,1024]{1,0:T(8,128)(2,1)S(1)} %get-tuple-element.57), channel_id=1, source_target_pairs={{0,14},{1,15},{2,12},{3,13},{4,10},{5,11},{6,8},{7,9},{8,6},{9,7},... | collective-permute-start | bytes 196616 | tf_op jit(solution)/shard_map/ppermute | solution.py:218
  44.0 5.9 %collective-permute-start.19 = (bf16[32,1024]{1,0:T(8,128)(2,1)S(1)}, bf16[32,1024]{1,0:T(8,128)(2,1)S(1)}, u32[]{:S(2)}, u32[]{:S(2)}) collective-permute-start(bf16[32,1024]{1,0:T(8,128)(2,1)S(1)} %get-tuple-element.58), channel_id=1, source_target_pairs={{0,2},{1,3},{2,0},{3,1},{4,6},{5,7},{6,4},{7,5},{8,10},{9,11},{10,... | collective-permute-start | bytes 196616 | tf_op jit(solution)/shard_map/ppermute | solution.py:218
  45.6 6.8 %collective-permute-start.20 = (bf16[32,1024]{1,0:T(8,128)(2,1)S(1)}, bf16[32,1024]{1,0:T(8,128)(2,1)S(1)}, u32[]{:S(2)}, u32[]{:S(2)}) collective-permute-start(bf16[32,1024]{1,0:T(8,128)(2,1)S(1)} %get-tuple-element.59), channel_id=1, source_target_pairs={{0,12},{1,13},{2,14},{3,15},{4,8},{5,9},{6,10},{7,11},{8,4},{9,5},... | collective-permute-start | bytes 196616 | tf_op jit(solution)/shard_map/ppermute | solution.py:218
  46.5 7.1 %collective-permute-start.21 = (bf16[32,1024]{1,0:T(8,128)(2,1)S(1)}, bf16[32,1024]{1,0:T(8,128)(2,1)S(1)}, u32[]{:S(2)}, u32[]{:S(2)}) collective-permute-start(bf16[32,1024]{1,0:T(8,128)(2,1)S(1)} %get-tuple-element.60), channel_id=1, source_target_pairs={{0,4},{1,5},{2,6},{3,7},{4,0},{5,1},{6,2},{7,3},{8,12},{9,13},{10,... | collective-permute-start | bytes 196616 | tf_op jit(solution)/shard_map/ppermute | solution.py:218
  46.5 8.0 %collective-permute-start.22 = (bf16[32,1024]{1,0:T(8,128)(2,1)S(1)}, bf16[32,1024]{1,0:T(8,128)(2,1)S(1)}, u32[]{:S(2)}, u32[]{:S(2)}) collective-permute-start(bf16[32,1024]{1,0:T(8,128)(2,1)S(1)} %get-tuple-element.61), channel_id=1, source_target_pairs={{0,10},{1,11},{2,8},{3,9},{4,14},{5,15},{6,12},{7,13},{8,2},{9,3},... | collective-permute-start | bytes 196616 | tf_op jit(solution)/shard_map/ppermute | solution.py:218
  49.9 5.4 %collective-permute-start.23 = (bf16[32,1024]{1,0:T(8,128)(2,1)S(1)}, bf16[32,1024]{1,0:T(8,128)(2,1)S(1)}, u32[]{:S(2)}, u32[]{:S(2)}) collective-permute-start(bf16[32,1024]{1,0:T(8,128)(2,1)S(1)} %get-tuple-element.62), channel_id=1, source_target_pairs={{0,8},{1,9},{2,10},{3,11},{4,12},{5,13},{6,14},{7,15},{8,0},{9,1},... | collective-permute-start | bytes 196616 | tf_op jit(solution)/shard_map/ppermute | solution.py:218
  57.7 9.6 %collective-permute-start.27 = (bf16[32,1024]{1,0:T(8,128)(2,1)S(1)}, bf16[32,1024]{1,0:T(8,128)(2,1)S(1)}, u32[]{:S(2)}, u32[]{:S(2)}) collective-permute-start(bf16[32,1024]{1,0:T(8,128)(2,1)S(1)} %get-tuple-element.67), channel_id=1, source_target_pairs={{0,14},{1,15},{2,12},{3,13},{4,10},{5,11},{6,8},{7,9},{8,6},{9,7},... | collective-permute-start | bytes 196616 | tf_op jit(solution)/shard_map/ppermute | solution.py:218
  61.4 6.1 %collective-permute-start.28 = (bf16[32,1024]{1,0:T(8,128)(2,1)S(1)}, bf16[32,1024]{1,0:T(8,128)(2,1)S(1)}, u32[]{:S(2)}, u32[]{:S(2)}) collective-permute-start(bf16[32,1024]{1,0:T(8,128)(2,1)S(1)} %get-tuple-element.68), channel_id=1, source_target_pairs={{0,2},{1,3},{2,0},{3,1},{4,6},{5,7},{6,4},{7,5},{8,10},{9,11},{10,... | collective-permute-start | bytes 196616 | tf_op jit(solution)/shard_map/ppermute | solution.py:218
  61.4 9.8 %collective-permute-start.29 = (bf16[32,1024]{1,0:T(8,128)(2,1)S(1)}, bf16[32,1024]{1,0:T(8,128)(2,1)S(1)}, u32[]{:S(2)}, u32[]{:S(2)}) collective-permute-start(bf16[32,1024]{1,0:T(8,128)(2,1)S(1)} %get-tuple-element.69), channel_id=1, source_target_pairs={{0,12},{1,13},{2,14},{3,15},{4,8},{5,9},{6,10},{7,11},{8,4},{9,5},... | collective-permute-start | bytes 196616 | tf_op jit(solution)/shard_map/ppermute | solution.py:218
  63.0 8.2 %collective-permute-start.30 = (bf16[32,1024]{1,0:T(8,128)(2,1)S(1)}, bf16[32,1024]{1,0:T(8,128)(2,1)S(1)}, u32[]{:S(2)}, u32[]{:S(2)}) collective-permute-start(bf16[32,1024]{1,0:T(8,128)(2,1)S(1)} %get-tuple-element.70), channel_id=1, source_target_pairs={{0,4},{1,5},{2,6},{3,7},{4,0},{5,1},{6,2},{7,3},{8,12},{9,13},{10,... | collective-permute-start | bytes 196616 | tf_op jit(solution)/shard_map/ppermute | solution.py:218
  63.0 10.2 %collective-permute-start.31 = (bf16[32,1024]{1,0:T(8,128)(2,1)S(1)}, bf16[32,1024]{1,0:T(8,128)(2,1)S(1)}, u32[]{:S(2)}, u32[]{:S(2)}) collective-permute-start(bf16[32,1024]{1,0:T(8,128)(2,1)S(1)} %get-tuple-element.71), channel_id=1, source_target_pairs={{0,10},{1,11},{2,8},{3,9},{4,14},{5,15},{6,12},{7,13},{8,2},{9,3},... | collective-permute-start | bytes 196616 | tf_op jit(solution)/shard_map/ppermute | solution.py:218
  67.2 6.3 %collective-permute-start.32 = (bf16[32,1024]{1,0:T(8,128)(2,1)S(1)}, bf16[32,1024]{1,0:T(8,128)(2,1)S(1)}, u32[]{:S(2)}, u32[]{:S(2)}) collective-permute-start(bf16[32,1024]{1,0:T(8,128)(2,1)S(1)} %get-tuple-element.72), channel_id=1, source_target_pairs={{0,8},{1,9},{2,10},{3,11},{4,12},{5,13},{6,14},{7,15},{8,0},{9,1},... | collective-permute-start | bytes 196616 | tf_op jit(solution)/shard_map/ppermute | solution.py:218
  67.4 6.1 %collective-permute-start.33 = (bf16[32,1024]{1,0:T(8,128)(2,1)S(1)}, bf16[32,1024]{1,0:T(8,128)(2,1)S(1)}, u32[]{:S(2)}, u32[]{:S(2)}) collective-permute-start(bf16[32,1024]{1,0:T(8,128)(2,1)S(1)} %get-tuple-element.64._), channel_id=1, source_target_pairs={{0,6},{1,7},{2,4},{3,5},{4,2},{5,3},{6,0},{7,1},{8,14},{9,15},{10,... | collective-permute-start | bytes 196616 | tf_op jit(solution)/shard_map/ppermute | solution.py:218
  (13 other events, 94.4 us)

commit v11 on v10

--- a/solution.py
+++ b/solution.py
@@ -24,12 +24,13 @@
 
 
 def offsets(m):
-    near, far = [*range(1, m // 2)], [*range(m - 1, m // 2 - 1, -1)]
+    near, far = [*range(m // 2 - 1, 0, -1)], [*range(m - 1, m // 2 - 1, -1)]
     return [0, far[0], near[0], far[1], near[1], *far[2:], *near[2:]]
 
 
 def rank(k, m):
-    near = jnp.where(k < 3, 2 * k, m // 2 + k)
+    near = jnp.where(k > m // 2 - 3, m - 2 * k, m - k)
+    near = jnp.where(k == 0, 0, near)
     far = jnp.where(k > m - 3, 2 * (m - 1 - k) + 1, m + 2 - k)
     return jnp.where(k < m // 2, near, far)
 
@@ -151,14 +152,14 @@
     r = r2 // 2
     rows = acts_ref.shape[0]
     dims_nt = (((1,), (1,)), ((), ()))
-    low_u = jnp.zeros((r, rows), F32)
-    low_h = jnp.zeros((r, rows), F32)
+    low_u = jnp.zeros((rows, r), F32)
+    low_h = jnp.zeros((rows, r), F32)
     for (x, k), factor in zip(ways, factors):
         cols = columns(share(groups, m // 2, x, k), w)
-        low_u += lax.dot_general(factor[0:r, :], acts_ref[:, cols], dims_nt, preferred_element_type=F32)
-        low_h += lax.dot_general(factor[r:r2, :], cot_ref[:, cols], dims_nt, preferred_element_type=F32)
-    low_u = low_u.astype(BF16)
-    low_h = low_h.astype(BF16)
+        low_u += lax.dot_general(acts_ref[:, cols], factor[0:r, :], dims_nt, preferred_element_type=F32)
+        low_h += lax.dot_general(cot_ref[:, cols], factor[r:r2, :], dims_nt, preferred_element_type=F32)
+    low_u = low_u.T.astype(BF16)
+    low_h = low_h.T.astype(BF16)
     low_ref[...] = low_h
     for k, out in zip(offsets(m), outs):
         cols = columns(p ^ k, out.shape[1])

time: 74.7 us -> 74.9 us (level)
  waiting for transfers between devices: 16.7 us -> 18.6 us
  starting transfers between devices: 46.3 us -> 44.6 us
    ppermute x22, waiting for transfers between devices: 7.64 us -> 9.51 us  [to_chip(): return lax.ppermute(block, 'fsdp', pairs)]
    ppermute x22, starting transfers between devices: 35.1 us -> 33.4 us  [to_chip(): return lax.ppermute(block, 'fsdp', pairs)]
  transfers between devices with their start and end apart: 34 -> 34, of which waited for: 12 -> 13; matrix products, arithmetic and copies ran while one was open for 0% -> 0% of each run, Pallas kernels for 4% -> 4%
where the time goes in v11:
time: 74.9 us; the launch traced here: 74.6 us
  starting transfers between devices  44.6 us (60%)
  waiting for transfers between devices  18.6 us (25%)
  Pallas kernels  8.97 us (12%)
  between operations  1.59 us (2%)
  local copies, waits for them, and re-layouts  0.89 us (1%)
    ppermute x22, starting transfers between devices, to_chip(): return lax.ppermute(block, 'fsdp', pairs)  33.4 us
    ppermute x8, starting transfers between devices, to_device(): return lax.ppermute(block, ('group', 'fsdp'), pairs)  11 us
    ppermute x22, waiting for transfers between devices, to_chip(): return lax.ppermute(block, 'fsdp', pairs)  9.51 us
    ppermute x8, waiting for transfers between devices, to_device(): return lax.ppermute(block, ('group', 'fsdp'), pairs)  6.69 us
    ppermute x4, waiting for transfers between devices, with_other_core(): lax.ppermute(half, 'fsdp', [(f, f ^ 1) for f in range(n)])  2.38 us
    pallas_call x1, Pallas kernels, shards(): call(functools.partial(pack_kernel, groups, h), [bf16(h // 2, *flat.shape...  2.37 us
    pallas_call x1, Pallas kernels, shards(): call(functools.partial(inputs_kernel, m, groups), bf16(*acts.shape), [VME...  2.04 us
    pallas_call x1, Pallas kernels, shards(): call(functools.partial(grads_kernel, m, groups), [bf16(r, acts.shape[0])]...  1.91 us
  transfers between devices with their start and end apart: 34, of which 13 were waited for; matrix products, arithmetic and copies ran while one was open for 0% of the time, Pallas kernels for 4%

profile of v11, /device:TPU:0, one launch (start us, length us, event | category | flops | bytes accessed | tf_op | source)
XLA Modules:
  0.0 74.6 jit_solution(13303999985569598350)
XLA Ops:
  1.4 2.4 %shard_map.85 = (bf16[2,272,128]{2,1,0:T(8,128)(2,1)}, bf16[272,128]{1,0:T(8,128)(2,1)}, bf16[272,128]{1,0:T(8,128)(2,1)}, bf16[272,128]{1,0:T(8,128)(2,1)}, bf16[272,128]{1,0:T(8,128)(2,1)}) custom-call(s32[1]{0:T(128)S(6)} %copy.9.id_ref, s32[16]{0:T(128)} %storage_ref.1, bf16[1,16,8192]{2,1,0:T(8,128)(2,1)} %down_hbm.1, bf16[1,16,8192]{2,1,0:T(8,128)(2,1)} %up_hbm.1), custom_call_target="tpu_custom_call" | custom-call | tf_op jit(solution)/shard_map/pallas_call | solution.py:245
  3.8 4.1 %collective-permute-start.4 = (bf16[2,272,128]{2,1,0:T(8,128)(2,1)}, bf16[2,272,128]{2,1,0:T(8,128)(2,1)S(1)}, u32[]{:S(2)}, u32[]{:S(2)}) collective-permute-start(bf16[2,272,128]{2,1,0:T(8,128)(2,1)} %get-tuple-element.44), channel_id=1, source_target_pairs={{0,8},{1,9},{2,10},{3,11},{4,12},{5,13},{6,14},{7,15},{8,0},{9,1},... | collective-permute-start | bytes 417800 | tf_op jit(solution)/shard_map/ppermute | solution.py:219
  7.9 2.5 %collective-permute-start.2 = (bf16[272,128]{1,0:T(8,128)(2,1)}, bf16[272,128]{1,0:T(8,128)(2,1)S(1)}, u32[]{:S(2)}, u32[]{:S(2)}) collective-permute-start(bf16[272,128]{1,0:T(8,128)(2,1)} %get-tuple-element.42), channel_id=1, source_target_pairs={{0,6},{1,7},{2,4},{3,5},{4,2},{5,3},{6,0},{7,1},{8,14},{9,15},{10,... | collective-permute-start | bytes 208904 | tf_op jit(solution)/shard_map/ppermute | solution.py:219
  11.5 2.4 %collective-permute-done.2.refs_3_ = bf16[272,128]{1,0:T(8,128)(2,1)S(1)} collective-permute-done((bf16[272,128]{1,0:T(8,128)(2,1)}, bf16[272,128]{1,0:T(8,128)(2,1)S(1)}, u32[]{:S(2)}, u32[]{:S(2)}) %collective-permute-start.2) | collective-permute-done | bytes 69664 | tf_op jit(solution)/shard_map/ppermute | solution.py:219
  13.9 3.1 %collective-permute-start.7 = (bf16[272,128]{1,0:T(8,128)(2,1)S(1)}, bf16[272,128]{1,0:T(8,128)(2,1)S(1)}, u32[]{:S(2)}, u32[]{:S(2)}) collective-permute-start(bf16[272,128]{1,0:T(8,128)(2,1)S(1)} %collective-permute-done.2.refs_3_), channel_id=1, source_target_pairs={{0,8},{1,9},{2,10},{3,11},{4,12},{5,13},{6,14},{7,15},{8,0},{9,1},... | collective-permute-start | bytes 208904 | tf_op jit(solution)/shard_map/ppermute | solution.py:219
  16.9 1.7 %collective-permute-start.5 = (bf16[272,128]{1,0:T(8,128)(2,1)S(1)}, bf16[272,128]{1,0:T(8,128)(2,1)S(1)}, u32[]{:S(2)}, u32[]{:S(2)}) collective-permute-start(bf16[272,128]{1,0:T(8,128)(2,1)S(1)} %get-tuple-element.45), channel_id=1, source_target_pairs={{0,2},{1,3},{2,0},{3,1},{4,6},{5,7},{6,4},{7,5},{8,10},{9,11},{10,... | collective-permute-start | bytes 208904 | tf_op jit(solution)/shard_map/ppermute | solution.py:219
  20.7 2.7 %collective-permute-done.8.refs_4_ = bf16[4,16,128]{2,1,0:T(8,128)(2,1)S(1)} collective-permute-done((bf16[4,16,128]{2,1,0:T(8,128)(2,1)S(1)}, bf16[4,16,128]{2,1,0:T(8,128)(2,1)S(1)}, u32[]{:S(2)}, u32[]{:S(2)}) %collective-permute-start.8) | collective-permute-done | bytes 16416 | tf_op jit(solution)/shard_map/ppermute | solution.py:228
  23.5 1.5 %collective-permute-done.10.other_b.refs_3_ = bf16[4,272,128]{2,1,0:T(8,128)(2,1)S(1)} collective-permute-done((bf16[4,272,128]{2,1,0:T(8,128)(2,1)S(1)}, bf16[4,272,128]{2,1,0:T(8,128)(2,1)S(1)}, u32[]{:S(2)}, u32[]{:S(2)}) %collective-permute-start.10) | collective-permute-done | bytes 278560 | tf_op jit(solution)/shard_map/ppermute | solution.py:234
  25.4 2.8 %collective-permute-start.11 = (bf16[32,1024]{1,0:T(8,128)(2,1)S(1)}, bf16[32,1024]{1,0:T(8,128)(2,1)S(1)}, u32[]{:S(2)}, u32[]{:S(2)}) collective-permute-start(bf16[32,1024]{1,0:T(8,128)(2,1)S(1)} %get-tuple-element.50), channel_id=1, source_target_pairs={{0,22},{1,23},{2,20},{3,21},{4,18},{5,19},{6,16},{7,17},{8,30},{9,... | collective-permute-start | bytes 196616 | tf_op jit(solution)/shard_map/ppermute | solution.py:228
  30.0 2.6 %collective-permute-start.14 = (bf16[32,1024]{1,0:T(8,128)(2,1)S(1)}, bf16[32,1024]{1,0:T(8,128)(2,1)S(1)}, u32[]{:S(2)}, u32[]{:S(2)}) collective-permute-start(bf16[32,1024]{1,0:T(8,128)(2,1)S(1)} %get-tuple-element.53), channel_id=1, source_target_pairs={{0,20},{1,21},{2,22},{3,23},{4,16},{5,17},{6,18},{7,19},{8,28},{9,... | collective-permute-start | bytes 196616 | tf_op jit(solution)/shard_map/ppermute | solution.py:228
  35.3 1.5 %collective-permute-done.15.refs_5_ = bf16[32,1024]{1,0:T(8,128)(2,1)S(1)} collective-permute-done((bf16[32,1024]{1,0:T(8,128)(2,1)S(1)}, bf16[32,1024]{1,0:T(8,128)(2,1)S(1)}, u32[]{:S(2)}, u32[]{:S(2)}) %collective-permute-start.15) | collective-permute-done | bytes 65568 | tf_op jit(solution)/shard_map/ppermute | solution.py:228
  37.9 1.4 %collective-permute-done.17.refs_7_ = bf16[32,1024]{1,0:T(8,128)(2,1)S(1)} collective-permute-done((bf16[32,1024]{1,0:T(8,128)(2,1)S(1)}, bf16[32,1024]{1,0:T(8,128)(2,1)S(1)}, u32[]{:S(2)}, u32[]{:S(2)}) %collective-permute-start.17) | collective-permute-done | bytes 65568 | tf_op jit(solution)/shard_map/ppermute | solution.py:228
  39.3 1.9 %shard_map.92 = (bf16[16,128]{1,0:T(8,128)(2,1)S(1)}, bf16[32,1024]{1,0:T(8,128)(2,1)S(1)}, bf16[32,1024]{1,0:T(8,128)(2,1)S(1)}, bf16[32,1024]{1,0:T(8,128)(2,1...) custom-call(f32[8,128]{1,0:T(8,128)S(1)} %shard_map.91._, ...), custom_call_target="tpu_custom_call" | custom-call | tf_op jit(solution)/shard_map/pallas_call | solution.py:284
  41.2 2.9 %collective-permute-start.18 = (bf16[32,1024]{1,0:T(8,128)(2,1)S(1)}, bf16[32,1024]{1,0:T(8,128)(2,1)S(1)}, u32[]{:S(2)}, u32[]{:S(2)}) collective-permute-start(bf16[32,1024]{1,0:T(8,128)(2,1)S(1)} %get-tuple-element.57), channel_id=1, source_target_pairs={{0,14},{1,15},{2,12},{3,13},{4,10},{5,11},{6,8},{7,9},{8,6},{9,7},... | collective-permute-start | bytes 196616 | tf_op jit(solution)/shard_map/ppermute | solution.py:219
  44.1 1.6 %collective-permute-start.19 = (bf16[32,1024]{1,0:T(8,128)(2,1)S(1)}, bf16[32,1024]{1,0:T(8,128)(2,1)S(1)}, u32[]{:S(2)}, u32[]{:S(2)}) collective-permute-start(bf16[32,1024]{1,0:T(8,128)(2,1)S(1)} %get-tuple-element.58), channel_id=1, source_target_pairs={{0,6},{1,7},{2,4},{3,5},{4,2},{5,3},{6,0},{7,1},{8,14},{9,15},{10,... | collective-permute-start | bytes 196616 | tf_op jit(solution)/shard_map/ppermute | solution.py:219
  47.1 2.4 %collective-permute-start.22 = (bf16[32,1024]{1,0:T(8,128)(2,1)S(1)}, bf16[32,1024]{1,0:T(8,128)(2,1)S(1)}, u32[]{:S(2)}, u32[]{:S(2)}) collective-permute-start(bf16[32,1024]{1,0:T(8,128)(2,1)S(1)} %get-tuple-element.61), channel_id=1, source_target_pairs={{0,10},{1,11},{2,8},{3,9},{4,14},{5,15},{6,12},{7,13},{8,2},{9,3},... | collective-permute-start | bytes 196616 | tf_op jit(solution)/shard_map/ppermute | solution.py:219
  50.2 1.5 %collective-permute-start.24 = (bf16[32,1024]{1,0:T(8,128)(2,1)S(1)}, bf16[32,1024]{1,0:T(8,128)(2,1)S(1)}, u32[]{:S(2)}, u32[]{:S(2)}) collective-permute-start(bf16[32,1024]{1,0:T(8,128)(2,1)S(1)} %get-tuple-element.63), channel_id=1, source_target_pairs={{0,2},{1,3},{2,0},{3,1},{4,6},{5,7},{6,4},{7,5},{8,10},{9,11},{10,... | collective-permute-start | bytes 196616 | tf_op jit(solution)/shard_map/ppermute | solution.py:219
  52.1 2.7 %collective-permute-done.22.refs_1_ = bf16[32,1024]{1,0:T(8,128)(2,1)S(1)} collective-permute-done((bf16[32,1024]{1,0:T(8,128)(2,1)S(1)}, bf16[32,1024]{1,0:T(8,128)(2,1)S(1)}, u32[]{:S(2)}, u32[]{:S(2)}) %collective-permute-start.22) | collective-permute-done | bytes 65568 | tf_op jit(solution)/shard_map/ppermute | solution.py:219
  58.0 2.9 %collective-permute-start.27 = (bf16[32,1024]{1,0:T(8,128)(2,1)S(1)}, bf16[32,1024]{1,0:T(8,128)(2,1)S(1)}, u32[]{:S(2)}, u32[]{:S(2)}) collective-permute-start(bf16[32,1024]{1,0:T(8,128)(2,1)S(1)} %get-tuple-element.67), channel_id=1, source_target_pairs={{0,14},{1,15},{2,12},{3,13},{4,10},{5,11},{6,8},{7,9},{8,6},{9,7},... | collective-permute-start | bytes 196616 | tf_op jit(solution)/shard_map/ppermute | solution.py:219
  60.9 2.1 %collective-permute-start.29 = (bf16[32,1024]{1,0:T(8,128)(2,1)S(1)}, bf16[32,1024]{1,0:T(8,128)(2,1)S(1)}, u32[]{:S(2)}, u32[]{:S(2)}) collective-permute-start(bf16[32,1024]{1,0:T(8,128)(2,1)S(1)} %get-tuple-element.69), channel_id=1, source_target_pairs={{0,12},{1,13},{2,14},{3,15},{4,8},{5,9},{6,10},{7,11},{8,4},{9,5},... | collective-permute-start | bytes 196616 | tf_op jit(solution)/shard_map/ppermute | solution.py:219
  63.9 2.6 %collective-permute-start.31 = (bf16[32,1024]{1,0:T(8,128)(2,1)S(1)}, bf16[32,1024]{1,0:T(8,128)(2,1)S(1)}, u32[]{:S(2)}, u32[]{:S(2)}) collective-permute-start(bf16[32,1024]{1,0:T(8,128)(2,1)S(1)} %get-tuple-element.71), channel_id=1, source_target_pairs={{0,10},{1,11},{2,8},{3,9},{4,14},{5,15},{6,12},{7,13},{8,2},{9,3},... | collective-permute-start | bytes 196616 | tf_op jit(solution)/shard_map/ppermute | solution.py:219
  66.5 1.5 %collective-permute-start.32 = (bf16[32,1024]{1,0:T(8,128)(2,1)S(1)}, bf16[32,1024]{1,0:T(8,128)(2,1)S(1)}, u32[]{:S(2)}, u32[]{:S(2)}) collective-permute-start(bf16[32,1024]{1,0:T(8,128)(2,1)S(1)} %get-tuple-element.72), channel_id=1, source_target_pairs={{0,8},{1,9},{2,10},{3,11},{4,12},{5,13},{6,14},{7,15},{8,0},{9,1},... | collective-permute-start | bytes 196616 | tf_op jit(solution)/shard_map/ppermute | solution.py:219
  69.0 2.0 %shard_map.96 = bf16[128,8192]{1,0:T(8,128)(2,1)} custom-call(bf16[32,1024]{1,0:T(8,128)(2,1)S(1)} %get-tuple-element.64._, bf16[16,128]{1,0:T(8,128)(2,1)S(1)} %get-tuple-element.65.low_ref, bf16[32,1024]{1,0:T(8,128)(2,1)S(1)} %get-tuple-element.49.refs_0_, bf16[32,1024]{1,0:T(8,128)(2,1)S(1)} %collective-permute-done.11.refs_1_, ...), custom_call_target="tpu_custom_call" | custom-call | flops 33554432 | bytes 2097152 | tf_op jit(solution)/shard_map/pallas_call | solution.py:294
  71.0 2.0 %collective-permute-done.31.refs_5_ = bf16[32,1024]{1,0:T(8,128)(2,1)S(1)} collective-permute-done((bf16[32,1024]{1,0:T(8,128)(2,1)S(1)}, bf16[32,1024]{1,0:T(8,128)(2,1)S(1)}, u32[]{:S(2)}, u32[]{:S(2)}) %collective-permute-start.31) | collective-permute-done | bytes 65568 | tf_op jit(solution)/shard_map/ppermute | solution.py:219
  (63 shorter events, 18.1 us)
Async XLA Ops:
  3.8 13.1 %collective-permute-start.4 = (bf16[2,272,128]{2,1,0:T(8,128)(2,1)}, bf16[2,272,128]{2,1,0:T(8,128)(2,1)S(1)}, u32[]{:S(2)}, u32[]{:S(2)}) collective-permute-start(bf16[2,272,128]{2,1,0:T(8,128)(2,1)} %get-tuple-element.44), channel_id=1, source_target_pairs={{0,8},{1,9},{2,10},{3,11},{4,12},{5,13},{6,14},{7,15},{8,0},{9,1},... | collective-permute-start | bytes 417800 | tf_op jit(solution)/shard_map/ppermute | solution.py:219
  7.9 5.9 %collective-permute-start.2 = (bf16[272,128]{1,0:T(8,128)(2,1)}, bf16[272,128]{1,0:T(8,128)(2,1)S(1)}, u32[]{:S(2)}, u32[]{:S(2)}) collective-permute-start(bf16[272,128]{1,0:T(8,128)(2,1)} %get-tuple-element.42), channel_id=1, source_target_pairs={{0,6},{1,7},{2,4},{3,5},{4,2},{5,3},{6,0},{7,1},{8,14},{9,15},{10,... | collective-permute-start | bytes 208904 | tf_op jit(solution)/shard_map/ppermute | solution.py:219
  10.4 8.2 %collective-permute-start = (bf16[272,128]{1,0:T(8,128)(2,1)}, bf16[272,128]{1,0:T(8,128)(2,1)S(1)}, u32[]{:S(2)}, u32[]{:S(2)}) collective-permute-start(bf16[272,128]{1,0:T(8,128)(2,1)} %get-tuple-element.40), channel_id=1, source_target_pairs={{0,2},{1,3},{2,0},{3,1},{4,6},{5,7},{6,4},{7,5},{8,10},{9,11},{10,... | collective-permute-start | bytes 208904 | tf_op jit(solution)/shard_map/ppermute | solution.py:219
  11.0 7.7 %collective-permute-start.1 = (bf16[272,128]{1,0:T(8,128)(2,1)}, bf16[272,128]{1,0:T(8,128)(2,1)S(1)}, u32[]{:S(2)}, u32[]{:S(2)}) collective-permute-start(bf16[272,128]{1,0:T(8,128)(2,1)} %get-tuple-element.41), channel_id=1, source_target_pairs={{0,4},{1,5},{2,6},{3,7},{4,0},{5,1},{6,2},{7,3},{8,12},{9,13},{10,... | collective-permute-start | bytes 208904 | tf_op jit(solution)/shard_map/ppermute | solution.py:219
  11.4 9.3 %collective-permute-start.3 = (bf16[272,128]{1,0:T(8,128)(2,1)}, bf16[272,128]{1,0:T(8,128)(2,1)S(1)}, u32[]{:S(2)}, u32[]{:S(2)}) collective-permute-start(bf16[272,128]{1,0:T(8,128)(2,1)} %get-tuple-element.39.refs_0_), channel_id=1, source_target_pairs={{0,8},{1,9},{2,10},{3,11},{4,12},{5,13},{6,14},{7,15},{8,0},{9,1},... | collective-permute-start | bytes 208904 | tf_op jit(solution)/shard_map/ppermute | solution.py:219
  13.9 9.5 %collective-permute-start.7 = (bf16[272,128]{1,0:T(8,128)(2,1)S(1)}, bf16[272,128]{1,0:T(8,128)(2,1)S(1)}, u32[]{:S(2)}, u32[]{:S(2)}) collective-permute-start(bf16[272,128]{1,0:T(8,128)(2,1)S(1)} %collective-permute-done.2.refs_3_), channel_id=1, source_target_pairs={{0,8},{1,9},{2,10},{3,11},{4,12},{5,13},{6,14},{7,15},{8,0},{9,1},... | collective-permute-start | bytes 208904 | tf_op jit(solution)/shard_map/ppermute | solution.py:219
  16.9 6.5 %collective-permute-start.5 = (bf16[272,128]{1,0:T(8,128)(2,1)S(1)}, bf16[272,128]{1,0:T(8,128)(2,1)S(1)}, u32[]{:S(2)}, u32[]{:S(2)}) collective-permute-start(bf16[272,128]{1,0:T(8,128)(2,1)S(1)} %get-tuple-element.45), channel_id=1, source_target_pairs={{0,2},{1,3},{2,0},{3,1},{4,6},{5,7},{6,4},{7,5},{8,10},{9,11},{10,... | collective-permute-start | bytes 208904 | tf_op jit(solution)/shard_map/ppermute | solution.py:219
  25.4 8.2 %collective-permute-start.11 = (bf16[32,1024]{1,0:T(8,128)(2,1)S(1)}, bf16[32,1024]{1,0:T(8,128)(2,1)S(1)}, u32[]{:S(2)}, u32[]{:S(2)}) collective-permute-start(bf16[32,1024]{1,0:T(8,128)(2,1)S(1)} %get-tuple-element.50), channel_id=1, source_target_pairs={{0,22},{1,23},{2,20},{3,21},{4,18},{5,19},{6,16},{7,17},{8,30},{9,... | collective-permute-start | bytes 196616 | tf_op jit(solution)/shard_map/ppermute | solution.py:228
  28.2 6.8 %collective-permute-start.12 = (bf16[32,1024]{1,0:T(8,128)(2,1)S(1)}, bf16[32,1024]{1,0:T(8,128)(2,1)S(1)}, u32[]{:S(2)}, u32[]{:S(2)}) collective-permute-start(bf16[32,1024]{1,0:T(8,128)(2,1)S(1)} %get-tuple-element.51), channel_id=1, source_target_pairs={{0,6},{1,7},{2,4},{3,5},{4,2},{5,3},{6,0},{7,1},{8,14},{9,15},{10,... | collective-permute-start | bytes 196616 | tf_op jit(solution)/shard_map/ppermute | solution.py:228
  28.8 6.5 %collective-permute-start.13 = (bf16[32,1024]{1,0:T(8,128)(2,1)S(1)}, bf16[32,1024]{1,0:T(8,128)(2,1)S(1)}, u32[]{:S(2)}, u32[]{:S(2)}) collective-permute-start(bf16[32,1024]{1,0:T(8,128)(2,1)S(1)} %get-tuple-element.52), channel_id=1, source_target_pairs={{0,18},{1,19},{2,16},{3,17},{4,22},{5,23},{6,20},{7,21},{8,26},{9,... | collective-permute-start | bytes 196616 | tf_op jit(solution)/shard_map/ppermute | solution.py:228
  41.2 8.3 %collective-permute-start.18 = (bf16[32,1024]{1,0:T(8,128)(2,1)S(1)}, bf16[32,1024]{1,0:T(8,128)(2,1)S(1)}, u32[]{:S(2)}, u32[]{:S(2)}) collective-permute-start(bf16[32,1024]{1,0:T(8,128)(2,1)S(1)} %get-tuple-element.57), channel_id=1, source_target_pairs={{0,14},{1,15},{2,12},{3,13},{4,10},{5,11},{6,8},{7,9},{8,6},{9,7},... | collective-permute-start | bytes 196616 | tf_op jit(solution)/shard_map/ppermute | solution.py:219
  44.1 6.1 %collective-permute-start.19 = (bf16[32,1024]{1,0:T(8,128)(2,1)S(1)}, bf16[32,1024]{1,0:T(8,128)(2,1)S(1)}, u32[]{:S(2)}, u32[]{:S(2)}) collective-permute-start(bf16[32,1024]{1,0:T(8,128)(2,1)S(1)} %get-tuple-element.58), channel_id=1, source_target_pairs={{0,6},{1,7},{2,4},{3,5},{4,2},{5,3},{6,0},{7,1},{8,14},{9,15},{10,... | collective-permute-start | bytes 196616 | tf_op jit(solution)/shard_map/ppermute | solution.py:219
  45.8 6.2 %collective-permute-start.20 = (bf16[32,1024]{1,0:T(8,128)(2,1)S(1)}, bf16[32,1024]{1,0:T(8,128)(2,1)S(1)}, u32[]{:S(2)}, u32[]{:S(2)}) collective-permute-start(bf16[32,1024]{1,0:T(8,128)(2,1)S(1)} %get-tuple-element.59), channel_id=1, source_target_pairs={{0,12},{1,13},{2,14},{3,15},{4,8},{5,9},{6,10},{7,11},{8,4},{9,5},... | collective-permute-start | bytes 196616 | tf_op jit(solution)/shard_map/ppermute | solution.py:219
  45.8 6.3 %collective-permute-start.21 = (bf16[32,1024]{1,0:T(8,128)(2,1)S(1)}, bf16[32,1024]{1,0:T(8,128)(2,1)S(1)}, u32[]{:S(2)}, u32[]{:S(2)}) collective-permute-start(bf16[32,1024]{1,0:T(8,128)(2,1)S(1)} %get-tuple-element.60), channel_id=1, source_target_pairs={{0,4},{1,5},{2,6},{3,7},{4,0},{5,1},{6,2},{7,3},{8,12},{9,13},{10,... | collective-permute-start | bytes 196616 | tf_op jit(solution)/shard_map/ppermute | solution.py:219
  47.1 7.7 %collective-permute-start.22 = (bf16[32,1024]{1,0:T(8,128)(2,1)S(1)}, bf16[32,1024]{1,0:T(8,128)(2,1)S(1)}, u32[]{:S(2)}, u32[]{:S(2)}) collective-permute-start(bf16[32,1024]{1,0:T(8,128)(2,1)S(1)} %get-tuple-element.61), channel_id=1, source_target_pairs={{0,10},{1,11},{2,8},{3,9},{4,14},{5,15},{6,12},{7,13},{8,2},{9,3},... | collective-permute-start | bytes 196616 | tf_op jit(solution)/shard_map/ppermute | solution.py:219
  49.5 6.2 %collective-permute-start.23 = (bf16[32,1024]{1,0:T(8,128)(2,1)S(1)}, bf16[32,1024]{1,0:T(8,128)(2,1)S(1)}, u32[]{:S(2)}, u32[]{:S(2)}) collective-permute-start(bf16[32,1024]{1,0:T(8,128)(2,1)S(1)} %get-tuple-element.62), channel_id=1, source_target_pairs={{0,8},{1,9},{2,10},{3,11},{4,12},{5,13},{6,14},{7,15},{8,0},{9,1},... | collective-permute-start | bytes 196616 | tf_op jit(solution)/shard_map/ppermute | solution.py:219
  50.2 5.5 %collective-permute-start.24 = (bf16[32,1024]{1,0:T(8,128)(2,1)S(1)}, bf16[32,1024]{1,0:T(8,128)(2,1)S(1)}, u32[]{:S(2)}, u32[]{:S(2)}) collective-permute-start(bf16[32,1024]{1,0:T(8,128)(2,1)S(1)} %get-tuple-element.63), channel_id=1, source_target_pairs={{0,2},{1,3},{2,0},{3,1},{4,6},{5,7},{6,4},{7,5},{8,10},{9,11},{10,... | collective-permute-start | bytes 196616 | tf_op jit(solution)/shard_map/ppermute | solution.py:219
  58.0 8.5 %collective-permute-start.27 = (bf16[32,1024]{1,0:T(8,128)(2,1)S(1)}, bf16[32,1024]{1,0:T(8,128)(2,1)S(1)}, u32[]{:S(2)}, u32[]{:S(2)}) collective-permute-start(bf16[32,1024]{1,0:T(8,128)(2,1)S(1)} %get-tuple-element.67), channel_id=1, source_target_pairs={{0,14},{1,15},{2,12},{3,13},{4,10},{5,11},{6,8},{7,9},{8,6},{9,7},... | collective-permute-start | bytes 196616 | tf_op jit(solution)/shard_map/ppermute | solution.py:219
  60.9 7.5 %collective-permute-start.28 = (bf16[32,1024]{1,0:T(8,128)(2,1)S(1)}, bf16[32,1024]{1,0:T(8,128)(2,1)S(1)}, u32[]{:S(2)}, u32[]{:S(2)}) collective-permute-start(bf16[32,1024]{1,0:T(8,128)(2,1)S(1)} %get-tuple-element.68), channel_id=1, source_target_pairs={{0,6},{1,7},{2,4},{3,5},{4,2},{5,3},{6,0},{7,1},{8,14},{9,15},{10,... | collective-permute-start | bytes 196616 | tf_op jit(solution)/shard_map/ppermute | solution.py:219
  60.9 10.1 %collective-permute-start.29 = (bf16[32,1024]{1,0:T(8,128)(2,1)S(1)}, bf16[32,1024]{1,0:T(8,128)(2,1)S(1)}, u32[]{:S(2)}, u32[]{:S(2)}) collective-permute-start(bf16[32,1024]{1,0:T(8,128)(2,1)S(1)} %get-tuple-element.69), channel_id=1, source_target_pairs={{0,12},{1,13},{2,14},{3,15},{4,8},{5,9},{6,10},{7,11},{8,4},{9,5},... | collective-permute-start | bytes 196616 | tf_op jit(solution)/shard_map/ppermute | solution.py:219
  63.0 8.0 %collective-permute-start.30 = (bf16[32,1024]{1,0:T(8,128)(2,1)S(1)}, bf16[32,1024]{1,0:T(8,128)(2,1)S(1)}, u32[]{:S(2)}, u32[]{:S(2)}) collective-permute-start(bf16[32,1024]{1,0:T(8,128)(2,1)S(1)} %get-tuple-element.70), channel_id=1, source_target_pairs={{0,4},{1,5},{2,6},{3,7},{4,0},{5,1},{6,2},{7,3},{8,12},{9,13},{10,... | collective-permute-start | bytes 196616 | tf_op jit(solution)/shard_map/ppermute | solution.py:219
  63.9 9.1 %collective-permute-start.31 = (bf16[32,1024]{1,0:T(8,128)(2,1)S(1)}, bf16[32,1024]{1,0:T(8,128)(2,1)S(1)}, u32[]{:S(2)}, u32[]{:S(2)}) collective-permute-start(bf16[32,1024]{1,0:T(8,128)(2,1)S(1)} %get-tuple-element.71), channel_id=1, source_target_pairs={{0,10},{1,11},{2,8},{3,9},{4,14},{5,15},{6,12},{7,13},{8,2},{9,3},... | collective-permute-start | bytes 196616 | tf_op jit(solution)/shard_map/ppermute | solution.py:219
  66.5 7.3 %collective-permute-start.32 = (bf16[32,1024]{1,0:T(8,128)(2,1)S(1)}, bf16[32,1024]{1,0:T(8,128)(2,1)S(1)}, u32[]{:S(2)}, u32[]{:S(2)}) collective-permute-start(bf16[32,1024]{1,0:T(8,128)(2,1)S(1)} %get-tuple-element.72), channel_id=1, source_target_pairs={{0,8},{1,9},{2,10},{3,11},{4,12},{5,13},{6,14},{7,15},{8,0},{9,1},... | collective-permute-start | bytes 196616 | tf_op jit(solution)/shard_map/ppermute | solution.py:219
  68.4 5.4 %collective-permute-start.33 = (bf16[32,1024]{1,0:T(8,128)(2,1)S(1)}, bf16[32,1024]{1,0:T(8,128)(2,1)S(1)}, u32[]{:S(2)}, u32[]{:S(2)}) collective-permute-start(bf16[32,1024]{1,0:T(8,128)(2,1)S(1)} %get-tuple-element.64._), channel_id=1, source_target_pairs={{0,2},{1,3},{2,0},{3,1},{4,6},{5,7},{6,4},{7,5},{8,10},{9,11},{10,... | collective-permute-start | bytes 196616 | tf_op jit(solution)/shard_map/ppermute | solution.py:219
  (13 other events, 95.1 us)

commit v12 on v11

--- a/solution.py
+++ b/solution.py
@@ -96,12 +96,12 @@
         out[...] = array_ref[at]
 
 
-def near_kernel(*refs):
-    *blocks, held_ref, marks_ref = refs
-    for at, ref in enumerate(blocks):
-        block = ref[...]
-        held_ref[at] = block
-        marks_ref[at] = block[block.shape[0] - ID_ROWS :, :]
+def marks_kernel(id_ref, storage_ref, *refs):
+    *blocks, marks_ref = refs
+    mark = jnp.full((ID_ROWS, LANES), storage_ref[id_ref[0]].astype(F32), F32).astype(BF16)
+    marks_ref[0] = mark
+    for at, block in enumerate(blocks):
+        marks_ref[at + 1] = block[block.shape[0] - ID_ROWS :, :]
 
 
 def pick(held, at, here, rows):
@@ -133,11 +133,13 @@
             out[:, b * LANES : (b + 1) * LANES] = pick(held, (slot // 2) ^ p, slot % 2 == c, rows)
 
 
-def inverse_kernel(own_a, own_b, other_a, other_b, tile_of):
+def inverse_kernel(m, own_a, own_b, other_a, other_b, plan_ref, tile_of):
     p, c = position()
     for near, far, core in ((own_a, own_b, c), (other_a, other_b, 1 - c)):
         for k, slot in enumerate(slots_of(near) + slots_of(far)):
             tile_of[slot] = 2 * (p ^ k) + core
+    for i, k in enumerate(offsets(m)):
+        plan_ref[i] = jnp.full(plan_ref.shape[1:], tile_of[2 * (p ^ k) + c], jnp.int32)
 
 
 def touch_kernel(after, array, token_ref):
@@ -176,11 +178,11 @@
         ).astype(BF16)
 
 
-def collect_kernel(m, tile_of, *refs):
+def collect_kernel(m, plan_ref, *refs):
     held, outs = refs[:4], refs[4:]
     p, c = position()
-    for out, k in zip(outs, offsets(m)):
-        tile = tile_of[2 * (p ^ k) + c]
+    tiles = [plan_ref[i][0, 0] for i in range(m)]
+    for out, tile in zip(outs, tiles):
         out[...] = pick(held, rank((tile // 2) ^ p, m), tile % 2 == c, slice(None))
 
 
@@ -261,11 +263,11 @@
     handed = call(split_kernel, [flat] * (h // 2), [VMEM], [VMEM] * (h // 2))(first)
     far = [to_chip(h, near[0])] + [to_chip(k + 1, block) for k, block in enumerate(handed)]
     far += [to_chip(h, block) for block in near[h // 2 + 1 :]]
-    near, marks = call(
-        near_kernel, [bf16(h, *flat.shape), bf16(h, ID_ROWS, LANES)], [VMEM] * h, [VMEM] * 2
-    )(*near)
+    marks = call(
+        marks_kernel, bf16(h, ID_ROWS, LANES), [SMEM] * 2 + [VMEM] * (h - 1), VMEM
+    )(adapter_per_tile, adapter_storage_slot, *near[1:])
     marks = [to_device(x, 0, marks) for x in range(1, groups)]
-    held = with_other_core(near, stack(far, *marks))
+    held = with_other_core(stack(near), stack(far, *marks))
     factors = call(
         functools.partial(deliver_kernel, groups),
         [bf16(2 * r, w)] * len(ways),
@@ -278,7 +280,13 @@
     factors = [factors[0]] + [
         to_device(x, k, block) for (x, k), block in zip(ways[1:], factors[1:])
     ]
-    tile_of = call(inverse_kernel, jax.ShapeDtypeStruct((n,), jnp.int32), [VMEM] * 4, SMEM)(*held)
+    plan = call(
+        functools.partial(inverse_kernel, m),
+        jax.ShapeDtypeStruct((m, 8, LANES), jnp.int32),
+        [VMEM] * 4,
+        VMEM,
+        scratch_shapes=[pltpu.SMEM((n,), jnp.int32)],
+    )(*held)
 
     wide = bf16(2 * r, d // m)
     low, *parts = call(
@@ -288,8 +296,8 @@
         [VMEM] * (m + 1),
     )(token, acts, cotangent, *factors)
     parts = exchange(parts)
-    owned = call(functools.partial(collect_kernel, m), [wide] * m, [SMEM] + [VMEM] * 4, [VMEM] * m)(
-        tile_of, *with_other_core(stack(parts[:h]), stack(parts[h:]))
+    owned = call(functools.partial(collect_kernel, m), [wide] * m, [VMEM] * 5, [VMEM] * m)(
+        plan, *with_other_core(stack(parts[:h]), stack(parts[h:]))
     )
     grad_x = call(
         functools.partial(inputs_kernel, m, groups),

time: 74.9 us -> 74.6 us (level)
    ppermute x8, waiting for transfers between devices: 6.69 us -> 5.7 us  [to_device(): return lax.ppermute(block, ('group', 'fsdp'), pairs)]
    unnamed x6 -> x8, local copies, waits for them, and re-layouts: 0.89 us -> 1.54 us
where the time goes in v12:
time: 74.6 us; the launch traced here: 74.4 us
  starting transfers between devices  44.7 us (60%)
  waiting for transfers between devices  18.2 us (24%)
  Pallas kernels  8.38 us (11%)
  between operations  1.62 us (2%)
  local copies, waits for them, and re-layouts  1.54 us (2%)
    ppermute x22, starting transfers between devices, to_chip(): return lax.ppermute(block, 'fsdp', pairs)  33.4 us
    ppermute x8, starting transfers between devices, to_device(): return lax.ppermute(block, ('group', 'fsdp'), pairs)  11 us
    ppermute x22, waiting for transfers between devices, to_chip(): return lax.ppermute(block, 'fsdp', pairs)  9.5 us
    ppermute x8, waiting for transfers between devices, to_device(): return lax.ppermute(block, ('group', 'fsdp'), pairs)  5.7 us
    ppermute x4, waiting for transfers between devices, with_other_core(): lax.ppermute(half, 'fsdp', [(f, f ^ 1) for f in range(n)])  2.96 us
    pallas_call x1, Pallas kernels, shards(): call(functools.partial(pack_kernel, groups, h), [bf16(h // 2, *flat.shape...  2.37 us
    pallas_call x1, Pallas kernels, shards(): call(functools.partial(inputs_kernel, m, groups), bf16(*acts.shape), [VME...  2.05 us
    pallas_call x1, Pallas kernels, shards(): call(functools.partial(grads_kernel, m, groups), [bf16(r, acts.shape[0])]...  1.91 us
  transfers between devices with their start and end apart: 34, of which 13 were waited for; matrix products, arithmetic and copies ran while one was open for 0% of the time, Pallas kernels for 4%

profile of v12, /device:TPU:0, one launch (start us, length us, event | category | flops | bytes accessed | tf_op | source)
XLA Modules:
  0.0 74.4 jit_solution(14862585065227271384)
XLA Ops:
  1.4 2.4 %shard_map.85 = (bf16[2,272,128]{2,1,0:T(8,128)(2,1)}, bf16[272,128]{1,0:T(8,128)(2,1)}, bf16[272,128]{1,0:T(8,128)(2,1)}, bf16[272,128]{1,0:T(8,128)(2,1)}, bf16[272,128]{1,0:T(8,128)(2,1)}) custom-call(s32[1]{0:T(128)S(6)} %copy.9.id_ref, s32[16]{0:T(128)} %storage_ref.3, bf16[1,16,8192]{2,1,0:T(8,128)(2,1)} %down_hbm.1, bf16[1,16,8192]{2,1,0:T(8,128)(2,1)} %up_hbm.1), custom_call_target="tpu_custom_call" | custom-call | tf_op jit(solution)/shard_map/pallas_call | solution.py:247
  3.8 4.1 %collective-permute-start.4 = (bf16[2,272,128]{2,1,0:T(8,128)(2,1)}, bf16[2,272,128]{2,1,0:T(8,128)(2,1)S(1)}, u32[]{:S(2)}, u32[]{:S(2)}) collective-permute-start(bf16[2,272,128]{2,1,0:T(8,128)(2,1)} %get-tuple-element.41), channel_id=1, source_target_pairs={{0,8},{1,9},{2,10},{3,11},{4,12},{5,13},{6,14},{7,15},{8,0},{9,1},... | collective-permute-start | bytes 417800 | tf_op jit(solution)/shard_map/ppermute | solution.py:221
  7.9 2.5 %collective-permute-start.2 = (bf16[272,128]{1,0:T(8,128)(2,1)}, bf16[272,128]{1,0:T(8,128)(2,1)S(1)}, u32[]{:S(2)}, u32[]{:S(2)}) collective-permute-start(bf16[272,128]{1,0:T(8,128)(2,1)} %get-tuple-element.40), channel_id=1, source_target_pairs={{0,6},{1,7},{2,4},{3,5},{4,2},{5,3},{6,0},{7,1},{8,14},{9,15},{10,... | collective-permute-start | bytes 208904 | tf_op jit(solution)/shard_map/ppermute | solution.py:221
  11.5 2.4 %collective-permute-done.2.refs_3_.refs_2_ = bf16[272,128]{1,0:T(8,128)(2,1)S(1)} collective-permute-done((bf16[272,128]{1,0:T(8,128)(2,1)}, bf16[272,128]{1,0:T(8,128)(2,1)S(1)}, u32[]{:S(2)}, u32[]{:S(2)}) %collective-permute-start.2) | collective-permute-done | bytes 69664 | tf_op jit(solution)/shard_map/ppermute | solution.py:221
  13.9 3.1 %collective-permute-start.7 = (bf16[272,128]{1,0:T(8,128)(2,1)S(1)}, bf16[272,128]{1,0:T(8,128)(2,1)S(1)}, u32[]{:S(2)}, u32[]{:S(2)}) collective-permute-start(bf16[272,128]{1,0:T(8,128)(2,1)S(1)} %collective-permute-done.2.refs_3_.refs_2_), channel_id=1, source_target_pairs={{0,8},{1,9},{2,10},{3,11},{4,12},{5,13},{6,14},{7,15},{8,0},{9,1},... | collective-permute-start | bytes 208904 | tf_op jit(solution)/shard_map/ppermute | solution.py:221
  16.9 1.7 %collective-permute-start.5 = (bf16[272,128]{1,0:T(8,128)(2,1)S(1)}, bf16[272,128]{1,0:T(8,128)(2,1)S(1)}, u32[]{:S(2)}, u32[]{:S(2)}) collective-permute-start(bf16[272,128]{1,0:T(8,128)(2,1)S(1)} %get-tuple-element.42), channel_id=1, source_target_pairs={{0,2},{1,3},{2,0},{3,1},{4,6},{5,7},{6,4},{7,5},{8,10},{9,11},{10,... | collective-permute-start | bytes 208904 | tf_op jit(solution)/shard_map/ppermute | solution.py:221
  22.0 1.7 %collective-permute-done.8.refs_4_ = bf16[4,16,128]{2,1,0:T(8,128)(2,1)S(1)} collective-permute-done((bf16[4,16,128]{2,1,0:T(8,128)(2,1)S(1)}, bf16[4,16,128]{2,1,0:T(8,128)(2,1)S(1)}, u32[]{:S(2)}, u32[]{:S(2)}) %collective-permute-start.8) | collective-permute-done | bytes 16416 | tf_op jit(solution)/shard_map/ppermute | solution.py:230
  23.8 1.5 %collective-permute-done.10.other_b.refs_3_ = bf16[4,272,128]{2,1,0:T(8,128)(2,1)S(1)} collective-permute-done((bf16[4,272,128]{2,1,0:T(8,128)(2,1)S(1)}, bf16[4,272,128]{2,1,0:T(8,128)(2,1)S(1)}, u32[]{:S(2)}, u32[]{:S(2)}) %collective-permute-start.10) | collective-permute-done | bytes 278560 | tf_op jit(solution)/shard_map/ppermute | solution.py:236
  25.7 2.8 %collective-permute-start.11 = (bf16[32,1024]{1,0:T(8,128)(2,1)S(1)}, bf16[32,1024]{1,0:T(8,128)(2,1)S(1)}, u32[]{:S(2)}, u32[]{:S(2)}) collective-permute-start(bf16[32,1024]{1,0:T(8,128)(2,1)S(1)} %get-tuple-element.46), channel_id=1, source_target_pairs={{0,22},{1,23},{2,20},{3,21},{4,18},{5,19},{6,16},{7,17},{8,30},{9,... | collective-permute-start | bytes 196616 | tf_op jit(solution)/shard_map/ppermute | solution.py:230
  30.2 2.7 %collective-permute-start.14 = (bf16[32,1024]{1,0:T(8,128)(2,1)S(1)}, bf16[32,1024]{1,0:T(8,128)(2,1)S(1)}, u32[]{:S(2)}, u32[]{:S(2)}) collective-permute-start(bf16[32,1024]{1,0:T(8,128)(2,1)S(1)} %get-tuple-element.49), channel_id=1, source_target_pairs={{0,20},{1,21},{2,22},{3,23},{4,16},{5,17},{6,18},{7,19},{8,28},{9,... | collective-permute-start | bytes 196616 | tf_op jit(solution)/shard_map/ppermute | solution.py:230
  35.6 1.5 %collective-permute-done.15.refs_5_ = bf16[32,1024]{1,0:T(8,128)(2,1)S(1)} collective-permute-done((bf16[32,1024]{1,0:T(8,128)(2,1)S(1)}, bf16[32,1024]{1,0:T(8,128)(2,1)S(1)}, u32[]{:S(2)}, u32[]{:S(2)}) %collective-permute-start.15) | collective-permute-done | bytes 65568 | tf_op jit(solution)/shard_map/ppermute | solution.py:230
  39.6 1.9 %shard_map.93 = (bf16[16,128]{1,0:T(8,128)(2,1)S(1)}, bf16[32,1024]{1,0:T(8,128)(2,1)S(1)}, bf16[32,1024]{1,0:T(8,128)(2,1)S(1)}, bf16[32,1024]{1,0:T(8,128)(2,1...) custom-call(f32[8,128]{1,0:T(8,128)S(1)} %shard_map.92._, ...), custom_call_target="tpu_custom_call" | custom-call | tf_op jit(solution)/shard_map/pallas_call | solution.py:292
  41.5 2.9 %collective-permute-start.18 = (bf16[32,1024]{1,0:T(8,128)(2,1)S(1)}, bf16[32,1024]{1,0:T(8,128)(2,1)S(1)}, u32[]{:S(2)}, u32[]{:S(2)}) collective-permute-start(bf16[32,1024]{1,0:T(8,128)(2,1)S(1)} %get-tuple-element.53), channel_id=1, source_target_pairs={{0,14},{1,15},{2,12},{3,13},{4,10},{5,11},{6,8},{7,9},{8,6},{9,7},... | collective-permute-start | bytes 196616 | tf_op jit(solution)/shard_map/ppermute | solution.py:221
  44.4 1.7 %collective-permute-start.19 = (bf16[32,1024]{1,0:T(8,128)(2,1)S(1)}, bf16[32,1024]{1,0:T(8,128)(2,1)S(1)}, u32[]{:S(2)}, u32[]{:S(2)}) collective-permute-start(bf16[32,1024]{1,0:T(8,128)(2,1)S(1)} %get-tuple-element.54), channel_id=1, source_target_pairs={{0,6},{1,7},{2,4},{3,5},{4,2},{5,3},{6,0},{7,1},{8,14},{9,15},{10,... | collective-permute-start | bytes 196616 | tf_op jit(solution)/shard_map/ppermute | solution.py:221
  47.4 2.4 %collective-permute-start.22 = (bf16[32,1024]{1,0:T(8,128)(2,1)S(1)}, bf16[32,1024]{1,0:T(8,128)(2,1)S(1)}, u32[]{:S(2)}, u32[]{:S(2)}) collective-permute-start(bf16[32,1024]{1,0:T(8,128)(2,1)S(1)} %get-tuple-element.57), channel_id=1, source_target_pairs={{0,10},{1,11},{2,8},{3,9},{4,14},{5,15},{6,12},{7,13},{8,2},{9,3},... | collective-permute-start | bytes 196616 | tf_op jit(solution)/shard_map/ppermute | solution.py:221
  50.5 1.5 %collective-permute-start.24 = (bf16[32,1024]{1,0:T(8,128)(2,1)S(1)}, bf16[32,1024]{1,0:T(8,128)(2,1)S(1)}, u32[]{:S(2)}, u32[]{:S(2)}) collective-permute-start(bf16[32,1024]{1,0:T(8,128)(2,1)S(1)} %get-tuple-element.59), channel_id=1, source_target_pairs={{0,2},{1,3},{2,0},{3,1},{4,6},{5,7},{6,4},{7,5},{8,10},{9,11},{10,... | collective-permute-start | bytes 196616 | tf_op jit(solution)/shard_map/ppermute | solution.py:221
  52.4 2.7 %collective-permute-done.22.refs_1_ = bf16[32,1024]{1,0:T(8,128)(2,1)S(1)} collective-permute-done((bf16[32,1024]{1,0:T(8,128)(2,1)S(1)}, bf16[32,1024]{1,0:T(8,128)(2,1)S(1)}, u32[]{:S(2)}, u32[]{:S(2)}) %collective-permute-start.22) | collective-permute-done | bytes 65568 | tf_op jit(solution)/shard_map/ppermute | solution.py:221
  56.2 1.4 %collective-permute-done.26.refs_3_ = bf16[4,32,1024]{2,1,0:T(8,128)(2,1)S(1)} collective-permute-done((bf16[4,32,1024]{2,1,0:T(8,128)(2,1)S(1)}, bf16[4,32,1024]{2,1,0:T(8,128)(2,1)S(1)}, u32[]{:S(2)}, u32[]{:S(2)}) %collective-permute-start.26) | collective-permute-done | bytes 262176 | tf_op jit(solution)/shard_map/ppermute | solution.py:236
  57.8 2.9 %collective-permute-start.27 = (bf16[32,1024]{1,0:T(8,128)(2,1)S(1)}, bf16[32,1024]{1,0:T(8,128)(2,1)S(1)}, u32[]{:S(2)}, u32[]{:S(2)}) collective-permute-start(bf16[32,1024]{1,0:T(8,128)(2,1)S(1)} %get-tuple-element.63), channel_id=1, source_target_pairs={{0,14},{1,15},{2,12},{3,13},{4,10},{5,11},{6,8},{7,9},{8,6},{9,7},... | collective-permute-start | bytes 196616 | tf_op jit(solution)/shard_map/ppermute | solution.py:221
  60.7 2.1 %collective-permute-start.29 = (bf16[32,1024]{1,0:T(8,128)(2,1)S(1)}, bf16[32,1024]{1,0:T(8,128)(2,1)S(1)}, u32[]{:S(2)}, u32[]{:S(2)}) collective-permute-start(bf16[32,1024]{1,0:T(8,128)(2,1)S(1)} %get-tuple-element.65), channel_id=1, source_target_pairs={{0,12},{1,13},{2,14},{3,15},{4,8},{5,9},{6,10},{7,11},{8,4},{9,5},... | collective-permute-start | bytes 196616 | tf_op jit(solution)/shard_map/ppermute | solution.py:221
  63.7 2.6 %collective-permute-start.31 = (bf16[32,1024]{1,0:T(8,128)(2,1)S(1)}, bf16[32,1024]{1,0:T(8,128)(2,1)S(1)}, u32[]{:S(2)}, u32[]{:S(2)}) collective-permute-start(bf16[32,1024]{1,0:T(8,128)(2,1)S(1)} %get-tuple-element.67), channel_id=1, source_target_pairs={{0,10},{1,11},{2,8},{3,9},{4,14},{5,15},{6,12},{7,13},{8,2},{9,3},... | collective-permute-start | bytes 196616 | tf_op jit(solution)/shard_map/ppermute | solution.py:221
  66.3 1.5 %collective-permute-start.32 = (bf16[32,1024]{1,0:T(8,128)(2,1)S(1)}, bf16[32,1024]{1,0:T(8,128)(2,1)S(1)}, u32[]{:S(2)}, u32[]{:S(2)}) collective-permute-start(bf16[32,1024]{1,0:T(8,128)(2,1)S(1)} %get-tuple-element.68), channel_id=1, source_target_pairs={{0,8},{1,9},{2,10},{3,11},{4,12},{5,13},{6,14},{7,15},{8,0},{9,1},... | collective-permute-start | bytes 196616 | tf_op jit(solution)/shard_map/ppermute | solution.py:221
  68.7 2.0 %shard_map.97 = bf16[128,8192]{1,0:T(8,128)(2,1)} custom-call(bf16[32,1024]{1,0:T(8,128)(2,1)S(1)} %get-tuple-element.60._, bf16[16,128]{1,0:T(8,128)(2,1)S(1)} %get-tuple-element.61.low_ref, bf16[32,1024]{1,0:T(8,128)(2,1)S(1)} %get-tuple-element.45.refs_0_, bf16[32,1024]{1,0:T(8,128)(2,1)S(1)} %collective-permute-done.11.refs_1_, ...), custom_call_target="tpu_custom_call" | custom-call | flops 33554432 | bytes 2097152 | tf_op jit(solution)/shard_map/pallas_call | solution.py:302
  70.8 2.0 %collective-permute-done.31.refs_5_ = bf16[32,1024]{1,0:T(8,128)(2,1)S(1)} collective-permute-done((bf16[32,1024]{1,0:T(8,128)(2,1)S(1)}, bf16[32,1024]{1,0:T(8,128)(2,1)S(1)}, u32[]{:S(2)}, u32[]{:S(2)}) %collective-permute-start.31) | collective-permute-done | bytes 65568 | tf_op jit(solution)/shard_map/ppermute | solution.py:221
  (66 shorter events, 18.7 us)
Async XLA Ops:
  3.8 13.1 %collective-permute-start.4 = (bf16[2,272,128]{2,1,0:T(8,128)(2,1)}, bf16[2,272,128]{2,1,0:T(8,128)(2,1)S(1)}, u32[]{:S(2)}, u32[]{:S(2)}) collective-permute-start(bf16[2,272,128]{2,1,0:T(8,128)(2,1)} %get-tuple-element.41), channel_id=1, source_target_pairs={{0,8},{1,9},{2,10},{3,11},{4,12},{5,13},{6,14},{7,15},{8,0},{9,1},... | collective-permute-start | bytes 417800 | tf_op jit(solution)/shard_map/ppermute | solution.py:221
  7.9 5.9 %collective-permute-start.2 = (bf16[272,128]{1,0:T(8,128)(2,1)}, bf16[272,128]{1,0:T(8,128)(2,1)S(1)}, u32[]{:S(2)}, u32[]{:S(2)}) collective-permute-start(bf16[272,128]{1,0:T(8,128)(2,1)} %get-tuple-element.40), channel_id=1, source_target_pairs={{0,6},{1,7},{2,4},{3,5},{4,2},{5,3},{6,0},{7,1},{8,14},{9,15},{10,... | collective-permute-start | bytes 208904 | tf_op jit(solution)/shard_map/ppermute | solution.py:221
  10.4 8.2 %collective-permute-start = (bf16[272,128]{1,0:T(8,128)(2,1)}, bf16[272,128]{1,0:T(8,128)(2,1)S(1)}, u32[]{:S(2)}, u32[]{:S(2)}) collective-permute-start(bf16[272,128]{1,0:T(8,128)(2,1)} %get-tuple-element.38), channel_id=1, source_target_pairs={{0,2},{1,3},{2,0},{3,1},{4,6},{5,7},{6,4},{7,5},{8,10},{9,11},{10,... | collective-permute-start | bytes 208904 | tf_op jit(solution)/shard_map/ppermute | solution.py:221
  11.0 7.7 %collective-permute-start.1 = (bf16[272,128]{1,0:T(8,128)(2,1)}, bf16[272,128]{1,0:T(8,128)(2,1)S(1)}, u32[]{:S(2)}, u32[]{:S(2)}) collective-permute-start(bf16[272,128]{1,0:T(8,128)(2,1)} %get-tuple-element.39), channel_id=1, source_target_pairs={{0,4},{1,5},{2,6},{3,7},{4,0},{5,1},{6,2},{7,3},{8,12},{9,13},{10,... | collective-permute-start | bytes 208904 | tf_op jit(solution)/shard_map/ppermute | solution.py:221
  11.4 10.5 %collective-permute-start.3 = (bf16[272,128]{1,0:T(8,128)(2,1)}, bf16[272,128]{1,0:T(8,128)(2,1)S(1)}, u32[]{:S(2)}, u32[]{:S(2)}) collective-permute-start(bf16[272,128]{1,0:T(8,128)(2,1)} %get-tuple-element.37.refs_0_), channel_id=1, source_target_pairs={{0,8},{1,9},{2,10},{3,11},{4,12},{5,13},{6,14},{7,15},{8,0},{9,1},... | collective-permute-start | bytes 208904 | tf_op jit(solution)/shard_map/ppermute | solution.py:221
  13.9 9.8 %collective-permute-start.7 = (bf16[272,128]{1,0:T(8,128)(2,1)S(1)}, bf16[272,128]{1,0:T(8,128)(2,1)S(1)}, u32[]{:S(2)}, u32[]{:S(2)}) collective-permute-start(bf16[272,128]{1,0:T(8,128)(2,1)S(1)} %collective-permute-done.2.refs_3_.refs_2_), channel_id=1, source_target_pairs={{0,8},{1,9},{2,10},{3,11},{4,12},{5,13},{6,14},{7,15},{8,0},{9,1},... | collective-permute-start | bytes 208904 | tf_op jit(solution)/shard_map/ppermute | solution.py:221
  16.9 6.8 %collective-permute-start.5 = (bf16[272,128]{1,0:T(8,128)(2,1)S(1)}, bf16[272,128]{1,0:T(8,128)(2,1)S(1)}, u32[]{:S(2)}, u32[]{:S(2)}) collective-permute-start(bf16[272,128]{1,0:T(8,128)(2,1)S(1)} %get-tuple-element.42), channel_id=1, source_target_pairs={{0,2},{1,3},{2,0},{3,1},{4,6},{5,7},{6,4},{7,5},{8,10},{9,11},{10,... | collective-permute-start | bytes 208904 | tf_op jit(solution)/shard_map/ppermute | solution.py:221
  25.7 8.2 %collective-permute-start.11 = (bf16[32,1024]{1,0:T(8,128)(2,1)S(1)}, bf16[32,1024]{1,0:T(8,128)(2,1)S(1)}, u32[]{:S(2)}, u32[]{:S(2)}) collective-permute-start(bf16[32,1024]{1,0:T(8,128)(2,1)S(1)} %get-tuple-element.46), channel_id=1, source_target_pairs={{0,22},{1,23},{2,20},{3,21},{4,18},{5,19},{6,16},{7,17},{8,30},{9,... | collective-permute-start | bytes 196616 | tf_op jit(solution)/shard_map/ppermute | solution.py:230
  28.5 6.8 %collective-permute-start.12 = (bf16[32,1024]{1,0:T(8,128)(2,1)S(1)}, bf16[32,1024]{1,0:T(8,128)(2,1)S(1)}, u32[]{:S(2)}, u32[]{:S(2)}) collective-permute-start(bf16[32,1024]{1,0:T(8,128)(2,1)S(1)} %get-tuple-element.47), channel_id=1, source_target_pairs={{0,6},{1,7},{2,4},{3,5},{4,2},{5,3},{6,0},{7,1},{8,14},{9,15},{10,... | collective-permute-start | bytes 196616 | tf_op jit(solution)/shard_map/ppermute | solution.py:230
  29.1 6.5 %collective-permute-start.13 = (bf16[32,1024]{1,0:T(8,128)(2,1)S(1)}, bf16[32,1024]{1,0:T(8,128)(2,1)S(1)}, u32[]{:S(2)}, u32[]{:S(2)}) collective-permute-start(bf16[32,1024]{1,0:T(8,128)(2,1)S(1)} %get-tuple-element.48), channel_id=1, source_target_pairs={{0,18},{1,19},{2,16},{3,17},{4,22},{5,23},{6,20},{7,21},{8,26},{9,... | collective-permute-start | bytes 196616 | tf_op jit(solution)/shard_map/ppermute | solution.py:230
  30.2 5.4 %collective-permute-start.14 = (bf16[32,1024]{1,0:T(8,128)(2,1)S(1)}, bf16[32,1024]{1,0:T(8,128)(2,1)S(1)}, u32[]{:S(2)}, u32[]{:S(2)}) collective-permute-start(bf16[32,1024]{1,0:T(8,128)(2,1)S(1)} %get-tuple-element.49), channel_id=1, source_target_pairs={{0,20},{1,21},{2,22},{3,23},{4,16},{5,17},{6,18},{7,19},{8,28},{9,... | collective-permute-start | bytes 196616 | tf_op jit(solution)/shard_map/ppermute | solution.py:230
  41.5 8.3 %collective-permute-start.18 = (bf16[32,1024]{1,0:T(8,128)(2,1)S(1)}, bf16[32,1024]{1,0:T(8,128)(2,1)S(1)}, u32[]{:S(2)}, u32[]{:S(2)}) collective-permute-start(bf16[32,1024]{1,0:T(8,128)(2,1)S(1)} %get-tuple-element.53), channel_id=1, source_target_pairs={{0,14},{1,15},{2,12},{3,13},{4,10},{5,11},{6,8},{7,9},{8,6},{9,7},... | collective-permute-start | bytes 196616 | tf_op jit(solution)/shard_map/ppermute | solution.py:221
  44.4 6.1 %collective-permute-start.19 = (bf16[32,1024]{1,0:T(8,128)(2,1)S(1)}, bf16[32,1024]{1,0:T(8,128)(2,1)S(1)}, u32[]{:S(2)}, u32[]{:S(2)}) collective-permute-start(bf16[32,1024]{1,0:T(8,128)(2,1)S(1)} %get-tuple-element.54), channel_id=1, source_target_pairs={{0,6},{1,7},{2,4},{3,5},{4,2},{5,3},{6,0},{7,1},{8,14},{9,15},{10,... | collective-permute-start | bytes 196616 | tf_op jit(solution)/shard_map/ppermute | solution.py:221
  46.1 6.2 %collective-permute-start.20 = (bf16[32,1024]{1,0:T(8,128)(2,1)S(1)}, bf16[32,1024]{1,0:T(8,128)(2,1)S(1)}, u32[]{:S(2)}, u32[]{:S(2)}) collective-permute-start(bf16[32,1024]{1,0:T(8,128)(2,1)S(1)} %get-tuple-element.55), channel_id=1, source_target_pairs={{0,12},{1,13},{2,14},{3,15},{4,8},{5,9},{6,10},{7,11},{8,4},{9,5},... | collective-permute-start | bytes 196616 | tf_op jit(solution)/shard_map/ppermute | solution.py:221
  46.1 6.3 %collective-permute-start.21 = (bf16[32,1024]{1,0:T(8,128)(2,1)S(1)}, bf16[32,1024]{1,0:T(8,128)(2,1)S(1)}, u32[]{:S(2)}, u32[]{:S(2)}) collective-permute-start(bf16[32,1024]{1,0:T(8,128)(2,1)S(1)} %get-tuple-element.56), channel_id=1, source_target_pairs={{0,4},{1,5},{2,6},{3,7},{4,0},{5,1},{6,2},{7,3},{8,12},{9,13},{10,... | collective-permute-start | bytes 196616 | tf_op jit(solution)/shard_map/ppermute | solution.py:221
  47.4 7.7 %collective-permute-start.22 = (bf16[32,1024]{1,0:T(8,128)(2,1)S(1)}, bf16[32,1024]{1,0:T(8,128)(2,1)S(1)}, u32[]{:S(2)}, u32[]{:S(2)}) collective-permute-start(bf16[32,1024]{1,0:T(8,128)(2,1)S(1)} %get-tuple-element.57), channel_id=1, source_target_pairs={{0,10},{1,11},{2,8},{3,9},{4,14},{5,15},{6,12},{7,13},{8,2},{9,3},... | collective-permute-start | bytes 196616 | tf_op jit(solution)/shard_map/ppermute | solution.py:221
  49.8 6.2 %collective-permute-start.23 = (bf16[32,1024]{1,0:T(8,128)(2,1)S(1)}, bf16[32,1024]{1,0:T(8,128)(2,1)S(1)}, u32[]{:S(2)}, u32[]{:S(2)}) collective-permute-start(bf16[32,1024]{1,0:T(8,128)(2,1)S(1)} %get-tuple-element.58), channel_id=1, source_target_pairs={{0,8},{1,9},{2,10},{3,11},{4,12},{5,13},{6,14},{7,15},{8,0},{9,1},... | collective-permute-start | bytes 196616 | tf_op jit(solution)/shard_map/ppermute | solution.py:221
  50.5 5.5 %collective-permute-start.24 = (bf16[32,1024]{1,0:T(8,128)(2,1)S(1)}, bf16[32,1024]{1,0:T(8,128)(2,1)S(1)}, u32[]{:S(2)}, u32[]{:S(2)}) collective-permute-start(bf16[32,1024]{1,0:T(8,128)(2,1)S(1)} %get-tuple-element.59), channel_id=1, source_target_pairs={{0,2},{1,3},{2,0},{3,1},{4,6},{5,7},{6,4},{7,5},{8,10},{9,11},{10,... | collective-permute-start | bytes 196616 | tf_op jit(solution)/shard_map/ppermute | solution.py:221
  57.8 8.5 %collective-permute-start.27 = (bf16[32,1024]{1,0:T(8,128)(2,1)S(1)}, bf16[32,1024]{1,0:T(8,128)(2,1)S(1)}, u32[]{:S(2)}, u32[]{:S(2)}) collective-permute-start(bf16[32,1024]{1,0:T(8,128)(2,1)S(1)} %get-tuple-element.63), channel_id=1, source_target_pairs={{0,14},{1,15},{2,12},{3,13},{4,10},{5,11},{6,8},{7,9},{8,6},{9,7},... | collective-permute-start | bytes 196616 | tf_op jit(solution)/shard_map/ppermute | solution.py:221
  60.7 7.5 %collective-permute-start.28 = (bf16[32,1024]{1,0:T(8,128)(2,1)S(1)}, bf16[32,1024]{1,0:T(8,128)(2,1)S(1)}, u32[]{:S(2)}, u32[]{:S(2)}) collective-permute-start(bf16[32,1024]{1,0:T(8,128)(2,1)S(1)} %get-tuple-element.64), channel_id=1, source_target_pairs={{0,6},{1,7},{2,4},{3,5},{4,2},{5,3},{6,0},{7,1},{8,14},{9,15},{10,... | collective-permute-start | bytes 196616 | tf_op jit(solution)/shard_map/ppermute | solution.py:221
  60.7 10.1 %collective-permute-start.29 = (bf16[32,1024]{1,0:T(8,128)(2,1)S(1)}, bf16[32,1024]{1,0:T(8,128)(2,1)S(1)}, u32[]{:S(2)}, u32[]{:S(2)}) collective-permute-start(bf16[32,1024]{1,0:T(8,128)(2,1)S(1)} %get-tuple-element.65), channel_id=1, source_target_pairs={{0,12},{1,13},{2,14},{3,15},{4,8},{5,9},{6,10},{7,11},{8,4},{9,5},... | collective-permute-start | bytes 196616 | tf_op jit(solution)/shard_map/ppermute | solution.py:221
  62.8 8.0 %collective-permute-start.30 = (bf16[32,1024]{1,0:T(8,128)(2,1)S(1)}, bf16[32,1024]{1,0:T(8,128)(2,1)S(1)}, u32[]{:S(2)}, u32[]{:S(2)}) collective-permute-start(bf16[32,1024]{1,0:T(8,128)(2,1)S(1)} %get-tuple-element.66), channel_id=1, source_target_pairs={{0,4},{1,5},{2,6},{3,7},{4,0},{5,1},{6,2},{7,3},{8,12},{9,13},{10,... | collective-permute-start | bytes 196616 | tf_op jit(solution)/shard_map/ppermute | solution.py:221
  63.7 9.1 %collective-permute-start.31 = (bf16[32,1024]{1,0:T(8,128)(2,1)S(1)}, bf16[32,1024]{1,0:T(8,128)(2,1)S(1)}, u32[]{:S(2)}, u32[]{:S(2)}) collective-permute-start(bf16[32,1024]{1,0:T(8,128)(2,1)S(1)} %get-tuple-element.67), channel_id=1, source_target_pairs={{0,10},{1,11},{2,8},{3,9},{4,14},{5,15},{6,12},{7,13},{8,2},{9,3},... | collective-permute-start | bytes 196616 | tf_op jit(solution)/shard_map/ppermute | solution.py:221
  66.3 7.3 %collective-permute-start.32 = (bf16[32,1024]{1,0:T(8,128)(2,1)S(1)}, bf16[32,1024]{1,0:T(8,128)(2,1)S(1)}, u32[]{:S(2)}, u32[]{:S(2)}) collective-permute-start(bf16[32,1024]{1,0:T(8,128)(2,1)S(1)} %get-tuple-element.68), channel_id=1, source_target_pairs={{0,8},{1,9},{2,10},{3,11},{4,12},{5,13},{6,14},{7,15},{8,0},{9,1},... | collective-permute-start | bytes 196616 | tf_op jit(solution)/shard_map/ppermute | solution.py:221
  (14 other events, 92.2 us)

commit v13 on v12

--- a/solution.py
+++ b/solution.py
@@ -91,17 +91,19 @@
         held_ref[at] = ref[...]
 
 
-def split_kernel(array_ref, *outs):
+def split_kernel(_, array_ref, *outs):
     for at, out in enumerate(outs):
         out[...] = array_ref[at]
 
 
-def marks_kernel(id_ref, storage_ref, *refs):
+def marks_kernel(*refs):
     *blocks, marks_ref = refs
-    mark = jnp.full((ID_ROWS, LANES), storage_ref[id_ref[0]].astype(F32), F32).astype(BF16)
-    marks_ref[0] = mark
     for at, block in enumerate(blocks):
-        marks_ref[at + 1] = block[block.shape[0] - ID_ROWS :, :]
+        marks_ref[at] = block[block.shape[0] - ID_ROWS :, :]
+
+
+def copy_kernel(in_ref, out_ref):
+    out_ref[...] = in_ref[...]
 
 
 def pick(held, at, here, rows):
@@ -260,12 +262,12 @@
     )(adapter_per_tile, adapter_storage_slot, down, up)
     first = to_chip(h, first)
     near = [spread[0]] + [to_chip(k, spread[k]) for k in range(1, h)]
-    handed = call(split_kernel, [flat] * (h // 2), [VMEM], [VMEM] * (h // 2))(first)
+    own = call(copy_kernel, flat, [VMEM], VMEM)(near[0])
+    handed = call(split_kernel, [flat] * (h // 2), [VMEM] * 2, [VMEM] * (h // 2))(own, first)
     far = [to_chip(h, near[0])] + [to_chip(k + 1, block) for k, block in enumerate(handed)]
     far += [to_chip(h, block) for block in near[h // 2 + 1 :]]
-    marks = call(
-        marks_kernel, bf16(h, ID_ROWS, LANES), [SMEM] * 2 + [VMEM] * (h - 1), VMEM
-    )(adapter_per_tile, adapter_storage_slot, *near[1:])
+    near[0] = own
+    marks = call(marks_kernel, bf16(h, ID_ROWS, LANES), [VMEM] * h, VMEM)(*near)
     marks = [to_device(x, 0, marks) for x in range(1, groups)]
     held = with_other_core(stack(near), stack(far, *marks))
     factors = call(

time: 74.6 us -> 73.4 us (0.984)
    unnamed x8 -> x6, local copies, waits for them, and re-layouts: 1.54 us -> 0.93 us
  transfers between devices with their start and end apart: 34 -> 34, of which waited for: 13 -> 16; matrix products, arithmetic and copies ran while one was open for 0% -> 0% of each run, Pallas kernels for 4% -> 3%
where the time goes in v13:
time: 73.4 us; the launch traced here: 73.2 us
  starting transfers between devices  44.4 us (60%)
  waiting for transfers between devices  18.4 us (25%)
  Pallas kernels  7.84 us (11%)
  between operations  1.6 us (2%)
  local copies, waits for them, and re-layouts  0.93 us (1%)
    ppermute x22, starting transfers between devices, to_chip(): return lax.ppermute(block, 'fsdp', pairs)  33.3 us
    ppermute x8, starting transfers between devices, to_device(): return lax.ppermute(block, ('group', 'fsdp'), pairs)  10.8 us
    ppermute x22, waiting for transfers between devices, to_chip(): return lax.ppermute(block, 'fsdp', pairs)  9.24 us
    ppermute x8, waiting for transfers between devices, to_device(): return lax.ppermute(block, ('group', 'fsdp'), pairs)  6.2 us
    ppermute x4, waiting for transfers between devices, with_other_core(): lax.ppermute(half, 'fsdp', [(f, f ^ 1) for f in range(n)])  2.96 us
    pallas_call x1, Pallas kernels, shards(): call(functools.partial(pack_kernel, groups, h), [bf16(h // 2, *flat.shape...  2.36 us
    pallas_call x1, Pallas kernels, shards(): call(functools.partial(inputs_kernel, m, groups), bf16(*acts.shape), [VME...  2.04 us
    pallas_call x1, Pallas kernels, shards(): call(functools.partial(grads_kernel, m, groups), [bf16(r, acts.shape[0])]...  1.92 us
  transfers between devices with their start and end apart: 34, of which 16 were waited for; matrix products, arithmetic and copies ran while one was open for 0% of the time, Pallas kernels for 3%

profile of v13, /device:TPU:0, one launch (start us, length us, event | category | flops | bytes accessed | tf_op | source)
XLA Modules:
  0.0 73.2 jit_solution(17843929653037052436)
XLA Ops:
  1.4 2.4 %shard_map.85 = (bf16[2,272,128]{2,1,0:T(8,128)(2,1)}, bf16[272,128]{1,0:T(8,128)(2,1)}, bf16[272,128]{1,0:T(8,128)(2,1)}, bf16[272,128]{1,0:T(8,128)(2,1)}, bf16[272,128]{1,0:T(8,128)(2,1)}) custom-call(s32[1]{0:T(128)S(6)} %copy.9.id_ref, s32[16]{0:T(128)} %storage_ref.1, bf16[1,16,8192]{2,1,0:T(8,128)(2,1)} %down_hbm.1, bf16[1,16,8192]{2,1,0:T(8,128)(2,1)} %up_hbm.1), custom_call_target="tpu_custom_call" | custom-call | tf_op jit(solution)/shard_map/pallas_call | solution.py:249
  3.8 4.1 %collective-permute-start.4 = (bf16[2,272,128]{2,1,0:T(8,128)(2,1)}, bf16[2,272,128]{2,1,0:T(8,128)(2,1)S(1)}, u32[]{:S(2)}, u32[]{:S(2)}) collective-permute-start(bf16[2,272,128]{2,1,0:T(8,128)(2,1)} %get-tuple-element.41), channel_id=1, source_target_pairs={{0,8},{1,9},{2,10},{3,11},{4,12},{5,13},{6,14},{7,15},{8,0},{9,1},... | collective-permute-start | bytes 417800 | tf_op jit(solution)/shard_map/ppermute | solution.py:223
  7.9 2.5 %collective-permute-start.2 = (bf16[272,128]{1,0:T(8,128)(2,1)}, bf16[272,128]{1,0:T(8,128)(2,1)S(1)}, u32[]{:S(2)}, u32[]{:S(2)}) collective-permute-start(bf16[272,128]{1,0:T(8,128)(2,1)} %get-tuple-element.40), channel_id=1, source_target_pairs={{0,6},{1,7},{2,4},{3,5},{4,2},{5,3},{6,0},{7,1},{8,14},{9,15},{10,... | collective-permute-start | bytes 208904 | tf_op jit(solution)/shard_map/ppermute | solution.py:223
  12.4 1.4 %collective-permute-done.2.refs_3_ = bf16[272,128]{1,0:T(8,128)(2,1)S(1)} collective-permute-done((bf16[272,128]{1,0:T(8,128)(2,1)}, bf16[272,128]{1,0:T(8,128)(2,1)S(1)}, u32[]{:S(2)}, u32[]{:S(2)}) %collective-permute-start.2) | collective-permute-done | bytes 69664 | tf_op jit(solution)/shard_map/ppermute | solution.py:223
  13.8 3.1 %collective-permute-start.7 = (bf16[272,128]{1,0:T(8,128)(2,1)S(1)}, bf16[272,128]{1,0:T(8,128)(2,1)S(1)}, u32[]{:S(2)}, u32[]{:S(2)}) collective-permute-start(bf16[272,128]{1,0:T(8,128)(2,1)S(1)} %collective-permute-done.2.refs_3_), channel_id=1, source_target_pairs={{0,8},{1,9},{2,10},{3,11},{4,12},{5,13},{6,14},{7,15},{8,0},{9,1},... | collective-permute-start | bytes 208904 | tf_op jit(solution)/shard_map/ppermute | solution.py:223
  16.9 1.7 %collective-permute-start.5 = (bf16[272,128]{1,0:T(8,128)(2,1)S(1)}, bf16[272,128]{1,0:T(8,128)(2,1)S(1)}, u32[]{:S(2)}, u32[]{:S(2)}) collective-permute-start(bf16[272,128]{1,0:T(8,128)(2,1)S(1)} %get-tuple-element.42), channel_id=1, source_target_pairs={{0,2},{1,3},{2,0},{3,1},{4,6},{5,7},{6,4},{7,5},{8,10},{9,11},{10,... | collective-permute-start | bytes 208904 | tf_op jit(solution)/shard_map/ppermute | solution.py:223
  20.2 2.3 %collective-permute-done.8.refs_4_ = bf16[4,16,128]{2,1,0:T(8,128)(2,1)S(1)} collective-permute-done((bf16[4,16,128]{2,1,0:T(8,128)(2,1)S(1)}, bf16[4,16,128]{2,1,0:T(8,128)(2,1)S(1)}, u32[]{:S(2)}, u32[]{:S(2)}) %collective-permute-start.8) | collective-permute-done | bytes 16416 | tf_op jit(solution)/shard_map/ppermute | solution.py:232
  23.1 1.5 %collective-permute-done.10.other_b.refs_3_ = bf16[4,272,128]{2,1,0:T(8,128)(2,1)S(1)} collective-permute-done((bf16[4,272,128]{2,1,0:T(8,128)(2,1)S(1)}, bf16[4,272,128]{2,1,0:T(8,128)(2,1)S(1)}, u32[]{:S(2)}, u32[]{:S(2)}) %collective-permute-start.10) | collective-permute-done | bytes 278560 | tf_op jit(solution)/shard_map/ppermute | solution.py:238
  24.9 2.3 %collective-permute-start.11 = (bf16[32,1024]{1,0:T(8,128)(2,1)S(1)}, bf16[32,1024]{1,0:T(8,128)(2,1)S(1)}, u32[]{:S(2)}, u32[]{:S(2)}) collective-permute-start(bf16[32,1024]{1,0:T(8,128)(2,1)S(1)} %get-tuple-element.46), channel_id=1, source_target_pairs={{0,22},{1,23},{2,20},{3,21},{4,18},{5,19},{6,16},{7,17},{8,30},{9,... | collective-permute-start | bytes 196616 | tf_op jit(solution)/shard_map/ppermute | solution.py:232
  28.2 1.7 %collective-permute-start.13 = (bf16[32,1024]{1,0:T(8,128)(2,1)S(1)}, bf16[32,1024]{1,0:T(8,128)(2,1)S(1)}, u32[]{:S(2)}, u32[]{:S(2)}) collective-permute-start(bf16[32,1024]{1,0:T(8,128)(2,1)S(1)} %get-tuple-element.48), channel_id=1, source_target_pairs={{0,18},{1,19},{2,16},{3,17},{4,22},{5,23},{6,20},{7,21},{8,26},{9,... | collective-permute-start | bytes 196616 | tf_op jit(solution)/shard_map/ppermute | solution.py:232
  29.9 1.7 %collective-permute-start.14 = (bf16[32,1024]{1,0:T(8,128)(2,1)S(1)}, bf16[32,1024]{1,0:T(8,128)(2,1)S(1)}, u32[]{:S(2)}, u32[]{:S(2)}) collective-permute-start(bf16[32,1024]{1,0:T(8,128)(2,1)S(1)} %get-tuple-element.49), channel_id=1, source_target_pairs={{0,20},{1,21},{2,22},{3,23},{4,16},{5,17},{6,18},{7,19},{8,28},{9,... | collective-permute-start | bytes 196616 | tf_op jit(solution)/shard_map/ppermute | solution.py:232
  38.3 1.9 %shard_map.94 = (bf16[16,128]{1,0:T(8,128)(2,1)S(1)}, bf16[32,1024]{1,0:T(8,128)(2,1)S(1)}, bf16[32,1024]{1,0:T(8,128)(2,1)S(1)}, bf16[32,1024]{1,0:T(8,128)(2,1...) custom-call(f32[8,128]{1,0:T(8,128)S(1)} %shard_map.93._, ...), custom_call_target="tpu_custom_call" | custom-call | tf_op jit(solution)/shard_map/pallas_call | solution.py:294
  40.2 3.2 %collective-permute-start.18 = (bf16[32,1024]{1,0:T(8,128)(2,1)S(1)}, bf16[32,1024]{1,0:T(8,128)(2,1)S(1)}, u32[]{:S(2)}, u32[]{:S(2)}) collective-permute-start(bf16[32,1024]{1,0:T(8,128)(2,1)S(1)} %get-tuple-element.53), channel_id=1, source_target_pairs={{0,14},{1,15},{2,12},{3,13},{4,10},{5,11},{6,8},{7,9},{8,6},{9,7},... | collective-permute-start | bytes 196616 | tf_op jit(solution)/shard_map/ppermute | solution.py:223
  43.4 1.4 %collective-permute-start.19 = (bf16[32,1024]{1,0:T(8,128)(2,1)S(1)}, bf16[32,1024]{1,0:T(8,128)(2,1)S(1)}, u32[]{:S(2)}, u32[]{:S(2)}) collective-permute-start(bf16[32,1024]{1,0:T(8,128)(2,1)S(1)} %get-tuple-element.54), channel_id=1, source_target_pairs={{0,6},{1,7},{2,4},{3,5},{4,2},{5,3},{6,0},{7,1},{8,14},{9,15},{10,... | collective-permute-start | bytes 196616 | tf_op jit(solution)/shard_map/ppermute | solution.py:223
  46.2 2.4 %collective-permute-start.22 = (bf16[32,1024]{1,0:T(8,128)(2,1)S(1)}, bf16[32,1024]{1,0:T(8,128)(2,1)S(1)}, u32[]{:S(2)}, u32[]{:S(2)}) collective-permute-start(bf16[32,1024]{1,0:T(8,128)(2,1)S(1)} %get-tuple-element.57), channel_id=1, source_target_pairs={{0,10},{1,11},{2,8},{3,9},{4,14},{5,15},{6,12},{7,13},{8,2},{9,3},... | collective-permute-start | bytes 196616 | tf_op jit(solution)/shard_map/ppermute | solution.py:223
  49.4 1.4 %collective-permute-start.24 = (bf16[32,1024]{1,0:T(8,128)(2,1)S(1)}, bf16[32,1024]{1,0:T(8,128)(2,1)S(1)}, u32[]{:S(2)}, u32[]{:S(2)}) collective-permute-start(bf16[32,1024]{1,0:T(8,128)(2,1)S(1)} %get-tuple-element.59), channel_id=1, source_target_pairs={{0,2},{1,3},{2,0},{3,1},{4,6},{5,7},{6,4},{7,5},{8,10},{9,11},{10,... | collective-permute-start | bytes 196616 | tf_op jit(solution)/shard_map/ppermute | solution.py:223
  51.2 2.9 %collective-permute-done.22.refs_1_ = bf16[32,1024]{1,0:T(8,128)(2,1)S(1)} collective-permute-done((bf16[32,1024]{1,0:T(8,128)(2,1)S(1)}, bf16[32,1024]{1,0:T(8,128)(2,1)S(1)}, u32[]{:S(2)}, u32[]{:S(2)}) %collective-permute-start.22) | collective-permute-done | bytes 65568 | tf_op jit(solution)/shard_map/ppermute | solution.py:223
  55.1 1.4 %collective-permute-done.26.refs_3_ = bf16[4,32,1024]{2,1,0:T(8,128)(2,1)S(1)} collective-permute-done((bf16[4,32,1024]{2,1,0:T(8,128)(2,1)S(1)}, bf16[4,32,1024]{2,1,0:T(8,128)(2,1)S(1)}, u32[]{:S(2)}, u32[]{:S(2)}) %collective-permute-start.26) | collective-permute-done | bytes 262176 | tf_op jit(solution)/shard_map/ppermute | solution.py:238
  56.7 2.9 %collective-permute-start.27 = (bf16[32,1024]{1,0:T(8,128)(2,1)S(1)}, bf16[32,1024]{1,0:T(8,128)(2,1)S(1)}, u32[]{:S(2)}, u32[]{:S(2)}) collective-permute-start(bf16[32,1024]{1,0:T(8,128)(2,1)S(1)} %get-tuple-element.63), channel_id=1, source_target_pairs={{0,14},{1,15},{2,12},{3,13},{4,10},{5,11},{6,8},{7,9},{8,6},{9,7},... | collective-permute-start | bytes 196616 | tf_op jit(solution)/shard_map/ppermute | solution.py:223
  59.6 2.0 %collective-permute-start.29 = (bf16[32,1024]{1,0:T(8,128)(2,1)S(1)}, bf16[32,1024]{1,0:T(8,128)(2,1)S(1)}, u32[]{:S(2)}, u32[]{:S(2)}) collective-permute-start(bf16[32,1024]{1,0:T(8,128)(2,1)S(1)} %get-tuple-element.65), channel_id=1, source_target_pairs={{0,12},{1,13},{2,14},{3,15},{4,8},{5,9},{6,10},{7,11},{8,4},{9,5},... | collective-permute-start | bytes 196616 | tf_op jit(solution)/shard_map/ppermute | solution.py:223
  62.6 2.4 %collective-permute-start.31 = (bf16[32,1024]{1,0:T(8,128)(2,1)S(1)}, bf16[32,1024]{1,0:T(8,128)(2,1)S(1)}, u32[]{:S(2)}, u32[]{:S(2)}) collective-permute-start(bf16[32,1024]{1,0:T(8,128)(2,1)S(1)} %get-tuple-element.67), channel_id=1, source_target_pairs={{0,10},{1,11},{2,8},{3,9},{4,14},{5,15},{6,12},{7,13},{8,2},{9,3},... | collective-permute-start | bytes 196616 | tf_op jit(solution)/shard_map/ppermute | solution.py:223
  65.0 1.5 %collective-permute-start.32 = (bf16[32,1024]{1,0:T(8,128)(2,1)S(1)}, bf16[32,1024]{1,0:T(8,128)(2,1)S(1)}, u32[]{:S(2)}, u32[]{:S(2)}) collective-permute-start(bf16[32,1024]{1,0:T(8,128)(2,1)S(1)} %get-tuple-element.68), channel_id=1, source_target_pairs={{0,8},{1,9},{2,10},{3,11},{4,12},{5,13},{6,14},{7,15},{8,0},{9,1},... | collective-permute-start | bytes 196616 | tf_op jit(solution)/shard_map/ppermute | solution.py:223
  67.5 2.0 %shard_map.98 = bf16[128,8192]{1,0:T(8,128)(2,1)} custom-call(bf16[32,1024]{1,0:T(8,128)(2,1)S(1)} %get-tuple-element.60._, bf16[16,128]{1,0:T(8,128)(2,1)S(1)} %get-tuple-element.61.low_ref, bf16[32,1024]{1,0:T(8,128)(2,1)S(1)} %get-tuple-element.45.refs_0_, bf16[32,1024]{1,0:T(8,128)(2,1)S(1)} %collective-permute-done.11.refs_1_, ...), custom_call_target="tpu_custom_call" | custom-call | flops 33554432 | bytes 2097152 | tf_op jit(solution)/shard_map/pallas_call | solution.py:304
  69.6 2.1 %collective-permute-done.31.refs_5_ = bf16[32,1024]{1,0:T(8,128)(2,1)S(1)} collective-permute-done((bf16[32,1024]{1,0:T(8,128)(2,1)S(1)}, bf16[32,1024]{1,0:T(8,128)(2,1)S(1)}, u32[]{:S(2)}, u32[]{:S(2)}) %collective-permute-start.31) | collective-permute-done | bytes 65568 | tf_op jit(solution)/shard_map/ppermute | solution.py:223
  (65 shorter events, 19.1 us)
Async XLA Ops:
  3.8 13.1 %collective-permute-start.4 = (bf16[2,272,128]{2,1,0:T(8,128)(2,1)}, bf16[2,272,128]{2,1,0:T(8,128)(2,1)S(1)}, u32[]{:S(2)}, u32[]{:S(2)}) collective-permute-start(bf16[2,272,128]{2,1,0:T(8,128)(2,1)} %get-tuple-element.41), channel_id=1, source_target_pairs={{0,8},{1,9},{2,10},{3,11},{4,12},{5,13},{6,14},{7,15},{8,0},{9,1},... | collective-permute-start | bytes 417800 | tf_op jit(solution)/shard_map/ppermute | solution.py:223
  7.9 5.9 %collective-permute-start.2 = (bf16[272,128]{1,0:T(8,128)(2,1)}, bf16[272,128]{1,0:T(8,128)(2,1)S(1)}, u32[]{:S(2)}, u32[]{:S(2)}) collective-permute-start(bf16[272,128]{1,0:T(8,128)(2,1)} %get-tuple-element.40), channel_id=1, source_target_pairs={{0,6},{1,7},{2,4},{3,5},{4,2},{5,3},{6,0},{7,1},{8,14},{9,15},{10,... | collective-permute-start | bytes 208904 | tf_op jit(solution)/shard_map/ppermute | solution.py:223
  10.4 8.2 %collective-permute-start = (bf16[272,128]{1,0:T(8,128)(2,1)}, bf16[272,128]{1,0:T(8,128)(2,1)S(1)}, u32[]{:S(2)}, u32[]{:S(2)}) collective-permute-start(bf16[272,128]{1,0:T(8,128)(2,1)} %get-tuple-element.38), channel_id=1, source_target_pairs={{0,2},{1,3},{2,0},{3,1},{4,6},{5,7},{6,4},{7,5},{8,10},{9,11},{10,... | collective-permute-start | bytes 208904 | tf_op jit(solution)/shard_map/ppermute | solution.py:223
  10.9 7.7 %collective-permute-start.1 = (bf16[272,128]{1,0:T(8,128)(2,1)}, bf16[272,128]{1,0:T(8,128)(2,1)S(1)}, u32[]{:S(2)}, u32[]{:S(2)}) collective-permute-start(bf16[272,128]{1,0:T(8,128)(2,1)} %get-tuple-element.39), channel_id=1, source_target_pairs={{0,4},{1,5},{2,6},{3,7},{4,0},{5,1},{6,2},{7,3},{8,12},{9,13},{10,... | collective-permute-start | bytes 208904 | tf_op jit(solution)/shard_map/ppermute | solution.py:223
  11.4 8.7 %collective-permute-start.3 = (bf16[272,128]{1,0:T(8,128)(2,1)}, bf16[272,128]{1,0:T(8,128)(2,1)S(1)}, u32[]{:S(2)}, u32[]{:S(2)}) collective-permute-start(bf16[272,128]{1,0:T(8,128)(2,1)} %get-tuple-element.37.in_ref), channel_id=1, source_target_pairs={{0,8},{1,9},{2,10},{3,11},{4,12},{5,13},{6,14},{7,15},{8,0},{9,1},... | collective-permute-start | bytes 208904 | tf_op jit(solution)/shard_map/ppermute | solution.py:223
  13.8 8.6 %collective-permute-start.7 = (bf16[272,128]{1,0:T(8,128)(2,1)S(1)}, bf16[272,128]{1,0:T(8,128)(2,1)S(1)}, u32[]{:S(2)}, u32[]{:S(2)}) collective-permute-start(bf16[272,128]{1,0:T(8,128)(2,1)S(1)} %collective-permute-done.2.refs_3_), channel_id=1, source_target_pairs={{0,8},{1,9},{2,10},{3,11},{4,12},{5,13},{6,14},{7,15},{8,0},{9,1},... | collective-permute-start | bytes 208904 | tf_op jit(solution)/shard_map/ppermute | solution.py:223
  16.9 5.6 %collective-permute-start.5 = (bf16[272,128]{1,0:T(8,128)(2,1)S(1)}, bf16[272,128]{1,0:T(8,128)(2,1)S(1)}, u32[]{:S(2)}, u32[]{:S(2)}) collective-permute-start(bf16[272,128]{1,0:T(8,128)(2,1)S(1)} %get-tuple-element.42), channel_id=1, source_target_pairs={{0,2},{1,3},{2,0},{3,1},{4,6},{5,7},{6,4},{7,5},{8,10},{9,11},{10,... | collective-permute-start | bytes 208904 | tf_op jit(solution)/shard_map/ppermute | solution.py:223
  24.9 7.8 %collective-permute-start.11 = (bf16[32,1024]{1,0:T(8,128)(2,1)S(1)}, bf16[32,1024]{1,0:T(8,128)(2,1)S(1)}, u32[]{:S(2)}, u32[]{:S(2)}) collective-permute-start(bf16[32,1024]{1,0:T(8,128)(2,1)S(1)} %get-tuple-element.46), channel_id=1, source_target_pairs={{0,22},{1,23},{2,20},{3,21},{4,18},{5,19},{6,16},{7,17},{8,30},{9,... | collective-permute-start | bytes 196616 | tf_op jit(solution)/shard_map/ppermute | solution.py:232
  27.3 6.7 %collective-permute-start.12 = (bf16[32,1024]{1,0:T(8,128)(2,1)S(1)}, bf16[32,1024]{1,0:T(8,128)(2,1)S(1)}, u32[]{:S(2)}, u32[]{:S(2)}) collective-permute-start(bf16[32,1024]{1,0:T(8,128)(2,1)S(1)} %get-tuple-element.47), channel_id=1, source_target_pairs={{0,6},{1,7},{2,4},{3,5},{4,2},{5,3},{6,0},{7,1},{8,14},{9,15},{10,... | collective-permute-start | bytes 196616 | tf_op jit(solution)/shard_map/ppermute | solution.py:232
  28.2 6.1 %collective-permute-start.13 = (bf16[32,1024]{1,0:T(8,128)(2,1)S(1)}, bf16[32,1024]{1,0:T(8,128)(2,1)S(1)}, u32[]{:S(2)}, u32[]{:S(2)}) collective-permute-start(bf16[32,1024]{1,0:T(8,128)(2,1)S(1)} %get-tuple-element.48), channel_id=1, source_target_pairs={{0,18},{1,19},{2,16},{3,17},{4,22},{5,23},{6,20},{7,21},{8,26},{9,... | collective-permute-start | bytes 196616 | tf_op jit(solution)/shard_map/ppermute | solution.py:232
  29.9 5.6 %collective-permute-start.14 = (bf16[32,1024]{1,0:T(8,128)(2,1)S(1)}, bf16[32,1024]{1,0:T(8,128)(2,1)S(1)}, u32[]{:S(2)}, u32[]{:S(2)}) collective-permute-start(bf16[32,1024]{1,0:T(8,128)(2,1)S(1)} %get-tuple-element.49), channel_id=1, source_target_pairs={{0,20},{1,21},{2,22},{3,23},{4,16},{5,17},{6,18},{7,19},{8,28},{9,... | collective-permute-start | bytes 196616 | tf_op jit(solution)/shard_map/ppermute | solution.py:232
  40.2 8.4 %collective-permute-start.18 = (bf16[32,1024]{1,0:T(8,128)(2,1)S(1)}, bf16[32,1024]{1,0:T(8,128)(2,1)S(1)}, u32[]{:S(2)}, u32[]{:S(2)}) collective-permute-start(bf16[32,1024]{1,0:T(8,128)(2,1)S(1)} %get-tuple-element.53), channel_id=1, source_target_pairs={{0,14},{1,15},{2,12},{3,13},{4,10},{5,11},{6,8},{7,9},{8,6},{9,7},... | collective-permute-start | bytes 196616 | tf_op jit(solution)/shard_map/ppermute | solution.py:223
  43.4 6.0 %collective-permute-start.19 = (bf16[32,1024]{1,0:T(8,128)(2,1)S(1)}, bf16[32,1024]{1,0:T(8,128)(2,1)S(1)}, u32[]{:S(2)}, u32[]{:S(2)}) collective-permute-start(bf16[32,1024]{1,0:T(8,128)(2,1)S(1)} %get-tuple-element.54), channel_id=1, source_target_pairs={{0,6},{1,7},{2,4},{3,5},{4,2},{5,3},{6,0},{7,1},{8,14},{9,15},{10,... | collective-permute-start | bytes 196616 | tf_op jit(solution)/shard_map/ppermute | solution.py:223
  44.8 6.2 %collective-permute-start.20 = (bf16[32,1024]{1,0:T(8,128)(2,1)S(1)}, bf16[32,1024]{1,0:T(8,128)(2,1)S(1)}, u32[]{:S(2)}, u32[]{:S(2)}) collective-permute-start(bf16[32,1024]{1,0:T(8,128)(2,1)S(1)} %get-tuple-element.55), channel_id=1, source_target_pairs={{0,12},{1,13},{2,14},{3,15},{4,8},{5,9},{6,10},{7,11},{8,4},{9,5},... | collective-permute-start | bytes 196616 | tf_op jit(solution)/shard_map/ppermute | solution.py:223
  44.8 6.3 %collective-permute-start.21 = (bf16[32,1024]{1,0:T(8,128)(2,1)S(1)}, bf16[32,1024]{1,0:T(8,128)(2,1)S(1)}, u32[]{:S(2)}, u32[]{:S(2)}) collective-permute-start(bf16[32,1024]{1,0:T(8,128)(2,1)S(1)} %get-tuple-element.56), channel_id=1, source_target_pairs={{0,4},{1,5},{2,6},{3,7},{4,0},{5,1},{6,2},{7,3},{8,12},{9,13},{10,... | collective-permute-start | bytes 196616 | tf_op jit(solution)/shard_map/ppermute | solution.py:223
  46.2 7.8 %collective-permute-start.22 = (bf16[32,1024]{1,0:T(8,128)(2,1)S(1)}, bf16[32,1024]{1,0:T(8,128)(2,1)S(1)}, u32[]{:S(2)}, u32[]{:S(2)}) collective-permute-start(bf16[32,1024]{1,0:T(8,128)(2,1)S(1)} %get-tuple-element.57), channel_id=1, source_target_pairs={{0,10},{1,11},{2,8},{3,9},{4,14},{5,15},{6,12},{7,13},{8,2},{9,3},... | collective-permute-start | bytes 196616 | tf_op jit(solution)/shard_map/ppermute | solution.py:223
  48.6 6.3 %collective-permute-start.23 = (bf16[32,1024]{1,0:T(8,128)(2,1)S(1)}, bf16[32,1024]{1,0:T(8,128)(2,1)S(1)}, u32[]{:S(2)}, u32[]{:S(2)}) collective-permute-start(bf16[32,1024]{1,0:T(8,128)(2,1)S(1)} %get-tuple-element.58), channel_id=1, source_target_pairs={{0,8},{1,9},{2,10},{3,11},{4,12},{5,13},{6,14},{7,15},{8,0},{9,1},... | collective-permute-start | bytes 196616 | tf_op jit(solution)/shard_map/ppermute | solution.py:223
  49.4 5.5 %collective-permute-start.24 = (bf16[32,1024]{1,0:T(8,128)(2,1)S(1)}, bf16[32,1024]{1,0:T(8,128)(2,1)S(1)}, u32[]{:S(2)}, u32[]{:S(2)}) collective-permute-start(bf16[32,1024]{1,0:T(8,128)(2,1)S(1)} %get-tuple-element.59), channel_id=1, source_target_pairs={{0,2},{1,3},{2,0},{3,1},{4,6},{5,7},{6,4},{7,5},{8,10},{9,11},{10,... | collective-permute-start | bytes 196616 | tf_op jit(solution)/shard_map/ppermute | solution.py:223
  56.7 8.4 %collective-permute-start.27 = (bf16[32,1024]{1,0:T(8,128)(2,1)S(1)}, bf16[32,1024]{1,0:T(8,128)(2,1)S(1)}, u32[]{:S(2)}, u32[]{:S(2)}) collective-permute-start(bf16[32,1024]{1,0:T(8,128)(2,1)S(1)} %get-tuple-element.63), channel_id=1, source_target_pairs={{0,14},{1,15},{2,12},{3,13},{4,10},{5,11},{6,8},{7,9},{8,6},{9,7},... | collective-permute-start | bytes 196616 | tf_op jit(solution)/shard_map/ppermute | solution.py:223
  59.6 7.4 %collective-permute-start.28 = (bf16[32,1024]{1,0:T(8,128)(2,1)S(1)}, bf16[32,1024]{1,0:T(8,128)(2,1)S(1)}, u32[]{:S(2)}, u32[]{:S(2)}) collective-permute-start(bf16[32,1024]{1,0:T(8,128)(2,1)S(1)} %get-tuple-element.64), channel_id=1, source_target_pairs={{0,6},{1,7},{2,4},{3,5},{4,2},{5,3},{6,0},{7,1},{8,14},{9,15},{10,... | collective-permute-start | bytes 196616 | tf_op jit(solution)/shard_map/ppermute | solution.py:223
  59.6 10.0 %collective-permute-start.29 = (bf16[32,1024]{1,0:T(8,128)(2,1)S(1)}, bf16[32,1024]{1,0:T(8,128)(2,1)S(1)}, u32[]{:S(2)}, u32[]{:S(2)}) collective-permute-start(bf16[32,1024]{1,0:T(8,128)(2,1)S(1)} %get-tuple-element.65), channel_id=1, source_target_pairs={{0,12},{1,13},{2,14},{3,15},{4,8},{5,9},{6,10},{7,11},{8,4},{9,5},... | collective-permute-start | bytes 196616 | tf_op jit(solution)/shard_map/ppermute | solution.py:223
  61.6 8.0 %collective-permute-start.30 = (bf16[32,1024]{1,0:T(8,128)(2,1)S(1)}, bf16[32,1024]{1,0:T(8,128)(2,1)S(1)}, u32[]{:S(2)}, u32[]{:S(2)}) collective-permute-start(bf16[32,1024]{1,0:T(8,128)(2,1)S(1)} %get-tuple-element.66), channel_id=1, source_target_pairs={{0,4},{1,5},{2,6},{3,7},{4,0},{5,1},{6,2},{7,3},{8,12},{9,13},{10,... | collective-permute-start | bytes 196616 | tf_op jit(solution)/shard_map/ppermute | solution.py:223
  62.6 9.1 %collective-permute-start.31 = (bf16[32,1024]{1,0:T(8,128)(2,1)S(1)}, bf16[32,1024]{1,0:T(8,128)(2,1)S(1)}, u32[]{:S(2)}, u32[]{:S(2)}) collective-permute-start(bf16[32,1024]{1,0:T(8,128)(2,1)S(1)} %get-tuple-element.67), channel_id=1, source_target_pairs={{0,10},{1,11},{2,8},{3,9},{4,14},{5,15},{6,12},{7,13},{8,2},{9,3},... | collective-permute-start | bytes 196616 | tf_op jit(solution)/shard_map/ppermute | solution.py:223
  65.0 7.3 %collective-permute-start.32 = (bf16[32,1024]{1,0:T(8,128)(2,1)S(1)}, bf16[32,1024]{1,0:T(8,128)(2,1)S(1)}, u32[]{:S(2)}, u32[]{:S(2)}) collective-permute-start(bf16[32,1024]{1,0:T(8,128)(2,1)S(1)} %get-tuple-element.68), channel_id=1, source_target_pairs={{0,8},{1,9},{2,10},{3,11},{4,12},{5,13},{6,14},{7,15},{8,0},{9,1},... | collective-permute-start | bytes 196616 | tf_op jit(solution)/shard_map/ppermute | solution.py:223
  (13 other events, 90.7 us)
